TPU v7x, 32 devices: a whole 2x2x4 slice. The times are simulated.
32 devices in a mesh: worker: 2 (over core), fsdp: 16 (over z, y, x).
Axes of the slice: x: 2, y: 2, z: 4, core: 2. Of those that a mesh axis runs over, the one named last changes fastest.
Arguments:
- features: bfloat16 [6144, 8192], P(('worker', 'fsdp')), may hold values from -6 to 6
- value_cotangent: bfloat16 [6144, 512], P(('worker', 'fsdp')), may hold values from -6 to 6
- value_weight: float32 [2, 8192, 512], P('worker', 'fsdp'), may hold values from -0.25 to 0.25
- first_moment: float32 [2, 8192, 512], P('worker', 'fsdp'), may hold values from -48 to 48
- second_moment: float32 [2, 8192, 512], P('worker', 'fsdp'), may hold values from 1000 to 10000
- fragment_local: float32 [2, 8192, 512], P('worker', 'fsdp'), may hold values from -6 to 6
- fragment_anchor: float32 [8192, 512], P('fsdp'), may hold values from -6 to 6
- outer_momentum: float32 [8192, 512], P('fsdp'), may hold values from -3 to 3
Outputs:
- feature_grad: float32 [6144, 8192], P(('worker', 'fsdp'))
- new_weight: float32 [2, 8192, 512], P('worker', 'fsdp')
- new_first: float32 [2, 8192, 512], P('worker', 'fsdp')
- new_second: float32 [2, 8192, 512], P('worker', 'fsdp')
- new_anchor: float32 [8192, 512], P('fsdp')
- new_momentum: float32 [8192, 512], P('fsdp')
All inputs are finite; a program needn't handle non-finite values.
Results may differ from a plain program's by a relative error of at most 0.0003.
Values may be sent and summed in bfloat16 or wider, within the bound.
No kernel may reach another device: no remote copies, remote signals or barrier semaphores. Data moves between devices by JAX's collectives and lax.ppermute only.
A program may use at most 128 MiB of HBM per device.

v0:
```python
import jax
import jax.numpy as jnp
from jax import lax
from jax.sharding import PartitionSpec as P

first_decay = 0.9
second_decay = 0.95
inner_rate = 0.001
weight_decay = 0.1
adam_epsilon = 1e-08
adam_count = 10.0
outer_rate = 0.7
outer_mass = 0.9


def on_device(
    features,
    value_cotangent,
    value_weight,
    first_moment,
    second_moment,
    fragment_local,
    fragment_anchor,
    outer_momentum,
):
    weight = value_weight[0]
    wide_cot = value_cotangent.astype(jnp.float32)
    feature_grad = jnp.dot(
        wide_cot,
        lax.all_gather(weight, "fsdp", axis=0, tiled=True).T,
        preferred_element_type=jnp.float32,
        precision=lax.Precision.HIGHEST,
    )
    gradient = lax.psum_scatter(
        lax.dot_general(
            features, value_cotangent, (((0,), (0,)), ((), ())), preferred_element_type=jnp.float32
        ),
        "fsdp",
        scatter_dimension=0,
        tiled=True,
    )
    first_new = first_decay * first_moment[0] + (1.0 - first_decay) * gradient
    second_new = second_decay * second_moment[0] + (1.0 - second_decay) * gradient * gradient
    first_hat = first_new / (1.0 - first_decay**adam_count)
    second_hat = second_new / (1.0 - second_decay**adam_count)
    weight_new = weight - inner_rate * (
        first_hat / (jnp.sqrt(second_hat) + adam_epsilon) + weight_decay * weight
    )
    workers = lax.axis_size("worker")
    pseudo_sum = lax.psum(fragment_anchor - fragment_local[0], "worker")
    pseudo_mean = pseudo_sum / workers
    new_momentum = outer_mass * outer_momentum + pseudo_mean
    new_anchor = fragment_anchor - outer_rate * (pseudo_mean + outer_mass * new_momentum)
    return (
        feature_grad,
        weight_new[None],
        first_new[None],
        second_new[None],
        new_anchor,
        new_momentum,
    )


def solution(mesh):
    placed = (
        P(("worker", "fsdp"), None),
        P(("worker", "fsdp"), None),
        P("worker", "fsdp", None),
        P("worker", "fsdp", None),
        P("worker", "fsdp", None),
        P("worker", "fsdp", None),
        P("fsdp", None),
        P("fsdp", None),
    )
    return jax.shard_map(
        on_device,
        mesh=mesh,
        in_specs=placed,
        out_specs=(
            P(("worker", "fsdp"), None),
            P("worker", "fsdp", None),
            P("worker", "fsdp", None),
            P("worker", "fsdp", None),
            P("fsdp", None),
            P("fsdp", None),
        ),
        check_vma=False,
    )
```

profile of v0, /device:TPU:0, one launch (start us, length us, event | category | flops | bytes accessed | tf_op | source)
XLA Modules:
  0.0 566.8 jit_solution(4783569768732979765)
XLA Ops:
  8.0 0.0 copy-start
  8.0 0.0 all-reduce.2.cloned.1.call-start
  8.1 2.9 bitcast_subtract_fusion
  10.9 0.0 all-reduce.2.cloned.1.call-update
  11.0 0.0 all-gather.3.cloned.1.call-start
  11.0 0.5 all-gather.3.cloned.1.call-update
  11.5 0.0 copy-start.1
  11.5 0.0 reduce-scatter.2.cloned.1.call-start
  11.6 0.0 copy-done
  11.6 9.2 %fusion.8 = f32[8192,512]{1,0:T(8,128)} fusion(bf16[192,8192]{1,0:T(8,128)(2,1)S(1)} %copy-done, bf16[192,512]{1,0:T(8,128)(2,1)} %param.9), kind=kOutput, calls=%fused_computation.15 | convolution fusion | flops 1610612736 | bytes 20119552 | tf_op jit(solution)/shard_map/dot_general | solution.py:35
  20.8 0.0 reduce-scatter.2.cloned.1.call-update
  20.9 13.2 %all-reduce.2.cloned.1.call-done = f32[512,512]{1,0:T(8,128)} async-done(((f32[512,512]{1,0:T(8,128)}), f32[512,512]{1,0:T(8,128)}) %all-reduce.2.cloned.1.call-update) | async-done | bytes 1048592 | tf_op jit(solution)/shard_map/psum | solution.py:50
  34.1 3.6 multiply_subtract_fusion
  37.7 170.4 %all-gather.3.cloned.1.call-done = f32[1,8192,512]{2,1,0:T(8,128)} async-done(((f32[1,512,512]{2,1,0:T(8,128)}), f32[1,8192,512]{2,1,0:T(8,128)}) %all-gather.3.cloned.1.call-update) | async-done | bytes 16777232 | tf_op jit(solution)/shard_map/all_gather | solution.py:30
  208.1 0.0 copy-done.1
  208.1 16.2 %fusion = f32[192,8192]{1,0:T(8,128)} fusion(bf16[192,512]{1,0:T(8,128)(2,1)S(1)} %copy-done.1, f32[1,8192,512]{2,1,0:T(8,128)} %all-gather.3.cloned.1.call-done), kind=kOutput, calls=%fused_computation | convolution fusion | flops 9663676416 | bytes 23265280 | tf_op jit(solution)/shard_map/dot_general | solution.py:28
  224.3 330.5 %reduce-scatter.2.cloned.1.call-done = f32[512,512]{1,0:T(8,128)} async-done(((f32[8192,512]{1,0:T(8,128)}), f32[512,512]{1,0:T(8,128)}) %reduce-scatter.2.cloned.1.call-update) | async-done | bytes 1048592 | tf_op jit(solution)/shard_map/reduce_scatter | solution.py:34
  554.8 4.6 fusion.7
Async XLA Ops:
  8.0 3.6 copy-start
  8.0 26.1 %all-reduce.2.cloned.1.call-start = ((), (), s32[]{:S(2)}) async-start(), calls=%async_computation.2 | async-start | bytes 2097152 | tf_op jit(solution)/shard_map/psum | solution.py:50
  11.0 197.1 %all-gather.3.cloned.1.call-start = ((), (), s32[]{:S(2)}) async-start(), calls=%async_computation.3 | async-start | bytes 17825792 | tf_op jit(solution)/shard_map/all_gather | solution.py:30
  11.5 196.6 %copy-start.1 = (bf16[192,512]{1,0:T(8,128)(2,1)S(1)}, bf16[192,512]{1,0:T(8,128)(2,1)}, u32[]{:S(2)}) copy-start(bf16[192,512]{1,0:T(8,128)(2,1)} %param.9) | copy-start | bytes 589828
  11.5 543.2 %reduce-scatter.2.cloned.1.call-start = ((), (), s32[]{:S(2)}) async-start(), calls=%async_computation.1 | async-start | bytes 17825792 | tf_op jit(solution)/shard_map/reduce_scatter | solution.py:34
Sparse Core Ops, SparseCore 0:
  11.8 22.2 all-reduce.1
Sparse Core Ops, SparseCore 1:
  14.2 193.8 all-gather.2
  210.3 344.4 reduce-scatter.1
where the time goes:
time: 571 us; the launch traced here: 567 us
  waiting for transfers between devices  515 us (90%)
  matrix products  25.4 us (4%)
  between operations  15.5 us (3%)
  other arithmetic  11.1 us (2%)
    reduce_scatter x1, waiting for transfers between devices, on_device(): lax.psum_scatter(lax.dot_general(features, value_cotangent, (((0,), (0,))...  330 us
    all_gather x1, waiting for transfers between devices, on_device(): lax.all_gather(weight, 'fsdp', axis=0, tiled=True)  170 us
    dot_general x1, matrix products, on_device(): jnp.dot(wide_cot, lax.all_gather(weight, 'fsdp', axis=0, tiled=True).T, p...  16.2 us
    psum x1, waiting for transfers between devices, on_device(): pseudo_sum = lax.psum(fragment_anchor - fragment_local[0], 'worker')  13.2 us
  transfers between devices with their start and end apart: 3, of which 3 were waited for; matrix products, arithmetic and copies ran while one was open for 5% of the time, Pallas kernels for 0%

commit v1 on v0

--- a/solution.py
+++ b/solution.py
@@ -1,6 +1,10 @@
+import functools
+
 import jax
 import jax.numpy as jnp
 from jax import lax
+from jax.experimental import pallas as pl
+from jax.experimental.pallas import tpu as pltpu
 from jax.sharding import PartitionSpec as P
 
 first_decay = 0.9
@@ -11,6 +15,162 @@
 adam_count = 10.0
 outer_rate = 0.7
 outer_mass = 0.9
+
+PLANE = 4
+WEIGHT_SCALE = 2.0**17
+WIRE = jnp.bfloat16
+
+
+def power_below(limit):
+    scale = 1.0
+    while scale * limit > 32768.0:
+        scale /= 2.0
+    while scale * limit < 16384.0:
+        scale *= 2.0
+    return scale
+
+
+def encode(x):
+    power = x * x
+    power = power * power
+    power = power * power
+    return jnp.where(x < 0.0, -power, power).astype(WIRE)
+
+
+def decode(code):
+    wide = code.astype(jnp.float32)
+    size = jnp.abs(wide)
+    root = jnp.where(size > 0.0, jnp.exp(jnp.log(size) * 0.125), 0.0)
+    return jnp.where(wide < 0.0, -root, root)
+
+
+def vmem(count):
+    return [pl.BlockSpec(memory_space=pltpu.VMEM)] * count
+
+
+def contract(left, right, dims):
+    return lax.dot_general(left, right, (dims, ((), ())), preferred_element_type=jnp.float32)
+
+
+def pack_kernel(columns, planes, axis, features, weight, coded, *outs_and_sem):
+    outs, sem = outs_and_sem[:-1], outs_and_sem[-1]
+    me = lax.axis_index(axis)
+    z, p = me // PLANE, me % PLANE
+    copies = []
+    for at in range(planes):
+        block = lax.rem(z + 2 * planes - 1 - at, planes)
+        for k in range(PLANE):
+            start = pl.multiple_of((block * PLANE + (p ^ k)) * columns, 128)
+            copy = pltpu.make_async_copy(
+                features.at[:, pl.ds(start, columns)], outs[at * PLANE + k], sem.at[at * PLANE + k]
+            )
+            copy.start()
+            copies.append(copy)
+    coded[...] = encode(weight[...] * WEIGHT_SCALE)
+    for copy in copies:
+        copy.wait()
+
+
+def pack(features, weight, columns, planes):
+    rows = features.shape[0]
+    count = planes * PLANE
+    coded, *outs = pl.pallas_call(
+        functools.partial(pack_kernel, columns, planes, "fsdp"),
+        out_shape=[jax.ShapeDtypeStruct(weight.shape, WIRE)]
+        + [jax.ShapeDtypeStruct((rows, columns), features.dtype)] * count,
+        in_specs=[pl.BlockSpec(memory_space=pl.ANY), *vmem(1)],
+        out_specs=vmem(1) + [pl.BlockSpec(memory_space=pl.ANY)] * count,
+        scratch_shapes=[pltpu.SemaphoreType.DMA((count,))],
+        name="pack",
+    )(features, weight)
+    return coded, [outs[at * PLANE : (at + 1) * PLANE] for at in range(planes)]
+
+
+def partial_kernel(scale, *refs):
+    parts, cots, so_far, out = refs[:PLANE], refs[PLANE : 2 * PLANE], refs[2 * PLANE : -1], refs[-1]
+    total = contract(parts[0][...], cots[0][...], ((0,), (0,)))
+    for part, cot in zip(parts[1:], cots[1:]):
+        total += contract(part[...], cot[...], ((0,), (0,)))
+    total = total * scale
+    for ref in so_far:
+        total += decode(ref[...])
+    out[...] = encode(total) if out.dtype == WIRE else total
+
+
+def plane_partial(parts, cots, so_far, scale, dtype):
+    shape = (parts[0].shape[1], cots[0].shape[1])
+    operands = [*parts, *cots, *so_far]
+    return pl.pallas_call(
+        functools.partial(partial_kernel, scale),
+        out_shape=jax.ShapeDtypeStruct(shape, dtype),
+        in_specs=vmem(len(operands)),
+        out_specs=pl.BlockSpec(memory_space=pltpu.VMEM),
+        compiler_params=pltpu.CompilerParams(vmem_limit_bytes=24 << 20),
+        name="plane_partial",
+    )(*operands)
+
+
+def product_kernel(factor, scale, *refs):
+    weight, cots, outs = refs[0], refs[1 : 1 + PLANE], refs[1 + PLANE :]
+    wide = decode(weight[...]) if weight.dtype == WIRE else weight[...]
+    high = wide.astype(jnp.bfloat16)
+    low = (wide - high.astype(jnp.float32)).astype(jnp.bfloat16)
+    for k in range(PLANE):
+        cot = cots[k][...]
+        result = contract(cot, high, ((1,), (1,))) + contract(cot, low, ((1,), (1,)))
+        outs[k][...] = result * factor if k == 0 else encode(result * (factor * scale))
+
+
+def plane_product(weight, cots, factor, scale):
+    shape = (cots[0].shape[0], weight.shape[0])
+    return pl.pallas_call(
+        functools.partial(product_kernel, factor, scale),
+        out_shape=[jax.ShapeDtypeStruct(shape, jnp.float32 if k == 0 else WIRE) for k in range(PLANE)],
+        in_specs=vmem(1 + PLANE),
+        out_specs=vmem(PLANE),
+        compiler_params=pltpu.CompilerParams(vmem_limit_bytes=24 << 20),
+        name="plane_product",
+    )(weight, *cots)
+
+
+def unpack_kernel(columns, planes, axis, factor, *refs):
+    count = planes * PLANE
+    pieces, out, buffer, sem = refs[:count], refs[count], refs[count + 1], refs[count + 2]
+    me = lax.axis_index(axis)
+    z, p = me // PLANE, me % PLANE
+    copies = []
+    for at in range(planes):
+        block = lax.rem(z + planes - at, planes)
+        for k in range(PLANE):
+            i = at * PLANE + k
+            if k == 0:
+                source = pieces[i]
+            else:
+                buffer[i] = decode(pieces[i][...]) * factor
+                source = buffer.at[i]
+            start = pl.multiple_of((block * PLANE + (p ^ k)) * columns, 128)
+            copy = pltpu.make_async_copy(source, out.at[:, pl.ds(start, columns)], sem.at[i])
+            copy.start()
+            copies.append(copy)
+    for copy in copies:
+        copy.wait()
+
+
+def unpack(pieces, planes, factor):
+    rows, columns = pieces[0].shape
+    count = planes * PLANE
+    return pl.pallas_call(
+        functools.partial(unpack_kernel, columns, planes, "fsdp", factor),
+        out_shape=jax.ShapeDtypeStruct((rows, columns * count), jnp.float32),
+        in_specs=vmem(count),
+        out_specs=pl.BlockSpec(memory_space=pl.ANY),
+        scratch_shapes=[
+            pltpu.VMEM((count, rows, columns), jnp.float32),
+            pltpu.SemaphoreType.DMA((count,)),
+        ],
+        compiler_params=pltpu.CompilerParams(vmem_limit_bytes=40 << 20),
+        name="unpack",
+    )(*pieces)
 
 
 def on_device(
@@ -23,22 +183,44 @@
     fragment_anchor,
     outer_momentum,
 ):
+    size = lax.axis_size("fsdp")
+    planes = size // PLANE
+    columns = features.shape[1] // size
+    tokens = features.shape[0] * size
+    gradient_scale = power_below(tokens * 24.0 * 6.0)
+    product_scale = power_below(value_cotangent.shape[1] * 6.0 * 0.25)
+
+    ring = [(i, (i + PLANE) % size) for i in range(size)]
+
+    def around(x):
+        return lax.ppermute(x, "fsdp", ring)
+
+    def across(x, k):
+        return lax.ppermute(x, "fsdp", [(i, i ^ k) for i in range(size)])
+
     weight = value_weight[0]
-    wide_cot = value_cotangent.astype(jnp.float32)
-    feature_grad = jnp.dot(
-        wide_cot,
-        lax.all_gather(weight, "fsdp", axis=0, tiled=True).T,
-        preferred_element_type=jnp.float32,
-        precision=lax.Precision.HIGHEST,
-    )
-    gradient = lax.psum_scatter(
-        lax.dot_general(
-            features, value_cotangent, (((0,), (0,)), ((), ())), preferred_element_type=jnp.float32
-        ),
-        "fsdp",
-        scatter_dimension=0,
-        tiled=True,
-    )
+    cots = [value_cotangent] + [across(value_cotangent, k) for k in range(1, PLANE)]
+    travelling, packed = pack(features, weight, columns, planes)
+    weights = [weight]
+    for _ in range(1, planes):
+        travelling = around(travelling)
+        weights.append(travelling)
+
+    received = [[part if k == 0 else across(part, k) for k, part in enumerate(parts)] for parts in packed]
+
+    pieces = []
+    for held in weights:
+        products = plane_product(held, cots, 1.0 if held is weight else 1.0 / WEIGHT_SCALE, product_scale)
+        pieces += [part if k == 0 else across(part, k) for k, part in enumerate(products)]
+    feature_grad = unpack(pieces, planes, 1.0 / product_scale)
+
+    running = []
+    for at, parts in enumerate(received):
+        last = at == planes - 1
+        total = plane_partial(parts, cots, running, gradient_scale, jnp.float32 if last else WIRE)
+        running = [total if last else around(total)]
+    gradient = running[0] * (1.0 / gradient_scale)
+
     first_new = first_decay * first_moment[0] + (1.0 - first_decay) * gradient
     second_new = second_decay * second_moment[0] + (1.0 - second_decay) * gradient * gradient
     first_hat = first_new / (1.0 - first_decay**adam_count)
@@ -47,7 +229,11 @@
         first_hat / (jnp.sqrt(second_hat) + adam_epsilon) + weight_decay * weight
     )
     workers = lax.axis_size("worker")
-    pseudo_sum = lax.psum(fragment_anchor - fragment_local[0], "worker")
+    difference = fragment_anchor - fragment_local[0]
+    if workers == 2:
+        pseudo_sum = difference + lax.ppermute(difference, "worker", [(0, 1), (1, 0)])
+    else:
+        pseudo_sum = lax.psum(difference, "worker")
     pseudo_mean = pseudo_sum / workers
     new_momentum = outer_mass * outer_momentum + pseudo_mean
     new_anchor = fragment_anchor - outer_rate * (pseudo_mean + outer_mass * new_momentum)

time: 571 us -> 215 us (0.38)
  waiting for transfers between devices: 515 us -> 50.6 us
  Pallas kernels: 0 us -> 113 us
  starting transfers between devices: 0.12 us -> 41.9 us
  matrix products: 25.4 us -> 0 us
  between operations: 15.5 us -> 1.05 us
  other arithmetic: 11.1 us -> 4.55 us
    reduce_scatter x1 -> x0, waiting for transfers between devices: 330 us -> none  [on_device(): lax.psum_scatter(lax.dot_general(features, value_cotangent, (((0,), (0,))...]
    all_gather x1 -> x0, waiting for transfers between devices: 170 us -> none  [on_device(): lax.all_gather(weight, 'fsdp', axis=0, tiled=True)]
    pallas_call x0 -> x10, Pallas kernels: none -> 113 us  [the longest x1 98.7 us: pack(): pl.pallas_call(functools.partial(pack_kernel, columns, planes, 'fsdp'), o...]
    ppermute x0 -> x34, waiting for transfers between devices: none -> 50.6 us  [the longest x27 40.8 us: across(): return lax.ppermute(x, 'fsdp', [(i, i ^ k) for i in range(size)])]
    ppermute x0 -> x34, starting transfers between devices: none -> 41.9 us  [the longest x27 35 us: across(): return lax.ppermute(x, 'fsdp', [(i, i ^ k) for i in range(size)])]
    dot_general x2 -> x0, matrix products: 25.4 us -> none  [the longest x1 16.2 us: on_device(): jnp.dot(wide_cot, lax.all_gather(weight, 'fsdp', axis=0, tiled=True).T, p...]
    psum x1 -> x0, waiting for transfers between devices: 13.2 us -> none  [on_device(): pseudo_sum = lax.psum(fragment_anchor - fragment_local[0], 'worker')]
  transfers between devices with their start and end apart: 3 -> 34, of which waited for: 3 -> 18; matrix products, arithmetic and copies ran while one was open for 5% -> 2% of each run, Pallas kernels for 0% -> 6%
where the time goes in v1:
time: 215 us; the launch traced here: 214 us
  Pallas kernels  113 us (53%)
  waiting for transfers between devices  50.6 us (24%)
  starting transfers between devices  41.9 us (19%)
  other arithmetic  4.55 us (2%)
  local copies, waits for them, and re-layouts  2.85 us (1%)
    pallas_call x1, Pallas kernels, pack(): pl.pallas_call(functools.partial(pack_kernel, columns, planes, 'fsdp'), o...  98.7 us
    ppermute x27, waiting for transfers between devices, across(): return lax.ppermute(x, 'fsdp', [(i, i ^ k) for i in range(size)])  40.8 us
    ppermute x27, starting transfers between devices, across(): return lax.ppermute(x, 'fsdp', [(i, i ^ k) for i in range(size)])  35 us
    ppermute x6, waiting for transfers between devices, around(): return lax.ppermute(x, 'fsdp', ring)  9.83 us
    pallas_call x4, Pallas kernels, plane_product(): pl.pallas_call(functools.partial(product_kernel, factor, scale), out_shap...  7.37 us
    ppermute x6, starting transfers between devices, around(): return lax.ppermute(x, 'fsdp', ring)  6.93 us
    pallas_call x4, Pallas kernels, plane_partial(): pl.pallas_call(functools.partial(partial_kernel, scale), out_shape=jax.Sh...  4.45 us
  transfers between devices with their start and end apart: 34, of which 18 were waited for; matrix products, arithmetic and copies ran while one was open for 2% of the time, Pallas kernels for 6%

profile of v1, /device:TPU:0, one launch (start us, length us, event | category | flops | bytes accessed | tf_op | source)
XLA Modules:
  0.0 214.4 jit_solution(4542028754356526776)
XLA Ops:
  0.7 98.7 %pack.1 = (bf16[512,512]{1,0:T(8,128)(2,1)}, bf16[192,512]{1,0:T(8,128)(2,1)}, bf16[192,512]{1,0:T(8,128)(2,1)}, bf16[192,512]{1,0:T(8,128)(2,1)}, bf16[192,512]...) custom-call(bf16[192,8192]{1,0:T(8,128)(2,1)} %features.1, ...), custom_call_target="tpu_custom_call" | custom-call | tf_op jit(solution)/shard_map/pack/pallas_call | solution.py:77
  99.4 3.0 %collective-permute-start.27 = (bf16[192,512]{1,0:T(8,128)(2,1)}, bf16[192,512]{1,0:T(8,128)(2,1)S(1)}, u32[]{:S(2)}, u32[]{:S(2)}) collective-permute-start(bf16[192,512]{1,0:T(8,128)(2,1)} %get-tuple-element.69), channel_id=1, source_target_pairs={{0,1},{1,0},{2,3},{3,2},{4,5},{5,4},{6,7},{7,6},{8,9},{9,8},{10,11... | collective-permute-start | bytes 589832 | tf_op jit(solution)/shard_map/ppermute | solution.py:199
  102.4 1.5 collective-permute-start.28
  103.9 1.9 collective-permute-start
  105.9 1.5 collective-permute-start.1
  108.3 3.0 %collective-permute-start.2 = (bf16[192,512]{1,0:T(8,128)(2,1)}, bf16[192,512]{1,0:T(8,128)(2,1)S(1)}, u32[]{:S(2)}, u32[]{:S(2)}) collective-permute-start(bf16[192,512]{1,0:T(8,128)(2,1)} %refs_4_.7), channel_id=1, source_target_pairs={{0,3},{1,2},{2,1},{3,0},{4,7},{5,6},{6,5},{7,4},{8,11},{9,10},{10,... | collective-permute-start | bytes 589832 | tf_op jit(solution)/shard_map/ppermute | solution.py:199
  111.4 3.3 %collective-permute-done.28.refs_2_ = bf16[192,512]{1,0:T(8,128)(2,1)S(1)} collective-permute-done((bf16[192,512]{1,0:T(8,128)(2,1)}, bf16[192,512]{1,0:T(8,128)(2,1)S(1)}, u32[]{:S(2)}, u32[]{:S(2)}) %collective-permute-start.28) | collective-permute-done | bytes 196640 | tf_op jit(solution)/shard_map/ppermute | solution.py:199
  114.7 1.6 collective-permute-start.6
  116.8 4.8 %collective-permute-done.1.refs_3_.refs_6_ = bf16[192,512]{1,0:T(8,128)(2,1)S(1)} collective-permute-done((bf16[192,512]{1,0:T(8,128)(2,1)}, bf16[192,512]{1,0:T(8,128)(2,1)S(1)}, u32[]{:S(2)}, u32[]{:S(2)}) %collective-permute-start.1) | collective-permute-done | bytes 196640 | tf_op jit(solution)/shard_map/ppermute | solution.py:199
  124.4 1.6 collective-permute-start.30
  129.7 4.2 %collective-permute-done.24.refs_1_ = bf16[192,512]{1,0:T(8,128)(2,1)S(1)} collective-permute-done((bf16[192,512]{1,0:T(8,128)(2,1)}, bf16[192,512]{1,0:T(8,128)(2,1)S(1)}, u32[]{:S(2)}, u32[]{:S(2)}) %collective-permute-start.24) | collective-permute-done | bytes 196640 | tf_op jit(solution)/shard_map/ppermute | solution.py:199
  133.9 1.6 collective-permute-start.10
  136.9 2.0 collective-permute-done.30.refs_8_
  141.3 1.8 collective-permute-start.21
  143.6 3.6 %collective-permute-done.21.refs_1_ = bf16[192,512]{1,0:T(8,128)(2,1)S(1)} collective-permute-done((bf16[192,512]{1,0:T(8,128)(2,1)S(1)}, bf16[192,512]{1,0:T(8,128)(2,1)S(1)}, u32[]{:S(2)}, u32[]{:S(2)}) %collective-permute-start.21) | collective-permute-done | bytes 196640 | tf_op jit(solution)/shard_map/ppermute | solution.py:199
  148.7 2.1 collective-permute-done.22.refs_2_
  150.8 1.9 collective-permute-start.14
  154.0 7.8 %collective-permute-done.31.refs_8_ = bf16[512,512]{1,0:T(8,128)(2,1)S(1)} collective-permute-done((bf16[512,512]{1,0:T(8,128)(2,1)S(1)}, bf16[512,512]{1,0:T(8,128)(2,1)S(1)}, u32[]{:S(2)}, u32[]{:S(2)}) %collective-permute-start.31) | collective-permute-done | bytes 524320 | tf_op jit(solution)/shard_map/ppermute | solution.py:196
  163.9 2.3 %collective-permute-start.20 = (bf16[192,512]{1,0:T(8,128)(2,1)S(1)}, bf16[192,512]{1,0:T(8,128)(2,1)S(1)}, u32[]{:S(2)}, u32[]{:S(2)}) collective-permute-start(bf16[192,512]{1,0:T(8,128)(2,1)S(1)} %copy-done.12), channel_id=1, source_target_pairs={{0,3},{1,2},{2,1},{3,0},{4,7},{5,6},{6,5},{7,4},{8,11},{9,10},{10,... | collective-permute-start | bytes 589832 | tf_op jit(solution)/shard_map/ppermute | solution.py:199
  166.2 1.6 plane_product.4
  167.8 6.0 %collective-permute-done.19.refs_2_ = bf16[192,512]{1,0:T(8,128)(2,1)S(1)} collective-permute-done((bf16[192,512]{1,0:T(8,128)(2,1)S(1)}, bf16[192,512]{1,0:T(8,128)(2,1)S(1)}, u32[]{:S(2)}, u32[]{:S(2)}) %collective-permute-start.19) | collective-permute-done | bytes 196640 | tf_op jit(solution)/shard_map/ppermute | solution.py:199
  175.9 1.9 plane_product.5
  177.8 1.9 plane_product.6
  179.8 1.5 collective-permute-start.5
  186.3 1.9 multiply_subtract_fusion
  188.2 1.9 plane_product.7
  194.9 2.3 %collective-permute-done.9.refs_7_ = bf16[192,512]{1,0:T(8,128)(2,1)S(1)} collective-permute-done((bf16[192,512]{1,0:T(8,128)(2,1)S(1)}, bf16[192,512]{1,0:T(8,128)(2,1)S(1)}, u32[]{:S(2)}, u32[]{:S(2)}) %collective-permute-start.9) | collective-permute-done | bytes 196640 | tf_op jit(solution)/shard_map/ppermute | solution.py:199
  198.6 2.7 %collective-permute-done.11.refs_9_ = bf16[192,512]{1,0:T(8,128)(2,1)S(1)} collective-permute-done((bf16[192,512]{1,0:T(8,128)(2,1)S(1)}, bf16[192,512]{1,0:T(8,128)(2,1)S(1)}, u32[]{:S(2)}, u32[]{:S(2)}) %collective-permute-start.11) | collective-permute-done | bytes 196640 | tf_op jit(solution)/shard_map/ppermute | solution.py:199
  202.4 2.5 %fusion.1 = (f32[1,512,512]{2,1,0:T(8,128)}, f32[1,512,512]{2,1,0:T(8,128)}, f32[1,512,512]{2,1,0:T(8,128)}) fusion(f32[512,512]{1,0:T(8,128)S(1)} %plane_partial.7, f32[1,512,512]{2,1,0:T(8,128)S(1)} %copy-done.9, f32[1,512,512]{2,1,0:T(8,128)S(1)} %copy-done.10, f32[1,512,512]{2,1,0:T(8,128)S(1)} %copy-done.2), kind=kLoop, calls=%fused_computation.8 | loop fusion | flops 4194304 | bytes 7340032 | tf_op jit(solution)/shard_map/broadcast_in_dim | solution.py:244
  205.6 3.5 %collective-permute-done.15.refs_13_ = bf16[192,512]{1,0:T(8,128)(2,1)S(1)} collective-permute-done((bf16[192,512]{1,0:T(8,128)(2,1)S(1)}, bf16[192,512]{1,0:T(8,128)(2,1)S(1)}, u32[]{:S(2)}, u32[]{:S(2)}) %collective-permute-start.15) | collective-permute-done | bytes 196640 | tf_op jit(solution)/shard_map/ppermute | solution.py:199
  209.1 2.3 %collective-permute-done.16.refs_14_ = bf16[192,512]{1,0:T(8,128)(2,1)S(1)} collective-permute-done((bf16[192,512]{1,0:T(8,128)(2,1)S(1)}, bf16[192,512]{1,0:T(8,128)(2,1)S(1)}, u32[]{:S(2)}, u32[]{:S(2)}) %collective-permute-start.16) | collective-permute-done | bytes 196640 | tf_op jit(solution)/shard_map/ppermute | solution.py:199
  211.4 2.9 %unpack.1 = f32[192,8192]{1,0:T(8,128)} custom-call(f32[192,512]{1,0:T(8,128)S(1)} %get-tuple-element.39.refs_0_, bf16[192,512]{1,0:T(8,128)(2,1)S(1)} %collective-permute-done.3.refs_1_, bf16[192,512]{1,0:T(8,128)(2,1)S(1)} %collective-permute-done.4.refs_2_, bf16[192,512]{1,0:T(8,128)(2,1)S(1)} %collective-permute-done.5.refs_3_, ...), custom_call_target="tpu_custom_call" | custom-call | tf_op jit(solution)/shard_map/unpack/pallas_call | solution.py:162
  (85 shorter events, 32.2 us)
Async XLA Ops:
  99.4 8.9 %collective-permute-start.27 = (bf16[192,512]{1,0:T(8,128)(2,1)}, bf16[192,512]{1,0:T(8,128)(2,1)S(1)}, u32[]{:S(2)}, u32[]{:S(2)}) collective-permute-start(bf16[192,512]{1,0:T(8,128)(2,1)} %get-tuple-element.69), channel_id=1, source_target_pairs={{0,1},{1,0},{2,3},{3,2},{4,5},{5,4},{6,7},{7,6},{8,9},{9,8},{10,11... | collective-permute-start | bytes 589832 | tf_op jit(solution)/shard_map/ppermute | solution.py:199
  102.4 12.2 %collective-permute-start.28 = (bf16[192,512]{1,0:T(8,128)(2,1)}, bf16[192,512]{1,0:T(8,128)(2,1)S(1)}, u32[]{:S(2)}, u32[]{:S(2)}) collective-permute-start(bf16[192,512]{1,0:T(8,128)(2,1)} %get-tuple-element.70), channel_id=1, source_target_pairs={{0,2},{1,3},{2,0},{3,1},{4,6},{5,7},{6,4},{7,5},{8,10},{9,11},{10,... | collective-permute-start | bytes 589832 | tf_op jit(solution)/shard_map/ppermute | solution.py:199
  103.9 12.3 %collective-permute-start.29 = (bf16[192,512]{1,0:T(8,128)(2,1)}, bf16[192,512]{1,0:T(8,128)(2,1)S(1)}, u32[]{:S(2)}, u32[]{:S(2)}) collective-permute-start(bf16[192,512]{1,0:T(8,128)(2,1)} %get-tuple-element.71), channel_id=1, source_target_pairs={{0,3},{1,2},{2,1},{3,0},{4,7},{5,6},{6,5},{7,4},{8,11},{9,10},{10,... | collective-permute-start | bytes 589832 | tf_op jit(solution)/shard_map/ppermute | solution.py:199
  103.9 12.9 %collective-permute-start = (bf16[192,512]{1,0:T(8,128)(2,1)}, bf16[192,512]{1,0:T(8,128)(2,1)S(1)}, u32[]{:S(2)}, u32[]{:S(2)}) collective-permute-start(bf16[192,512]{1,0:T(8,128)(2,1)} %refs_4_.7), channel_id=1, source_target_pairs={{0,1},{1,0},{2,3},{3,2},{4,5},{5,4},{6,7},{7,6},{8,9},{9,8},{10,11... | collective-permute-start | bytes 589832 | tf_op jit(solution)/shard_map/ppermute | solution.py:199
  105.9 15.7 %collective-permute-start.1 = (bf16[192,512]{1,0:T(8,128)(2,1)}, bf16[192,512]{1,0:T(8,128)(2,1)S(1)}, u32[]{:S(2)}, u32[]{:S(2)}) collective-permute-start(bf16[192,512]{1,0:T(8,128)(2,1)} %refs_4_.7), channel_id=1, source_target_pairs={{0,2},{1,3},{2,0},{3,1},{4,6},{5,7},{6,4},{7,5},{8,10},{9,11},{10,... | collective-permute-start | bytes 589832 | tf_op jit(solution)/shard_map/ppermute | solution.py:199
  108.3 13.3 %collective-permute-start.2 = (bf16[192,512]{1,0:T(8,128)(2,1)}, bf16[192,512]{1,0:T(8,128)(2,1)S(1)}, u32[]{:S(2)}, u32[]{:S(2)}) collective-permute-start(bf16[192,512]{1,0:T(8,128)(2,1)} %refs_4_.7), channel_id=1, source_target_pairs={{0,3},{1,2},{2,1},{3,0},{4,7},{5,6},{6,5},{7,4},{8,11},{9,10},{10,... | collective-permute-start | bytes 589832 | tf_op jit(solution)/shard_map/ppermute | solution.py:199
  114.7 19.3 %collective-permute-start.6 = (bf16[512,512]{1,0:T(8,128)(2,1)}, bf16[512,512]{1,0:T(8,128)(2,1)S(1)}, u32[]{:S(2)}, u32[]{:S(2)}) collective-permute-start(bf16[512,512]{1,0:T(8,128)(2,1)} %get-tuple-element.43), channel_id=1, source_target_pairs={{0,4},{1,5},{2,6},{3,7},{4,8},{5,9},{6,10},{7,11},{8,12},{9,13},{1... | collective-permute-start | bytes 1572872 | tf_op jit(solution)/shard_map/ppermute | solution.py:196
  124.4 14.6 %collective-permute-start.30 = (bf16[512,512]{1,0:T(8,128)(2,1)S(1)}, bf16[512,512]{1,0:T(8,128)(2,1)S(1)}, u32[]{:S(2)}, u32[]{:S(2)}) collective-permute-start(bf16[512,512]{1,0:T(8,128)(2,1)S(1)} %plane_partial.4), channel_id=1, source_target_pairs={{0,4},{1,5},{2,6},{3,7},{4,8},{5,9},{6,10},{7,11},{8,12},{9,13},{1... | collective-permute-start | bytes 1572872 | tf_op jit(solution)/shard_map/ppermute | solution.py:196
  126.0 7.9 %collective-permute-start.24 = (bf16[192,512]{1,0:T(8,128)(2,1)}, bf16[192,512]{1,0:T(8,128)(2,1)S(1)}, u32[]{:S(2)}, u32[]{:S(2)}) collective-permute-start(bf16[192,512]{1,0:T(8,128)(2,1)} %get-tuple-element.65), channel_id=1, source_target_pairs={{0,1},{1,0},{2,3},{3,2},{4,5},{5,4},{6,7},{7,6},{8,9},{9,8},{10,11... | collective-permute-start | bytes 589832 | tf_op jit(solution)/shard_map/ppermute | solution.py:199
  127.3 9.6 %collective-permute-start.25 = (bf16[192,512]{1,0:T(8,128)(2,1)}, bf16[192,512]{1,0:T(8,128)(2,1)S(1)}, u32[]{:S(2)}, u32[]{:S(2)}) collective-permute-start(bf16[192,512]{1,0:T(8,128)(2,1)} %get-tuple-element.66), channel_id=1, source_target_pairs={{0,2},{1,3},{2,0},{3,1},{4,6},{5,7},{6,4},{7,5},{8,10},{9,11},{10,... | collective-permute-start | bytes 589832 | tf_op jit(solution)/shard_map/ppermute | solution.py:199
  128.1 8.9 %collective-permute-start.26 = (bf16[192,512]{1,0:T(8,128)(2,1)}, bf16[192,512]{1,0:T(8,128)(2,1)S(1)}, u32[]{:S(2)}, u32[]{:S(2)}) collective-permute-start(bf16[192,512]{1,0:T(8,128)(2,1)} %get-tuple-element.67), channel_id=1, source_target_pairs={{0,3},{1,2},{2,1},{3,0},{4,7},{5,6},{6,5},{7,4},{8,11},{9,10},{10,... | collective-permute-start | bytes 589832 | tf_op jit(solution)/shard_map/ppermute | solution.py:199
  133.9 48.9 %collective-permute-start.33 = (f32[512,512]{1,0:T(8,128)S(1)}, f32[512,512]{1,0:T(8,128)S(1)}, u32[]{:S(2)}, u32[]{:S(2)}) collective-permute-start(f32[512,512]{1,0:T(8,128)S(1)} %bitcast_subtract_fusion), channel_id=1, source_target_pairs={{0,16},{16,0},{1,17},{17,1},{2,18},{18,2},{3,19},{19,3},{4,20},{20... | collective-permute-start | bytes 3145736 | tf_op jit(solution)/shard_map/ppermute | solution.py:234
  133.9 16.9 %collective-permute-start.10 = (bf16[512,512]{1,0:T(8,128)(2,1)S(1)}, bf16[512,512]{1,0:T(8,128)(2,1)S(1)}, u32[]{:S(2)}, u32[]{:S(2)}) collective-permute-start(bf16[512,512]{1,0:T(8,128)(2,1)S(1)} %collective-permute-done.6.refs_0_), channel_id=1, source_target_pairs={{0,4},{1,5},{2,6},{3,7},{4,8},{5,9},{6,10},{7,11},{8,12},{9,13},{1... | collective-permute-start | bytes 1572872 | tf_op jit(solution)/shard_map/ppermute | solution.py:196
  141.2 20.6 %collective-permute-start.31 = (bf16[512,512]{1,0:T(8,128)(2,1)S(1)}, bf16[512,512]{1,0:T(8,128)(2,1)S(1)}, u32[]{:S(2)}, u32[]{:S(2)}) collective-permute-start(bf16[512,512]{1,0:T(8,128)(2,1)S(1)} %plane_partial.5), channel_id=1, source_target_pairs={{0,4},{1,5},{2,6},{3,7},{4,8},{5,9},{6,10},{7,11},{8,12},{9,13},{1... | collective-permute-start | bytes 1572872 | tf_op jit(solution)/shard_map/ppermute | solution.py:196
  143.0 7.8 %collective-permute-start.22 = (bf16[192,512]{1,0:T(8,128)(2,1)S(1)}, bf16[192,512]{1,0:T(8,128)(2,1)S(1)}, u32[]{:S(2)}, u32[]{:S(2)}) collective-permute-start(bf16[192,512]{1,0:T(8,128)(2,1)S(1)} %copy-done.16), channel_id=1, source_target_pairs={{0,2},{1,3},{2,0},{3,1},{4,6},{5,7},{6,4},{7,5},{8,10},{9,11},{10,... | collective-permute-start | bytes 589832 | tf_op jit(solution)/shard_map/ppermute | solution.py:199
  147.2 6.8 %collective-permute-start.23 = (bf16[192,512]{1,0:T(8,128)(2,1)S(1)}, bf16[192,512]{1,0:T(8,128)(2,1)S(1)}, u32[]{:S(2)}, u32[]{:S(2)}) collective-permute-start(bf16[192,512]{1,0:T(8,128)(2,1)S(1)} %copy-done.15), channel_id=1, source_target_pairs={{0,3},{1,2},{2,1},{3,0},{4,7},{5,6},{6,5},{7,4},{8,11},{9,10},{10,... | collective-permute-start | bytes 589832 | tf_op jit(solution)/shard_map/ppermute | solution.py:199
  150.8 13.1 %collective-permute-start.18 = (bf16[192,512]{1,0:T(8,128)(2,1)S(1)}, bf16[192,512]{1,0:T(8,128)(2,1)S(1)}, u32[]{:S(2)}, u32[]{:S(2)}) collective-permute-start(bf16[192,512]{1,0:T(8,128)(2,1)S(1)} %copy-done.14), channel_id=1, source_target_pairs={{0,1},{1,0},{2,3},{3,2},{4,5},{5,4},{6,7},{7,6},{8,9},{9,8},{10,11... | collective-permute-start | bytes 589832 | tf_op jit(solution)/shard_map/ppermute | solution.py:199
  150.8 32.5 %collective-permute-start.14 = (bf16[512,512]{1,0:T(8,128)(2,1)S(1)}, bf16[512,512]{1,0:T(8,128)(2,1)S(1)}, u32[]{:S(2)}, u32[]{:S(2)}) collective-permute-start(bf16[512,512]{1,0:T(8,128)(2,1)S(1)} %collective-permute-done.10.refs_0_), channel_id=1, source_target_pairs={{0,4},{1,5},{2,6},{3,7},{4,8},{5,9},{6,10},{7,11},{8,12},{9,13},{1... | collective-permute-start | bytes 1572872 | tf_op jit(solution)/shard_map/ppermute | solution.py:196
  163.0 21.8 %collective-permute-start.32 = (bf16[512,512]{1,0:T(8,128)(2,1)S(1)}, bf16[512,512]{1,0:T(8,128)(2,1)S(1)}, u32[]{:S(2)}, u32[]{:S(2)}) collective-permute-start(bf16[512,512]{1,0:T(8,128)(2,1)S(1)} %plane_partial.6), channel_id=1, source_target_pairs={{0,4},{1,5},{2,6},{3,7},{4,8},{5,9},{6,10},{7,11},{8,12},{9,13},{1... | collective-permute-start | bytes 1572872 | tf_op jit(solution)/shard_map/ppermute | solution.py:196
  163.3 10.5 %collective-permute-start.19 = (bf16[192,512]{1,0:T(8,128)(2,1)S(1)}, bf16[192,512]{1,0:T(8,128)(2,1)S(1)}, u32[]{:S(2)}, u32[]{:S(2)}) collective-permute-start(bf16[192,512]{1,0:T(8,128)(2,1)S(1)} %copy-done.13), channel_id=1, source_target_pairs={{0,2},{1,3},{2,0},{3,1},{4,6},{5,7},{6,4},{7,5},{8,10},{9,11},{10,... | collective-permute-start | bytes 589832 | tf_op jit(solution)/shard_map/ppermute | solution.py:199
  163.9 11.4 %collective-permute-start.20 = (bf16[192,512]{1,0:T(8,128)(2,1)S(1)}, bf16[192,512]{1,0:T(8,128)(2,1)S(1)}, u32[]{:S(2)}, u32[]{:S(2)}) collective-permute-start(bf16[192,512]{1,0:T(8,128)(2,1)S(1)} %copy-done.12), channel_id=1, source_target_pairs={{0,3},{1,2},{2,1},{3,0},{4,7},{5,6},{6,5},{7,4},{8,11},{9,10},{10,... | collective-permute-start | bytes 589832 | tf_op jit(solution)/shard_map/ppermute | solution.py:199
  175.3 6.0 %collective-permute-start.4 = (bf16[192,512]{1,0:T(8,128)(2,1)S(1)}, bf16[192,512]{1,0:T(8,128)(2,1)S(1)}, u32[]{:S(2)}, u32[]{:S(2)}) collective-permute-start(bf16[192,512]{1,0:T(8,128)(2,1)S(1)} %get-tuple-element.41), channel_id=1, source_target_pairs={{0,2},{1,3},{2,0},{3,1},{4,6},{5,7},{6,4},{7,5},{8,10},{9,11},{10,... | collective-permute-start | bytes 589832 | tf_op jit(solution)/shard_map/ppermute | solution.py:199
  179.8 11.4 %collective-permute-start.5 = (bf16[192,512]{1,0:T(8,128)(2,1)S(1)}, bf16[192,512]{1,0:T(8,128)(2,1)S(1)}, u32[]{:S(2)}, u32[]{:S(2)}) collective-permute-start(bf16[192,512]{1,0:T(8,128)(2,1)S(1)} %get-tuple-element.42), channel_id=1, source_target_pairs={{0,3},{1,2},{2,1},{3,0},{4,7},{5,6},{6,5},{7,4},{8,11},{9,10},{10,... | collective-permute-start | bytes 589832 | tf_op jit(solution)/shard_map/ppermute | solution.py:199
  181.3 11.6 %collective-permute-start.7 = (bf16[192,512]{1,0:T(8,128)(2,1)S(1)}, bf16[192,512]{1,0:T(8,128)(2,1)S(1)}, u32[]{:S(2)}, u32[]{:S(2)}) collective-permute-start(bf16[192,512]{1,0:T(8,128)(2,1)S(1)} %get-tuple-element.45), channel_id=1, source_target_pairs={{0,1},{1,0},{2,3},{3,2},{4,5},{5,4},{6,7},{7,6},{8,9},{9,8},{10,11... | collective-permute-start | bytes 589832 | tf_op jit(solution)/shard_map/ppermute | solution.py:199
  182.8 11.2 %collective-permute-start.8 = (bf16[192,512]{1,0:T(8,128)(2,1)S(1)}, bf16[192,512]{1,0:T(8,128)(2,1)S(1)}, u32[]{:S(2)}, u32[]{:S(2)}) collective-permute-start(bf16[192,512]{1,0:T(8,128)(2,1)S(1)} %get-tuple-element.46), channel_id=1, source_target_pairs={{0,2},{1,3},{2,0},{3,1},{4,6},{5,7},{6,4},{7,5},{8,10},{9,11},{10,... | collective-permute-start | bytes 589832 | tf_op jit(solution)/shard_map/ppermute | solution.py:199
  183.3 13.8 %collective-permute-start.9 = (bf16[192,512]{1,0:T(8,128)(2,1)S(1)}, bf16[192,512]{1,0:T(8,128)(2,1)S(1)}, u32[]{:S(2)}, u32[]{:S(2)}) collective-permute-start(bf16[192,512]{1,0:T(8,128)(2,1)S(1)} %get-tuple-element.47), channel_id=1, source_target_pairs={{0,3},{1,2},{2,1},{3,0},{4,7},{5,6},{6,5},{7,4},{8,11},{9,10},{10,... | collective-permute-start | bytes 589832 | tf_op jit(solution)/shard_map/ppermute | solution.py:199
  184.8 16.5 %collective-permute-start.11 = (bf16[192,512]{1,0:T(8,128)(2,1)S(1)}, bf16[192,512]{1,0:T(8,128)(2,1)S(1)}, u32[]{:S(2)}, u32[]{:S(2)}) collective-permute-start(bf16[192,512]{1,0:T(8,128)(2,1)S(1)} %get-tuple-element.49), channel_id=1, source_target_pairs={{0,1},{1,0},{2,3},{3,2},{4,5},{5,4},{6,7},{7,6},{8,9},{9,8},{10,11... | collective-permute-start | bytes 589832 | tf_op jit(solution)/shard_map/ppermute | solution.py:199
  191.2 13.7 %collective-permute-start.12 = (bf16[192,512]{1,0:T(8,128)(2,1)S(1)}, bf16[192,512]{1,0:T(8,128)(2,1)S(1)}, u32[]{:S(2)}, u32[]{:S(2)}) collective-permute-start(bf16[192,512]{1,0:T(8,128)(2,1)S(1)} %get-tuple-element.50), channel_id=1, source_target_pairs={{0,2},{1,3},{2,0},{3,1},{4,6},{5,7},{6,4},{7,5},{8,10},{9,11},{10,... | collective-permute-start | bytes 589832 | tf_op jit(solution)/shard_map/ppermute | solution.py:199
  192.9 12.8 %collective-permute-start.13 = (bf16[192,512]{1,0:T(8,128)(2,1)S(1)}, bf16[192,512]{1,0:T(8,128)(2,1)S(1)}, u32[]{:S(2)}, u32[]{:S(2)}) collective-permute-start(bf16[192,512]{1,0:T(8,128)(2,1)S(1)} %get-tuple-element.51), channel_id=1, source_target_pairs={{0,3},{1,2},{2,1},{3,0},{4,7},{5,6},{6,5},{7,4},{8,11},{9,10},{10,... | collective-permute-start | bytes 589832 | tf_op jit(solution)/shard_map/ppermute | solution.py:199
  194.0 15.1 %collective-permute-start.15 = (bf16[192,512]{1,0:T(8,128)(2,1)S(1)}, bf16[192,512]{1,0:T(8,128)(2,1)S(1)}, u32[]{:S(2)}, u32[]{:S(2)}) collective-permute-start(bf16[192,512]{1,0:T(8,128)(2,1)S(1)} %get-tuple-element.53), channel_id=1, source_target_pairs={{0,1},{1,0},{2,3},{3,2},{4,5},{5,4},{6,7},{7,6},{8,9},{9,8},{10,11... | collective-permute-start | bytes 589832 | tf_op jit(solution)/shard_map/ppermute | solution.py:199
  197.2 14.2 %collective-permute-start.16 = (bf16[192,512]{1,0:T(8,128)(2,1)S(1)}, bf16[192,512]{1,0:T(8,128)(2,1)S(1)}, u32[]{:S(2)}, u32[]{:S(2)}) collective-permute-start(bf16[192,512]{1,0:T(8,128)(2,1)S(1)} %get-tuple-element.54), channel_id=1, source_target_pairs={{0,2},{1,3},{2,0},{3,1},{4,6},{5,7},{6,4},{7,5},{8,10},{9,11},{10,... | collective-permute-start | bytes 589832 | tf_op jit(solution)/shard_map/ppermute | solution.py:199
  201.3 10.1 %collective-permute-start.17 = (bf16[192,512]{1,0:T(8,128)(2,1)S(1)}, bf16[192,512]{1,0:T(8,128)(2,1)S(1)}, u32[]{:S(2)}, u32[]{:S(2)}) collective-permute-start(bf16[192,512]{1,0:T(8,128)(2,1)S(1)} %get-tuple-element.55), channel_id=1, source_target_pairs={{0,3},{1,2},{2,1},{3,0},{4,7},{5,6},{6,5},{7,4},{8,11},{9,10},{10,... | collective-permute-start | bytes 589832 | tf_op jit(solution)/shard_map/ppermute | solution.py:199
  (20 other events, 944.9 us)

commit v2 on v1

v2 whole, which is shorter than its diff:
```python
import functools

import jax
import jax.numpy as jnp
from jax import lax
from jax.experimental import pallas as pl
from jax.experimental.pallas import tpu as pltpu
from jax.sharding import PartitionSpec as P

first_decay = 0.9
second_decay = 0.95
inner_rate = 0.001
weight_decay = 0.1
adam_epsilon = 1e-08
adam_count = 10.0
outer_rate = 0.7
outer_mass = 0.9

PLANE = 4
WEIGHT_SCALE = 2.0**17
WIRE = jnp.bfloat16


def power_below(limit):
    scale = 1.0
    while scale * limit > 32768.0:
        scale /= 2.0
    while scale * limit < 16384.0:
        scale *= 2.0
    return scale


def encode(x):
    power = x * x
    power = power * power
    power = power * power
    return jnp.where(x < 0.0, -power, power).astype(WIRE)


def decode(code):
    wide = code.astype(jnp.float32)
    size = jnp.abs(wide)
    root = jnp.where(size > 0.0, jnp.exp(jnp.log(size) * 0.125), 0.0)
    return jnp.where(wide < 0.0, -root, root)


def vmem(count):
    return [pl.BlockSpec(memory_space=pltpu.VMEM)] * count


def contract(left, right, dims):
    return lax.dot_general(left, right, (dims, ((), ())), preferred_element_type=jnp.float32)


def pack_kernel(columns, planes, axis, features, cot, weight, coded, own, *chunks):
    me = lax.axis_index(axis)
    z, p = me // PLANE, me % PLANE
    coded[...] = encode(weight[...] * WEIGHT_SCALE)
    for k in range(PLANE):
        if k > 0:
            first, rest = chunks[2 * k - 2], chunks[2 * k - 1]
            first[:, : cot.shape[1]] = cot[...]
        for at in range(planes):
            block = lax.rem(z + 2 * planes - 1 - at, planes)
            start = pl.multiple_of((block * PLANE + (p ^ k)) * columns, 128)
            value = features[:, pl.ds(start, columns)]
            if k == 0:
                own[:, at * columns : (at + 1) * columns] = value
            elif at == 0:
                first[:, cot.shape[1] :] = value
            else:
                rest[:, (at - 1) * columns : at * columns] = value


def pack(features, cot, weight, columns, planes):
    rows = features.shape[0]
    widths = [planes * columns] + [cot.shape[1] + columns, (planes - 1) * columns] * (PLANE - 1)
    coded, own, *chunks = pl.pallas_call(
        functools.partial(pack_kernel, columns, planes, "fsdp"),
        out_shape=[jax.ShapeDtypeStruct(weight.shape, WIRE)]
        + [jax.ShapeDtypeStruct((rows, width), features.dtype) for width in widths],
        in_specs=vmem(3),
        out_specs=vmem(1 + len(widths)),
        compiler_params=pltpu.CompilerParams(vmem_limit_bytes=32 << 20),
        name="pack",
    )(features, cot, weight)
    return coded, own, [chunks[2 * k : 2 * k + 2] for k in range(PLANE - 1)]


def partial_kernel(at, columns, scale, own, cot, *refs):
    firsts, others, so_far, out = refs[:3], refs[3:-1], (), refs[-1]
    if at > 0:
        others, so_far = refs[3:6], refs[6:-1]
    depth = cot.shape[1]
    total = contract(own[:, at * columns : (at + 1) * columns], cot[...], ((0,), (0,)))
    for i, first in enumerate(firsts):
        if at == 0:
            part = first[:, depth:]
        else:
            part = others[i][:, (at - 1) * columns : at * columns]
        total += contract(part, first[:, :depth], ((0,), (0,)))
    total = total * scale
    for ref in so_far:
        total += decode(ref[...])
    out[...] = encode(total) if out.dtype == WIRE else total


def plane_partial(at, own, cot, firsts, others, so_far, columns, scale, dtype):
    operands = [own, cot, *firsts, *others, *so_far]
    return pl.pallas_call(
        functools.partial(partial_kernel, at, columns, scale),
        out_shape=jax.ShapeDtypeStruct((columns, cot.shape[1]), dtype),
        in_specs=vmem(len(operands)),
        out_specs=pl.BlockSpec(memory_space=pltpu.VMEM),
        compiler_params=pltpu.CompilerParams(vmem_limit_bytes=32 << 20),
        name="plane_partial",
    )(*operands)


def product_kernel(count, scale, *refs):
    weights, cot, firsts, outs = refs[:count], refs[count], refs[count + 1 : count + PLANE], refs[count + PLANE :]
    depth = cot.shape[1]
    for i, weight in enumerate(weights):
        if weight.dtype == WIRE:
            wide, factor = decode(weight[...]), 1.0 / WEIGHT_SCALE
        else:
            wide, factor = weight[...], 1.0
        high = wide.astype(jnp.bfloat16)
        low = (wide - high.astype(jnp.float32)).astype(jnp.bfloat16)
        columns = weight.shape[0]
        for k in range(PLANE):
            rows = cot[...] if k == 0 else firsts[k - 1][:, :depth]
            result = contract(rows, high, ((1,), (1,))) + contract(rows, low, ((1,), (1,)))
            result = result * factor if k == 0 else encode(result * (factor * scale))
            outs[k][:, i * columns : (i + 1) * columns] = result


def plane_product(weights, cot, firsts, scale):
    shape = (cot.shape[0], weights[0].shape[0] * len(weights))
    return pl.pallas_call(
        functools.partial(product_kernel, len(weights), scale),
        out_shape=[jax.ShapeDtypeStruct(shape, jnp.float32 if k == 0 else WIRE) for k in range(PLANE)],
        in_specs=vmem(len(weights) + PLANE),
        out_specs=vmem(PLANE),
        compiler_params=pltpu.CompilerParams(vmem_limit_bytes=32 << 20),
        name="plane_product",
    )(*weights, cot, *firsts)


def unpack_kernel(columns, planes, axis, factor, widths, *refs):
    pieces, out, buffer, sem = refs[:-3], refs[-3], refs[-2], refs[-1]
    me = lax.axis_index(axis)
    z, p = me // PLANE, me % PLANE
    copies = []
    at = 0
    for chunk, width in enumerate(widths):
        for inner in range(width):
            block = lax.rem(z + planes - at, planes)
            for k in range(PLANE):
                i = at * PLANE + k
                piece = pieces[chunk * PLANE + k]
                span = slice(inner * columns, (inner + 1) * columns)
                if k == 0:
                    source = piece.at[:, span]
                else:
                    buffer[i] = decode(piece[:, span]) * factor
                    source = buffer.at[i]
                start = pl.multiple_of((block * PLANE + (p ^ k)) * columns, 128)
                copy = pltpu.make_async_copy(source, out.at[:, pl.ds(start, columns)], sem.at[i])
                copy.start()
                copies.append(copy)
            at += 1
    for copy in copies:
        copy.wait()


def unpack(pieces, columns, planes, factor):
    rows = pieces[0].shape[0]
    count = planes * PLANE
    widths = [piece.shape[1] // columns for piece in pieces[::PLANE]]
    return pl.pallas_call(
        functools.partial(unpack_kernel, columns, planes, "fsdp", factor, widths),
        out_shape=jax.ShapeDtypeStruct((rows, columns * count), jnp.float32),
        in_specs=vmem(len(pieces)),
        out_specs=pl.BlockSpec(memory_space=pl.ANY),
        scratch_shapes=[
            pltpu.VMEM((count, rows, columns), jnp.float32),
            pltpu.SemaphoreType.DMA((count,)),
        ],
        compiler_params=pltpu.CompilerParams(vmem_limit_bytes=40 << 20),
        name="unpack",
    )(*pieces)


def on_device(
    features,
    value_cotangent,
    value_weight,
    first_moment,
    second_moment,
    fragment_local,
    fragment_anchor,
    outer_momentum,
):
    size = lax.axis_size("fsdp")
    planes = size // PLANE
    columns = features.shape[1] // size
    tokens = features.shape[0] * size
    gradient_scale = power_below(tokens * 24.0 * 6.0)
    product_scale = power_below(value_cotangent.shape[1] * 6.0 * 0.25)

    ring = [(i, (i + PLANE) % size) for i in range(size)]

    def around(x):
        return lax.ppermute(x, "fsdp", ring)

    def across(x, k):
        return lax.ppermute(x, "fsdp", [(i, i ^ k) for i in range(size)])

    weight = value_weight[0]
    travelling, own, chunks = pack(features, value_cotangent, weight, columns, planes)
    weights = [weight]
    for _ in range(1, planes):
        travelling = around(travelling)
        weights.append(travelling)
    firsts = [across(first, k + 1) for k, (first, _) in enumerate(chunks)]
    others = [across(rest, k + 1) for k, (_, rest) in enumerate(chunks)]

    pieces = []
    for half in (weights[: planes // 2], weights[planes // 2 :]):
        products = plane_product(half, value_cotangent, firsts, product_scale)
        pieces += [part if k == 0 else across(part, k) for k, part in enumerate(products)]
    feature_grad = unpack(pieces, columns, planes, 1.0 / product_scale)

    running = []
    for at in range(planes):
        last = at == planes - 1
        total = plane_partial(
            at,
            own,
            value_cotangent,
            firsts,
            others if at > 0 else [],
            running,
            columns,
            gradient_scale,
            jnp.float32 if last else WIRE,
        )
        running = [total if last else around(total)]
    gradient = running[0] * (1.0 / gradient_scale)

    first_new = first_decay * first_moment[0] + (1.0 - first_decay) * gradient
    second_new = second_decay * second_moment[0] + (1.0 - second_decay) * gradient * gradient
    first_hat = first_new / (1.0 - first_decay**adam_count)
    second_hat = second_new / (1.0 - second_decay**adam_count)
    weight_new = weight - inner_rate * (
        first_hat / (jnp.sqrt(second_hat) + adam_epsilon) + weight_decay * weight
    )
    workers = lax.axis_size("worker")
    difference = fragment_anchor - fragment_local[0]
    if workers == 2:
        pseudo_sum = difference + lax.ppermute(difference, "worker", [(0, 1), (1, 0)])
    else:
        pseudo_sum = lax.psum(difference, "worker")
    pseudo_mean = pseudo_sum / workers
    new_momentum = outer_mass * outer_momentum + pseudo_mean
    new_anchor = fragment_anchor - outer_rate * (pseudo_mean + outer_mass * new_momentum)
    return (
        feature_grad,
        weight_new[None],
        first_new[None],
        second_new[None],
        new_anchor,
        new_momentum,
    )


def solution(mesh):
    placed = (
        P(("worker", "fsdp"), None),
        P(("worker", "fsdp"), None),
        P("worker", "fsdp", None),
        P("worker", "fsdp", None),
        P("worker", "fsdp", None),
        P("worker", "fsdp", None),
        P("fsdp", None),
        P("fsdp", None),
    )
    return jax.shard_map(
        on_device,
        mesh=mesh,
        in_specs=placed,
        out_specs=(
            P(("worker", "fsdp"), None),
            P("worker", "fsdp", None),
            P("worker", "fsdp", None),
            P("worker", "fsdp", None),
            P("fsdp", None),
            P("fsdp", None),
        ),
        check_vma=False,
    )
```

time: 215 us -> 115 us (0.53)
  Pallas kernels: 113 us -> 14.9 us
  starting transfers between devices: 41.9 us -> 24 us
  waiting for transfers between devices: 50.6 us -> 66.8 us
    pallas_call x1, Pallas kernels: 98.7 us -> 0.48 us  [pack(): pl.pallas_call(functools.partial(pack_kernel, columns, planes, 'fsdp'), o...]
    ppermute x27 -> x12, starting transfers between devices: 35 us -> 14.3 us  [across(): return lax.ppermute(x, 'fsdp', [(i, i ^ k) for i in range(size)])]
    ppermute x27 -> x12, waiting for transfers between devices: 40.8 us -> 49 us  [across(): return lax.ppermute(x, 'fsdp', [(i, i ^ k) for i in range(size)])]
    ppermute x6, waiting for transfers between devices: 9.83 us -> 17.8 us  [around(): return lax.ppermute(x, 'fsdp', ring)]
    ppermute x6, starting transfers between devices: 6.93 us -> 9.72 us  [around(): return lax.ppermute(x, 'fsdp', ring)]
    pallas_call x8 -> x6, Pallas kernels: 11.8 us -> 11.5 us  [the longest x2 7.1 us: plane_product(): pl.pallas_call(functools.partial(product_kernel, len(weights), scale), ou...]
  transfers between devices with their start and end apart: 34 -> 19, of which waited for: 18 -> 10; matrix products, arithmetic and copies ran while one was open for 2% -> 2% of each run, Pallas kernels for 6% -> 12%
where the time goes in v2:
time: 115 us
  waiting for transfers between devices  66.8 us (58%)
  starting transfers between devices  24 us (21%)
  Pallas kernels  14.9 us (13%)
  other arithmetic  4.53 us (4%)
  local copies, waits for them, and re-layouts  4.06 us (4%)
    ppermute x12, waiting for transfers between devices, across(): return lax.ppermute(x, 'fsdp', [(i, i ^ k) for i in range(size)])  49 us
    ppermute x6, waiting for transfers between devices, around(): return lax.ppermute(x, 'fsdp', ring)  17.8 us
    ppermute x12, starting transfers between devices, across(): return lax.ppermute(x, 'fsdp', [(i, i ^ k) for i in range(size)])  14.3 us
    ppermute x6, starting transfers between devices, around(): return lax.ppermute(x, 'fsdp', ring)  9.72 us
    pallas_call x2, Pallas kernels, plane_product(): pl.pallas_call(functools.partial(product_kernel, len(weights), scale), ou...  7.1 us
    pallas_call x4, Pallas kernels, plane_partial(): pl.pallas_call(functools.partial(partial_kernel, at, columns, scale), out...  4.45 us
    unnamed x20, local copies, waits for them, and re-layouts  4.06 us
    pallas_call x1, Pallas kernels, unpack(): pl.pallas_call(functools.partial(unpack_kernel, columns, planes, 'fsdp',...  2.91 us
  transfers between devices with their start and end apart: 19, of which 10 were waited for; matrix products, arithmetic and copies ran while one was open for 2% of the time, Pallas kernels for 12%

profile of v2, /device:TPU:0, one launch (start us, length us, event | category | flops | bytes accessed | tf_op | source)
XLA Modules:
  0.0 115.1 jit_solution(9726827717598994977)
XLA Ops:
  1.6 1.2 %copy-done.2 = f32[1,512,512]{2,1,0:T(8,128)S(1)} copy-done((f32[1,512,512]{2,1,0:T(8,128)S(1)}, f32[1,512,512]{2,1,0:T(8,128)}, u32[]{:S(2)}) %copy-start.2) | copy-done | bytes 1048600
  2.8 1.9 %copy-done.4 = bf16[192,8192]{1,0:T(8,128)(2,1)S(1)} copy-done((bf16[192,8192]{1,0:T(8,128)(2,1)S(1)}, bf16[192,8192]{1,0:T(8,128)(2,1)}, u32[]{:S(2)}) %copy-start.4) | copy-done | bytes 3145752
  5.2 3.1 %collective-permute-start = (bf16[512,512]{1,0:T(8,128)(2,1)S(1)}, bf16[512,512]{1,0:T(8,128)(2,1)S(1)}, u32[]{:S(2)}, u32[]{:S(2)}) collective-permute-start(bf16[512,512]{1,0:T(8,128)(2,1)S(1)} %get-tuple-element.22), channel_id=1, source_target_pairs={{0,4},{1,5},{2,6},{3,7},{4,8},{5,9},{6,10},{7,11},{8,12},{9,13},{1... | collective-permute-start | bytes 1572872 | tf_op jit(solution)/shard_map/ppermute | solution.py:215
  8.3 1.5 %collective-permute-start.1 = (bf16[192,1024]{1,0:T(8,128)(2,1)S(1)}, bf16[192,1024]{1,0:T(8,128)(2,1)S(1)}, u32[]{:S(2)}, u32[]{:S(2)}) collective-permute-start(bf16[192,1024]{1,0:T(8,128)(2,1)S(1)} %get-tuple-element.23), channel_id=1, source_target_pairs={{0,1},{1,0},{2,3},{3,2},{4,5},{5,4},{6,7},{7,6},{8,9},{9,8},{10,11... | collective-permute-start | bytes 1179656 | tf_op jit(solution)/shard_map/ppermute | solution.py:218
  9.8 1.5 %collective-permute-start.2 = (bf16[192,1024]{1,0:T(8,128)(2,1)S(1)}, bf16[192,1024]{1,0:T(8,128)(2,1)S(1)}, u32[]{:S(2)}, u32[]{:S(2)}) collective-permute-start(bf16[192,1024]{1,0:T(8,128)(2,1)S(1)} %get-tuple-element.24), channel_id=1, source_target_pairs={{0,2},{1,3},{2,0},{3,1},{4,6},{5,7},{6,4},{7,5},{8,10},{9,11},{10,... | collective-permute-start | bytes 1179656 | tf_op jit(solution)/shard_map/ppermute | solution.py:218
  11.7 1.5 %collective-permute-start.12 = (bf16[192,1536]{1,0:T(8,128)(2,1)S(1)}, bf16[192,1536]{1,0:T(8,128)(2,1)S(1)}, u32[]{:S(2)}, u32[]{:S(2)}) collective-permute-start(bf16[192,1536]{1,0:T(8,128)(2,1)S(1)} %get-tuple-element.35), channel_id=1, source_target_pairs={{0,1},{1,0},{2,3},{3,2},{4,5},{5,4},{6,7},{7,6},{8,9},{9,8},{10,11... | collective-permute-start | bytes 1769480 | tf_op jit(solution)/shard_map/ppermute | solution.py:218
  13.2 7.1 %collective-permute-done.1.refs_3_.refs_0_ = bf16[192,1024]{1,0:T(8,128)(2,1)S(1)} collective-permute-done((bf16[192,1024]{1,0:T(8,128)(2,1)S(1)}, bf16[192,1024]{1,0:T(8,128)(2,1)S(1)}, u32[]{:S(2)}, u32[]{:S(2)}) %collective-permute-start.1) | collective-permute-done | bytes 393248 | tf_op jit(solution)/shard_map/ppermute | solution.py:218
  20.3 1.5 %collective-permute-start.13 = (bf16[192,1536]{1,0:T(8,128)(2,1)S(1)}, bf16[192,1536]{1,0:T(8,128)(2,1)S(1)}, u32[]{:S(2)}, u32[]{:S(2)}) collective-permute-start(bf16[192,1536]{1,0:T(8,128)(2,1)S(1)} %get-tuple-element.36), channel_id=1, source_target_pairs={{0,2},{1,3},{2,0},{3,1},{4,6},{5,7},{6,4},{7,5},{8,10},{9,11},{10,... | collective-permute-start | bytes 1769480 | tf_op jit(solution)/shard_map/ppermute | solution.py:218
  21.8 7.0 %collective-permute-done.2.refs_4_.refs_1_ = bf16[192,1024]{1,0:T(8,128)(2,1)S(1)} collective-permute-done((bf16[192,1024]{1,0:T(8,128)(2,1)S(1)}, bf16[192,1024]{1,0:T(8,128)(2,1)S(1)}, u32[]{:S(2)}, u32[]{:S(2)}) %collective-permute-start.2) | collective-permute-done | bytes 393248 | tf_op jit(solution)/shard_map/ppermute | solution.py:218
  30.6 1.6 %collective-permute-start.15 = (bf16[512,512]{1,0:T(8,128)(2,1)S(1)}, bf16[512,512]{1,0:T(8,128)(2,1)S(1)}, u32[]{:S(2)}, u32[]{:S(2)}) collective-permute-start(bf16[512,512]{1,0:T(8,128)(2,1)S(1)} %plane_partial.4), channel_id=1, source_target_pairs={{0,4},{1,5},{2,6},{3,7},{4,8},{5,9},{6,10},{7,11},{8,12},{9,13},{1... | collective-permute-start | bytes 1572872 | tf_op jit(solution)/shard_map/ppermute | solution.py:215
  32.2 1.6 %collective-permute-start.7 = (bf16[512,512]{1,0:T(8,128)(2,1)S(1)}, bf16[512,512]{1,0:T(8,128)(2,1)S(1)}, u32[]{:S(2)}, u32[]{:S(2)}) collective-permute-start(bf16[512,512]{1,0:T(8,128)(2,1)S(1)} %collective-permute-done.refs_1_), channel_id=1, source_target_pairs={{0,4},{1,5},{2,6},{3,7},{4,8},{5,9},{6,10},{7,11},{8,12},{9,13},{1... | collective-permute-start | bytes 1572872 | tf_op jit(solution)/shard_map/ppermute | solution.py:215
  34.0 7.4 %collective-permute-done.12.refs_3_ = bf16[192,1536]{1,0:T(8,128)(2,1)S(1)} collective-permute-done((bf16[192,1536]{1,0:T(8,128)(2,1)S(1)}, bf16[192,1536]{1,0:T(8,128)(2,1)S(1)}, u32[]{:S(2)}, u32[]{:S(2)}) %collective-permute-start.12) | collective-permute-done | bytes 589856 | tf_op jit(solution)/shard_map/ppermute | solution.py:218
  41.4 12.3 %collective-permute-done.13.refs_4_ = bf16[192,1536]{1,0:T(8,128)(2,1)S(1)} collective-permute-done((bf16[192,1536]{1,0:T(8,128)(2,1)S(1)}, bf16[192,1536]{1,0:T(8,128)(2,1)S(1)}, u32[]{:S(2)}, u32[]{:S(2)}) %collective-permute-start.13) | collective-permute-done | bytes 589856 | tf_op jit(solution)/shard_map/ppermute | solution.py:218
  53.8 1.3 %plane_partial.5 = bf16[512,512]{1,0:T(8,128)(2,1)S(1)} custom-call(bf16[192,2048]{1,0:T(8,128)(2,1)S(1)} %get-tuple-element.34.own, bf16[192,512]{1,0:T(8,128)(2,1)S(1)} %copy-done.1, bf16[192,1024]{1,0:T(8,128)(2,1)S(1)} %collective-permute-done.1.refs_3_.refs_0_, bf16[192,1024]{1,0:T(8,128)(2,1)S(1)} %collective-permute-done.2.refs_4_.refs_1_, ...), custom_call_target="tpu_custom_call" | custom-call | tf_op jit(solution)/shard_map/plane_partial/pallas_call | solution.py:110
  55.0 1.6 %collective-permute-start.16 = (bf16[512,512]{1,0:T(8,128)(2,1)S(1)}, bf16[512,512]{1,0:T(8,128)(2,1)S(1)}, u32[]{:S(2)}, u32[]{:S(2)}) collective-permute-start(bf16[512,512]{1,0:T(8,128)(2,1)S(1)} %plane_partial.5), channel_id=1, source_target_pairs={{0,4},{1,5},{2,6},{3,7},{4,8},{5,9},{6,10},{7,11},{8,12},{9,13},{1... | collective-permute-start | bytes 1572872 | tf_op jit(solution)/shard_map/ppermute | solution.py:215
  56.7 1.6 %collective-permute-start.8 = (bf16[512,512]{1,0:T(8,128)(2,1)S(1)}, bf16[512,512]{1,0:T(8,128)(2,1)S(1)}, u32[]{:S(2)}, u32[]{:S(2)}) collective-permute-start(bf16[512,512]{1,0:T(8,128)(2,1)S(1)} %collective-permute-done.7.refs_0_), channel_id=1, source_target_pairs={{0,4},{1,5},{2,6},{3,7},{4,8},{5,9},{6,10},{7,11},{8,12},{9,13},{1... | collective-permute-start | bytes 1572872 | tf_op jit(solution)/shard_map/ppermute | solution.py:215
  58.3 3.4 %plane_product.2 = (f32[192,1024]{1,0:T(8,128)S(1)}, bf16[192,1024]{1,0:T(8,128)(2,1)S(1)}, bf16[192,1024]{1,0:T(8,128)(2,1)S(1)}, bf16[192,1024]{1,0:T(8,128)(2,1)S(1)}) custom-call(f32[512,512]{1,0:T(8,128)S(1)} %bitcast.23, bf16[512,512]{1,0:T(8,128)(2,1)S(1)} %collective-permute-done.refs_1_, bf16[192,512]{1,0:T(8,128)(2,1)S(1)} %copy-done.1, ...), custom_call_target="tpu_custom_call" | custom-call | tf_op jit(solution)/shard_map/plane_product/pallas_call | solution.py:140
  61.6 1.3 %collective-permute-start.4 = (bf16[192,1024]{1,0:T(8,128)(2,1)S(1)}, bf16[192,1024]{1,0:T(8,128)(2,1)S(1)}, u32[]{:S(2)}, u32[]{:S(2)}) collective-permute-start(bf16[192,1024]{1,0:T(8,128)(2,1)S(1)} %get-tuple-element.27), channel_id=1, source_target_pairs={{0,1},{1,0},{2,3},{3,2},{4,5},{5,4},{6,7},{7,6},{8,9},{9,8},{10,11... | collective-permute-start | bytes 1179656 | tf_op jit(solution)/shard_map/ppermute | solution.py:218
  63.7 8.0 %collective-permute-done.16.refs_6_ = bf16[512,512]{1,0:T(8,128)(2,1)S(1)} collective-permute-done((bf16[512,512]{1,0:T(8,128)(2,1)S(1)}, bf16[512,512]{1,0:T(8,128)(2,1)S(1)}, u32[]{:S(2)}, u32[]{:S(2)}) %collective-permute-start.16) | collective-permute-done | bytes 524320 | tf_op jit(solution)/shard_map/ppermute | solution.py:215
  71.8 1.3 %plane_partial.6 = bf16[512,512]{1,0:T(8,128)(2,1)S(1)} custom-call(bf16[192,2048]{1,0:T(8,128)(2,1)S(1)} %get-tuple-element.34.own, bf16[192,512]{1,0:T(8,128)(2,1)S(1)} %copy-done.1, bf16[192,1024]{1,0:T(8,128)(2,1)S(1)} %collective-permute-done.1.refs_3_.refs_0_, bf16[192,1024]{1,0:T(8,128)(2,1)S(1)} %collective-permute-done.2.refs_4_.refs_1_, ...), custom_call_target="tpu_custom_call" | custom-call | tf_op jit(solution)/shard_map/plane_partial/pallas_call | solution.py:110
  73.3 9.7 %collective-permute-done.8.refs_1_ = bf16[512,512]{1,0:T(8,128)(2,1)S(1)} collective-permute-done((bf16[512,512]{1,0:T(8,128)(2,1)S(1)}, bf16[512,512]{1,0:T(8,128)(2,1)S(1)}, u32[]{:S(2)}, u32[]{:S(2)}) %collective-permute-start.8) | collective-permute-done | bytes 524320 | tf_op jit(solution)/shard_map/ppermute | solution.py:215
  83.0 1.5 %collective-permute-start.6 = (bf16[192,1024]{1,0:T(8,128)(2,1)S(1)}, bf16[192,1024]{1,0:T(8,128)(2,1)S(1)}, u32[]{:S(2)}, u32[]{:S(2)}) collective-permute-start(bf16[192,1024]{1,0:T(8,128)(2,1)S(1)} %get-tuple-element.29), channel_id=1, source_target_pairs={{0,3},{1,2},{2,1},{3,0},{4,7},{5,6},{6,5},{7,4},{8,11},{9,10},{10,... | collective-permute-start | bytes 1179656 | tf_op jit(solution)/shard_map/ppermute | solution.py:218
  84.5 3.7 %plane_product.3 = (f32[192,1024]{1,0:T(8,128)S(1)}, bf16[192,1024]{1,0:T(8,128)(2,1)S(1)}, bf16[192,1024]{1,0:T(8,128)(2,1)S(1)}, bf16[192,1024]{1,0:T(8,128)(2,1)S(1)}) custom-call(bf16[512,512]{1,0:T(8,128)(2,1)S(1)} %collective-permute-done.7.refs_0_, bf16[512,512]{1,0:T(8,128)(2,1)S(1)} %collective-permute-done.8.refs_1_, ...), custom_call_target="tpu_custom_call" | custom-call | tf_op jit(solution)/shard_map/plane_product/pallas_call | solution.py:140
  88.2 1.3 %collective-permute-start.10 = (bf16[192,1024]{1,0:T(8,128)(2,1)S(1)}, bf16[192,1024]{1,0:T(8,128)(2,1)S(1)}, u32[]{:S(2)}, u32[]{:S(2)}) collective-permute-start(bf16[192,1024]{1,0:T(8,128)(2,1)S(1)} %get-tuple-element.32), channel_id=1, source_target_pairs={{0,2},{1,3},{2,0},{3,1},{4,6},{5,7},{6,4},{7,5},{8,10},{9,11},{10,... | collective-permute-start | bytes 1179656 | tf_op jit(solution)/shard_map/ppermute | solution.py:218
  89.6 1.7 %collective-permute-start.11 = (bf16[192,1024]{1,0:T(8,128)(2,1)S(1)}, bf16[192,1024]{1,0:T(8,128)(2,1)S(1)}, u32[]{:S(2)}, u32[]{:S(2)}) collective-permute-start(bf16[192,1024]{1,0:T(8,128)(2,1)S(1)} %get-tuple-element.33), channel_id=1, source_target_pairs={{0,3},{1,2},{2,1},{3,0},{4,7},{5,6},{6,5},{7,4},{8,11},{9,10},{10,... | collective-permute-start | bytes 1179656 | tf_op jit(solution)/shard_map/ppermute | solution.py:218
  91.8 1.8 %multiply_subtract_fusion = (f32[512,512]{1,0:T(8,128)}, f32[512,512]{1,0:T(8,128)}) fusion(f32[512,512]{1,0:T(8,128)S(1)} %copy-done.5, f32[512,512]{1,0:T(8,128)S(1)} %bitcast_subtract_fusion, f32[512,512]{1,0:T(8,128)S(1)} %collective-permute-done.18, f32[512,512]{1,0:T(8,128)S(1)} %copy-done.9), kind=kLoop, calls=%fused_computation.3 | loop fusion | flops 2097152 | bytes 6291456 | tf_op jit(solution)/shard_map/sub | solution.py:267
  93.7 2.1 %collective-permute-done.6.refs_3_ = bf16[192,1024]{1,0:T(8,128)(2,1)S(1)} collective-permute-done((bf16[192,1024]{1,0:T(8,128)(2,1)S(1)}, bf16[192,1024]{1,0:T(8,128)(2,1)S(1)}, u32[]{:S(2)}, u32[]{:S(2)}) %collective-permute-start.6) | collective-permute-done | bytes 393248 | tf_op jit(solution)/shard_map/ppermute | solution.py:218
  95.7 11.7 %collective-permute-done.10.refs_6_ = bf16[192,1024]{1,0:T(8,128)(2,1)S(1)} collective-permute-done((bf16[192,1024]{1,0:T(8,128)(2,1)S(1)}, bf16[192,1024]{1,0:T(8,128)(2,1)S(1)}, u32[]{:S(2)}, u32[]{:S(2)}) %collective-permute-start.10) | collective-permute-done | bytes 393248 | tf_op jit(solution)/shard_map/ppermute | solution.py:218
  107.4 1.2 %collective-permute-done.9.refs_5_ = bf16[192,1024]{1,0:T(8,128)(2,1)S(1)} collective-permute-done((bf16[192,1024]{1,0:T(8,128)(2,1)S(1)}, bf16[192,1024]{1,0:T(8,128)(2,1)S(1)}, u32[]{:S(2)}, u32[]{:S(2)}) %collective-permute-start.9) | collective-permute-done | bytes 393248 | tf_op jit(solution)/shard_map/ppermute | solution.py:218
  108.6 2.9 %unpack.1 = f32[192,8192]{1,0:T(8,128)} custom-call(f32[192,1024]{1,0:T(8,128)S(1)} %get-tuple-element.26.refs_0_, bf16[192,1024]{1,0:T(8,128)(2,1)S(1)} %collective-permute-done.4.refs_1_, bf16[192,1024]{1,0:T(8,128)(2,1)S(1)} %collective-permute-done.5.refs_2_, bf16[192,1024]{1,0:T(8,128)(2,1)S(1)} %collective-permute-done.6.refs_3_, ...), custom_call_target="tpu_custom_call" | custom-call | tf_op jit(solution)/shard_map/unpack/pallas_call | solution.py:181
  111.5 1.1 plane_partial.7
  112.6 2.5 %fusion.1 = (f32[1,512,512]{2,1,0:T(8,128)}, f32[1,512,512]{2,1,0:T(8,128)}, f32[1,512,512]{2,1,0:T(8,128)}) fusion(f32[512,512]{1,0:T(8,128)S(1)} %plane_partial.7, f32[1,512,512]{2,1,0:T(8,128)S(1)} %copy-done.7, f32[1,512,512]{2,1,0:T(8,128)S(1)} %copy-done.8, f32[1,512,512]{2,1,0:T(8,128)S(1)} %copy-done.3), kind=kLoop, calls=%fused_computation.8 | loop fusion | flops 4194304 | bytes 7340032 | tf_op jit(solution)/shard_map/broadcast_in_dim | solution.py:272
  (37 shorter events, 5.5 us)
Async XLA Ops:
  0.6 0.9 copy-start
  1.6 1.2 %copy-start.2 = (f32[1,512,512]{2,1,0:T(8,128)S(1)}, f32[1,512,512]{2,1,0:T(8,128)}, u32[]{:S(2)}) copy-start(f32[1,512,512]{2,1,0:T(8,128)} %param.10) | copy-start | bytes 3145732
  2.8 1.9 %copy-start.4 = (bf16[192,8192]{1,0:T(8,128)(2,1)S(1)}, bf16[192,8192]{1,0:T(8,128)(2,1)}, u32[]{:S(2)}) copy-start(bf16[192,8192]{1,0:T(8,128)(2,1)} %features.1) | copy-start | bytes 9437188
  4.7 29.1 %copy-start.5 = (f32[512,512]{1,0:T(8,128)S(1)}, f32[512,512]{1,0:T(8,128)}, u32[]{:S(2)}) copy-start(f32[512,512]{1,0:T(8,128)} %param.14) | copy-start | bytes 3145732
  4.7 29.1 %copy-start.6 = (f32[1,512,512]{2,1,0:T(8,128)S(1)}, f32[1,512,512]{2,1,0:T(8,128)}, u32[]{:S(2)}) copy-start(f32[1,512,512]{2,1,0:T(8,128)} %param.13) | copy-start | bytes 3145732
  4.7 49.1 %copy-start.1 = (bf16[192,512]{1,0:T(8,128)(2,1)S(1)}, bf16[192,512]{1,0:T(8,128)(2,1)}, u32[]{:S(2)}) copy-start(bf16[192,512]{1,0:T(8,128)(2,1)} %cot.9) | copy-start | bytes 589828
  5.2 53.1 %copy-start.3 = (f32[1,512,512]{2,1,0:T(8,128)S(1)}, f32[1,512,512]{2,1,0:T(8,128)}, u32[]{:S(2)}) copy-start(f32[1,512,512]{2,1,0:T(8,128)} %param.10) | copy-start | bytes 3145732
  5.2 27.1 %collective-permute-start = (bf16[512,512]{1,0:T(8,128)(2,1)S(1)}, bf16[512,512]{1,0:T(8,128)(2,1)S(1)}, u32[]{:S(2)}, u32[]{:S(2)}) collective-permute-start(bf16[512,512]{1,0:T(8,128)(2,1)S(1)} %get-tuple-element.22), channel_id=1, source_target_pairs={{0,4},{1,5},{2,6},{3,7},{4,8},{5,9},{6,10},{7,11},{8,12},{9,13},{1... | collective-permute-start | bytes 1572872 | tf_op jit(solution)/shard_map/ppermute | solution.py:215
  8.3 12.0 %collective-permute-start.1 = (bf16[192,1024]{1,0:T(8,128)(2,1)S(1)}, bf16[192,1024]{1,0:T(8,128)(2,1)S(1)}, u32[]{:S(2)}, u32[]{:S(2)}) collective-permute-start(bf16[192,1024]{1,0:T(8,128)(2,1)S(1)} %get-tuple-element.23), channel_id=1, source_target_pairs={{0,1},{1,0},{2,3},{3,2},{4,5},{5,4},{6,7},{7,6},{8,9},{9,8},{10,11... | collective-permute-start | bytes 1179656 | tf_op jit(solution)/shard_map/ppermute | solution.py:218
  9.8 19.0 %collective-permute-start.2 = (bf16[192,1024]{1,0:T(8,128)(2,1)S(1)}, bf16[192,1024]{1,0:T(8,128)(2,1)S(1)}, u32[]{:S(2)}, u32[]{:S(2)}) collective-permute-start(bf16[192,1024]{1,0:T(8,128)(2,1)S(1)} %get-tuple-element.24), channel_id=1, source_target_pairs={{0,2},{1,3},{2,0},{3,1},{4,6},{5,7},{6,4},{7,5},{8,10},{9,11},{10,... | collective-permute-start | bytes 1179656 | tf_op jit(solution)/shard_map/ppermute | solution.py:218
  11.3 18.5 %collective-permute-start.3 = (bf16[192,1024]{1,0:T(8,128)(2,1)S(1)}, bf16[192,1024]{1,0:T(8,128)(2,1)S(1)}, u32[]{:S(2)}, u32[]{:S(2)}) collective-permute-start(bf16[192,1024]{1,0:T(8,128)(2,1)S(1)} %get-tuple-element.25), channel_id=1, source_target_pairs={{0,3},{1,2},{2,1},{3,0},{4,7},{5,6},{6,5},{7,4},{8,11},{9,10},{10,... | collective-permute-start | bytes 1179656 | tf_op jit(solution)/shard_map/ppermute | solution.py:218
  11.7 29.7 %collective-permute-start.12 = (bf16[192,1536]{1,0:T(8,128)(2,1)S(1)}, bf16[192,1536]{1,0:T(8,128)(2,1)S(1)}, u32[]{:S(2)}, u32[]{:S(2)}) collective-permute-start(bf16[192,1536]{1,0:T(8,128)(2,1)S(1)} %get-tuple-element.35), channel_id=1, source_target_pairs={{0,1},{1,0},{2,3},{3,2},{4,5},{5,4},{6,7},{7,6},{8,9},{9,8},{10,11... | collective-permute-start | bytes 1769480 | tf_op jit(solution)/shard_map/ppermute | solution.py:218
  20.3 33.5 %collective-permute-start.13 = (bf16[192,1536]{1,0:T(8,128)(2,1)S(1)}, bf16[192,1536]{1,0:T(8,128)(2,1)S(1)}, u32[]{:S(2)}, u32[]{:S(2)}) collective-permute-start(bf16[192,1536]{1,0:T(8,128)(2,1)S(1)} %get-tuple-element.36), channel_id=1, source_target_pairs={{0,2},{1,3},{2,0},{3,1},{4,6},{5,7},{6,4},{7,5},{8,10},{9,11},{10,... | collective-permute-start | bytes 1769480 | tf_op jit(solution)/shard_map/ppermute | solution.py:218
  28.8 25.0 %collective-permute-start.14 = (bf16[192,1536]{1,0:T(8,128)(2,1)S(1)}, bf16[192,1536]{1,0:T(8,128)(2,1)S(1)}, u32[]{:S(2)}, u32[]{:S(2)}) collective-permute-start(bf16[192,1536]{1,0:T(8,128)(2,1)S(1)} %get-tuple-element.37), channel_id=1, source_target_pairs={{0,3},{1,2},{2,1},{3,0},{4,7},{5,6},{6,5},{7,4},{8,11},{9,10},{10,... | collective-permute-start | bytes 1769480 | tf_op jit(solution)/shard_map/ppermute | solution.py:218
  30.6 23.2 %collective-permute-start.15 = (bf16[512,512]{1,0:T(8,128)(2,1)S(1)}, bf16[512,512]{1,0:T(8,128)(2,1)S(1)}, u32[]{:S(2)}, u32[]{:S(2)}) collective-permute-start(bf16[512,512]{1,0:T(8,128)(2,1)S(1)} %plane_partial.4), channel_id=1, source_target_pairs={{0,4},{1,5},{2,6},{3,7},{4,8},{5,9},{6,10},{7,11},{8,12},{9,13},{1... | collective-permute-start | bytes 1572872 | tf_op jit(solution)/shard_map/ppermute | solution.py:215
  32.2 24.4 %collective-permute-start.7 = (bf16[512,512]{1,0:T(8,128)(2,1)S(1)}, bf16[512,512]{1,0:T(8,128)(2,1)S(1)}, u32[]{:S(2)}, u32[]{:S(2)}) collective-permute-start(bf16[512,512]{1,0:T(8,128)(2,1)S(1)} %collective-permute-done.refs_1_), channel_id=1, source_target_pairs={{0,4},{1,5},{2,6},{3,7},{4,8},{5,9},{6,10},{7,11},{8,12},{9,13},{1... | collective-permute-start | bytes 1572872 | tf_op jit(solution)/shard_map/ppermute | solution.py:215
  41.4 49.9 %collective-permute-start.18 = (f32[512,512]{1,0:T(8,128)S(1)}, f32[512,512]{1,0:T(8,128)S(1)}, u32[]{:S(2)}, u32[]{:S(2)}) collective-permute-start(f32[512,512]{1,0:T(8,128)S(1)} %bitcast_subtract_fusion), channel_id=1, source_target_pairs={{0,16},{16,0},{1,17},{17,1},{2,18},{18,2},{3,19},{19,3},{4,20},{20... | collective-permute-start | bytes 3145736 | tf_op jit(solution)/shard_map/ppermute | solution.py:262
  55.0 36.8 %copy-start.9 = (f32[512,512]{1,0:T(8,128)S(1)}, f32[512,512]{1,0:T(8,128)}, u32[]{:S(2)}) copy-start(f32[512,512]{1,0:T(8,128)} %param.15) | copy-start | bytes 3145732
  55.0 16.7 %collective-permute-start.16 = (bf16[512,512]{1,0:T(8,128)(2,1)S(1)}, bf16[512,512]{1,0:T(8,128)(2,1)S(1)}, u32[]{:S(2)}, u32[]{:S(2)}) collective-permute-start(bf16[512,512]{1,0:T(8,128)(2,1)S(1)} %plane_partial.5), channel_id=1, source_target_pairs={{0,4},{1,5},{2,6},{3,7},{4,8},{5,9},{6,10},{7,11},{8,12},{9,13},{1... | collective-permute-start | bytes 1572872 | tf_op jit(solution)/shard_map/ppermute | solution.py:215
  56.7 26.3 %collective-permute-start.8 = (bf16[512,512]{1,0:T(8,128)(2,1)S(1)}, bf16[512,512]{1,0:T(8,128)(2,1)S(1)}, u32[]{:S(2)}, u32[]{:S(2)}) collective-permute-start(bf16[512,512]{1,0:T(8,128)(2,1)S(1)} %collective-permute-done.7.refs_0_), channel_id=1, source_target_pairs={{0,4},{1,5},{2,6},{3,7},{4,8},{5,9},{6,10},{7,11},{8,12},{9,13},{1... | collective-permute-start | bytes 1572872 | tf_op jit(solution)/shard_map/ppermute | solution.py:215
  61.6 26.6 %collective-permute-start.4 = (bf16[192,1024]{1,0:T(8,128)(2,1)S(1)}, bf16[192,1024]{1,0:T(8,128)(2,1)S(1)}, u32[]{:S(2)}, u32[]{:S(2)}) collective-permute-start(bf16[192,1024]{1,0:T(8,128)(2,1)S(1)} %get-tuple-element.27), channel_id=1, source_target_pairs={{0,1},{1,0},{2,3},{3,2},{4,5},{5,4},{6,7},{7,6},{8,9},{9,8},{10,11... | collective-permute-start | bytes 1179656 | tf_op jit(solution)/shard_map/ppermute | solution.py:218
  63.0 26.6 %collective-permute-start.5 = (bf16[192,1024]{1,0:T(8,128)(2,1)S(1)}, bf16[192,1024]{1,0:T(8,128)(2,1)S(1)}, u32[]{:S(2)}, u32[]{:S(2)}) collective-permute-start(bf16[192,1024]{1,0:T(8,128)(2,1)S(1)} %get-tuple-element.28), channel_id=1, source_target_pairs={{0,2},{1,3},{2,0},{3,1},{4,6},{5,7},{6,4},{7,5},{8,10},{9,11},{10,... | collective-permute-start | bytes 1179656 | tf_op jit(solution)/shard_map/ppermute | solution.py:218
  73.0 38.5 %collective-permute-start.17 = (bf16[512,512]{1,0:T(8,128)(2,1)S(1)}, bf16[512,512]{1,0:T(8,128)(2,1)S(1)}, u32[]{:S(2)}, u32[]{:S(2)}) collective-permute-start(bf16[512,512]{1,0:T(8,128)(2,1)S(1)} %plane_partial.6), channel_id=1, source_target_pairs={{0,4},{1,5},{2,6},{3,7},{4,8},{5,9},{6,10},{7,11},{8,12},{9,13},{1... | collective-permute-start | bytes 1572872 | tf_op jit(solution)/shard_map/ppermute | solution.py:215
  83.0 12.7 %collective-permute-start.6 = (bf16[192,1024]{1,0:T(8,128)(2,1)S(1)}, bf16[192,1024]{1,0:T(8,128)(2,1)S(1)}, u32[]{:S(2)}, u32[]{:S(2)}) collective-permute-start(bf16[192,1024]{1,0:T(8,128)(2,1)S(1)} %get-tuple-element.29), channel_id=1, source_target_pairs={{0,3},{1,2},{2,1},{3,0},{4,7},{5,6},{6,5},{7,4},{8,11},{9,10},{10,... | collective-permute-start | bytes 1179656 | tf_op jit(solution)/shard_map/ppermute | solution.py:218
  88.2 19.1 %collective-permute-start.10 = (bf16[192,1024]{1,0:T(8,128)(2,1)S(1)}, bf16[192,1024]{1,0:T(8,128)(2,1)S(1)}, u32[]{:S(2)}, u32[]{:S(2)}) collective-permute-start(bf16[192,1024]{1,0:T(8,128)(2,1)S(1)} %get-tuple-element.32), channel_id=1, source_target_pairs={{0,2},{1,3},{2,0},{3,1},{4,6},{5,7},{6,4},{7,5},{8,10},{9,11},{10,... | collective-permute-start | bytes 1179656 | tf_op jit(solution)/shard_map/ppermute | solution.py:218
  89.6 17.8 %collective-permute-start.11 = (bf16[192,1024]{1,0:T(8,128)(2,1)S(1)}, bf16[192,1024]{1,0:T(8,128)(2,1)S(1)}, u32[]{:S(2)}, u32[]{:S(2)}) collective-permute-start(bf16[192,1024]{1,0:T(8,128)(2,1)S(1)} %get-tuple-element.33), channel_id=1, source_target_pairs={{0,3},{1,2},{2,1},{3,0},{4,7},{5,6},{6,5},{7,4},{8,11},{9,10},{10,... | collective-permute-start | bytes 1179656 | tf_op jit(solution)/shard_map/ppermute | solution.py:218
  91.3 17.3 %collective-permute-start.9 = (bf16[192,1024]{1,0:T(8,128)(2,1)S(1)}, bf16[192,1024]{1,0:T(8,128)(2,1)S(1)}, u32[]{:S(2)}, u32[]{:S(2)}) collective-permute-start(bf16[192,1024]{1,0:T(8,128)(2,1)S(1)} %get-tuple-element.31), channel_id=1, source_target_pairs={{0,1},{1,0},{2,3},{3,2},{4,5},{5,4},{6,7},{7,6},{8,9},{9,8},{10,11... | collective-permute-start | bytes 1179656 | tf_op jit(solution)/shard_map/ppermute | solution.py:218
  108.6 4.0 %copy-start.7 = (f32[1,512,512]{2,1,0:T(8,128)S(1)}, f32[1,512,512]{2,1,0:T(8,128)}, u32[]{:S(2)}) copy-start(f32[1,512,512]{2,1,0:T(8,128)} %param.12) | copy-start | bytes 3145732
  108.6 4.0 %copy-start.8 = (f32[1,512,512]{2,1,0:T(8,128)S(1)}, f32[1,512,512]{2,1,0:T(8,128)}, u32[]{:S(2)}) copy-start(f32[1,512,512]{2,1,0:T(8,128)} %param.11) | copy-start | bytes 3145732

commit v3 on v2

--- a/solution.py
+++ b/solution.py
@@ -19,6 +19,7 @@
 PLANE = 4
 WEIGHT_SCALE = 2.0**17
 WIRE = jnp.bfloat16
+SPAN = pl.CostEstimate(flops=1 << 36, bytes_accessed=1 << 30, transcendentals=0)
 
 
 def power_below(limit):
@@ -52,10 +53,20 @@
     return lax.dot_general(left, right, (dims, ((), ())), preferred_element_type=jnp.float32)
 
 
-def pack_kernel(columns, planes, axis, features, cot, weight, coded, own, *chunks):
+def pack_kernel(columns, planes, axis, features_far, cot_in, weight_far, coded, weight, cot, own, *refs):
+    chunks, (features, sem) = refs[:-2], refs[-2:]
     me = lax.axis_index(axis)
     z, p = me // PLANE, me % PLANE
+    copies = [
+        pltpu.make_async_copy(weight_far.at[0], weight, sem.at[0]),
+        pltpu.make_async_copy(features_far, features, sem.at[1]),
+    ]
+    for copy in copies:
+        copy.start()
+    cot[...] = cot_in[...]
+    copies[0].wait()
     coded[...] = encode(weight[...] * WEIGHT_SCALE)
+    copies[1].wait()
     for k in range(PLANE):
         if k > 0:
             first, rest = chunks[2 * k - 2], chunks[2 * k - 1]
@@ -75,16 +86,22 @@
 def pack(features, cot, weight, columns, planes):
     rows = features.shape[0]
     widths = [planes * columns] + [cot.shape[1] + columns, (planes - 1) * columns] * (PLANE - 1)
-    coded, own, *chunks = pl.pallas_call(
+    coded, weight, cot, own, *chunks = pl.pallas_call(
         functools.partial(pack_kernel, columns, planes, "fsdp"),
-        out_shape=[jax.ShapeDtypeStruct(weight.shape, WIRE)]
+        out_shape=[
+            jax.ShapeDtypeStruct(weight.shape[1:], WIRE),
+            jax.ShapeDtypeStruct(weight.shape[1:], weight.dtype),
+            jax.ShapeDtypeStruct(cot.shape, cot.dtype),
+        ]
         + [jax.ShapeDtypeStruct((rows, width), features.dtype) for width in widths],
-        in_specs=vmem(3),
-        out_specs=vmem(1 + len(widths)),
-        compiler_params=pltpu.CompilerParams(vmem_limit_bytes=32 << 20),
+        in_specs=[pl.BlockSpec(memory_space=pltpu.HBM), *vmem(1), pl.BlockSpec(memory_space=pltpu.HBM)],
+        out_specs=vmem(3 + len(widths)),
+        scratch_shapes=[pltpu.VMEM(features.shape, features.dtype), pltpu.SemaphoreType.DMA((2,))],
+        cost_estimate=SPAN,
+        compiler_params=pltpu.CompilerParams(vmem_limit_bytes=48 << 20),
         name="pack",
     )(features, cot, weight)
-    return coded, own, [chunks[2 * k : 2 * k + 2] for k in range(PLANE - 1)]
+    return coded, weight, cot, own, [chunks[2 * k : 2 * k + 2] for k in range(PLANE - 1)]
 
 
 def partial_kernel(at, columns, scale, own, cot, *refs):
@@ -112,13 +129,14 @@
         out_shape=jax.ShapeDtypeStruct((columns, cot.shape[1]), dtype),
         in_specs=vmem(len(operands)),
         out_specs=pl.BlockSpec(memory_space=pltpu.VMEM),
+        cost_estimate=SPAN,
         compiler_params=pltpu.CompilerParams(vmem_limit_bytes=32 << 20),
         name="plane_partial",
     )(*operands)
 
 
 def product_kernel(count, scale, *refs):
-    weights, cot, firsts, outs = refs[:count], refs[count], refs[count + 1 : count + PLANE], refs[count + PLANE :]
+    weights, cot, firsts, outs = refs[:count], refs[count], refs[count + 1 : count + PLANE], refs[-PLANE:]
     depth = cot.shape[1]
     for i, weight in enumerate(weights):
         if weight.dtype == WIRE:
@@ -135,61 +153,64 @@
             outs[k][:, i * columns : (i + 1) * columns] = result
 
 
-def plane_product(weights, cot, firsts, scale):
+def product_shapes(weights, cot):
     shape = (cot.shape[0], weights[0].shape[0] * len(weights))
+    return [jax.ShapeDtypeStruct(shape, jnp.float32 if k == 0 else WIRE) for k in range(PLANE)]
+
+
+def plane_product(weights, cot, firsts, after, scale):
     return pl.pallas_call(
         functools.partial(product_kernel, len(weights), scale),
-        out_shape=[jax.ShapeDtypeStruct(shape, jnp.float32 if k == 0 else WIRE) for k in range(PLANE)],
-        in_specs=vmem(len(weights) + PLANE),
+        out_shape=product_shapes(weights, cot),
+        in_specs=vmem(len(weights) + PLANE) + [pl.BlockSpec(memory_space=pl.ANY)],
         out_specs=vmem(PLANE),
+        cost_estimate=SPAN,
         compiler_params=pltpu.CompilerParams(vmem_limit_bytes=32 << 20),
         name="plane_product",
-    )(*weights, cot, *firsts)
-
-
-def unpack_kernel(columns, planes, axis, factor, widths, *refs):
-    pieces, out, buffer, sem = refs[:-3], refs[-3], refs[-2], refs[-1]
+    )(*weights, cot, *firsts, after)
+
+
+def unpack_kernel(columns, planes, axis, factor, offsets, *refs):
+    pieces, out, buffer, sem = refs[:PLANE], refs[-3], refs[-2], refs[-1]
     me = lax.axis_index(axis)
     z, p = me // PLANE, me % PLANE
     copies = []
-    at = 0
-    for chunk, width in enumerate(widths):
-        for inner in range(width):
-            block = lax.rem(z + planes - at, planes)
-            for k in range(PLANE):
-                i = at * PLANE + k
-                piece = pieces[chunk * PLANE + k]
-                span = slice(inner * columns, (inner + 1) * columns)
-                if k == 0:
-                    source = piece.at[:, span]
-                else:
-                    buffer[i] = decode(piece[:, span]) * factor
-                    source = buffer.at[i]
-                start = pl.multiple_of((block * PLANE + (p ^ k)) * columns, 128)
-                copy = pltpu.make_async_copy(source, out.at[:, pl.ds(start, columns)], sem.at[i])
-                copy.start()
-                copies.append(copy)
-            at += 1
+    for inner, offset in enumerate(offsets):
+        block = lax.rem(z + planes - offset, planes)
+        for k in range(PLANE):
+            i = inner * PLANE + k
+            span = slice(inner * columns, (inner + 1) * columns)
+            if k == 0:
+                source = pieces[k].at[:, span]
+            else:
+                buffer[i] = decode(pieces[k][:, span]) * factor
+                source = buffer.at[i]
+            start = pl.multiple_of((block * PLANE + (p ^ k)) * columns, 128)
+            copy = pltpu.make_async_copy(source, out.at[:, pl.ds(start, columns)], sem.at[i])
+            copy.start()
+            copies.append(copy)
     for copy in copies:
         copy.wait()
 
 
-def unpack(pieces, columns, planes, factor):
+def unpack(pieces, out, after, offsets, columns, planes, factor):
     rows = pieces[0].shape[0]
-    count = planes * PLANE
-    widths = [piece.shape[1] // columns for piece in pieces[::PLANE]]
+    count = len(offsets) * PLANE
+    others = [*out, *after]
     return pl.pallas_call(
-        functools.partial(unpack_kernel, columns, planes, "fsdp", factor, widths),
-        out_shape=jax.ShapeDtypeStruct((rows, columns * count), jnp.float32),
-        in_specs=vmem(len(pieces)),
+        functools.partial(unpack_kernel, columns, planes, "fsdp", factor, offsets),
+        out_shape=jax.ShapeDtypeStruct((rows, columns * planes * PLANE), jnp.float32),
+        in_specs=vmem(PLANE) + [pl.BlockSpec(memory_space=pl.ANY)] * len(others),
         out_specs=pl.BlockSpec(memory_space=pl.ANY),
         scratch_shapes=[
             pltpu.VMEM((count, rows, columns), jnp.float32),
             pltpu.SemaphoreType.DMA((count,)),
         ],
-        compiler_params=pltpu.CompilerParams(vmem_limit_bytes=40 << 20),
+        input_output_aliases={PLANE: 0} if out else {},
+        cost_estimate=SPAN,
+        compiler_params=pltpu.CompilerParams(vmem_limit_bytes=32 << 20),
         name="unpack",
-    )(*pieces)
+    )(*pieces, *others)
 
 
 def on_device(
@@ -214,40 +235,41 @@
     def around(x):
         return lax.ppermute(x, "fsdp", ring)
 
+    def back(x):
+        return lax.ppermute(x, "fsdp", [(to, source) for source, to in ring])
+
     def across(x, k):
         return lax.ppermute(x, "fsdp", [(i, i ^ k) for i in range(size)])
 
-    weight = value_weight[0]
-    travelling, own, chunks = pack(features, value_cotangent, weight, columns, planes)
-    weights = [weight]
-    for _ in range(1, planes):
-        travelling = around(travelling)
-        weights.append(travelling)
+    workers = lax.axis_size("worker")
+    coded, weight, cot, own, chunks = pack(features, value_cotangent, value_weight, columns, planes)
     firsts = [across(first, k + 1) for k, (first, _) in enumerate(chunks)]
     others = [across(rest, k + 1) for k, (_, rest) in enumerate(chunks)]
 
-    pieces = []
-    for half in (weights[: planes // 2], weights[planes // 2 :]):
-        products = plane_product(half, value_cotangent, firsts, product_scale)
-        pieces += [part if k == 0 else across(part, k) for k, part in enumerate(products)]
-    feature_grad = unpack(pieces, columns, planes, 1.0 / product_scale)
-
-    running = []
-    for at in range(planes):
+    early_offsets, late_offsets = (0, 1, planes - 1), tuple(range(2, planes - 1))
+    travelling, ahead = around(coded), back(coded)
+    travelling, firsts = lax.optimization_barrier((travelling, firsts))
+    early_weights, late_weights = [weight, travelling, ahead], []
+    for _ in late_offsets:
+        travelling = around(travelling)
+        late_weights.append(travelling)
+
+    total = plane_partial(0, own, cot, firsts, [], [], columns, gradient_scale, WIRE)
+    products = plane_product(early_weights, cot, firsts, total, product_scale)
+    early = [part if k == 0 else across(part, k) for k, part in enumerate(products)]
+    for at in range(1, planes):
+        running = around(total)
+        if at == 1:
+            running, early[0] = lax.optimization_barrier((running, early[0]))
         last = at == planes - 1
-        total = plane_partial(
-            at,
-            own,
-            value_cotangent,
-            firsts,
-            others if at > 0 else [],
-            running,
-            columns,
-            gradient_scale,
-            jnp.float32 if last else WIRE,
-        )
-        running = [total if last else around(total)]
-    gradient = running[0] * (1.0 / gradient_scale)
+        dtype = jnp.float32 if last else WIRE
+        total = plane_partial(at, own, cot, firsts, others, [running], columns, gradient_scale, dtype)
+        if at == planes - 2:
+            total, fragment_local = lax.optimization_barrier((total, fragment_local))
+            mark = total
+            products = plane_product(late_weights, cot, firsts, mark, product_scale)
+            late = [part if k == 0 else across(part, k) for k, part in enumerate(products)]
+    gradient = total * (1.0 / gradient_scale)
 
     first_new = first_decay * first_moment[0] + (1.0 - first_decay) * gradient
     second_new = second_decay * second_moment[0] + (1.0 - second_decay) * gradient * gradient
@@ -256,15 +278,21 @@
     weight_new = weight - inner_rate * (
         first_hat / (jnp.sqrt(second_hat) + adam_epsilon) + weight_decay * weight
     )
-    workers = lax.axis_size("worker")
     difference = fragment_anchor - fragment_local[0]
     if workers == 2:
-        pseudo_sum = difference + lax.ppermute(difference, "worker", [(0, 1), (1, 0)])
+        partner_local = lax.ppermute(fragment_local, "worker", [(0, 1), (1, 0)])
+        pseudo_sum = difference + (fragment_anchor - partner_local[0])
     else:
         pseudo_sum = lax.psum(difference, "worker")
     pseudo_mean = pseudo_sum / workers
     new_momentum = outer_mass * outer_momentum + pseudo_mean
     new_anchor = fragment_anchor - outer_rate * (pseudo_mean + outer_mass * new_momentum)
+
+    factor = 1.0 / product_scale
+    feature_grad = unpack(early, [], [mark], early_offsets, columns, planes, factor)
+    feature_grad = unpack(
+        late, [feature_grad], [first_new, new_momentum], late_offsets, columns, planes, factor
+    )
     return (
         feature_grad,
         weight_new[None],

time: 115 us -> 97.2 us (0.85)
  waiting for transfers between devices: 66.8 us -> 48.6 us
  local copies, waits for them, and re-layouts: 4.06 us -> 0.96 us
  Pallas kernels: 14.9 us -> 17.9 us
    ppermute x12, waiting for transfers between devices: 49 us -> 22.3 us  [across(): return lax.ppermute(x, 'fsdp', [(i, i ^ k) for i in range(size)])]
    ppermute x6 -> x5, waiting for transfers between devices: 17.8 us -> 26.3 us  [around(): return lax.ppermute(x, 'fsdp', ring)]
    unnamed x20 -> x16, local copies, waits for them, and re-layouts: 4.06 us -> 0.96 us
    ppermute x1 -> x2, starting transfers between devices: 0.01 us -> 2.11 us  [the longest x1 2.1 us: back(): return lax.ppermute(x, 'fsdp', [(to, source) for source, to in ring])]
    pallas_call x1, Pallas kernels: 0.48 us -> 2.52 us  [pack(): pl.pallas_call(functools.partial(pack_kernel, columns, planes, 'fsdp'), o...]
    ppermute x6 -> x5, starting transfers between devices: 9.72 us -> 8.15 us  [around(): return lax.ppermute(x, 'fsdp', ring)]
    pallas_call x1 -> x2, Pallas kernels: 2.91 us -> 3.88 us  [unpack(): pl.pallas_call(functools.partial(unpack_kernel, columns, planes, 'fsdp',...]
  transfers between devices with their start and end apart: 19 -> 19, of which waited for: 10 -> 7; matrix products, arithmetic and copies ran while one was open for 2% -> 4% of each run, Pallas kernels for 12% -> 13%
where the time goes in v3:
time: 97.2 us; the launch traced here: 97 us
  waiting for transfers between devices  48.6 us (50%)
  starting transfers between devices  24.8 us (26%)
  Pallas kernels  17.9 us (18%)
  other arithmetic  3.65 us (4%)
  between operations  0.98 us (1%)
    ppermute x5, waiting for transfers between devices, around(): return lax.ppermute(x, 'fsdp', ring)  26.3 us
    ppermute x12, waiting for transfers between devices, across(): return lax.ppermute(x, 'fsdp', [(i, i ^ k) for i in range(size)])  22.3 us
    ppermute x12, starting transfers between devices, across(): return lax.ppermute(x, 'fsdp', [(i, i ^ k) for i in range(size)])  14.6 us
    ppermute x5, starting transfers between devices, around(): return lax.ppermute(x, 'fsdp', ring)  8.15 us
    pallas_call x2, Pallas kernels, plane_product(): pl.pallas_call(functools.partial(product_kernel, len(weights), scale), ou...  7.11 us
    pallas_call x4, Pallas kernels, plane_partial(): pl.pallas_call(functools.partial(partial_kernel, at, columns, scale), out...  4.44 us
    pallas_call x2, Pallas kernels, unpack(): pl.pallas_call(functools.partial(unpack_kernel, columns, planes, 'fsdp',...  3.88 us
    pallas_call x1, Pallas kernels, pack(): pl.pallas_call(functools.partial(pack_kernel, columns, planes, 'fsdp'), o...  2.52 us
  transfers between devices with their start and end apart: 19, of which 7 were waited for; matrix products, arithmetic and copies ran while one was open for 4% of the time, Pallas kernels for 13%

profile of v3, /device:TPU:0, one launch (start us, length us, event | category | flops | bytes accessed | tf_op | source)
XLA Modules:
  0.0 97.0 jit_solution(7293394195296951647)
XLA Ops:
  0.6 0.9 copy-done.2
  1.6 2.5 %pack.1 = (bf16[512,512]{1,0:T(8,128)(2,1)S(1)}, f32[512,512]{1,0:T(8,128)S(1)}, bf16[192,512]{1,0:T(8,128)(2,1)S(1)}, bf16[192,2048]{1,0:T(8,128)(2,1)S(1)}, bf...) custom-call(bf16[192,8192]{1,0:T(8,128)(2,1)} %features_far.1, ...), custom_call_target="tpu_custom_call" | custom-call | flops 68719476736 | bytes 1073741824 | tf_op jit(solution)/shard_map/pack/pallas_call | solution.py:89
  4.1 3.1 %collective-permute-start = (bf16[512,512]{1,0:T(8,128)(2,1)S(1)}, bf16[512,512]{1,0:T(8,128)(2,1)S(1)}, u32[]{:S(2)}, u32[]{:S(2)}) collective-permute-start(bf16[512,512]{1,0:T(8,128)(2,1)S(1)} %get-tuple-element.32), channel_id=1, source_target_pairs={{0,4},{1,5},{2,6},{3,7},{4,8},{5,9},{6,10},{7,11},{8,12},{9,13},{1... | collective-permute-start | bytes 1572872 | tf_op jit(solution)/shard_map/ppermute | solution.py:236
  7.2 1.5 %collective-permute-start.1 = (bf16[192,1024]{1,0:T(8,128)(2,1)S(1)}, bf16[192,1024]{1,0:T(8,128)(2,1)S(1)}, u32[]{:S(2)}, u32[]{:S(2)}) collective-permute-start(bf16[192,1024]{1,0:T(8,128)(2,1)S(1)} %get-tuple-element.33), channel_id=1, source_target_pairs={{0,1},{1,0},{2,3},{3,2},{4,5},{5,4},{6,7},{7,6},{8,9},{9,8},{10,11... | collective-permute-start | bytes 1179656 | tf_op jit(solution)/shard_map/ppermute | solution.py:242
  8.7 1.5 %collective-permute-start.2 = (bf16[192,1024]{1,0:T(8,128)(2,1)S(1)}, bf16[192,1024]{1,0:T(8,128)(2,1)S(1)}, u32[]{:S(2)}, u32[]{:S(2)}) collective-permute-start(bf16[192,1024]{1,0:T(8,128)(2,1)S(1)} %get-tuple-element.34), channel_id=1, source_target_pairs={{0,2},{1,3},{2,0},{3,1},{4,6},{5,7},{6,4},{7,5},{8,10},{9,11},{10,... | collective-permute-start | bytes 1179656 | tf_op jit(solution)/shard_map/ppermute | solution.py:242
  10.7 2.1 %collective-permute-start.9 = (bf16[512,512]{1,0:T(8,128)(2,1)S(1)}, bf16[512,512]{1,0:T(8,128)(2,1)S(1)}, u32[]{:S(2)}, u32[]{:S(2)}) collective-permute-start(bf16[512,512]{1,0:T(8,128)(2,1)S(1)} %get-tuple-element.32), channel_id=1, source_target_pairs={{4,0},{5,1},{6,2},{7,3},{8,4},{9,5},{10,6},{11,7},{12,8},{13,9},{1... | collective-permute-start | bytes 1572872 | tf_op jit(solution)/shard_map/ppermute | solution.py:239
  12.8 6.4 %collective-permute-done.1.refs_0_.refs_4_.refs_2_ = bf16[192,1024]{1,0:T(8,128)(2,1)S(1)} collective-permute-done((bf16[192,1024]{1,0:T(8,128)(2,1)S(1)}, bf16[192,1024]{1,0:T(8,128)(2,1)S(1)}, u32[]{:S(2)}, u32[]{:S(2)}) %collective-permute-start.1) | collective-permute-done | bytes 393248 | tf_op jit(solution)/shard_map/ppermute | solution.py:242
  19.2 1.5 %collective-permute-start.5 = (bf16[192,1536]{1,0:T(8,128)(2,1)S(1)}, bf16[192,1536]{1,0:T(8,128)(2,1)S(1)}, u32[]{:S(2)}, u32[]{:S(2)}) collective-permute-start(bf16[192,1536]{1,0:T(8,128)(2,1)S(1)} %get-tuple-element.42), channel_id=1, source_target_pairs={{0,1},{1,0},{2,3},{3,2},{4,5},{5,4},{6,7},{7,6},{8,9},{9,8},{10,11... | collective-permute-start | bytes 1769480 | tf_op jit(solution)/shard_map/ppermute | solution.py:242
  20.7 6.8 %collective-permute-done.2.refs_1_.refs_5_.refs_3_ = bf16[192,1024]{1,0:T(8,128)(2,1)S(1)} collective-permute-done((bf16[192,1024]{1,0:T(8,128)(2,1)S(1)}, bf16[192,1024]{1,0:T(8,128)(2,1)S(1)}, u32[]{:S(2)}, u32[]{:S(2)}) %collective-permute-start.2) | collective-permute-done | bytes 393248 | tf_op jit(solution)/shard_map/ppermute | solution.py:242
  27.5 2.5 %collective-permute-start.6 = (bf16[192,1536]{1,0:T(8,128)(2,1)S(1)}, bf16[192,1536]{1,0:T(8,128)(2,1)S(1)}, u32[]{:S(2)}, u32[]{:S(2)}) collective-permute-start(bf16[192,1536]{1,0:T(8,128)(2,1)S(1)} %get-tuple-element.43), channel_id=1, source_target_pairs={{0,2},{1,3},{2,0},{3,1},{4,6},{5,7},{6,4},{7,5},{8,10},{9,11},{10,... | collective-permute-start | bytes 1769480 | tf_op jit(solution)/shard_map/ppermute | solution.py:242
  30.1 0.9 plane_partial.4.refs_7_
  31.0 1.6 %collective-permute-start.8 = (bf16[512,512]{1,0:T(8,128)(2,1)S(1)}, bf16[512,512]{1,0:T(8,128)(2,1)S(1)}, u32[]{:S(2)}, u32[]{:S(2)}) collective-permute-start(bf16[512,512]{1,0:T(8,128)(2,1)S(1)} %plane_partial.4.refs_7_), channel_id=1, source_target_pairs={{0,4},{1,5},{2,6},{3,7},{4,8},{5,9},{6,10},{7,11},{8,12},{9,13},{1... | collective-permute-start | bytes 1572872 | tf_op jit(solution)/shard_map/ppermute | solution.py:236
  32.6 5.1 %plane_product.2 = (f32[192,1536]{1,0:T(8,128)S(1)}, bf16[192,1536]{1,0:T(8,128)(2,1)S(1)}, bf16[192,1536]{1,0:T(8,128)(2,1)S(1)}, bf16[192,1536]{1,0:T(8,128)(2,1)S(1)}) custom-call(f32[512,512]{1,0:T(8,128)S(1)} %get-tuple-element.45.refs_0_, bf16[512,512]{1,0:T(8,128)(2,1)S(1)} %collective-permute-done.refs_1_, ...), custom_call_target="tpu_custom_call" | custom-call | flops 68719476736 | bytes 1073741824 | tf_op jit(solution)/shard_map/plane_product/pallas_call | solution.py:162
  37.7 5.9 %collective-permute-done.8.refs_6_ = bf16[512,512]{1,0:T(8,128)(2,1)S(1)} collective-permute-done((bf16[512,512]{1,0:T(8,128)(2,1)S(1)}, bf16[512,512]{1,0:T(8,128)(2,1)S(1)}, u32[]{:S(2)}, u32[]{:S(2)}) %collective-permute-start.8) | collective-permute-done | bytes 524320 | tf_op jit(solution)/shard_map/ppermute | solution.py:236
  43.6 9.0 %collective-permute-done.6.refs_4_ = bf16[192,1536]{1,0:T(8,128)(2,1)S(1)} collective-permute-done((bf16[192,1536]{1,0:T(8,128)(2,1)S(1)}, bf16[192,1536]{1,0:T(8,128)(2,1)S(1)}, u32[]{:S(2)}, u32[]{:S(2)}) %collective-permute-start.6) | collective-permute-done | bytes 589856 | tf_op jit(solution)/shard_map/ppermute | solution.py:242
  52.7 1.3 %plane_partial.5 = bf16[512,512]{1,0:T(8,128)(2,1)S(1)} custom-call(bf16[192,2048]{1,0:T(8,128)(2,1)S(1)} %get-tuple-element.41.own, bf16[192,512]{1,0:T(8,128)(2,1)S(1)} %get-tuple-element.37.cot.refs_3_.refs_1_, bf16[192,1024]{1,0:T(8,128)(2,1)S(1)} %collective-permute-done.1.refs_0_.refs_4_.refs_2_, ...), custom_call_target="tpu_custom_call" | custom-call | flops 68719476736 | bytes 1073741824 | tf_op jit(solution)/shard_map/plane_partial/pallas_call | solution.py:127
  53.9 1.6 %collective-permute-start.10 = (bf16[512,512]{1,0:T(8,128)(2,1)S(1)}, bf16[512,512]{1,0:T(8,128)(2,1)S(1)}, u32[]{:S(2)}, u32[]{:S(2)}) collective-permute-start(bf16[512,512]{1,0:T(8,128)(2,1)S(1)} %plane_partial.5), channel_id=1, source_target_pairs={{0,4},{1,5},{2,6},{3,7},{4,8},{5,9},{6,10},{7,11},{8,12},{9,13},{1... | collective-permute-start | bytes 1572872 | tf_op jit(solution)/shard_map/ppermute | solution.py:236
  55.6 1.6 %collective-permute-start.4 = (bf16[512,512]{1,0:T(8,128)(2,1)S(1)}, bf16[512,512]{1,0:T(8,128)(2,1)S(1)}, u32[]{:S(2)}, u32[]{:S(2)}) collective-permute-start(bf16[512,512]{1,0:T(8,128)(2,1)S(1)} %collective-permute-done.refs_1_), channel_id=1, source_target_pairs={{0,4},{1,5},{2,6},{3,7},{4,8},{5,9},{6,10},{7,11},{8,12},{9,13},{1... | collective-permute-start | bytes 1572872 | tf_op jit(solution)/shard_map/ppermute | solution.py:236
  57.1 1.3 %collective-permute-start.14 = (bf16[192,1536]{1,0:T(8,128)(2,1)S(1)}, bf16[192,1536]{1,0:T(8,128)(2,1)S(1)}, u32[]{:S(2)}, u32[]{:S(2)}) collective-permute-start(bf16[192,1536]{1,0:T(8,128)(2,1)S(1)} %get-tuple-element.54), channel_id=1, source_target_pairs={{0,1},{1,0},{2,3},{3,2},{4,5},{5,4},{6,7},{7,6},{8,9},{9,8},{10,11... | collective-permute-start | bytes 1769480 | tf_op jit(solution)/shard_map/ppermute | solution.py:242
  59.2 1.4 %collective-permute-start.16 = (bf16[192,1536]{1,0:T(8,128)(2,1)S(1)}, bf16[192,1536]{1,0:T(8,128)(2,1)S(1)}, u32[]{:S(2)}, u32[]{:S(2)}) collective-permute-start(bf16[192,1536]{1,0:T(8,128)(2,1)S(1)} %get-tuple-element.56), channel_id=1, source_target_pairs={{0,3},{1,2},{2,1},{3,0},{4,7},{5,6},{6,5},{7,4},{8,11},{9,10},{10,... | collective-permute-start | bytes 1769480 | tf_op jit(solution)/shard_map/ppermute | solution.py:242
  60.6 10.0 %collective-permute-done.10.refs_6_ = bf16[512,512]{1,0:T(8,128)(2,1)S(1)} collective-permute-done((bf16[512,512]{1,0:T(8,128)(2,1)S(1)}, bf16[512,512]{1,0:T(8,128)(2,1)S(1)}, u32[]{:S(2)}, u32[]{:S(2)}) %collective-permute-start.10) | collective-permute-done | bytes 524320 | tf_op jit(solution)/shard_map/ppermute | solution.py:236
  70.6 1.3 %plane_partial.6.refs_5_.refs_4_ = bf16[512,512]{1,0:T(8,128)(2,1)S(1)} custom-call(bf16[192,2048]{1,0:T(8,128)(2,1)S(1)} %get-tuple-element.41.own, bf16[192,512]{1,0:T(8,128)(2,1)S(1)} %get-tuple-element.37.cot.refs_3_.refs_1_, bf16[192,1024]{1,0:T(8,128)(2,1)S(1)} %collective-permute-done.1.refs_0_.refs_4_.refs_2_, ...), custom_call_target="tpu_custom_call" | custom-call | flops 68719476736 | bytes 1073741824 | tf_op jit(solution)/shard_map/plane_partial/pallas_call | solution.py:127
  72.2 9.7 %collective-permute-done.4.refs_0_ = bf16[512,512]{1,0:T(8,128)(2,1)S(1)} collective-permute-done((bf16[512,512]{1,0:T(8,128)(2,1)S(1)}, bf16[512,512]{1,0:T(8,128)(2,1)S(1)}, u32[]{:S(2)}, u32[]{:S(2)}) %collective-permute-start.4) | collective-permute-done | bytes 524320 | tf_op jit(solution)/shard_map/ppermute | solution.py:236
  81.9 2.0 %plane_product.3 = (f32[192,512]{1,0:T(8,128)S(1)}, bf16[192,512]{1,0:T(8,128)(2,1)S(1)}, bf16[192,512]{1,0:T(8,128)(2,1)S(1)}, bf16[192,512]{1,0:T(8,128)(2,1)S(1)}) custom-call(bf16[512,512]{1,0:T(8,128)(2,1)S(1)} %collective-permute-done.4.refs_0_, bf16[192,512]{1,0:T(8,128)(2,1)S(1)} %get-tuple-element.37.cot.refs_3_.refs_1_, ...), custom_call_target="tpu_custom_call" | custom-call | flops 68719476736 | bytes 1073741824 | tf_op jit(solution)/shard_map/plane_product/pallas_call | solution.py:162
  83.9 1.3 %collective-permute-start.11 = (bf16[192,512]{1,0:T(8,128)(2,1)S(1)}, bf16[192,512]{1,0:T(8,128)(2,1)S(1)}, u32[]{:S(2)}, u32[]{:S(2)}) collective-permute-start(bf16[192,512]{1,0:T(8,128)(2,1)S(1)} %get-tuple-element.50), channel_id=1, source_target_pairs={{0,1},{1,0},{2,3},{3,2},{4,5},{5,4},{6,7},{7,6},{8,9},{9,8},{10,11... | collective-permute-start | bytes 589832 | tf_op jit(solution)/shard_map/ppermute | solution.py:242
  85.2 0.8 collective-permute-start.12
  86.0 1.4 %collective-permute-start.13 = (bf16[192,512]{1,0:T(8,128)(2,1)S(1)}, bf16[192,512]{1,0:T(8,128)(2,1)S(1)}, u32[]{:S(2)}, u32[]{:S(2)}) collective-permute-start(bf16[192,512]{1,0:T(8,128)(2,1)S(1)} %get-tuple-element.52), channel_id=1, source_target_pairs={{0,3},{1,2},{2,1},{3,0},{4,7},{5,6},{6,5},{7,4},{8,11},{9,10},{10,... | collective-permute-start | bytes 589832 | tf_op jit(solution)/shard_map/ppermute | solution.py:242
  87.5 2.4 %unpack.2.refs_4_ = f32[192,8192]{1,0:T(8,128)} custom-call(f32[192,1536]{1,0:T(8,128)S(1)} %get-tuple-element.53.refs_0_, bf16[192,1536]{1,0:T(8,128)(2,1)S(1)} %collective-permute-done.14.refs_1_, bf16[192,1536]{1,0:T(8,128)(2,1)S(1)} %collective-permute-done.15.refs_2_, bf16[192,1536]{1,0:T(8,128)(2,1)S(1)} %collective-permute-done.16.refs_3_, ...), custom_call_target="tpu_custom_call" | custom-call | flops 68719476736 | bytes 1073741824 | tf_op jit(solution)/shard_map/unpack/pallas_call | solution.py:200
  90.6 1.0 %plane_partial.7 = f32[512,512]{1,0:T(8,128)S(1)} custom-call(bf16[192,2048]{1,0:T(8,128)(2,1)S(1)} %get-tuple-element.41.own, bf16[192,512]{1,0:T(8,128)(2,1)S(1)} %get-tuple-element.37.cot.refs_3_.refs_1_, bf16[192,1024]{1,0:T(8,128)(2,1)S(1)} %collective-permute-done.1.refs_0_.refs_4_.refs_2_, ...), custom_call_target="tpu_custom_call" | custom-call | flops 68719476736 | bytes 1073741824 | tf_op jit(solution)/shard_map/plane_partial/pallas_call | solution.py:127
  91.7 2.1 %subtract_bitcast_fusion = (f32[1,512,512]{2,1,0:T(8,128)}, f32[512,512]{1,0:T(8,128)S(1)}, f32[1,512,512]{2,1,0:T(8,128)}) fusion(f32[512,512]{1,0:T(8,128)S(1)} %get-tuple-element.45.refs_0_, f32[512,512]{1,0:T(8,128)S(1)} %plane_partial.7, f32[1,512,512]{2,1,0:T(8,128)S(1)} %copy-done.3, f32[1,512,512]{2,1,0:T(8,128)S(1)} %copy-done.4), kind=kLoop, calls=%fused_computation.7 | loop fusion | flops 4194304 | bytes 7340032 | tf_op jit(solution)/shard_map/broadcast_in_dim | solution.py:298
  93.8 1.5 %multiply_subtract_fusion = (f32[512,512]{1,0:T(8,128)}, f32[512,512]{1,0:T(8,128)S(1)}) fusion(f32[512,512]{1,0:T(8,128)S(1)} %copy-done.5, f32[1,512,512]{2,1,0:T(8,128)S(1)} %collective-permute-done.18, f32[1,512,512]{2,1,0:T(8,128)S(1)} %copy-done.6, f32[512,512]{1,0:T(8,128)S(1)} %copy-done.7), kind=kLoop, calls=%fused_computation.6 | loop fusion | flops 2621440 | bytes 6291456 | tf_op jit(solution)/shard_map/sub | solution.py:289
  95.3 1.5 %unpack.3 = f32[192,8192]{1,0:T(8,128)} custom-call(f32[192,512]{1,0:T(8,128)S(1)} %get-tuple-element.49.refs_0_, bf16[192,512]{1,0:T(8,128)(2,1)S(1)} %collective-permute-done.11.refs_1_, bf16[192,512]{1,0:T(8,128)(2,1)S(1)} %collective-permute-done.12.refs_2_, ...), custom_call_target="tpu_custom_call", output_to_operand_aliasing={{}: (4, {})} | custom-call | flops 68719476736 | bytes 1073741824 | tf_op jit(solution)/shard_map/unpack/pallas_call | solution.py:200
  (33 shorter events, 2.3 us)
Async XLA Ops:
  0.6 0.9 copy-start.2
  4.1 26.0 %collective-permute-start = (bf16[512,512]{1,0:T(8,128)(2,1)S(1)}, bf16[512,512]{1,0:T(8,128)(2,1)S(1)}, u32[]{:S(2)}, u32[]{:S(2)}) collective-permute-start(bf16[512,512]{1,0:T(8,128)(2,1)S(1)} %get-tuple-element.32), channel_id=1, source_target_pairs={{0,4},{1,5},{2,6},{3,7},{4,8},{5,9},{6,10},{7,11},{8,12},{9,13},{1... | collective-permute-start | bytes 1572872 | tf_op jit(solution)/shard_map/ppermute | solution.py:236
  7.2 12.0 %collective-permute-start.1 = (bf16[192,1024]{1,0:T(8,128)(2,1)S(1)}, bf16[192,1024]{1,0:T(8,128)(2,1)S(1)}, u32[]{:S(2)}, u32[]{:S(2)}) collective-permute-start(bf16[192,1024]{1,0:T(8,128)(2,1)S(1)} %get-tuple-element.33), channel_id=1, source_target_pairs={{0,1},{1,0},{2,3},{3,2},{4,5},{5,4},{6,7},{7,6},{8,9},{9,8},{10,11... | collective-permute-start | bytes 1179656 | tf_op jit(solution)/shard_map/ppermute | solution.py:242
  8.7 18.8 %collective-permute-start.2 = (bf16[192,1024]{1,0:T(8,128)(2,1)S(1)}, bf16[192,1024]{1,0:T(8,128)(2,1)S(1)}, u32[]{:S(2)}, u32[]{:S(2)}) collective-permute-start(bf16[192,1024]{1,0:T(8,128)(2,1)S(1)} %get-tuple-element.34), channel_id=1, source_target_pairs={{0,2},{1,3},{2,0},{3,1},{4,6},{5,7},{6,4},{7,5},{8,10},{9,11},{10,... | collective-permute-start | bytes 1179656 | tf_op jit(solution)/shard_map/ppermute | solution.py:242
  10.2 19.8 %collective-permute-start.3 = (bf16[192,1024]{1,0:T(8,128)(2,1)S(1)}, bf16[192,1024]{1,0:T(8,128)(2,1)S(1)}, u32[]{:S(2)}, u32[]{:S(2)}) collective-permute-start(bf16[192,1024]{1,0:T(8,128)(2,1)S(1)} %get-tuple-element.35), channel_id=1, source_target_pairs={{0,3},{1,2},{2,1},{3,0},{4,7},{5,6},{6,5},{7,4},{8,11},{9,10},{10,... | collective-permute-start | bytes 1179656 | tf_op jit(solution)/shard_map/ppermute | solution.py:242
  10.7 21.9 %collective-permute-start.9 = (bf16[512,512]{1,0:T(8,128)(2,1)S(1)}, bf16[512,512]{1,0:T(8,128)(2,1)S(1)}, u32[]{:S(2)}, u32[]{:S(2)}) collective-permute-start(bf16[512,512]{1,0:T(8,128)(2,1)S(1)} %get-tuple-element.32), channel_id=1, source_target_pairs={{4,0},{5,1},{6,2},{7,3},{8,4},{9,5},{10,6},{11,7},{12,8},{13,9},{1... | collective-permute-start | bytes 1572872 | tf_op jit(solution)/shard_map/ppermute | solution.py:239
  19.2 24.4 %collective-permute-start.5 = (bf16[192,1536]{1,0:T(8,128)(2,1)S(1)}, bf16[192,1536]{1,0:T(8,128)(2,1)S(1)}, u32[]{:S(2)}, u32[]{:S(2)}) collective-permute-start(bf16[192,1536]{1,0:T(8,128)(2,1)S(1)} %get-tuple-element.42), channel_id=1, source_target_pairs={{0,1},{1,0},{2,3},{3,2},{4,5},{5,4},{6,7},{7,6},{8,9},{9,8},{10,11... | collective-permute-start | bytes 1769480 | tf_op jit(solution)/shard_map/ppermute | solution.py:242
  27.5 25.2 %collective-permute-start.6 = (bf16[192,1536]{1,0:T(8,128)(2,1)S(1)}, bf16[192,1536]{1,0:T(8,128)(2,1)S(1)}, u32[]{:S(2)}, u32[]{:S(2)}) collective-permute-start(bf16[192,1536]{1,0:T(8,128)(2,1)S(1)} %get-tuple-element.43), channel_id=1, source_target_pairs={{0,2},{1,3},{2,0},{3,1},{4,6},{5,7},{6,4},{7,5},{8,10},{9,11},{10,... | collective-permute-start | bytes 1769480 | tf_op jit(solution)/shard_map/ppermute | solution.py:242
  30.0 22.7 %collective-permute-start.7 = (bf16[192,1536]{1,0:T(8,128)(2,1)S(1)}, bf16[192,1536]{1,0:T(8,128)(2,1)S(1)}, u32[]{:S(2)}, u32[]{:S(2)}) collective-permute-start(bf16[192,1536]{1,0:T(8,128)(2,1)S(1)} %get-tuple-element.44), channel_id=1, source_target_pairs={{0,3},{1,2},{2,1},{3,0},{4,7},{5,6},{6,5},{7,4},{8,11},{9,10},{10,... | collective-permute-start | bytes 1769480 | tf_op jit(solution)/shard_map/ppermute | solution.py:242
  31.0 12.7 %collective-permute-start.8 = (bf16[512,512]{1,0:T(8,128)(2,1)S(1)}, bf16[512,512]{1,0:T(8,128)(2,1)S(1)}, u32[]{:S(2)}, u32[]{:S(2)}) collective-permute-start(bf16[512,512]{1,0:T(8,128)(2,1)S(1)} %plane_partial.4.refs_7_), channel_id=1, source_target_pairs={{0,4},{1,5},{2,6},{3,7},{4,8},{5,9},{6,10},{7,11},{8,12},{9,13},{1... | collective-permute-start | bytes 1572872 | tf_op jit(solution)/shard_map/ppermute | solution.py:236
  53.9 16.7 %collective-permute-start.10 = (bf16[512,512]{1,0:T(8,128)(2,1)S(1)}, bf16[512,512]{1,0:T(8,128)(2,1)S(1)}, u32[]{:S(2)}, u32[]{:S(2)}) collective-permute-start(bf16[512,512]{1,0:T(8,128)(2,1)S(1)} %plane_partial.5), channel_id=1, source_target_pairs={{0,4},{1,5},{2,6},{3,7},{4,8},{5,9},{6,10},{7,11},{8,12},{9,13},{1... | collective-permute-start | bytes 1572872 | tf_op jit(solution)/shard_map/ppermute | solution.py:236
  55.6 26.3 %collective-permute-start.4 = (bf16[512,512]{1,0:T(8,128)(2,1)S(1)}, bf16[512,512]{1,0:T(8,128)(2,1)S(1)}, u32[]{:S(2)}, u32[]{:S(2)}) collective-permute-start(bf16[512,512]{1,0:T(8,128)(2,1)S(1)} %collective-permute-done.refs_1_), channel_id=1, source_target_pairs={{0,4},{1,5},{2,6},{3,7},{4,8},{5,9},{6,10},{7,11},{8,12},{9,13},{1... | collective-permute-start | bytes 1572872 | tf_op jit(solution)/shard_map/ppermute | solution.py:236
  57.1 28.1 %collective-permute-start.14 = (bf16[192,1536]{1,0:T(8,128)(2,1)S(1)}, bf16[192,1536]{1,0:T(8,128)(2,1)S(1)}, u32[]{:S(2)}, u32[]{:S(2)}) collective-permute-start(bf16[192,1536]{1,0:T(8,128)(2,1)S(1)} %get-tuple-element.54), channel_id=1, source_target_pairs={{0,1},{1,0},{2,3},{3,2},{4,5},{5,4},{6,7},{7,6},{8,9},{9,8},{10,11... | collective-permute-start | bytes 1769480 | tf_op jit(solution)/shard_map/ppermute | solution.py:242
  58.4 27.6 %collective-permute-start.15 = (bf16[192,1536]{1,0:T(8,128)(2,1)S(1)}, bf16[192,1536]{1,0:T(8,128)(2,1)S(1)}, u32[]{:S(2)}, u32[]{:S(2)}) collective-permute-start(bf16[192,1536]{1,0:T(8,128)(2,1)S(1)} %get-tuple-element.55), channel_id=1, source_target_pairs={{0,2},{1,3},{2,0},{3,1},{4,6},{5,7},{6,4},{7,5},{8,10},{9,11},{10,... | collective-permute-start | bytes 1769480 | tf_op jit(solution)/shard_map/ppermute | solution.py:242
  59.2 28.3 %collective-permute-start.16 = (bf16[192,1536]{1,0:T(8,128)(2,1)S(1)}, bf16[192,1536]{1,0:T(8,128)(2,1)S(1)}, u32[]{:S(2)}, u32[]{:S(2)}) collective-permute-start(bf16[192,1536]{1,0:T(8,128)(2,1)S(1)} %get-tuple-element.56), channel_id=1, source_target_pairs={{0,3},{1,2},{2,1},{3,0},{4,7},{5,6},{6,5},{7,4},{8,11},{9,10},{10,... | collective-permute-start | bytes 1769480 | tf_op jit(solution)/shard_map/ppermute | solution.py:242
  71.9 15.5 %copy-start.6 = (f32[1,512,512]{2,1,0:T(8,128)S(1)}, f32[1,512,512]{2,1,0:T(8,128)}, u32[]{:S(2)}) copy-start(f32[1,512,512]{2,1,0:T(8,128)} %param.13) | copy-start | bytes 3145732
  71.9 18.6 %collective-permute-start.17 = (bf16[512,512]{1,0:T(8,128)(2,1)S(1)}, bf16[512,512]{1,0:T(8,128)(2,1)S(1)}, u32[]{:S(2)}, u32[]{:S(2)}) collective-permute-start(bf16[512,512]{1,0:T(8,128)(2,1)S(1)} %plane_partial.6.refs_5_.refs_4_), channel_id=1, source_target_pairs={{0,4},{1,5},{2,6},{3,7},{4,8},{5,9},{6,10},{7,11},{8,12},{9,13},{1... | collective-permute-start | bytes 1572872 | tf_op jit(solution)/shard_map/ppermute | solution.py:236
  83.9 11.4 %collective-permute-start.11 = (bf16[192,512]{1,0:T(8,128)(2,1)S(1)}, bf16[192,512]{1,0:T(8,128)(2,1)S(1)}, u32[]{:S(2)}, u32[]{:S(2)}) collective-permute-start(bf16[192,512]{1,0:T(8,128)(2,1)S(1)} %get-tuple-element.50), channel_id=1, source_target_pairs={{0,1},{1,0},{2,3},{3,2},{4,5},{5,4},{6,7},{7,6},{8,9},{9,8},{10,11... | collective-permute-start | bytes 589832 | tf_op jit(solution)/shard_map/ppermute | solution.py:242
  85.2 10.1 %collective-permute-start.12 = (bf16[192,512]{1,0:T(8,128)(2,1)S(1)}, bf16[192,512]{1,0:T(8,128)(2,1)S(1)}, u32[]{:S(2)}, u32[]{:S(2)}) collective-permute-start(bf16[192,512]{1,0:T(8,128)(2,1)S(1)} %get-tuple-element.51), channel_id=1, source_target_pairs={{0,2},{1,3},{2,0},{3,1},{4,6},{5,7},{6,4},{7,5},{8,10},{9,11},{10,... | collective-permute-start | bytes 589832 | tf_op jit(solution)/shard_map/ppermute | solution.py:242
  86.0 9.3 %collective-permute-start.13 = (bf16[192,512]{1,0:T(8,128)(2,1)S(1)}, bf16[192,512]{1,0:T(8,128)(2,1)S(1)}, u32[]{:S(2)}, u32[]{:S(2)}) collective-permute-start(bf16[192,512]{1,0:T(8,128)(2,1)S(1)} %get-tuple-element.52), channel_id=1, source_target_pairs={{0,3},{1,2},{2,1},{3,0},{4,7},{5,6},{6,5},{7,4},{8,11},{9,10},{10,... | collective-permute-start | bytes 589832 | tf_op jit(solution)/shard_map/ppermute | solution.py:242
  87.5 6.3 %collective-permute-start.18 = (f32[1,512,512]{2,1,0:T(8,128)S(1)}, f32[1,512,512]{2,1,0:T(8,128)S(1)}, u32[]{:S(2)}, u32[]{:S(2)}) collective-permute-start(f32[1,512,512]{2,1,0:T(8,128)S(1)} %copy-done.6), channel_id=1, source_target_pairs={{0,16},{16,0},{1,17},{17,1},{2,18},{18,2},{3,19},{19,3},{4,20},{20... | collective-permute-start | bytes 3145736 | tf_op jit(solution)/shard_map/ppermute | solution.py:283
  89.9 1.8 %copy-start.3 = (f32[1,512,512]{2,1,0:T(8,128)S(1)}, f32[1,512,512]{2,1,0:T(8,128)}, u32[]{:S(2)}) copy-start(f32[1,512,512]{2,1,0:T(8,128)} %param.12) | copy-start | bytes 3145732
  89.9 1.8 %copy-start.4 = (f32[1,512,512]{2,1,0:T(8,128)S(1)}, f32[1,512,512]{2,1,0:T(8,128)}, u32[]{:S(2)}) copy-start(f32[1,512,512]{2,1,0:T(8,128)} %param.11) | copy-start | bytes 3145732
  91.6 2.2 %copy-start.5 = (f32[512,512]{1,0:T(8,128)S(1)}, f32[512,512]{1,0:T(8,128)}, u32[]{:S(2)}) copy-start(f32[512,512]{1,0:T(8,128)} %param.14) | copy-start | bytes 3145732
  91.6 2.2 %copy-start.7 = (f32[512,512]{1,0:T(8,128)S(1)}, f32[512,512]{1,0:T(8,128)}, u32[]{:S(2)}) copy-start(f32[512,512]{1,0:T(8,128)} %param.15) | copy-start | bytes 3145732
  93.8 3.1 %copy-start = (f32[512,512]{1,0:T(8,128)}, f32[512,512]{1,0:T(8,128)S(1)}, u32[]{:S(2)}) copy-start(f32[512,512]{1,0:T(8,128)S(1)} %get-tuple-element.61.refs_5_) | copy-start | bytes 3145732
  95.3 1.5 %copy-start.1 = (f32[512,512]{1,0:T(8,128)}, f32[512,512]{1,0:T(8,128)S(1)}, u32[]{:S(2)}) copy-start(f32[512,512]{1,0:T(8,128)S(1)} %get-tuple-element.59.refs_6_) | copy-start | bytes 3145732

commit v4 on v3

v4 whole, which is shorter than its diff:
```python
import functools

import jax
import jax.numpy as jnp
from jax import lax
from jax.experimental import pallas as pl
from jax.experimental.pallas import tpu as pltpu
from jax.sharding import PartitionSpec as P

first_decay = 0.9
second_decay = 0.95
inner_rate = 0.001
weight_decay = 0.1
adam_epsilon = 1e-08
adam_count = 10.0
outer_rate = 0.7
outer_mass = 0.9

PLANE = 4
WEIGHT_SCALE = 2.0**17
WIRE = jnp.bfloat16
C_PARTIAL, C_PRODUCT, C_UNPACK = (33, 36, 34), (33, 20), (32, 30)


def cost(log_flops):
    return pl.CostEstimate(flops=1 << log_flops, bytes_accessed=1 << 20, transcendentals=0)


def power_below(limit):
    scale = 1.0
    while scale * limit > 32768.0:
        scale /= 2.0
    while scale * limit < 16384.0:
        scale *= 2.0
    return scale


def encode(x):
    power = x * x
    power = power * power
    power = power * power
    return jnp.where(x < 0.0, -power, power).astype(WIRE)


def decode(code):
    wide = code.astype(jnp.float32)
    size = jnp.abs(wide)
    root = jnp.where(size > 0.0, jnp.exp(jnp.log(size) * 0.125), 0.0)
    return jnp.where(wide < 0.0, -root, root)


def vmem(count):
    return [pl.BlockSpec(memory_space=pltpu.VMEM)] * count


def contract(left, right, dims):
    return lax.dot_general(left, right, (dims, ((), ())), preferred_element_type=jnp.float32)


def pack_kernel(columns, distances, axis, features_far, cot_in, weight_far, coded, weight, cot, own, *refs):
    chunks, (features, sem) = refs[:-2], refs[-2:]
    me = lax.axis_index(axis)
    z, p, planes = me // PLANE, me % PLANE, len(distances)
    copies = [
        pltpu.make_async_copy(weight_far.at[0], weight, sem.at[0]),
        pltpu.make_async_copy(features_far, features, sem.at[1]),
    ]
    for copy in copies:
        copy.start()
    cot[...] = cot_in[...]
    copies[0].wait()
    coded[...] = encode(weight[...] * WEIGHT_SCALE)
    copies[1].wait()
    for k in range(PLANE):
        if k > 0:
            first, rest = chunks[2 * k - 2], chunks[2 * k - 1]
            first[:, : cot.shape[1]] = cot[...]
        for at, distance in enumerate(distances):
            block = lax.rem(z + planes + distance, planes)
            start = pl.multiple_of((block * PLANE + (p ^ k)) * columns, 128)
            value = features[:, pl.ds(start, columns)]
            if k == 0:
                own[:, at * columns : (at + 1) * columns] = value
            elif at == 0:
                first[:, cot.shape[1] :] = value
            else:
                rest[:, (at - 1) * columns : at * columns] = value


def pack(features, cot, weight, columns, distances):
    rows, planes = features.shape[0], len(distances)
    widths = [planes * columns] + [cot.shape[1] + columns, (planes - 1) * columns] * (PLANE - 1)
    coded, weight, cot, own, *chunks = pl.pallas_call(
        functools.partial(pack_kernel, columns, distances, "fsdp"),
        out_shape=[
            jax.ShapeDtypeStruct(weight.shape[1:], WIRE),
            jax.ShapeDtypeStruct(weight.shape[1:], weight.dtype),
            jax.ShapeDtypeStruct(cot.shape, cot.dtype),
        ]
        + [jax.ShapeDtypeStruct((rows, width), features.dtype) for width in widths],
        in_specs=[pl.BlockSpec(memory_space=pltpu.HBM), *vmem(1), pl.BlockSpec(memory_space=pltpu.HBM)],
        out_specs=vmem(3 + len(widths)),
        scratch_shapes=[pltpu.VMEM(features.shape, features.dtype), pltpu.SemaphoreType.DMA((2,))],
        cost_estimate=cost(36),
        compiler_params=pltpu.CompilerParams(vmem_limit_bytes=48 << 20),
        name="pack",
    )(features, cot, weight)
    return coded, weight, cot, own, [chunks[2 * k : 2 * k + 2] for k in range(PLANE - 1)]


def partial_kernel(columns, scale, spread, own, cot, *refs):
    firsts, refs = refs[: PLANE - 1], refs[PLANE - 1 :]
    others = refs[: PLANE - 1] if any(at > 0 for at, _, _ in spread) else ()
    rest, outs = refs[len(others) : -len(spread)], refs[-len(spread) :]
    depth = cot.shape[1]
    for (at, count, rides), out in zip(spread, outs):
        total = contract(own[:, at * columns : (at + 1) * columns], cot[...], ((0,), (0,)))
        for i, first in enumerate(firsts):
            if at == 0:
                part = first[:, depth:]
            else:
                part = others[i][:, (at - 1) * columns : at * columns]
            total += contract(part, first[:, :depth], ((0,), (0,)))
        total = total * scale
        for ref in rest[:count]:
            total += decode(ref[:columns, :])
        out[:columns, :] = encode(total) if out.dtype == WIRE else total
        if rides:
            out[columns:, :] = rest[count][-columns:, :]
        rest = rest[count + rides :]


def plane_partial(spread, own, cot, firsts, others, rest, columns, scale, dtype, span):
    operands = [own, cot, *firsts, *others, *rest]
    outs = pl.pallas_call(
        functools.partial(partial_kernel, columns, scale, spread),
        out_shape=[jax.ShapeDtypeStruct((columns * (1 + rides), cot.shape[1]), dtype) for _, _, rides in spread],
        in_specs=vmem(len(operands)),
        out_specs=vmem(len(spread)),
        cost_estimate=cost(span),
        compiler_params=pltpu.CompilerParams(vmem_limit_bytes=32 << 20),
        name="plane_partial",
    )(*operands)
    return list(outs)


def product_kernel(columns, count, scale, *refs):
    weights, cot, firsts, outs = refs[:count], refs[count], refs[count + 1 : count + PLANE], refs[-PLANE:]
    depth = cot.shape[1]
    for i, weight in enumerate(weights):
        if weight.dtype == WIRE:
            wide, factor = decode(weight[-columns:, :]), 1.0 / WEIGHT_SCALE
        else:
            wide, factor = weight[...], 1.0
        high = wide.astype(jnp.bfloat16)
        low = (wide - high.astype(jnp.float32)).astype(jnp.bfloat16)
        for k in range(PLANE):
            rows = cot[...] if k == 0 else firsts[k - 1][:, :depth]
            result = contract(rows, high, ((1,), (1,))) + contract(rows, low, ((1,), (1,)))
            result = result * factor if k == 0 else encode(result * (factor * scale))
            outs[k][:, i * columns : (i + 1) * columns] = result


def plane_product(weights, cot, firsts, after, columns, scale, span):
    shape = (cot.shape[0], columns * len(weights))
    outs = pl.pallas_call(
        functools.partial(product_kernel, columns, len(weights), scale),
        out_shape=[jax.ShapeDtypeStruct(shape, jnp.float32 if k == 0 else WIRE) for k in range(PLANE)],
        in_specs=vmem(len(weights) + PLANE) + [pl.BlockSpec(memory_space=pl.ANY)],
        out_specs=vmem(PLANE),
        cost_estimate=cost(span),
        compiler_params=pltpu.CompilerParams(vmem_limit_bytes=32 << 20),
        name="plane_product",
    )(*weights, cot, *firsts, after)
    return list(outs)


def unpack_kernel(columns, planes, axis, factor, offsets, *refs):
    pieces, out, buffer, sem = refs[:PLANE], refs[-3], refs[-2], refs[-1]
    me = lax.axis_index(axis)
    z, p = me // PLANE, me % PLANE
    copies = []
    for inner, offset in enumerate(offsets):
        block = lax.rem(z + planes + offset, planes)
        for k in range(PLANE):
            i = inner * PLANE + k
            span = slice(inner * columns, (inner + 1) * columns)
            if k == 0:
                source = pieces[k].at[:, span]
            else:
                buffer[i] = decode(pieces[k][:, span]) * factor
                source = buffer.at[i]
            start = pl.multiple_of((block * PLANE + (p ^ k)) * columns, 128)
            copy = pltpu.make_async_copy(source, out.at[:, pl.ds(start, columns)], sem.at[i])
            copy.start()
            copies.append(copy)
    for copy in copies:
        copy.wait()


def unpack(pieces, out, after, offsets, columns, planes, factor, span):
    rows = pieces[0].shape[0]
    count = len(offsets) * PLANE
    others = [*out, *after]
    return pl.pallas_call(
        functools.partial(unpack_kernel, columns, planes, "fsdp", factor, offsets),
        out_shape=jax.ShapeDtypeStruct((rows, columns * planes * PLANE), jnp.float32),
        in_specs=vmem(PLANE) + [pl.BlockSpec(memory_space=pl.ANY)] * len(others),
        out_specs=pl.BlockSpec(memory_space=pl.ANY),
        scratch_shapes=[
            pltpu.VMEM((count, rows, columns), jnp.float32),
            pltpu.SemaphoreType.DMA((count,)),
        ],
        input_output_aliases={PLANE: 0} if out else {},
        cost_estimate=cost(span),
        compiler_params=pltpu.CompilerParams(vmem_limit_bytes=32 << 20),
        name="unpack",
    )(*pieces, *others)


def on_device(
    features,
    value_cotangent,
    value_weight,
    first_moment,
    second_moment,
    fragment_local,
    fragment_anchor,
    outer_momentum,
):
    size = lax.axis_size("fsdp")
    planes = size // PLANE
    columns = features.shape[1] // size
    tokens = features.shape[0] * size
    gradient_scale = power_below(tokens * 24.0 * 6.0)
    product_scale = power_below(value_cotangent.shape[1] * 6.0 * 0.25)

    ring = [(i, (i + PLANE) % size) for i in range(size)]

    def around(x):
        return lax.ppermute(x, "fsdp", ring)

    def back(x):
        return lax.ppermute(x, "fsdp", [(to, source) for source, to in ring])

    def across(x, k):
        return lax.ppermute(x, "fsdp", [(i, i ^ k) for i in range(size)])

    workers = lax.axis_size("worker")
    half = planes // 2
    distances = [half]
    for step in range(half - 1, 0, -1):
        distances += [step, -step]
    distances.append(0)
    coded, weight, cot, own, chunks = pack(features, value_cotangent, value_weight, columns, distances)
    firsts = [across(first, k + 1) for k, (first, _) in enumerate(chunks)]
    others = [across(rest, k + 1) for k, (_, rest) in enumerate(chunks)]

    difference = fragment_anchor - fragment_local[0]
    if workers == 2:
        partner_local = lax.ppermute(fragment_local, "worker", [(0, 1), (1, 0)])
        pseudo_sum = difference + (fragment_anchor - partner_local[0])
    else:
        pseudo_sum = lax.psum(difference, "worker")
    pseudo_mean = pseudo_sum / workers
    new_momentum = outer_mass * outer_momentum + pseudo_mean
    new_anchor = fragment_anchor - outer_rate * (pseudo_mean + outer_mass * new_momentum)

    behind, ahead = around(coded), back(coded)
    behind, firsts = lax.optimization_barrier((behind, firsts))
    weights, offsets = [weight, behind, ahead], [0, -1, 1]

    def partials(spread, others, rest, dtype, span):
        return plane_partial(spread, own, cot, firsts, others, rest, columns, gradient_scale, dtype, span)

    plus, minus = partials([(0, 0, half > 1)], [], [behind], WIRE, C_PARTIAL[0])[0], None
    early = plane_product(weights, cot, firsts, new_momentum, columns, product_scale, C_PRODUCT[0])
    early = [part if k == 0 else across(part, k) for k, part in enumerate(early)]
    late_weights, late_offsets = [], []
    for step in range(half - 1, 0, -1):
        plus = around(plus)
        late_weights.append(plus)
        late_offsets.append(step - half - 1)
        spread, rest = [(planes - 1 - 2 * step, 1, step > 1)], [plus]
        if step > 1:
            rest.append(plus)
        if minus is None:
            carried = ahead
            spread.append((planes - 2 * step, 0, step > 1))
        else:
            carried = minus = back(minus)
            late_weights.append(minus)
            late_offsets.append(half - step)
            spread.append((planes - 2 * step, 1, step > 1))
            rest.append(minus)
        if step > 1:
            rest.append(carried)
        if step == half - 1:
            pass
        plus, minus = partials(spread, others, rest, WIRE, C_PARTIAL[1])
    factor = 1.0 / product_scale
    late = plane_product(late_weights, cot, firsts, plus, columns, product_scale, C_PRODUCT[1])
    for k in range(1, PLANE):
        late[k], early[k] = lax.optimization_barrier((late[k], early[k]))
        late[k] = across(late[k], k)
    feature_grad = unpack(early, [], [], offsets, columns, planes, factor, C_UNPACK[0])
    so_far = [around(plus), back(minus)]
    so_far[0], feature_grad = lax.optimization_barrier((so_far[0], feature_grad))
    (total,) = partials([(planes - 1, 2, False)], others, so_far, jnp.float32, C_PARTIAL[2])
    gradient = total * (1.0 / gradient_scale)

    first_new = first_decay * first_moment[0] + (1.0 - first_decay) * gradient
    second_new = second_decay * second_moment[0] + (1.0 - second_decay) * gradient * gradient
    first_hat = first_new / (1.0 - first_decay**adam_count)
    second_hat = second_new / (1.0 - second_decay**adam_count)
    weight_new = weight - inner_rate * (
        first_hat / (jnp.sqrt(second_hat) + adam_epsilon) + weight_decay * weight
    )
    feature_grad = unpack(
        late, [feature_grad], [first_new], late_offsets, columns, planes, factor, C_UNPACK[1]
    )
    return (
        feature_grad,
        weight_new[None],
        first_new[None],
        second_new[None],
        new_anchor,
        new_momentum,
    )


def solution(mesh):
    placed = (
        P(("worker", "fsdp"), None),
        P(("worker", "fsdp"), None),
        P("worker", "fsdp", None),
        P("worker", "fsdp", None),
        P("worker", "fsdp", None),
        P("worker", "fsdp", None),
        P("fsdp", None),
        P("fsdp", None),
    )
    return jax.shard_map(
        on_device,
        mesh=mesh,
        in_specs=placed,
        out_specs=(
            P(("worker", "fsdp"), None),
            P("worker", "fsdp", None),
            P("worker", "fsdp", None),
            P("worker", "fsdp", None),
            P("fsdp", None),
            P("fsdp", None),
        ),
        check_vma=False,
    )
```

time: 97.2 us -> 92.8 us (0.955)
  starting transfers between devices: 24.8 us -> 21.9 us
  waiting for transfers between devices: 48.6 us -> 47.3 us
    ppermute x5 -> x3, waiting for transfers between devices: 26.3 us -> 0.01 us  [around(): return lax.ppermute(x, 'fsdp', ring)]
    ppermute x12, waiting for transfers between devices: 22.3 us -> 47.3 us  [across(): return lax.ppermute(x, 'fsdp', [(i, i ^ k) for i in range(size)])]
    ppermute x12, starting transfers between devices: 14.6 us -> 11.3 us  [across(): return lax.ppermute(x, 'fsdp', [(i, i ^ k) for i in range(size)])]
    ppermute x1 -> x2, starting transfers between devices: 2.1 us -> 4.31 us  [back(): return lax.ppermute(x, 'fsdp', [(to, source) for source, to in ring])]
    ppermute x5 -> x3, starting transfers between devices: 8.15 us -> 6.34 us  [around(): return lax.ppermute(x, 'fsdp', ring)]
    pallas_call x7 -> x6, Pallas kernels: 14.1 us -> 14 us  [the longest x2 7.11 us: plane_product(): pl.pallas_call(functools.partial(product_kernel, columns, len(weights), s...]
  transfers between devices with their start and end apart: 19 -> 18, of which waited for: 7 -> 8; matrix products, arithmetic and copies ran while one was open for 4% -> 4% of each run, Pallas kernels for 13% -> 15%
where the time goes in v4:
time: 92.8 us; the launch traced here: 92.6 us
  waiting for transfers between devices  47.3 us (51%)
  starting transfers between devices  21.9 us (24%)
  Pallas kernels  17.8 us (19%)
  other arithmetic  3.64 us (4%)
  local copies, waits for them, and re-layouts  0.96 us (1%)
  between operations  0.94 us (1%)
    ppermute x12, waiting for transfers between devices, across(): return lax.ppermute(x, 'fsdp', [(i, i ^ k) for i in range(size)])  47.3 us
    ppermute x12, starting transfers between devices, across(): return lax.ppermute(x, 'fsdp', [(i, i ^ k) for i in range(size)])  11.3 us
    pallas_call x2, Pallas kernels, plane_product(): pl.pallas_call(functools.partial(product_kernel, columns, len(weights), s...  7.11 us
    ppermute x3, starting transfers between devices, around(): return lax.ppermute(x, 'fsdp', ring)  6.34 us
    pallas_call x3, Pallas kernels, plane_partial(): pl.pallas_call(functools.partial(partial_kernel, columns, scale, spread),...  4.32 us
    ppermute x2, starting transfers between devices, back(): return lax.ppermute(x, 'fsdp', [(to, source) for source, to in ring])  4.31 us
    pallas_call x2, Pallas kernels, unpack(): pl.pallas_call(functools.partial(unpack_kernel, columns, planes, 'fsdp',...  3.79 us
    pallas_call x1, Pallas kernels, pack(): pl.pallas_call(functools.partial(pack_kernel, columns, distances, 'fsdp')...  2.6 us
  transfers between devices with their start and end apart: 18, of which 8 were waited for; matrix products, arithmetic and copies ran while one was open for 4% of the time, Pallas kernels for 15%

profile of v4, /device:TPU:0, one launch (start us, length us, event | category | flops | bytes accessed | tf_op | source)
XLA Modules:
  0.0 92.6 jit_solution(9524061674841746733)
XLA Ops:
  0.6 0.9 copy-done.2
  1.6 2.6 %pack.1 = (bf16[512,512]{1,0:T(8,128)(2,1)S(1)}, f32[512,512]{1,0:T(8,128)S(1)}, bf16[192,512]{1,0:T(8,128)(2,1)S(1)}, bf16[192,2048]{1,0:T(8,128)(2,1)S(1)}, bf...) custom-call(bf16[192,8192]{1,0:T(8,128)(2,1)} %features_far.1, ...), custom_call_target="tpu_custom_call" | custom-call | flops 68719476736 | bytes 1048576 | tf_op jit(solution)/shard_map/pack/pallas_call | solution.py:93
  4.2 3.1 %collective-permute-start = (bf16[512,512]{1,0:T(8,128)(2,1)S(1)}, bf16[512,512]{1,0:T(8,128)(2,1)S(1)}, u32[]{:S(2)}, u32[]{:S(2)}) collective-permute-start(bf16[512,512]{1,0:T(8,128)(2,1)S(1)} %get-tuple-element.40), channel_id=1, source_target_pairs={{0,4},{1,5},{2,6},{3,7},{4,8},{5,9},{6,10},{7,11},{8,12},{9,13},{1... | collective-permute-start | bytes 1572872 | tf_op jit(solution)/shard_map/ppermute | solution.py:241
  7.3 1.5 %collective-permute-start.1 = (bf16[192,1024]{1,0:T(8,128)(2,1)S(1)}, bf16[192,1024]{1,0:T(8,128)(2,1)S(1)}, u32[]{:S(2)}, u32[]{:S(2)}) collective-permute-start(bf16[192,1024]{1,0:T(8,128)(2,1)S(1)} %get-tuple-element.41), channel_id=1, source_target_pairs={{0,1},{1,0},{2,3},{3,2},{4,5},{5,4},{6,7},{7,6},{8,9},{9,8},{10,11... | collective-permute-start | bytes 1179656 | tf_op jit(solution)/shard_map/ppermute | solution.py:247
  8.7 1.5 %collective-permute-start.2 = (bf16[192,1024]{1,0:T(8,128)(2,1)S(1)}, bf16[192,1024]{1,0:T(8,128)(2,1)S(1)}, u32[]{:S(2)}, u32[]{:S(2)}) collective-permute-start(bf16[192,1024]{1,0:T(8,128)(2,1)S(1)} %get-tuple-element.42), channel_id=1, source_target_pairs={{0,2},{1,3},{2,0},{3,1},{4,6},{5,7},{6,4},{7,5},{8,10},{9,11},{10,... | collective-permute-start | bytes 1179656 | tf_op jit(solution)/shard_map/ppermute | solution.py:247
  10.3 0.5 collective-permute-start.3
  10.7 8.5 %collective-permute-done.1.refs_0_.refs_2_.refs_4_ = bf16[192,1024]{1,0:T(8,128)(2,1)S(1)} collective-permute-done((bf16[192,1024]{1,0:T(8,128)(2,1)S(1)}, bf16[192,1024]{1,0:T(8,128)(2,1)S(1)}, u32[]{:S(2)}, u32[]{:S(2)}) %collective-permute-start.1) | collective-permute-done | bytes 393248 | tf_op jit(solution)/shard_map/ppermute | solution.py:247
  19.3 2.1 %collective-permute-start.8 = (bf16[512,512]{1,0:T(8,128)(2,1)S(1)}, bf16[512,512]{1,0:T(8,128)(2,1)S(1)}, u32[]{:S(2)}, u32[]{:S(2)}) collective-permute-start(bf16[512,512]{1,0:T(8,128)(2,1)S(1)} %get-tuple-element.40), channel_id=1, source_target_pairs={{4,0},{5,1},{6,2},{7,3},{8,4},{9,5},{10,6},{11,7},{12,8},{13,9},{1... | collective-permute-start | bytes 1572872 | tf_op jit(solution)/shard_map/ppermute | solution.py:244
  21.4 4.9 %collective-permute-done.2.refs_1_.refs_3_.refs_5_ = bf16[192,1024]{1,0:T(8,128)(2,1)S(1)} collective-permute-done((bf16[192,1024]{1,0:T(8,128)(2,1)S(1)}, bf16[192,1024]{1,0:T(8,128)(2,1)S(1)}, u32[]{:S(2)}, u32[]{:S(2)}) %collective-permute-start.2) | collective-permute-done | bytes 393248 | tf_op jit(solution)/shard_map/ppermute | solution.py:247
  26.2 2.5 %collective-permute-done.3.refs_2_.refs_4_.refs_6_ = bf16[192,1024]{1,0:T(8,128)(2,1)S(1)} collective-permute-done((bf16[192,1024]{1,0:T(8,128)(2,1)S(1)}, bf16[192,1024]{1,0:T(8,128)(2,1)S(1)}, u32[]{:S(2)}, u32[]{:S(2)}) %collective-permute-start.3) | collective-permute-done | bytes 393248 | tf_op jit(solution)/shard_map/ppermute | solution.py:247
  28.7 0.5 collective-permute-start.6
  29.2 2.4 %collective-permute-start.7 = (bf16[192,1536]{1,0:T(8,128)(2,1)S(1)}, bf16[192,1536]{1,0:T(8,128)(2,1)S(1)}, u32[]{:S(2)}, u32[]{:S(2)}) collective-permute-start(bf16[192,1536]{1,0:T(8,128)(2,1)S(1)} %get-tuple-element.50), channel_id=1, source_target_pairs={{0,3},{1,2},{2,1},{3,0},{4,7},{5,6},{6,5},{7,4},{8,11},{9,10},{10,... | collective-permute-start | bytes 1769480 | tf_op jit(solution)/shard_map/ppermute | solution.py:247
  31.6 0.9 plane_partial.3
  32.5 1.6 %collective-permute-start.4 = (bf16[1024,512]{1,0:T(8,128)(2,1)S(1)}, bf16[1024,512]{1,0:T(8,128)(2,1)S(1)}, u32[]{:S(2)}, u32[]{:S(2)}) collective-permute-start(bf16[1024,512]{1,0:T(8,128)(2,1)S(1)} %plane_partial.3), channel_id=1, source_target_pairs={{0,4},{1,5},{2,6},{3,7},{4,8},{5,9},{6,10},{7,11},{8,12},{9,13},{1... | collective-permute-start | bytes 3145736 | tf_op jit(solution)/shard_map/ppermute | solution.py:241
  34.2 1.5 %multiply_subtract_fusion = (f32[512,512]{1,0:T(8,128)}, f32[512,512]{1,0:T(8,128)S(1)}) fusion(f32[512,512]{1,0:T(8,128)S(1)} %copy-done.5, f32[1,512,512]{2,1,0:T(8,128)S(1)} %collective-permute-done.9, f32[1,512,512]{2,1,0:T(8,128)S(1)} %copy-done.6, f32[512,512]{1,0:T(8,128)S(1)} %copy-done.7), kind=kLoop, calls=%fused_computation.6 | loop fusion | flops 2621440 | bytes 6291456 | tf_op jit(solution)/shard_map/sub | solution.py:267
  35.7 5.1 %plane_product.3 = (f32[192,1536]{1,0:T(8,128)S(1)}, bf16[192,1536]{1,0:T(8,128)(2,1)S(1)}, bf16[192,1536]{1,0:T(8,128)(2,1)S(1)}, bf16[192,1536]{1,0:T(8,128)(2,1)S(1)}) custom-call(f32[512,512]{1,0:T(8,128)S(1)} %get-tuple-element.54.refs_0_, bf16[512,512]{1,0:T(8,128)(2,1)S(1)} %collective-permute-done.refs_3_.refs_1_, ...), custom_call_target="tpu_custom_call" | custom-call | flops 8589934592 | bytes 1048576 | tf_op jit(solution)/shard_map/plane_product/pallas_call | solution.py:166
  40.8 0.7 collective-permute-start.10
  41.5 1.0 %collective-permute-done.5.refs_3_ = bf16[192,1536]{1,0:T(8,128)(2,1)S(1)} collective-permute-done((bf16[192,1536]{1,0:T(8,128)(2,1)S(1)}, bf16[192,1536]{1,0:T(8,128)(2,1)S(1)}, u32[]{:S(2)}, u32[]{:S(2)}) %collective-permute-start.5) | collective-permute-done | bytes 589856 | tf_op jit(solution)/shard_map/ppermute | solution.py:247
  42.5 2.5 %collective-permute-start.12 = (bf16[192,1536]{1,0:T(8,128)(2,1)S(1)}, bf16[192,1536]{1,0:T(8,128)(2,1)S(1)}, u32[]{:S(2)}, u32[]{:S(2)}) collective-permute-start(bf16[192,1536]{1,0:T(8,128)(2,1)S(1)} %get-tuple-element.58), channel_id=1, source_target_pairs={{0,2},{1,3},{2,0},{3,1},{4,6},{5,7},{6,4},{7,5},{8,10},{9,11},{10,... | collective-permute-start | bytes 1769480 | tf_op jit(solution)/shard_map/ppermute | solution.py:247
  45.0 12.3 %collective-permute-done.6.refs_4_ = bf16[192,1536]{1,0:T(8,128)(2,1)S(1)} collective-permute-done((bf16[192,1536]{1,0:T(8,128)(2,1)S(1)}, bf16[192,1536]{1,0:T(8,128)(2,1)S(1)}, u32[]{:S(2)}, u32[]{:S(2)}) %collective-permute-start.6) | collective-permute-done | bytes 589856 | tf_op jit(solution)/shard_map/ppermute | solution.py:247
  57.3 0.2 collective-permute-start.14
  57.5 2.0 %plane_partial.4 = (bf16[512,512]{1,0:T(8,128)(2,1)S(1)}, bf16[512,512]{1,0:T(8,128)(2,1)S(1)}) custom-call(bf16[192,2048]{1,0:T(8,128)(2,1)S(1)} %get-tuple-element.38.own, bf16[192,512]{1,0:T(8,128)(2,1)S(1)} %get-tuple-element.39.cot.refs_1_.refs_3_, bf16[192,1024]{1,0:T(8,128)(2,1)S(1)} %collective-permute-done.1.refs_0_.refs_2_.refs_4_, ...), custom_call_target="tpu_custom_call" | custom-call | flops 68719476736 | bytes 1048576 | tf_op jit(solution)/shard_map/plane_partial/pallas_call | solution.py:135
  59.5 1.6 %collective-permute-start.16 = (bf16[512,512]{1,0:T(8,128)(2,1)S(1)}, bf16[512,512]{1,0:T(8,128)(2,1)S(1)}, u32[]{:S(2)}, u32[]{:S(2)}) collective-permute-start(bf16[512,512]{1,0:T(8,128)(2,1)S(1)} %get-tuple-element.51.refs_5_), channel_id=1, source_target_pairs={{0,4},{1,5},{2,6},{3,7},{4,8},{5,9},{6,10},{7,11},{8,12},{9,13},{1... | collective-permute-start | bytes 1572872 | tf_op jit(solution)/shard_map/ppermute | solution.py:241
  61.1 2.2 %collective-permute-start.17 = (bf16[512,512]{1,0:T(8,128)(2,1)S(1)}, bf16[512,512]{1,0:T(8,128)(2,1)S(1)}, u32[]{:S(2)}, u32[]{:S(2)}) collective-permute-start(bf16[512,512]{1,0:T(8,128)(2,1)S(1)} %get-tuple-element.69), channel_id=1, source_target_pairs={{4,0},{5,1},{6,2},{7,3},{8,4},{9,5},{10,6},{11,7},{12,8},{13,9},{1... | collective-permute-start | bytes 1572872 | tf_op jit(solution)/shard_map/ppermute | solution.py:244
  63.4 2.0 %plane_product.2 = (f32[192,512]{1,0:T(8,128)S(1)}, bf16[192,512]{1,0:T(8,128)(2,1)S(1)}, bf16[192,512]{1,0:T(8,128)(2,1)S(1)}, bf16[192,512]{1,0:T(8,128)(2,1)S(1)}) custom-call(bf16[1024,512]{1,0:T(8,128)(2,1)S(1)} %collective-permute-done.4.refs_6_.refs_0_, bf16[192,512]{1,0:T(8,128)(2,1)S(1)} %get-tuple-element.39.cot.refs_1_.refs_3_, ...), custom_call_target="tpu_custom_call" | custom-call | flops 1048576 | bytes 1048576 | tf_op jit(solution)/shard_map/plane_product/pallas_call | solution.py:166
  65.4 2.4 %collective-permute-done.10.refs_1_ = bf16[192,1536]{1,0:T(8,128)(2,1)S(1)} collective-permute-done((bf16[192,1536]{1,0:T(8,128)(2,1)S(1)}, bf16[192,1536]{1,0:T(8,128)(2,1)S(1)}, u32[]{:S(2)}, u32[]{:S(2)}) %collective-permute-start.10) | collective-permute-done | bytes 589856 | tf_op jit(solution)/shard_map/ppermute | solution.py:247
  67.8 15.5 %collective-permute-done.12.refs_2_ = bf16[192,1536]{1,0:T(8,128)(2,1)S(1)} collective-permute-done((bf16[192,1536]{1,0:T(8,128)(2,1)S(1)}, bf16[192,1536]{1,0:T(8,128)(2,1)S(1)}, u32[]{:S(2)}, u32[]{:S(2)}) %collective-permute-start.12) | collective-permute-done | bytes 589856 | tf_op jit(solution)/shard_map/ppermute | solution.py:247
  83.3 1.5 %collective-permute-start.15 = (bf16[192,512]{1,0:T(8,128)(2,1)S(1)}, bf16[192,512]{1,0:T(8,128)(2,1)S(1)}, u32[]{:S(2)}, u32[]{:S(2)}) collective-permute-start(bf16[192,512]{1,0:T(8,128)(2,1)S(1)} %get-tuple-element.62), channel_id=1, source_target_pairs={{0,3},{1,2},{2,1},{3,0},{4,7},{5,6},{6,5},{7,4},{8,11},{9,10},{10,... | collective-permute-start | bytes 589832 | tf_op jit(solution)/shard_map/ppermute | solution.py:247
  84.8 2.4 %unpack.2.refs_4_ = f32[192,8192]{1,0:T(8,128)} custom-call(f32[192,1536]{1,0:T(8,128)S(1)} %get-tuple-element.63.refs_0_, bf16[192,1536]{1,0:T(8,128)(2,1)S(1)} %collective-permute-done.10.refs_1_, bf16[192,1536]{1,0:T(8,128)(2,1)S(1)} %collective-permute-done.12.refs_2_, bf16[192,1536]{1,0:T(8,128)(2,1)S(1)} %collective-permute-done.14.refs_3_), custom_call_target="tpu_custom_call" | custom-call | flops 4294967296 | bytes 1048576 | tf_op jit(solution)/shard_map/unpack/pallas_call | solution.py:205
  87.3 1.5 %plane_partial.5 = f32[512,512]{1,0:T(8,128)S(1)} custom-call(bf16[192,2048]{1,0:T(8,128)(2,1)S(1)} %get-tuple-element.38.own, bf16[192,512]{1,0:T(8,128)(2,1)S(1)} %get-tuple-element.39.cot.refs_1_.refs_3_, bf16[192,1024]{1,0:T(8,128)(2,1)S(1)} %collective-permute-done.1.refs_0_.refs_2_.refs_4_, ...), custom_call_target="tpu_custom_call" | custom-call | flops 17179869184 | bytes 1048576 | tf_op jit(solution)/shard_map/plane_partial/pallas_call | solution.py:135
  88.8 2.1 %subtract_bitcast_fusion = (f32[1,512,512]{2,1,0:T(8,128)}, f32[512,512]{1,0:T(8,128)S(1)}, f32[1,512,512]{2,1,0:T(8,128)}) fusion(f32[512,512]{1,0:T(8,128)S(1)} %get-tuple-element.54.refs_0_, f32[512,512]{1,0:T(8,128)S(1)} %plane_partial.5, f32[1,512,512]{2,1,0:T(8,128)S(1)} %copy-done.3, f32[1,512,512]{2,1,0:T(8,128)S(1)} %copy-done.4), kind=kLoop, calls=%fused_computation.7 | loop fusion | flops 4194304 | bytes 7340032 | tf_op jit(solution)/shard_map/broadcast_in_dim | solution.py:324
  91.1 1.4 %unpack.3 = f32[192,8192]{1,0:T(8,128)} custom-call(f32[192,512]{1,0:T(8,128)S(1)} %get-tuple-element.52.refs_0_, bf16[192,512]{1,0:T(8,128)(2,1)S(1)} %collective-permute-done.11.refs_1_, bf16[192,512]{1,0:T(8,128)(2,1)S(1)} %collective-permute-done.13.refs_2_, ...), custom_call_target="tpu_custom_call", output_to_operand_aliasing={{}: (4, {})} | custom-call | flops 1073741824 | bytes 1048576 | tf_op jit(solution)/shard_map/unpack/pallas_call | solution.py:205
  (30 shorter events, 0.2 us)
Async XLA Ops:
  0.6 0.9 %copy-start.2 = (bf16[192,512]{1,0:T(8,128)(2,1)S(1)}, bf16[192,512]{1,0:T(8,128)(2,1)}, u32[]{:S(2)}) copy-start(bf16[192,512]{1,0:T(8,128)(2,1)} %cot_in.1) | copy-start | bytes 589828
  1.6 9.2 %copy-start.6 = (f32[1,512,512]{2,1,0:T(8,128)S(1)}, f32[1,512,512]{2,1,0:T(8,128)}, u32[]{:S(2)}) copy-start(f32[1,512,512]{2,1,0:T(8,128)} %param.13) | copy-start | bytes 3145732
  4.2 25.1 %collective-permute-start = (bf16[512,512]{1,0:T(8,128)(2,1)S(1)}, bf16[512,512]{1,0:T(8,128)(2,1)S(1)}, u32[]{:S(2)}, u32[]{:S(2)}) collective-permute-start(bf16[512,512]{1,0:T(8,128)(2,1)S(1)} %get-tuple-element.40), channel_id=1, source_target_pairs={{0,4},{1,5},{2,6},{3,7},{4,8},{5,9},{6,10},{7,11},{8,12},{9,13},{1... | collective-permute-start | bytes 1572872 | tf_op jit(solution)/shard_map/ppermute | solution.py:241
  7.3 12.0 %collective-permute-start.1 = (bf16[192,1024]{1,0:T(8,128)(2,1)S(1)}, bf16[192,1024]{1,0:T(8,128)(2,1)S(1)}, u32[]{:S(2)}, u32[]{:S(2)}) collective-permute-start(bf16[192,1024]{1,0:T(8,128)(2,1)S(1)} %get-tuple-element.41), channel_id=1, source_target_pairs={{0,1},{1,0},{2,3},{3,2},{4,5},{5,4},{6,7},{7,6},{8,9},{9,8},{10,11... | collective-permute-start | bytes 1179656 | tf_op jit(solution)/shard_map/ppermute | solution.py:247
  8.7 17.5 %collective-permute-start.2 = (bf16[192,1024]{1,0:T(8,128)(2,1)S(1)}, bf16[192,1024]{1,0:T(8,128)(2,1)S(1)}, u32[]{:S(2)}, u32[]{:S(2)}) collective-permute-start(bf16[192,1024]{1,0:T(8,128)(2,1)S(1)} %get-tuple-element.42), channel_id=1, source_target_pairs={{0,2},{1,3},{2,0},{3,1},{4,6},{5,7},{6,4},{7,5},{8,10},{9,11},{10,... | collective-permute-start | bytes 1179656 | tf_op jit(solution)/shard_map/ppermute | solution.py:247
  10.3 18.5 %collective-permute-start.3 = (bf16[192,1024]{1,0:T(8,128)(2,1)S(1)}, bf16[192,1024]{1,0:T(8,128)(2,1)S(1)}, u32[]{:S(2)}, u32[]{:S(2)}) collective-permute-start(bf16[192,1024]{1,0:T(8,128)(2,1)S(1)} %get-tuple-element.43), channel_id=1, source_target_pairs={{0,3},{1,2},{2,1},{3,0},{4,7},{5,6},{6,5},{7,4},{8,11},{9,10},{10,... | collective-permute-start | bytes 1179656 | tf_op jit(solution)/shard_map/ppermute | solution.py:247
  10.7 21.8 %collective-permute-start.9 = (f32[1,512,512]{2,1,0:T(8,128)S(1)}, f32[1,512,512]{2,1,0:T(8,128)S(1)}, u32[]{:S(2)}, u32[]{:S(2)}) collective-permute-start(f32[1,512,512]{2,1,0:T(8,128)S(1)} %copy-done.6), channel_id=1, source_target_pairs={{0,16},{16,0},{1,17},{17,1},{2,18},{18,2},{3,19},{19,3},{4,20},{20... | collective-permute-start | bytes 3145736 | tf_op jit(solution)/shard_map/ppermute | solution.py:261
  19.3 16.4 %collective-permute-start.8 = (bf16[512,512]{1,0:T(8,128)(2,1)S(1)}, bf16[512,512]{1,0:T(8,128)(2,1)S(1)}, u32[]{:S(2)}, u32[]{:S(2)}) collective-permute-start(bf16[512,512]{1,0:T(8,128)(2,1)S(1)} %get-tuple-element.40), channel_id=1, source_target_pairs={{4,0},{5,1},{6,2},{7,3},{8,4},{9,5},{10,6},{11,7},{12,8},{13,9},{1... | collective-permute-start | bytes 1572872 | tf_op jit(solution)/shard_map/ppermute | solution.py:244
  26.2 16.3 %collective-permute-start.5 = (bf16[192,1536]{1,0:T(8,128)(2,1)S(1)}, bf16[192,1536]{1,0:T(8,128)(2,1)S(1)}, u32[]{:S(2)}, u32[]{:S(2)}) collective-permute-start(bf16[192,1536]{1,0:T(8,128)(2,1)S(1)} %get-tuple-element.48), channel_id=1, source_target_pairs={{0,1},{1,0},{2,3},{3,2},{4,5},{5,4},{6,7},{7,6},{8,9},{9,8},{10,11... | collective-permute-start | bytes 1769480 | tf_op jit(solution)/shard_map/ppermute | solution.py:247
  28.7 28.6 %collective-permute-start.6 = (bf16[192,1536]{1,0:T(8,128)(2,1)S(1)}, bf16[192,1536]{1,0:T(8,128)(2,1)S(1)}, u32[]{:S(2)}, u32[]{:S(2)}) collective-permute-start(bf16[192,1536]{1,0:T(8,128)(2,1)S(1)} %get-tuple-element.49), channel_id=1, source_target_pairs={{0,2},{1,3},{2,0},{3,1},{4,6},{5,7},{6,4},{7,5},{8,10},{9,11},{10,... | collective-permute-start | bytes 1769480 | tf_op jit(solution)/shard_map/ppermute | solution.py:247
  29.2 28.3 %collective-permute-start.7 = (bf16[192,1536]{1,0:T(8,128)(2,1)S(1)}, bf16[192,1536]{1,0:T(8,128)(2,1)S(1)}, u32[]{:S(2)}, u32[]{:S(2)}) collective-permute-start(bf16[192,1536]{1,0:T(8,128)(2,1)S(1)} %get-tuple-element.50), channel_id=1, source_target_pairs={{0,3},{1,2},{2,1},{3,0},{4,7},{5,6},{6,5},{7,4},{8,11},{9,10},{10,... | collective-permute-start | bytes 1769480 | tf_op jit(solution)/shard_map/ppermute | solution.py:247
  31.6 2.5 %copy-start.5 = (f32[512,512]{1,0:T(8,128)S(1)}, f32[512,512]{1,0:T(8,128)}, u32[]{:S(2)}) copy-start(f32[512,512]{1,0:T(8,128)} %param.14) | copy-start | bytes 3145732
  31.6 2.5 %copy-start.7 = (f32[512,512]{1,0:T(8,128)S(1)}, f32[512,512]{1,0:T(8,128)}, u32[]{:S(2)}) copy-start(f32[512,512]{1,0:T(8,128)} %param.15) | copy-start | bytes 3145732
  32.5 25.0 %collective-permute-start.4 = (bf16[1024,512]{1,0:T(8,128)(2,1)S(1)}, bf16[1024,512]{1,0:T(8,128)(2,1)S(1)}, u32[]{:S(2)}, u32[]{:S(2)}) collective-permute-start(bf16[1024,512]{1,0:T(8,128)(2,1)S(1)} %plane_partial.3), channel_id=1, source_target_pairs={{0,4},{1,5},{2,6},{3,7},{4,8},{5,9},{6,10},{7,11},{8,12},{9,13},{1... | collective-permute-start | bytes 3145736 | tf_op jit(solution)/shard_map/ppermute | solution.py:241
  35.7 5.1 %copy-start.1 = (f32[512,512]{1,0:T(8,128)}, f32[512,512]{1,0:T(8,128)S(1)}, u32[]{:S(2)}) copy-start(f32[512,512]{1,0:T(8,128)S(1)} %get-tuple-element.71.refs_7_) | copy-start | bytes 3145732
  40.8 27.0 %collective-permute-start.10 = (bf16[192,1536]{1,0:T(8,128)(2,1)S(1)}, bf16[192,1536]{1,0:T(8,128)(2,1)S(1)}, u32[]{:S(2)}, u32[]{:S(2)}) collective-permute-start(bf16[192,1536]{1,0:T(8,128)(2,1)S(1)} %get-tuple-element.55), channel_id=1, source_target_pairs={{0,1},{1,0},{2,3},{3,2},{4,5},{5,4},{6,7},{7,6},{8,9},{9,8},{10,11... | collective-permute-start | bytes 1769480 | tf_op jit(solution)/shard_map/ppermute | solution.py:247
  42.5 40.8 %collective-permute-start.12 = (bf16[192,1536]{1,0:T(8,128)(2,1)S(1)}, bf16[192,1536]{1,0:T(8,128)(2,1)S(1)}, u32[]{:S(2)}, u32[]{:S(2)}) collective-permute-start(bf16[192,1536]{1,0:T(8,128)(2,1)S(1)} %get-tuple-element.58), channel_id=1, source_target_pairs={{0,2},{1,3},{2,0},{3,1},{4,6},{5,7},{6,4},{7,5},{8,10},{9,11},{10,... | collective-permute-start | bytes 1769480 | tf_op jit(solution)/shard_map/ppermute | solution.py:247
  57.3 26.0 %collective-permute-start.14 = (bf16[192,1536]{1,0:T(8,128)(2,1)S(1)}, bf16[192,1536]{1,0:T(8,128)(2,1)S(1)}, u32[]{:S(2)}, u32[]{:S(2)}) collective-permute-start(bf16[192,1536]{1,0:T(8,128)(2,1)S(1)} %get-tuple-element.61), channel_id=1, source_target_pairs={{0,3},{1,2},{2,1},{3,0},{4,7},{5,6},{6,5},{7,4},{8,11},{9,10},{10,... | collective-permute-start | bytes 1769480 | tf_op jit(solution)/shard_map/ppermute | solution.py:247
  59.5 27.7 %collective-permute-start.16 = (bf16[512,512]{1,0:T(8,128)(2,1)S(1)}, bf16[512,512]{1,0:T(8,128)(2,1)S(1)}, u32[]{:S(2)}, u32[]{:S(2)}) collective-permute-start(bf16[512,512]{1,0:T(8,128)(2,1)S(1)} %get-tuple-element.51.refs_5_), channel_id=1, source_target_pairs={{0,4},{1,5},{2,6},{3,7},{4,8},{5,9},{6,10},{7,11},{8,12},{9,13},{1... | collective-permute-start | bytes 1572872 | tf_op jit(solution)/shard_map/ppermute | solution.py:241
  61.1 26.1 %collective-permute-start.17 = (bf16[512,512]{1,0:T(8,128)(2,1)S(1)}, bf16[512,512]{1,0:T(8,128)(2,1)S(1)}, u32[]{:S(2)}, u32[]{:S(2)}) collective-permute-start(bf16[512,512]{1,0:T(8,128)(2,1)S(1)} %get-tuple-element.69), channel_id=1, source_target_pairs={{4,0},{5,1},{6,2},{7,3},{8,4},{9,5},{10,6},{11,7},{12,8},{13,9},{1... | collective-permute-start | bytes 1572872 | tf_op jit(solution)/shard_map/ppermute | solution.py:244
  67.8 23.1 %collective-permute-start.11 = (bf16[192,512]{1,0:T(8,128)(2,1)S(1)}, bf16[192,512]{1,0:T(8,128)(2,1)S(1)}, u32[]{:S(2)}, u32[]{:S(2)}) collective-permute-start(bf16[192,512]{1,0:T(8,128)(2,1)S(1)} %get-tuple-element.56), channel_id=1, source_target_pairs={{0,1},{1,0},{2,3},{3,2},{4,5},{5,4},{6,7},{7,6},{8,9},{9,8},{10,11... | collective-permute-start | bytes 589832 | tf_op jit(solution)/shard_map/ppermute | solution.py:247
  83.3 7.8 %collective-permute-start.13 = (bf16[192,512]{1,0:T(8,128)(2,1)S(1)}, bf16[192,512]{1,0:T(8,128)(2,1)S(1)}, u32[]{:S(2)}, u32[]{:S(2)}) collective-permute-start(bf16[192,512]{1,0:T(8,128)(2,1)S(1)} %get-tuple-element.59), channel_id=1, source_target_pairs={{0,2},{1,3},{2,0},{3,1},{4,6},{5,7},{6,4},{7,5},{8,10},{9,11},{10,... | collective-permute-start | bytes 589832 | tf_op jit(solution)/shard_map/ppermute | solution.py:247
  83.3 7.8 %collective-permute-start.15 = (bf16[192,512]{1,0:T(8,128)(2,1)S(1)}, bf16[192,512]{1,0:T(8,128)(2,1)S(1)}, u32[]{:S(2)}, u32[]{:S(2)}) collective-permute-start(bf16[192,512]{1,0:T(8,128)(2,1)S(1)} %get-tuple-element.62), channel_id=1, source_target_pairs={{0,3},{1,2},{2,1},{3,0},{4,7},{5,6},{6,5},{7,4},{8,11},{9,10},{10,... | collective-permute-start | bytes 589832 | tf_op jit(solution)/shard_map/ppermute | solution.py:247
  87.2 1.5 %copy-start.3 = (f32[1,512,512]{2,1,0:T(8,128)S(1)}, f32[1,512,512]{2,1,0:T(8,128)}, u32[]{:S(2)}) copy-start(f32[1,512,512]{2,1,0:T(8,128)} %param.12) | copy-start | bytes 3145732
  87.2 1.5 %copy-start.4 = (f32[1,512,512]{2,1,0:T(8,128)S(1)}, f32[1,512,512]{2,1,0:T(8,128)}, u32[]{:S(2)}) copy-start(f32[1,512,512]{2,1,0:T(8,128)} %param.11) | copy-start | bytes 3145732
  90.9 1.6 %copy-start = (f32[512,512]{1,0:T(8,128)}, f32[512,512]{1,0:T(8,128)S(1)}, u32[]{:S(2)}) copy-start(f32[512,512]{1,0:T(8,128)S(1)} %get-tuple-element.73.refs_5_) | copy-start | bytes 3145732

commit v5 on v4

--- a/solution.py
+++ b/solution.py
@@ -19,7 +19,8 @@
 PLANE = 4
 WEIGHT_SCALE = 2.0**17
 WIRE = jnp.bfloat16
-C_PARTIAL, C_PRODUCT, C_UNPACK = (33, 36, 34), (33, 20), (32, 30)
+ORDER = (3, 1, 2)
+C_PARTIAL, C_PRODUCT, C_UNPACK = (33, 34, 20), (33, 20), (36, 30)
 
 
 def cost(log_flops):
@@ -73,7 +74,7 @@
     copies[1].wait()
     for k in range(PLANE):
         if k > 0:
-            first, rest = chunks[2 * k - 2], chunks[2 * k - 1]
+            first, middle, last = chunks[3 * k - 3 : 3 * k]
             first[:, : cot.shape[1]] = cot[...]
         for at, distance in enumerate(distances):
             block = lax.rem(z + planes + distance, planes)
@@ -83,13 +84,15 @@
                 own[:, at * columns : (at + 1) * columns] = value
             elif at == 0:
                 first[:, cot.shape[1] :] = value
+            elif at == planes - 1:
+                last[...] = value
             else:
-                rest[:, (at - 1) * columns : at * columns] = value
+                middle[:, (at - 1) * columns : at * columns] = value
 
 
 def pack(features, cot, weight, columns, distances):
     rows, planes = features.shape[0], len(distances)
-    widths = [planes * columns] + [cot.shape[1] + columns, (planes - 1) * columns] * (PLANE - 1)
+    widths = [planes * columns] + [cot.shape[1] + columns, (planes - 2) * columns, columns] * (PLANE - 1)
     coded, weight, cot, own, *chunks = pl.pallas_call(
         functools.partial(pack_kernel, columns, distances, "fsdp"),
         out_shape=[
@@ -105,22 +108,17 @@
         compiler_params=pltpu.CompilerParams(vmem_limit_bytes=48 << 20),
         name="pack",
     )(features, cot, weight)
-    return coded, weight, cot, own, [chunks[2 * k : 2 * k + 2] for k in range(PLANE - 1)]
+    return coded, weight, cot, own, [chunks[k::3] for k in range(3)]
 
 
 def partial_kernel(columns, scale, spread, own, cot, *refs):
-    firsts, refs = refs[: PLANE - 1], refs[PLANE - 1 :]
-    others = refs[: PLANE - 1] if any(at > 0 for at, _, _ in spread) else ()
-    rest, outs = refs[len(others) : -len(spread)], refs[-len(spread) :]
+    firsts, parts = refs[: PLANE - 1], refs[PLANE - 1 : 2 * PLANE - 2]
+    rest, outs = refs[2 * PLANE - 2 : -len(spread)], refs[-len(spread) :]
     depth = cot.shape[1]
-    for (at, count, rides), out in zip(spread, outs):
-        total = contract(own[:, at * columns : (at + 1) * columns], cot[...], ((0,), (0,)))
-        for i, first in enumerate(firsts):
-            if at == 0:
-                part = first[:, depth:]
-            else:
-                part = others[i][:, (at - 1) * columns : at * columns]
-            total += contract(part, first[:, :depth], ((0,), (0,)))
+    for (at, start, count, rides), out in zip(spread, outs):
+        total = contract(own[:, at : at + columns], cot[...], ((0,), (0,)))
+        for part, first in zip(parts, firsts):
+            total += contract(part[:, start : start + columns], first[:, :depth], ((0,), (0,)))
         total = total * scale
         for ref in rest[:count]:
             total += decode(ref[:columns, :])
@@ -130,11 +128,13 @@
         rest = rest[count + rides :]
 
 
-def plane_partial(spread, own, cot, firsts, others, rest, columns, scale, dtype, span):
-    operands = [own, cot, *firsts, *others, *rest]
+def plane_partial(spread, own, cot, firsts, parts, rest, columns, scale, dtype, span):
+    operands = [own, cot, *firsts, *parts, *rest]
     outs = pl.pallas_call(
         functools.partial(partial_kernel, columns, scale, spread),
-        out_shape=[jax.ShapeDtypeStruct((columns * (1 + rides), cot.shape[1]), dtype) for _, _, rides in spread],
+        out_shape=[
+            jax.ShapeDtypeStruct((columns * (1 + rides), cot.shape[1]), dtype) for *_, rides in spread
+        ],
         in_specs=vmem(len(operands)),
         out_specs=vmem(len(spread)),
         cost_estimate=cost(span),
@@ -146,6 +146,8 @@
 
 def product_kernel(columns, count, scale, *refs):
     weights, cot, firsts, outs = refs[:count], refs[count], refs[count + 1 : count + PLANE], refs[-PLANE:]
+    for rider, out in zip(refs[count + PLANE : -PLANE - 1], outs[1:]):
+        out[:, count * columns :] = rider[...]
     depth = cot.shape[1]
     for i, weight in enumerate(weights):
         if weight.dtype == WIRE:
@@ -161,17 +163,20 @@
             outs[k][:, i * columns : (i + 1) * columns] = result
 
 
-def plane_product(weights, cot, firsts, after, columns, scale, span):
-    shape = (cot.shape[0], columns * len(weights))
+def plane_product(weights, cot, firsts, riders, after, columns, scale, span):
+    rows, width = cot.shape[0], columns * len(weights)
+    sizes = [width] + [width + (columns if riders else 0)] * (PLANE - 1)
     outs = pl.pallas_call(
         functools.partial(product_kernel, columns, len(weights), scale),
-        out_shape=[jax.ShapeDtypeStruct(shape, jnp.float32 if k == 0 else WIRE) for k in range(PLANE)],
-        in_specs=vmem(len(weights) + PLANE) + [pl.BlockSpec(memory_space=pl.ANY)],
+        out_shape=[
+            jax.ShapeDtypeStruct((rows, size), jnp.float32 if k == 0 else WIRE) for k, size in enumerate(sizes)
+        ],
+        in_specs=vmem(len(weights) + PLANE + len(riders)) + [pl.BlockSpec(memory_space=pl.ANY)],
         out_specs=vmem(PLANE),
         cost_estimate=cost(span),
         compiler_params=pltpu.CompilerParams(vmem_limit_bytes=32 << 20),
         name="plane_product",
-    )(*weights, cot, *firsts, after)
+    )(*weights, cot, *firsts, *riders, after)
     return list(outs)
 
 
@@ -246,6 +251,10 @@
     def across(x, k):
         return lax.ppermute(x, "fsdp", [(i, i ^ k) for i in range(size)])
 
+    def across_all(parts):
+        moved = {k: across(parts[k - 1], k) for k in ORDER}
+        return [moved[k] for k in range(1, PLANE)]
+
     workers = lax.axis_size("worker")
     half = planes // 2
     distances = [half]
@@ -253,8 +262,9 @@
         distances += [step, -step]
     distances.append(0)
     coded, weight, cot, own, chunks = pack(features, value_cotangent, value_weight, columns, distances)
-    firsts = [across(first, k + 1) for k, (first, _) in enumerate(chunks)]
-    others = [across(rest, k + 1) for k, (_, rest) in enumerate(chunks)]
+    firsts, middles, riders = chunks
+    firsts = across_all(firsts)
+    middles = across_all(middles)
 
     difference = fragment_anchor - fragment_local[0]
     if workers == 2:
@@ -270,43 +280,43 @@
     behind, firsts = lax.optimization_barrier((behind, firsts))
     weights, offsets = [weight, behind, ahead], [0, -1, 1]
 
-    def partials(spread, others, rest, dtype, span):
-        return plane_partial(spread, own, cot, firsts, others, rest, columns, gradient_scale, dtype, span)
-
-    plus, minus = partials([(0, 0, half > 1)], [], [behind], WIRE, C_PARTIAL[0])[0], None
-    early = plane_product(weights, cot, firsts, new_momentum, columns, product_scale, C_PRODUCT[0])
-    early = [part if k == 0 else across(part, k) for k, part in enumerate(early)]
+    def partials(spread, parts, rest, dtype, span):
+        return plane_partial(spread, own, cot, firsts, parts, rest, columns, gradient_scale, dtype, span)
+
+    plus, minus = partials([(0, cot.shape[1], 0, half > 1)], firsts, [behind], WIRE, C_PARTIAL[0])[0], None
+    early = plane_product(weights, cot, firsts, riders, new_momentum, columns, product_scale, C_PRODUCT[0])
+    early[1:] = across_all(early[1:])
     late_weights, late_offsets = [], []
     for step in range(half - 1, 0, -1):
         plus = around(plus)
         late_weights.append(plus)
         late_offsets.append(step - half - 1)
-        spread, rest = [(planes - 1 - 2 * step, 1, step > 1)], [plus]
+        at = (planes - 1 - 2 * step) * columns
+        spread, rest = [(at, at - columns, 1, step > 1)], [plus]
         if step > 1:
             rest.append(plus)
         if minus is None:
             carried = ahead
-            spread.append((planes - 2 * step, 0, step > 1))
+            spread.append((at + columns, at, 0, step > 1))
         else:
             carried = minus = back(minus)
             late_weights.append(minus)
             late_offsets.append(half - step)
-            spread.append((planes - 2 * step, 1, step > 1))
+            spread.append((at + columns, at, 1, step > 1))
             rest.append(minus)
         if step > 1:
             rest.append(carried)
-        if step == half - 1:
-            pass
-        plus, minus = partials(spread, others, rest, WIRE, C_PARTIAL[1])
+        plus, minus = partials(spread, middles, rest, WIRE, C_PARTIAL[1])
     factor = 1.0 / product_scale
-    late = plane_product(late_weights, cot, firsts, plus, columns, product_scale, C_PRODUCT[1])
+    late = plane_product(late_weights, cot, firsts, [], plus, columns, product_scale, C_PRODUCT[1])
     for k in range(1, PLANE):
         late[k], early[k] = lax.optimization_barrier((late[k], early[k]))
-        late[k] = across(late[k], k)
+    late[1:] = across_all(late[1:])
     feature_grad = unpack(early, [], [], offsets, columns, planes, factor, C_UNPACK[0])
     so_far = [around(plus), back(minus)]
     so_far[0], feature_grad = lax.optimization_barrier((so_far[0], feature_grad))
-    (total,) = partials([(planes - 1, 2, False)], others, so_far, jnp.float32, C_PARTIAL[2])
+    (total,) = partials(
+        [((planes - 1) * columns, len(weights) * columns, 2, False)], early[1:], so_far, jnp.float32, C_PARTIAL[2])
     gradient = total * (1.0 / gradient_scale)
 
     first_new = first_decay * first_moment[0] + (1.0 - first_decay) * gradient

time: 92.8 us -> 89.5 us (0.964)
  waiting for transfers between devices: 47.3 us -> 44.8 us
    ppermute x12, waiting for transfers between devices: 47.3 us -> 37 us  [across(): return lax.ppermute(x, 'fsdp', [(i, i ^ k) for i in range(size)])]
    ppermute x3, waiting for transfers between devices: 0.01 us -> 7.78 us  [around(): return lax.ppermute(x, 'fsdp', ring)]
    ppermute x12, starting transfers between devices: 11.3 us -> 12.4 us  [across(): return lax.ppermute(x, 'fsdp', [(i, i ^ k) for i in range(size)])]
    ppermute x2, starting transfers between devices: 4.31 us -> 3.28 us  [back(): return lax.ppermute(x, 'fsdp', [(to, source) for source, to in ring])]
  transfers between devices with their start and end apart: 18 -> 18, of which waited for: 8 -> 10; matrix products, arithmetic and copies ran while one was open for 4% -> 4% of each run, Pallas kernels for 15% -> 15%
where the time goes in v5:
time: 89.5 us; the launch traced here: 89.4 us
  waiting for transfers between devices  44.8 us (50%)
  starting transfers between devices  21.3 us (24%)
  Pallas kernels  17.7 us (20%)
  other arithmetic  3.63 us (4%)
  local copies, waits for them, and re-layouts  0.95 us (1%)
  between operations  0.95 us (1%)
    ppermute x12, waiting for transfers between devices, across(): return lax.ppermute(x, 'fsdp', [(i, i ^ k) for i in range(size)])  37 us
    ppermute x12, starting transfers between devices, across(): return lax.ppermute(x, 'fsdp', [(i, i ^ k) for i in range(size)])  12.4 us
    ppermute x3, waiting for transfers between devices, around(): return lax.ppermute(x, 'fsdp', ring)  7.78 us
    pallas_call x2, Pallas kernels, plane_product(): pl.pallas_call(functools.partial(product_kernel, columns, len(weights), s...  7.11 us
    ppermute x3, starting transfers between devices, around(): return lax.ppermute(x, 'fsdp', ring)  5.57 us
    pallas_call x3, Pallas kernels, plane_partial(): pl.pallas_call(functools.partial(partial_kernel, columns, scale, spread),...  4.33 us
    pallas_call x2, Pallas kernels, unpack(): pl.pallas_call(functools.partial(unpack_kernel, columns, planes, 'fsdp',...  3.67 us
    ppermute x2, starting transfers between devices, back(): return lax.ppermute(x, 'fsdp', [(to, source) for source, to in ring])  3.28 us
  transfers between devices with their start and end apart: 18, of which 10 were waited for; matrix products, arithmetic and copies ran while one was open for 4% of the time, Pallas kernels for 15%

profile of v5, /device:TPU:0, one launch (start us, length us, event | category | flops | bytes accessed | tf_op | source)
XLA Modules:
  0.0 89.4 jit_solution(5281535746082059702)
XLA Ops:
  0.6 0.9 %copy-done.2 = bf16[192,512]{1,0:T(8,128)(2,1)S(1)} copy-done((bf16[192,512]{1,0:T(8,128)(2,1)S(1)}, bf16[192,512]{1,0:T(8,128)(2,1)}, u32[]{:S(2)}) %copy-start.2) | copy-done | bytes 196632
  1.6 2.6 %pack.1 = (bf16[512,512]{1,0:T(8,128)(2,1)S(1)}, f32[512,512]{1,0:T(8,128)S(1)}, bf16[192,512]{1,0:T(8,128)(2,1)S(1)}, bf16[192,2048]{1,0:T(8,128)(2,1)S(1)}, bf...) custom-call(bf16[192,8192]{1,0:T(8,128)(2,1)} %features_far.1, ...), custom_call_target="tpu_custom_call" | custom-call | flops 68719476736 | bytes 1048576 | tf_op jit(solution)/shard_map/pack/pallas_call | solution.py:96
  4.2 3.1 %collective-permute-start = (bf16[512,512]{1,0:T(8,128)(2,1)S(1)}, bf16[512,512]{1,0:T(8,128)(2,1)S(1)}, u32[]{:S(2)}, u32[]{:S(2)}) collective-permute-start(bf16[512,512]{1,0:T(8,128)(2,1)S(1)} %get-tuple-element.43), channel_id=1, source_target_pairs={{0,4},{1,5},{2,6},{3,7},{4,8},{5,9},{6,10},{7,11},{8,12},{9,13},{1... | collective-permute-start | bytes 1572872 | tf_op jit(solution)/shard_map/ppermute | solution.py:246
  7.3 1.5 %collective-permute-start.1 = (bf16[192,1024]{1,0:T(8,128)(2,1)S(1)}, bf16[192,1024]{1,0:T(8,128)(2,1)S(1)}, u32[]{:S(2)}, u32[]{:S(2)}) collective-permute-start(bf16[192,1024]{1,0:T(8,128)(2,1)S(1)} %get-tuple-element.44), channel_id=1, source_target_pairs={{0,1},{1,0},{2,3},{3,2},{4,5},{5,4},{6,7},{7,6},{8,9},{9,8},{10,11... | collective-permute-start | bytes 1179656 | tf_op jit(solution)/shard_map/ppermute | solution.py:252
  8.7 1.5 %collective-permute-start.2 = (bf16[192,1024]{1,0:T(8,128)(2,1)S(1)}, bf16[192,1024]{1,0:T(8,128)(2,1)S(1)}, u32[]{:S(2)}, u32[]{:S(2)}) collective-permute-start(bf16[192,1024]{1,0:T(8,128)(2,1)S(1)} %get-tuple-element.45), channel_id=1, source_target_pairs={{0,2},{1,3},{2,0},{3,1},{4,6},{5,7},{6,4},{7,5},{8,10},{9,11},{10,... | collective-permute-start | bytes 1179656 | tf_op jit(solution)/shard_map/ppermute | solution.py:252
  10.7 8.5 %collective-permute-done.1.refs_0_.refs_3_.refs_2_.refs_4_ = bf16[192,1024]{1,0:T(8,128)(2,1)S(1)} collective-permute-done((bf16[192,1024]{1,0:T(8,128)(2,1)S(1)}, bf16[192,1024]{1,0:T(8,128)(2,1)S(1)}, u32[]{:S(2)}, u32[]{:S(2)}) %collective-permute-start.1) | collective-permute-done | bytes 393248 | tf_op jit(solution)/shard_map/ppermute | solution.py:252
  19.3 2.1 %collective-permute-start.8 = (bf16[512,512]{1,0:T(8,128)(2,1)S(1)}, bf16[512,512]{1,0:T(8,128)(2,1)S(1)}, u32[]{:S(2)}, u32[]{:S(2)}) collective-permute-start(bf16[512,512]{1,0:T(8,128)(2,1)S(1)} %get-tuple-element.43), channel_id=1, source_target_pairs={{4,0},{5,1},{6,2},{7,3},{8,4},{9,5},{10,6},{11,7},{12,8},{13,9},{1... | collective-permute-start | bytes 1572872 | tf_op jit(solution)/shard_map/ppermute | solution.py:249
  21.4 4.9 %collective-permute-done.2.refs_1_.refs_4_.refs_3_.refs_5_ = bf16[192,1024]{1,0:T(8,128)(2,1)S(1)} collective-permute-done((bf16[192,1024]{1,0:T(8,128)(2,1)S(1)}, bf16[192,1024]{1,0:T(8,128)(2,1)S(1)}, u32[]{:S(2)}, u32[]{:S(2)}) %collective-permute-start.2) | collective-permute-done | bytes 393248 | tf_op jit(solution)/shard_map/ppermute | solution.py:252
  26.2 2.5 %collective-permute-done.3.refs_2_.refs_5_.refs_4_.refs_6_ = bf16[192,1024]{1,0:T(8,128)(2,1)S(1)} collective-permute-done((bf16[192,1024]{1,0:T(8,128)(2,1)S(1)}, bf16[192,1024]{1,0:T(8,128)(2,1)S(1)}, u32[]{:S(2)}, u32[]{:S(2)}) %collective-permute-start.3) | collective-permute-done | bytes 393248 | tf_op jit(solution)/shard_map/ppermute | solution.py:252
  28.7 0.5 collective-permute-start.6
  29.2 2.4 %collective-permute-start.7 = (bf16[192,1024]{1,0:T(8,128)(2,1)S(1)}, bf16[192,1024]{1,0:T(8,128)(2,1)S(1)}, u32[]{:S(2)}, u32[]{:S(2)}) collective-permute-start(bf16[192,1024]{1,0:T(8,128)(2,1)S(1)} %get-tuple-element.53), channel_id=1, source_target_pairs={{0,3},{1,2},{2,1},{3,0},{4,7},{5,6},{6,5},{7,4},{8,11},{9,10},{10,... | collective-permute-start | bytes 1179656 | tf_op jit(solution)/shard_map/ppermute | solution.py:252
  31.6 0.9 plane_partial.3
  32.5 1.6 %collective-permute-start.4 = (bf16[1024,512]{1,0:T(8,128)(2,1)S(1)}, bf16[1024,512]{1,0:T(8,128)(2,1)S(1)}, u32[]{:S(2)}, u32[]{:S(2)}) collective-permute-start(bf16[1024,512]{1,0:T(8,128)(2,1)S(1)} %plane_partial.3), channel_id=1, source_target_pairs={{0,4},{1,5},{2,6},{3,7},{4,8},{5,9},{6,10},{7,11},{8,12},{9,13},{1... | collective-permute-start | bytes 3145736 | tf_op jit(solution)/shard_map/ppermute | solution.py:246
  34.2 1.5 %multiply_subtract_fusion = (f32[512,512]{1,0:T(8,128)}, f32[512,512]{1,0:T(8,128)S(1)}) fusion(f32[512,512]{1,0:T(8,128)S(1)} %copy-done.5, f32[1,512,512]{2,1,0:T(8,128)S(1)} %collective-permute-done.9, f32[1,512,512]{2,1,0:T(8,128)S(1)} %copy-done.6, f32[512,512]{1,0:T(8,128)S(1)} %copy-done.7), kind=kLoop, calls=%fused_computation.6 | loop fusion | flops 2621440 | bytes 6291456 | tf_op jit(solution)/shard_map/sub | solution.py:277
  35.7 5.1 %plane_product.3 = (f32[192,1536]{1,0:T(8,128)S(1)}, bf16[192,2048]{1,0:T(8,128)(2,1)S(1)}, bf16[192,2048]{1,0:T(8,128)(2,1)S(1)}, bf16[192,2048]{1,0:T(8,128)(2,1)S(1)}) custom-call(f32[512,512]{1,0:T(8,128)S(1)} %get-tuple-element.57.refs_0_, bf16[512,512]{1,0:T(8,128)(2,1)S(1)} %collective-permute-done.refs_6_.refs_1_, ...), custom_call_target="tpu_custom_call" | custom-call | flops 8589934592 | bytes 1048576 | tf_op jit(solution)/shard_map/plane_product/pallas_call | solution.py:169
  40.8 0.6 collective-permute-start.10
  41.5 0.5 collective-permute-start.12
  42.0 2.9 %collective-permute-done.6.refs_4_ = bf16[192,1024]{1,0:T(8,128)(2,1)S(1)} collective-permute-done((bf16[192,1024]{1,0:T(8,128)(2,1)S(1)}, bf16[192,1024]{1,0:T(8,128)(2,1)S(1)}, u32[]{:S(2)}, u32[]{:S(2)}) %collective-permute-start.6) | collective-permute-done | bytes 393248 | tf_op jit(solution)/shard_map/ppermute | solution.py:252
  44.9 3.2 %collective-permute-start.14 = (bf16[192,2048]{1,0:T(8,128)(2,1)S(1)}, bf16[192,2048]{1,0:T(8,128)(2,1)S(1)}, u32[]{:S(2)}, u32[]{:S(2)}) collective-permute-start(bf16[192,2048]{1,0:T(8,128)(2,1)S(1)} %get-tuple-element.67), channel_id=1, source_target_pairs={{0,3},{1,2},{2,1},{3,0},{4,7},{5,6},{6,5},{7,4},{8,11},{9,10},{10,... | collective-permute-start | bytes 2359304 | tf_op jit(solution)/shard_map/ppermute | solution.py:252
  48.3 7.8 %collective-permute-done.4.refs_6_.refs_0_ = bf16[1024,512]{1,0:T(8,128)(2,1)S(1)} collective-permute-done((bf16[1024,512]{1,0:T(8,128)(2,1)S(1)}, bf16[1024,512]{1,0:T(8,128)(2,1)S(1)}, u32[]{:S(2)}, u32[]{:S(2)}) %collective-permute-start.4) | collective-permute-done | bytes 1048608 | tf_op jit(solution)/shard_map/ppermute | solution.py:246
  56.1 2.0 %plane_partial.4 = (bf16[512,512]{1,0:T(8,128)(2,1)S(1)}, bf16[512,512]{1,0:T(8,128)(2,1)S(1)}) custom-call(bf16[192,2048]{1,0:T(8,128)(2,1)S(1)} %get-tuple-element.41.own, bf16[192,512]{1,0:T(8,128)(2,1)S(1)} %get-tuple-element.42.cot.refs_1_.refs_3_, bf16[192,1024]{1,0:T(8,128)(2,1)S(1)} %collective-permute-done.1.refs_0_.refs_3_.refs_2_.refs_4_, ...), custom_call_target="tpu_custom_call" | custom-call | flops 17179869184 | bytes 1048576 | tf_op jit(solution)/shard_map/plane_partial/pallas_call | solution.py:133
  58.1 1.2 %collective-permute-start.17 = (bf16[512,512]{1,0:T(8,128)(2,1)S(1)}, bf16[512,512]{1,0:T(8,128)(2,1)S(1)}, u32[]{:S(2)}, u32[]{:S(2)}) collective-permute-start(bf16[512,512]{1,0:T(8,128)(2,1)S(1)} %get-tuple-element.75), channel_id=1, source_target_pairs={{4,0},{5,1},{6,2},{7,3},{8,4},{9,5},{10,6},{11,7},{12,8},{13,9},{1... | collective-permute-start | bytes 1572872 | tf_op jit(solution)/shard_map/ppermute | solution.py:249
  59.3 0.9 collective-permute-start.16
  60.2 2.0 %plane_product.2 = (f32[192,512]{1,0:T(8,128)S(1)}, bf16[192,512]{1,0:T(8,128)(2,1)S(1)}, bf16[192,512]{1,0:T(8,128)(2,1)S(1)}, bf16[192,512]{1,0:T(8,128)(2,1)S(1)}) custom-call(bf16[1024,512]{1,0:T(8,128)(2,1)S(1)} %collective-permute-done.4.refs_6_.refs_0_, bf16[192,512]{1,0:T(8,128)(2,1)S(1)} %get-tuple-element.42.cot.refs_1_.refs_3_, ...), custom_call_target="tpu_custom_call" | custom-call | flops 1048576 | bytes 1048576 | tf_op jit(solution)/shard_map/plane_product/pallas_call | solution.py:169
  62.2 1.2 %collective-permute-done.10.refs_1_.refs_3_ = bf16[192,2048]{1,0:T(8,128)(2,1)S(1)} collective-permute-done((bf16[192,2048]{1,0:T(8,128)(2,1)S(1)}, bf16[192,2048]{1,0:T(8,128)(2,1)S(1)}, u32[]{:S(2)}, u32[]{:S(2)}) %collective-permute-start.10) | collective-permute-done | bytes 786464 | tf_op jit(solution)/shard_map/ppermute | solution.py:252
  63.6 12.6 %collective-permute-done.12.refs_2_.refs_4_ = bf16[192,2048]{1,0:T(8,128)(2,1)S(1)} collective-permute-done((bf16[192,2048]{1,0:T(8,128)(2,1)S(1)}, bf16[192,2048]{1,0:T(8,128)(2,1)S(1)}, u32[]{:S(2)}, u32[]{:S(2)}) %collective-permute-start.12) | collective-permute-done | bytes 786464 | tf_op jit(solution)/shard_map/ppermute | solution.py:252
  76.2 1.4 %collective-permute-start.13 = (bf16[192,512]{1,0:T(8,128)(2,1)S(1)}, bf16[192,512]{1,0:T(8,128)(2,1)S(1)}, u32[]{:S(2)}, u32[]{:S(2)}) collective-permute-start(bf16[192,512]{1,0:T(8,128)(2,1)S(1)} %get-tuple-element.65), channel_id=1, source_target_pairs={{0,2},{1,3},{2,0},{3,1},{4,6},{5,7},{6,4},{7,5},{8,10},{9,11},{10,... | collective-permute-start | bytes 589832 | tf_op jit(solution)/shard_map/ppermute | solution.py:252
  77.6 3.7 %collective-permute-done.14.refs_3_.refs_5_ = bf16[192,2048]{1,0:T(8,128)(2,1)S(1)} collective-permute-done((bf16[192,2048]{1,0:T(8,128)(2,1)S(1)}, bf16[192,2048]{1,0:T(8,128)(2,1)S(1)}, u32[]{:S(2)}, u32[]{:S(2)}) %collective-permute-start.14) | collective-permute-done | bytes 786464 | tf_op jit(solution)/shard_map/ppermute | solution.py:252
  81.4 2.4 %unpack.2.refs_4_ = f32[192,8192]{1,0:T(8,128)} custom-call(f32[192,1536]{1,0:T(8,128)S(1)} %get-tuple-element.69.refs_0_, bf16[192,2048]{1,0:T(8,128)(2,1)S(1)} %collective-permute-done.10.refs_1_.refs_3_, bf16[192,2048]{1,0:T(8,128)(2,1)S(1)} %collective-permute-done.12.refs_2_.refs_4_, bf16[192,2048]{1,0:T(8,128)(2,1)S(1)} %collective-permute-done.14.refs_3_.refs_5_), custom_call_target="tpu_custom_call" | custom-call | flops 68719476736 | bytes 1048576 | tf_op jit(solution)/shard_map/unpack/pallas_call | solution.py:210
  83.8 1.5 %plane_partial.5 = f32[512,512]{1,0:T(8,128)S(1)} custom-call(bf16[192,2048]{1,0:T(8,128)(2,1)S(1)} %get-tuple-element.41.own, bf16[192,512]{1,0:T(8,128)(2,1)S(1)} %get-tuple-element.42.cot.refs_1_.refs_3_, bf16[192,1024]{1,0:T(8,128)(2,1)S(1)} %collective-permute-done.1.refs_0_.refs_3_.refs_2_.refs_4_, ...), custom_call_target="tpu_custom_call" | custom-call | flops 1048576 | bytes 1048576 | tf_op jit(solution)/shard_map/plane_partial/pallas_call | solution.py:133
  85.4 2.1 %subtract_bitcast_fusion = (f32[1,512,512]{2,1,0:T(8,128)}, f32[512,512]{1,0:T(8,128)S(1)}, f32[1,512,512]{2,1,0:T(8,128)}) fusion(f32[512,512]{1,0:T(8,128)S(1)} %get-tuple-element.57.refs_0_, f32[512,512]{1,0:T(8,128)S(1)} %plane_partial.5, f32[1,512,512]{2,1,0:T(8,128)S(1)} %copy-done.3, f32[1,512,512]{2,1,0:T(8,128)S(1)} %copy-done.4), kind=kLoop, calls=%fused_computation.7 | loop fusion | flops 4194304 | bytes 7340032 | tf_op jit(solution)/shard_map/broadcast_in_dim | solution.py:334
  87.9 1.3 %unpack.3 = f32[192,8192]{1,0:T(8,128)} custom-call(f32[192,512]{1,0:T(8,128)S(1)} %get-tuple-element.55.refs_0_, bf16[192,512]{1,0:T(8,128)(2,1)S(1)} %collective-permute-done.11.refs_1_, bf16[192,512]{1,0:T(8,128)(2,1)S(1)} %collective-permute-done.13.refs_2_, ...), custom_call_target="tpu_custom_call", output_to_operand_aliasing={{}: (4, {})} | custom-call | flops 1073741824 | bytes 1048576 | tf_op jit(solution)/shard_map/unpack/pallas_call | solution.py:210
  (30 shorter events, 1.5 us)
Async XLA Ops:
  0.6 0.9 %copy-start.2 = (bf16[192,512]{1,0:T(8,128)(2,1)S(1)}, bf16[192,512]{1,0:T(8,128)(2,1)}, u32[]{:S(2)}) copy-start(bf16[192,512]{1,0:T(8,128)(2,1)} %cot_in.1) | copy-start | bytes 589828
  1.6 9.2 %copy-start.6 = (f32[1,512,512]{2,1,0:T(8,128)S(1)}, f32[1,512,512]{2,1,0:T(8,128)}, u32[]{:S(2)}) copy-start(f32[1,512,512]{2,1,0:T(8,128)} %param.13) | copy-start | bytes 3145732
  4.2 25.1 %collective-permute-start = (bf16[512,512]{1,0:T(8,128)(2,1)S(1)}, bf16[512,512]{1,0:T(8,128)(2,1)S(1)}, u32[]{:S(2)}, u32[]{:S(2)}) collective-permute-start(bf16[512,512]{1,0:T(8,128)(2,1)S(1)} %get-tuple-element.43), channel_id=1, source_target_pairs={{0,4},{1,5},{2,6},{3,7},{4,8},{5,9},{6,10},{7,11},{8,12},{9,13},{1... | collective-permute-start | bytes 1572872 | tf_op jit(solution)/shard_map/ppermute | solution.py:246
  7.3 12.0 %collective-permute-start.1 = (bf16[192,1024]{1,0:T(8,128)(2,1)S(1)}, bf16[192,1024]{1,0:T(8,128)(2,1)S(1)}, u32[]{:S(2)}, u32[]{:S(2)}) collective-permute-start(bf16[192,1024]{1,0:T(8,128)(2,1)S(1)} %get-tuple-element.44), channel_id=1, source_target_pairs={{0,1},{1,0},{2,3},{3,2},{4,5},{5,4},{6,7},{7,6},{8,9},{9,8},{10,11... | collective-permute-start | bytes 1179656 | tf_op jit(solution)/shard_map/ppermute | solution.py:252
  8.7 17.5 %collective-permute-start.2 = (bf16[192,1024]{1,0:T(8,128)(2,1)S(1)}, bf16[192,1024]{1,0:T(8,128)(2,1)S(1)}, u32[]{:S(2)}, u32[]{:S(2)}) collective-permute-start(bf16[192,1024]{1,0:T(8,128)(2,1)S(1)} %get-tuple-element.45), channel_id=1, source_target_pairs={{0,2},{1,3},{2,0},{3,1},{4,6},{5,7},{6,4},{7,5},{8,10},{9,11},{10,... | collective-permute-start | bytes 1179656 | tf_op jit(solution)/shard_map/ppermute | solution.py:252
  10.3 18.5 %collective-permute-start.3 = (bf16[192,1024]{1,0:T(8,128)(2,1)S(1)}, bf16[192,1024]{1,0:T(8,128)(2,1)S(1)}, u32[]{:S(2)}, u32[]{:S(2)}) collective-permute-start(bf16[192,1024]{1,0:T(8,128)(2,1)S(1)} %get-tuple-element.46), channel_id=1, source_target_pairs={{0,3},{1,2},{2,1},{3,0},{4,7},{5,6},{6,5},{7,4},{8,11},{9,10},{10,... | collective-permute-start | bytes 1179656 | tf_op jit(solution)/shard_map/ppermute | solution.py:252
  10.7 21.8 %collective-permute-start.9 = (f32[1,512,512]{2,1,0:T(8,128)S(1)}, f32[1,512,512]{2,1,0:T(8,128)S(1)}, u32[]{:S(2)}, u32[]{:S(2)}) collective-permute-start(f32[1,512,512]{2,1,0:T(8,128)S(1)} %copy-done.6), channel_id=1, source_target_pairs={{0,16},{16,0},{1,17},{17,1},{2,18},{18,2},{3,19},{19,3},{4,20},{20... | collective-permute-start | bytes 3145736 | tf_op jit(solution)/shard_map/ppermute | solution.py:271
  19.3 16.4 %collective-permute-start.8 = (bf16[512,512]{1,0:T(8,128)(2,1)S(1)}, bf16[512,512]{1,0:T(8,128)(2,1)S(1)}, u32[]{:S(2)}, u32[]{:S(2)}) collective-permute-start(bf16[512,512]{1,0:T(8,128)(2,1)S(1)} %get-tuple-element.43), channel_id=1, source_target_pairs={{4,0},{5,1},{6,2},{7,3},{8,4},{9,5},{10,6},{11,7},{12,8},{13,9},{1... | collective-permute-start | bytes 1572872 | tf_op jit(solution)/shard_map/ppermute | solution.py:249
  26.2 15.2 %collective-permute-start.5 = (bf16[192,1024]{1,0:T(8,128)(2,1)S(1)}, bf16[192,1024]{1,0:T(8,128)(2,1)S(1)}, u32[]{:S(2)}, u32[]{:S(2)}) collective-permute-start(bf16[192,1024]{1,0:T(8,128)(2,1)S(1)} %get-tuple-element.51), channel_id=1, source_target_pairs={{0,1},{1,0},{2,3},{3,2},{4,5},{5,4},{6,7},{7,6},{8,9},{9,8},{10,11... | collective-permute-start | bytes 1179656 | tf_op jit(solution)/shard_map/ppermute | solution.py:252
  28.7 16.2 %collective-permute-start.6 = (bf16[192,1024]{1,0:T(8,128)(2,1)S(1)}, bf16[192,1024]{1,0:T(8,128)(2,1)S(1)}, u32[]{:S(2)}, u32[]{:S(2)}) collective-permute-start(bf16[192,1024]{1,0:T(8,128)(2,1)S(1)} %get-tuple-element.52), channel_id=1, source_target_pairs={{0,2},{1,3},{2,0},{3,1},{4,6},{5,7},{6,4},{7,5},{8,10},{9,11},{10,... | collective-permute-start | bytes 1179656 | tf_op jit(solution)/shard_map/ppermute | solution.py:252
  29.2 19.1 %collective-permute-start.7 = (bf16[192,1024]{1,0:T(8,128)(2,1)S(1)}, bf16[192,1024]{1,0:T(8,128)(2,1)S(1)}, u32[]{:S(2)}, u32[]{:S(2)}) collective-permute-start(bf16[192,1024]{1,0:T(8,128)(2,1)S(1)} %get-tuple-element.53), channel_id=1, source_target_pairs={{0,3},{1,2},{2,1},{3,0},{4,7},{5,6},{6,5},{7,4},{8,11},{9,10},{10,... | collective-permute-start | bytes 1179656 | tf_op jit(solution)/shard_map/ppermute | solution.py:252
  31.6 2.5 %copy-start.5 = (f32[512,512]{1,0:T(8,128)S(1)}, f32[512,512]{1,0:T(8,128)}, u32[]{:S(2)}) copy-start(f32[512,512]{1,0:T(8,128)} %param.14) | copy-start | bytes 3145732
  31.6 2.5 %copy-start.7 = (f32[512,512]{1,0:T(8,128)S(1)}, f32[512,512]{1,0:T(8,128)}, u32[]{:S(2)}) copy-start(f32[512,512]{1,0:T(8,128)} %param.15) | copy-start | bytes 3145732
  32.5 23.6 %collective-permute-start.4 = (bf16[1024,512]{1,0:T(8,128)(2,1)S(1)}, bf16[1024,512]{1,0:T(8,128)(2,1)S(1)}, u32[]{:S(2)}, u32[]{:S(2)}) collective-permute-start(bf16[1024,512]{1,0:T(8,128)(2,1)S(1)} %plane_partial.3), channel_id=1, source_target_pairs={{0,4},{1,5},{2,6},{3,7},{4,8},{5,9},{6,10},{7,11},{8,12},{9,13},{1... | collective-permute-start | bytes 3145736 | tf_op jit(solution)/shard_map/ppermute | solution.py:246
  35.7 5.1 %copy-start.1 = (f32[512,512]{1,0:T(8,128)}, f32[512,512]{1,0:T(8,128)S(1)}, u32[]{:S(2)}) copy-start(f32[512,512]{1,0:T(8,128)S(1)} %get-tuple-element.77.refs_10_) | copy-start | bytes 3145732
  40.8 22.6 %collective-permute-start.10 = (bf16[192,2048]{1,0:T(8,128)(2,1)S(1)}, bf16[192,2048]{1,0:T(8,128)(2,1)S(1)}, u32[]{:S(2)}, u32[]{:S(2)}) collective-permute-start(bf16[192,2048]{1,0:T(8,128)(2,1)S(1)} %get-tuple-element.61), channel_id=1, source_target_pairs={{0,1},{1,0},{2,3},{3,2},{4,5},{5,4},{6,7},{7,6},{8,9},{9,8},{10,11... | collective-permute-start | bytes 2359304 | tf_op jit(solution)/shard_map/ppermute | solution.py:252
  41.5 34.8 %collective-permute-start.12 = (bf16[192,2048]{1,0:T(8,128)(2,1)S(1)}, bf16[192,2048]{1,0:T(8,128)(2,1)S(1)}, u32[]{:S(2)}, u32[]{:S(2)}) collective-permute-start(bf16[192,2048]{1,0:T(8,128)(2,1)S(1)} %get-tuple-element.64), channel_id=1, source_target_pairs={{0,2},{1,3},{2,0},{3,1},{4,6},{5,7},{6,4},{7,5},{8,10},{9,11},{10,... | collective-permute-start | bytes 2359304 | tf_op jit(solution)/shard_map/ppermute | solution.py:252
  44.9 36.4 %collective-permute-start.14 = (bf16[192,2048]{1,0:T(8,128)(2,1)S(1)}, bf16[192,2048]{1,0:T(8,128)(2,1)S(1)}, u32[]{:S(2)}, u32[]{:S(2)}) collective-permute-start(bf16[192,2048]{1,0:T(8,128)(2,1)S(1)} %get-tuple-element.67), channel_id=1, source_target_pairs={{0,3},{1,2},{2,1},{3,0},{4,7},{5,6},{6,5},{7,4},{8,11},{9,10},{10,... | collective-permute-start | bytes 2359304 | tf_op jit(solution)/shard_map/ppermute | solution.py:252
  58.1 25.7 %collective-permute-start.17 = (bf16[512,512]{1,0:T(8,128)(2,1)S(1)}, bf16[512,512]{1,0:T(8,128)(2,1)S(1)}, u32[]{:S(2)}, u32[]{:S(2)}) collective-permute-start(bf16[512,512]{1,0:T(8,128)(2,1)S(1)} %get-tuple-element.75), channel_id=1, source_target_pairs={{4,0},{5,1},{6,2},{7,3},{8,4},{9,5},{10,6},{11,7},{12,8},{13,9},{1... | collective-permute-start | bytes 1572872 | tf_op jit(solution)/shard_map/ppermute | solution.py:249
  59.3 24.5 %collective-permute-start.16 = (bf16[512,512]{1,0:T(8,128)(2,1)S(1)}, bf16[512,512]{1,0:T(8,128)(2,1)S(1)}, u32[]{:S(2)}, u32[]{:S(2)}) collective-permute-start(bf16[512,512]{1,0:T(8,128)(2,1)S(1)} %get-tuple-element.54.refs_5_), channel_id=1, source_target_pairs={{0,4},{1,5},{2,6},{3,7},{4,8},{5,9},{6,10},{7,11},{8,12},{9,13},{1... | collective-permute-start | bytes 1572872 | tf_op jit(solution)/shard_map/ppermute | solution.py:246
  63.4 24.1 %collective-permute-start.11 = (bf16[192,512]{1,0:T(8,128)(2,1)S(1)}, bf16[192,512]{1,0:T(8,128)(2,1)S(1)}, u32[]{:S(2)}, u32[]{:S(2)}) collective-permute-start(bf16[192,512]{1,0:T(8,128)(2,1)S(1)} %get-tuple-element.62), channel_id=1, source_target_pairs={{0,1},{1,0},{2,3},{3,2},{4,5},{5,4},{6,7},{7,6},{8,9},{9,8},{10,11... | collective-permute-start | bytes 589832 | tf_op jit(solution)/shard_map/ppermute | solution.py:252
  76.2 11.3 %collective-permute-start.13 = (bf16[192,512]{1,0:T(8,128)(2,1)S(1)}, bf16[192,512]{1,0:T(8,128)(2,1)S(1)}, u32[]{:S(2)}, u32[]{:S(2)}) collective-permute-start(bf16[192,512]{1,0:T(8,128)(2,1)S(1)} %get-tuple-element.65), channel_id=1, source_target_pairs={{0,2},{1,3},{2,0},{3,1},{4,6},{5,7},{6,4},{7,5},{8,10},{9,11},{10,... | collective-permute-start | bytes 589832 | tf_op jit(solution)/shard_map/ppermute | solution.py:252
  81.3 6.6 %collective-permute-start.15 = (bf16[192,512]{1,0:T(8,128)(2,1)S(1)}, bf16[192,512]{1,0:T(8,128)(2,1)S(1)}, u32[]{:S(2)}, u32[]{:S(2)}) collective-permute-start(bf16[192,512]{1,0:T(8,128)(2,1)S(1)} %get-tuple-element.68), channel_id=1, source_target_pairs={{0,3},{1,2},{2,1},{3,0},{4,7},{5,6},{6,5},{7,4},{8,11},{9,10},{10,... | collective-permute-start | bytes 589832 | tf_op jit(solution)/shard_map/ppermute | solution.py:252
  83.8 1.5 %copy-start.3 = (f32[1,512,512]{2,1,0:T(8,128)S(1)}, f32[1,512,512]{2,1,0:T(8,128)}, u32[]{:S(2)}) copy-start(f32[1,512,512]{2,1,0:T(8,128)} %param.12) | copy-start | bytes 3145732
  83.8 1.5 %copy-start.4 = (f32[1,512,512]{2,1,0:T(8,128)S(1)}, f32[1,512,512]{2,1,0:T(8,128)}, u32[]{:S(2)}) copy-start(f32[1,512,512]{2,1,0:T(8,128)} %param.11) | copy-start | bytes 3145732
  87.5 1.7 %copy-start = (f32[512,512]{1,0:T(8,128)}, f32[512,512]{1,0:T(8,128)S(1)}, u32[]{:S(2)}) copy-start(f32[512,512]{1,0:T(8,128)S(1)} %get-tuple-element.79.refs_5_) | copy-start | bytes 3145732

commit v6 on v5

--- a/solution.py
+++ b/solution.py
@@ -19,8 +19,8 @@
 PLANE = 4
 WEIGHT_SCALE = 2.0**17
 WIRE = jnp.bfloat16
-ORDER = (3, 1, 2)
-C_PARTIAL, C_PRODUCT, C_UNPACK = (33, 34, 20), (33, 20), (36, 30)
+ORDER = (1, 2, 3)
+C_PARTIAL, C_PRODUCT, C_UNPACK = (36, 32, 34), (36, 20), (32, 20)
 
 
 def cost(log_flops):
@@ -263,12 +263,14 @@
     distances.append(0)
     coded, weight, cot, own, chunks = pack(features, value_cotangent, value_weight, columns, distances)
     firsts, middles, riders = chunks
+    if workers == 2:
+        partner_local = lax.ppermute(fragment_local, "worker", [(0, 1), (1, 0)])
+        firsts[-1], partner_local = lax.optimization_barrier((firsts[-1], partner_local))
     firsts = across_all(firsts)
     middles = across_all(middles)
 
     difference = fragment_anchor - fragment_local[0]
     if workers == 2:
-        partner_local = lax.ppermute(fragment_local, "worker", [(0, 1), (1, 0)])
         pseudo_sum = difference + (fragment_anchor - partner_local[0])
     else:
         pseudo_sum = lax.psum(difference, "worker")

time: 89.5 us -> 90.9 us (1.016)
  starting transfers between devices: 21.3 us -> 24.2 us
  waiting for transfers between devices: 44.8 us -> 43.2 us
    ppermute x12, waiting for transfers between devices: 37 us -> 33.9 us  [across(): return lax.ppermute(x, 'fsdp', [(i, i ^ k) for i in range(size)])]
    ppermute x2, starting transfers between devices: 3.28 us -> 6.15 us  [back(): return lax.ppermute(x, 'fsdp', [(to, source) for source, to in ring])]
    ppermute x3, starting transfers between devices: 5.57 us -> 4.33 us  [around(): return lax.ppermute(x, 'fsdp', ring)]
    ppermute x2, waiting for transfers between devices: 0.01 us -> 0.92 us  [back(): return lax.ppermute(x, 'fsdp', [(to, source) for source, to in ring])]
  transfers between devices with their start and end apart: 18 -> 18, of which waited for: 10 -> 7; matrix products, arithmetic and copies ran while one was open for 4% -> 4% of each run, Pallas kernels for 15% -> 18%
where the time goes in v6:
time: 90.9 us; the launch traced here: 90.7 us
  waiting for transfers between devices  43.2 us (48%)
  starting transfers between devices  24.2 us (27%)
  Pallas kernels  17.8 us (20%)
  other arithmetic  3.65 us (4%)
  local copies, waits for them, and re-layouts  0.96 us (1%)
  between operations  0.94 us (1%)
    ppermute x12, waiting for transfers between devices, across(): return lax.ppermute(x, 'fsdp', [(i, i ^ k) for i in range(size)])  33.9 us
    ppermute x12, starting transfers between devices, across(): return lax.ppermute(x, 'fsdp', [(i, i ^ k) for i in range(size)])  13.2 us
    ppermute x3, waiting for transfers between devices, around(): return lax.ppermute(x, 'fsdp', ring)  8.39 us
    pallas_call x2, Pallas kernels, plane_product(): pl.pallas_call(functools.partial(product_kernel, columns, len(weights), s...  7.1 us
    ppermute x2, starting transfers between devices, back(): return lax.ppermute(x, 'fsdp', [(to, source) for source, to in ring])  6.15 us
    pallas_call x3, Pallas kernels, plane_partial(): pl.pallas_call(functools.partial(partial_kernel, columns, scale, spread),...  4.33 us
    ppermute x3, starting transfers between devices, around(): return lax.ppermute(x, 'fsdp', ring)  4.33 us
    pallas_call x2, Pallas kernels, unpack(): pl.pallas_call(functools.partial(unpack_kernel, columns, planes, 'fsdp',...  3.67 us
  transfers between devices with their start and end apart: 18, of which 7 were waited for; matrix products, arithmetic and copies ran while one was open for 4% of the time, Pallas kernels for 18%

profile of v6, /device:TPU:0, one launch (start us, length us, event | category | flops | bytes accessed | tf_op | source)
XLA Modules:
  0.0 90.7 jit_solution(10641018785424610624)
XLA Ops:
  0.6 0.5 collective-permute-start.3
  1.2 0.9 %copy-done.2 = bf16[192,512]{1,0:T(8,128)(2,1)S(1)} copy-done((bf16[192,512]{1,0:T(8,128)(2,1)S(1)}, bf16[192,512]{1,0:T(8,128)(2,1)}, u32[]{:S(2)}) %copy-start.2) | copy-done | bytes 196632
  2.1 2.7 %pack.1 = (bf16[512,512]{1,0:T(8,128)(2,1)S(1)}, f32[512,512]{1,0:T(8,128)S(1)}, bf16[192,512]{1,0:T(8,128)(2,1)S(1)}, bf16[192,2048]{1,0:T(8,128)(2,1)S(1)}, bf...) custom-call(bf16[192,8192]{1,0:T(8,128)(2,1)} %features_far.1, ...), custom_call_target="tpu_custom_call" | custom-call | flops 68719476736 | bytes 1048576 | tf_op jit(solution)/shard_map/pack/pallas_call | solution.py:96
  4.8 2.6 %collective-permute-start = (bf16[512,512]{1,0:T(8,128)(2,1)S(1)}, bf16[512,512]{1,0:T(8,128)(2,1)S(1)}, u32[]{:S(2)}, u32[]{:S(2)}) collective-permute-start(bf16[512,512]{1,0:T(8,128)(2,1)S(1)} %get-tuple-element.45), channel_id=1, source_target_pairs={{0,4},{1,5},{2,6},{3,7},{4,8},{5,9},{6,10},{7,11},{8,12},{9,13},{1... | collective-permute-start | bytes 1572872 | tf_op jit(solution)/shard_map/ppermute | solution.py:246
  7.4 1.5 %collective-permute-start.1 = (bf16[192,1024]{1,0:T(8,128)(2,1)S(1)}, bf16[192,1024]{1,0:T(8,128)(2,1)S(1)}, u32[]{:S(2)}, u32[]{:S(2)}) collective-permute-start(bf16[192,1024]{1,0:T(8,128)(2,1)S(1)} %get-tuple-element.46), channel_id=1, source_target_pairs={{0,1},{1,0},{2,3},{3,2},{4,5},{5,4},{6,7},{7,6},{8,9},{9,8},{10,11... | collective-permute-start | bytes 1179656 | tf_op jit(solution)/shard_map/ppermute | solution.py:252
  8.9 1.5 %collective-permute-start.2 = (bf16[192,1024]{1,0:T(8,128)(2,1)S(1)}, bf16[192,1024]{1,0:T(8,128)(2,1)S(1)}, u32[]{:S(2)}, u32[]{:S(2)}) collective-permute-start(bf16[192,1024]{1,0:T(8,128)(2,1)S(1)} %get-tuple-element.47), channel_id=1, source_target_pairs={{0,2},{1,3},{2,0},{3,1},{4,6},{5,7},{6,4},{7,5},{8,10},{9,11},{10,... | collective-permute-start | bytes 1179656 | tf_op jit(solution)/shard_map/ppermute | solution.py:252
  10.4 0.5 collective-permute-start.4
  10.9 2.1 %collective-permute-start.9 = (bf16[512,512]{1,0:T(8,128)(2,1)S(1)}, bf16[512,512]{1,0:T(8,128)(2,1)S(1)}, u32[]{:S(2)}, u32[]{:S(2)}) collective-permute-start(bf16[512,512]{1,0:T(8,128)(2,1)S(1)} %get-tuple-element.45), channel_id=1, source_target_pairs={{4,0},{5,1},{6,2},{7,3},{8,4},{9,5},{10,6},{11,7},{12,8},{13,9},{1... | collective-permute-start | bytes 1572872 | tf_op jit(solution)/shard_map/ppermute | solution.py:249
  13.0 1.5 %multiply_subtract_fusion = (f32[512,512]{1,0:T(8,128)}, f32[512,512]{1,0:T(8,128)S(1)}) fusion(f32[512,512]{1,0:T(8,128)S(1)} %copy-done.5, f32[1,512,512]{2,1,0:T(8,128)S(1)} %collective-permute-done.3, f32[1,512,512]{2,1,0:T(8,128)S(1)} %copy-done.6, f32[512,512]{1,0:T(8,128)S(1)} %copy-done.7), kind=kLoop, calls=%fused_computation.6 | loop fusion | flops 2621440 | bytes 6291456 | tf_op jit(solution)/shard_map/sub | solution.py:279
  14.5 4.8 %collective-permute-done.1.refs_0_.refs_3_.refs_2_.refs_4_ = bf16[192,1024]{1,0:T(8,128)(2,1)S(1)} collective-permute-done((bf16[192,1024]{1,0:T(8,128)(2,1)S(1)}, bf16[192,1024]{1,0:T(8,128)(2,1)S(1)}, u32[]{:S(2)}, u32[]{:S(2)}) %collective-permute-start.1) | collective-permute-done | bytes 393248 | tf_op jit(solution)/shard_map/ppermute | solution.py:252
  19.3 1.5 %collective-permute-start.6 = (bf16[192,1024]{1,0:T(8,128)(2,1)S(1)}, bf16[192,1024]{1,0:T(8,128)(2,1)S(1)}, u32[]{:S(2)}, u32[]{:S(2)}) collective-permute-start(bf16[192,1024]{1,0:T(8,128)(2,1)S(1)} %get-tuple-element.54), channel_id=1, source_target_pairs={{0,1},{1,0},{2,3},{3,2},{4,5},{5,4},{6,7},{7,6},{8,9},{9,8},{10,11... | collective-permute-start | bytes 1179656 | tf_op jit(solution)/shard_map/ppermute | solution.py:252
  20.8 6.9 %collective-permute-done.2.refs_1_.refs_4_.refs_3_.refs_5_ = bf16[192,1024]{1,0:T(8,128)(2,1)S(1)} collective-permute-done((bf16[192,1024]{1,0:T(8,128)(2,1)S(1)}, bf16[192,1024]{1,0:T(8,128)(2,1)S(1)}, u32[]{:S(2)}, u32[]{:S(2)}) %collective-permute-start.2) | collective-permute-done | bytes 393248 | tf_op jit(solution)/shard_map/ppermute | solution.py:252
  27.8 2.0 %collective-permute-start.7 = (bf16[192,1024]{1,0:T(8,128)(2,1)S(1)}, bf16[192,1024]{1,0:T(8,128)(2,1)S(1)}, u32[]{:S(2)}, u32[]{:S(2)}) collective-permute-start(bf16[192,1024]{1,0:T(8,128)(2,1)S(1)} %get-tuple-element.55), channel_id=1, source_target_pairs={{0,2},{1,3},{2,0},{3,1},{4,6},{5,7},{6,4},{7,5},{8,10},{9,11},{10,... | collective-permute-start | bytes 1179656 | tf_op jit(solution)/shard_map/ppermute | solution.py:252
  29.8 0.9 plane_partial.3
  30.7 1.6 %collective-permute-start.5 = (bf16[1024,512]{1,0:T(8,128)(2,1)S(1)}, bf16[1024,512]{1,0:T(8,128)(2,1)S(1)}, u32[]{:S(2)}, u32[]{:S(2)}) collective-permute-start(bf16[1024,512]{1,0:T(8,128)(2,1)S(1)} %plane_partial.3), channel_id=1, source_target_pairs={{0,4},{1,5},{2,6},{3,7},{4,8},{5,9},{6,10},{7,11},{8,12},{9,13},{1... | collective-permute-start | bytes 3145736 | tf_op jit(solution)/shard_map/ppermute | solution.py:246
  32.3 0.9 %collective-permute-done.9.refs_2_ = bf16[512,512]{1,0:T(8,128)(2,1)S(1)} collective-permute-done((bf16[512,512]{1,0:T(8,128)(2,1)S(1)}, bf16[512,512]{1,0:T(8,128)(2,1)S(1)}, u32[]{:S(2)}, u32[]{:S(2)}) %collective-permute-start.9) | collective-permute-done | bytes 524320 | tf_op jit(solution)/shard_map/ppermute | solution.py:249
  33.2 5.1 %plane_product.3 = (f32[192,1536]{1,0:T(8,128)S(1)}, bf16[192,2048]{1,0:T(8,128)(2,1)S(1)}, bf16[192,2048]{1,0:T(8,128)(2,1)S(1)}, bf16[192,2048]{1,0:T(8,128)(2,1)S(1)}) custom-call(f32[512,512]{1,0:T(8,128)S(1)} %get-tuple-element.60.refs_0_, bf16[512,512]{1,0:T(8,128)(2,1)S(1)} %collective-permute-done.refs_6_.refs_1_, ...), custom_call_target="tpu_custom_call" | custom-call | flops 68719476736 | bytes 1048576 | tf_op jit(solution)/shard_map/plane_product/pallas_call | solution.py:169
  38.4 1.6 %collective-permute-start.10 = (bf16[192,2048]{1,0:T(8,128)(2,1)S(1)}, bf16[192,2048]{1,0:T(8,128)(2,1)S(1)}, u32[]{:S(2)}, u32[]{:S(2)}) collective-permute-start(bf16[192,2048]{1,0:T(8,128)(2,1)S(1)} %get-tuple-element.65), channel_id=1, source_target_pairs={{0,1},{1,0},{2,3},{3,2},{4,5},{5,4},{6,7},{7,6},{8,9},{9,8},{10,11... | collective-permute-start | bytes 2359304 | tf_op jit(solution)/shard_map/ppermute | solution.py:252
  39.9 1.5 %collective-permute-start.12 = (bf16[192,2048]{1,0:T(8,128)(2,1)S(1)}, bf16[192,2048]{1,0:T(8,128)(2,1)S(1)}, u32[]{:S(2)}, u32[]{:S(2)}) collective-permute-start(bf16[192,2048]{1,0:T(8,128)(2,1)S(1)} %get-tuple-element.68), channel_id=1, source_target_pairs={{0,2},{1,3},{2,0},{3,1},{4,6},{5,7},{6,4},{7,5},{8,10},{9,11},{10,... | collective-permute-start | bytes 2359304 | tf_op jit(solution)/shard_map/ppermute | solution.py:252
  41.4 6.0 %collective-permute-done.7.refs_4_ = bf16[192,1024]{1,0:T(8,128)(2,1)S(1)} collective-permute-done((bf16[192,1024]{1,0:T(8,128)(2,1)S(1)}, bf16[192,1024]{1,0:T(8,128)(2,1)S(1)}, u32[]{:S(2)}, u32[]{:S(2)}) %collective-permute-start.7) | collective-permute-done | bytes 393248 | tf_op jit(solution)/shard_map/ppermute | solution.py:252
  47.5 8.4 %collective-permute-done.5.refs_6_.refs_0_ = bf16[1024,512]{1,0:T(8,128)(2,1)S(1)} collective-permute-done((bf16[1024,512]{1,0:T(8,128)(2,1)S(1)}, bf16[1024,512]{1,0:T(8,128)(2,1)S(1)}, u32[]{:S(2)}, u32[]{:S(2)}) %collective-permute-start.5) | collective-permute-done | bytes 1048608 | tf_op jit(solution)/shard_map/ppermute | solution.py:246
  55.9 2.0 %plane_partial.4 = (bf16[512,512]{1,0:T(8,128)(2,1)S(1)}, bf16[512,512]{1,0:T(8,128)(2,1)S(1)}) custom-call(bf16[192,2048]{1,0:T(8,128)(2,1)S(1)} %get-tuple-element.43.own, bf16[192,512]{1,0:T(8,128)(2,1)S(1)} %get-tuple-element.44.cot.refs_1_.refs_3_, bf16[192,1024]{1,0:T(8,128)(2,1)S(1)} %collective-permute-done.1.refs_0_.refs_3_.refs_2_.refs_4_, ...), custom_call_target="tpu_custom_call" | custom-call | flops 4294967296 | bytes 1048576 | tf_op jit(solution)/shard_map/plane_partial/pallas_call | solution.py:133
  57.9 4.0 %collective-permute-start.17 = (bf16[512,512]{1,0:T(8,128)(2,1)S(1)}, bf16[512,512]{1,0:T(8,128)(2,1)S(1)}, u32[]{:S(2)}, u32[]{:S(2)}) collective-permute-start(bf16[512,512]{1,0:T(8,128)(2,1)S(1)} %get-tuple-element.79), channel_id=1, source_target_pairs={{4,0},{5,1},{6,2},{7,3},{8,4},{9,5},{10,6},{11,7},{12,8},{13,9},{1... | collective-permute-start | bytes 1572872 | tf_op jit(solution)/shard_map/ppermute | solution.py:249
  62.0 2.0 %plane_product.2 = (f32[192,512]{1,0:T(8,128)S(1)}, bf16[192,512]{1,0:T(8,128)(2,1)S(1)}, bf16[192,512]{1,0:T(8,128)(2,1)S(1)}, bf16[192,512]{1,0:T(8,128)(2,1)S(1)}) custom-call(bf16[1024,512]{1,0:T(8,128)(2,1)S(1)} %collective-permute-done.5.refs_6_.refs_0_, bf16[192,512]{1,0:T(8,128)(2,1)S(1)} %get-tuple-element.44.cot.refs_1_.refs_3_, ...), custom_call_target="tpu_custom_call" | custom-call | flops 1048576 | bytes 1048576 | tf_op jit(solution)/shard_map/plane_product/pallas_call | solution.py:169
  64.0 1.3 %collective-permute-start.11 = (bf16[192,512]{1,0:T(8,128)(2,1)S(1)}, bf16[192,512]{1,0:T(8,128)(2,1)S(1)}, u32[]{:S(2)}, u32[]{:S(2)}) collective-permute-start(bf16[192,512]{1,0:T(8,128)(2,1)S(1)} %get-tuple-element.66), channel_id=1, source_target_pairs={{0,1},{1,0},{2,3},{3,2},{4,5},{5,4},{6,7},{7,6},{8,9},{9,8},{10,11... | collective-permute-start | bytes 589832 | tf_op jit(solution)/shard_map/ppermute | solution.py:252
  65.3 14.5 %collective-permute-done.12.refs_2_.refs_4_ = bf16[192,2048]{1,0:T(8,128)(2,1)S(1)} collective-permute-done((bf16[192,2048]{1,0:T(8,128)(2,1)S(1)}, bf16[192,2048]{1,0:T(8,128)(2,1)S(1)}, u32[]{:S(2)}, u32[]{:S(2)}) %collective-permute-start.12) | collective-permute-done | bytes 786464 | tf_op jit(solution)/shard_map/ppermute | solution.py:252
  79.7 1.8 %collective-permute-start.13 = (bf16[192,512]{1,0:T(8,128)(2,1)S(1)}, bf16[192,512]{1,0:T(8,128)(2,1)S(1)}, u32[]{:S(2)}, u32[]{:S(2)}) collective-permute-start(bf16[192,512]{1,0:T(8,128)(2,1)S(1)} %get-tuple-element.69), channel_id=1, source_target_pairs={{0,2},{1,3},{2,0},{3,1},{4,6},{5,7},{6,4},{7,5},{8,10},{9,11},{10,... | collective-permute-start | bytes 589832 | tf_op jit(solution)/shard_map/ppermute | solution.py:252
  81.6 2.4 %unpack.2.refs_4_ = f32[192,8192]{1,0:T(8,128)} custom-call(f32[192,1536]{1,0:T(8,128)S(1)} %get-tuple-element.73.refs_0_, bf16[192,2048]{1,0:T(8,128)(2,1)S(1)} %collective-permute-done.10.refs_1_.refs_3_, bf16[192,2048]{1,0:T(8,128)(2,1)S(1)} %collective-permute-done.12.refs_2_.refs_4_, bf16[192,2048]{1,0:T(8,128)(2,1)S(1)} %collective-permute-done.14.refs_3_.refs_5_), custom_call_target="tpu_custom_call" | custom-call | flops 4294967296 | bytes 1048576 | tf_op jit(solution)/shard_map/unpack/pallas_call | solution.py:210
  84.0 1.5 %plane_partial.5 = f32[512,512]{1,0:T(8,128)S(1)} custom-call(bf16[192,2048]{1,0:T(8,128)(2,1)S(1)} %get-tuple-element.43.own, bf16[192,512]{1,0:T(8,128)(2,1)S(1)} %get-tuple-element.44.cot.refs_1_.refs_3_, bf16[192,1024]{1,0:T(8,128)(2,1)S(1)} %collective-permute-done.1.refs_0_.refs_3_.refs_2_.refs_4_, ...), custom_call_target="tpu_custom_call" | custom-call | flops 17179869184 | bytes 1048576 | tf_op jit(solution)/shard_map/plane_partial/pallas_call | solution.py:133
  85.5 2.1 %subtract_bitcast_fusion = (f32[1,512,512]{2,1,0:T(8,128)}, f32[512,512]{1,0:T(8,128)S(1)}, f32[1,512,512]{2,1,0:T(8,128)}) fusion(f32[512,512]{1,0:T(8,128)S(1)} %get-tuple-element.60.refs_0_, f32[512,512]{1,0:T(8,128)S(1)} %plane_partial.5, f32[1,512,512]{2,1,0:T(8,128)S(1)} %copy-done.3, f32[1,512,512]{2,1,0:T(8,128)S(1)} %copy-done.4), kind=kLoop, calls=%fused_computation.7 | loop fusion | flops 4194304 | bytes 7340032 | tf_op jit(solution)/shard_map/broadcast_in_dim | solution.py:336
  87.6 1.6 %collective-permute-done.13.refs_2_ = bf16[192,512]{1,0:T(8,128)(2,1)S(1)} collective-permute-done((bf16[192,512]{1,0:T(8,128)(2,1)S(1)}, bf16[192,512]{1,0:T(8,128)(2,1)S(1)}, u32[]{:S(2)}, u32[]{:S(2)}) %collective-permute-start.13) | collective-permute-done | bytes 196640 | tf_op jit(solution)/shard_map/ppermute | solution.py:252
  89.3 1.3 %unpack.3 = f32[192,8192]{1,0:T(8,128)} custom-call(f32[192,512]{1,0:T(8,128)S(1)} %get-tuple-element.58.refs_0_, bf16[192,512]{1,0:T(8,128)(2,1)S(1)} %collective-permute-done.11.refs_1_, bf16[192,512]{1,0:T(8,128)(2,1)S(1)} %collective-permute-done.13.refs_2_, ...), custom_call_target="tpu_custom_call", output_to_operand_aliasing={{}: (4, {})} | custom-call | flops 1048576 | bytes 1048576 | tf_op jit(solution)/shard_map/unpack/pallas_call | solution.py:210
  (30 shorter events, 0.1 us)
Async XLA Ops:
  0.6 9.8 %collective-permute-start.3 = (f32[1,512,512]{2,1,0:T(8,128)}, f32[1,512,512]{2,1,0:T(8,128)S(1)}, u32[]{:S(2)}, u32[]{:S(2)}) collective-permute-start(f32[1,512,512]{2,1,0:T(8,128)} %param.13), channel_id=1, source_target_pairs={{0,16},{16,0},{1,17},{17,1},{2,18},{18,2},{3,19},{19,3},{4,20},{20... | collective-permute-start | bytes 3145736 | tf_op jit(solution)/shard_map/ppermute | solution.py:267
  1.2 0.9 %copy-start.2 = (bf16[192,512]{1,0:T(8,128)(2,1)S(1)}, bf16[192,512]{1,0:T(8,128)(2,1)}, u32[]{:S(2)}) copy-start(bf16[192,512]{1,0:T(8,128)(2,1)} %cot_in.1) | copy-start | bytes 589828
  2.1 10.9 %copy-start.5 = (f32[512,512]{1,0:T(8,128)S(1)}, f32[512,512]{1,0:T(8,128)}, u32[]{:S(2)}) copy-start(f32[512,512]{1,0:T(8,128)} %param.14) | copy-start | bytes 3145732
  2.1 10.9 %copy-start.6 = (f32[1,512,512]{2,1,0:T(8,128)S(1)}, f32[1,512,512]{2,1,0:T(8,128)}, u32[]{:S(2)}) copy-start(f32[1,512,512]{2,1,0:T(8,128)} %param.13) | copy-start | bytes 3145732
  2.1 10.9 %copy-start.7 = (f32[512,512]{1,0:T(8,128)S(1)}, f32[512,512]{1,0:T(8,128)}, u32[]{:S(2)}) copy-start(f32[512,512]{1,0:T(8,128)} %param.15) | copy-start | bytes 3145732
  4.8 25.0 %collective-permute-start = (bf16[512,512]{1,0:T(8,128)(2,1)S(1)}, bf16[512,512]{1,0:T(8,128)(2,1)S(1)}, u32[]{:S(2)}, u32[]{:S(2)}) collective-permute-start(bf16[512,512]{1,0:T(8,128)(2,1)S(1)} %get-tuple-element.45), channel_id=1, source_target_pairs={{0,4},{1,5},{2,6},{3,7},{4,8},{5,9},{6,10},{7,11},{8,12},{9,13},{1... | collective-permute-start | bytes 1572872 | tf_op jit(solution)/shard_map/ppermute | solution.py:246
  7.4 11.9 %collective-permute-start.1 = (bf16[192,1024]{1,0:T(8,128)(2,1)S(1)}, bf16[192,1024]{1,0:T(8,128)(2,1)S(1)}, u32[]{:S(2)}, u32[]{:S(2)}) collective-permute-start(bf16[192,1024]{1,0:T(8,128)(2,1)S(1)} %get-tuple-element.46), channel_id=1, source_target_pairs={{0,1},{1,0},{2,3},{3,2},{4,5},{5,4},{6,7},{7,6},{8,9},{9,8},{10,11... | collective-permute-start | bytes 1179656 | tf_op jit(solution)/shard_map/ppermute | solution.py:252
  8.9 18.9 %collective-permute-start.2 = (bf16[192,1024]{1,0:T(8,128)(2,1)S(1)}, bf16[192,1024]{1,0:T(8,128)(2,1)S(1)}, u32[]{:S(2)}, u32[]{:S(2)}) collective-permute-start(bf16[192,1024]{1,0:T(8,128)(2,1)S(1)} %get-tuple-element.47), channel_id=1, source_target_pairs={{0,2},{1,3},{2,0},{3,1},{4,6},{5,7},{6,4},{7,5},{8,10},{9,11},{10,... | collective-permute-start | bytes 1179656 | tf_op jit(solution)/shard_map/ppermute | solution.py:252
  10.4 19.4 %collective-permute-start.4 = (bf16[192,1024]{1,0:T(8,128)(2,1)S(1)}, bf16[192,1024]{1,0:T(8,128)(2,1)S(1)}, u32[]{:S(2)}, u32[]{:S(2)}) collective-permute-start(bf16[192,1024]{1,0:T(8,128)(2,1)S(1)} %get-tuple-element.49), channel_id=1, source_target_pairs={{0,3},{1,2},{2,1},{3,0},{4,7},{5,6},{6,5},{7,4},{8,11},{9,10},{10,... | collective-permute-start | bytes 1179656 | tf_op jit(solution)/shard_map/ppermute | solution.py:252
  10.9 22.4 %collective-permute-start.9 = (bf16[512,512]{1,0:T(8,128)(2,1)S(1)}, bf16[512,512]{1,0:T(8,128)(2,1)S(1)}, u32[]{:S(2)}, u32[]{:S(2)}) collective-permute-start(bf16[512,512]{1,0:T(8,128)(2,1)S(1)} %get-tuple-element.45), channel_id=1, source_target_pairs={{4,0},{5,1},{6,2},{7,3},{8,4},{9,5},{10,6},{11,7},{12,8},{13,9},{1... | collective-permute-start | bytes 1572872 | tf_op jit(solution)/shard_map/ppermute | solution.py:249
  14.5 18.7 %copy-start.1 = (f32[512,512]{1,0:T(8,128)}, f32[512,512]{1,0:T(8,128)S(1)}, u32[]{:S(2)}) copy-start(f32[512,512]{1,0:T(8,128)S(1)} %get-tuple-element.81.refs_10_) | copy-start | bytes 3145732
  19.3 20.6 %collective-permute-start.6 = (bf16[192,1024]{1,0:T(8,128)(2,1)S(1)}, bf16[192,1024]{1,0:T(8,128)(2,1)S(1)}, u32[]{:S(2)}, u32[]{:S(2)}) collective-permute-start(bf16[192,1024]{1,0:T(8,128)(2,1)S(1)} %get-tuple-element.54), channel_id=1, source_target_pairs={{0,1},{1,0},{2,3},{3,2},{4,5},{5,4},{6,7},{7,6},{8,9},{9,8},{10,11... | collective-permute-start | bytes 1179656 | tf_op jit(solution)/shard_map/ppermute | solution.py:252
  27.8 19.7 %collective-permute-start.7 = (bf16[192,1024]{1,0:T(8,128)(2,1)S(1)}, bf16[192,1024]{1,0:T(8,128)(2,1)S(1)}, u32[]{:S(2)}, u32[]{:S(2)}) collective-permute-start(bf16[192,1024]{1,0:T(8,128)(2,1)S(1)} %get-tuple-element.55), channel_id=1, source_target_pairs={{0,2},{1,3},{2,0},{3,1},{4,6},{5,7},{6,4},{7,5},{8,10},{9,11},{10,... | collective-permute-start | bytes 1179656 | tf_op jit(solution)/shard_map/ppermute | solution.py:252
  29.8 17.7 %collective-permute-start.8 = (bf16[192,1024]{1,0:T(8,128)(2,1)S(1)}, bf16[192,1024]{1,0:T(8,128)(2,1)S(1)}, u32[]{:S(2)}, u32[]{:S(2)}) collective-permute-start(bf16[192,1024]{1,0:T(8,128)(2,1)S(1)} %get-tuple-element.56), channel_id=1, source_target_pairs={{0,3},{1,2},{2,1},{3,0},{4,7},{5,6},{6,5},{7,4},{8,11},{9,10},{10,... | collective-permute-start | bytes 1179656 | tf_op jit(solution)/shard_map/ppermute | solution.py:252
  30.7 25.2 %collective-permute-start.5 = (bf16[1024,512]{1,0:T(8,128)(2,1)S(1)}, bf16[1024,512]{1,0:T(8,128)(2,1)S(1)}, u32[]{:S(2)}, u32[]{:S(2)}) collective-permute-start(bf16[1024,512]{1,0:T(8,128)(2,1)S(1)} %plane_partial.3), channel_id=1, source_target_pairs={{0,4},{1,5},{2,6},{3,7},{4,8},{5,9},{6,10},{7,11},{8,12},{9,13},{1... | collective-permute-start | bytes 3145736 | tf_op jit(solution)/shard_map/ppermute | solution.py:246
  38.4 25.6 %collective-permute-start.10 = (bf16[192,2048]{1,0:T(8,128)(2,1)S(1)}, bf16[192,2048]{1,0:T(8,128)(2,1)S(1)}, u32[]{:S(2)}, u32[]{:S(2)}) collective-permute-start(bf16[192,2048]{1,0:T(8,128)(2,1)S(1)} %get-tuple-element.65), channel_id=1, source_target_pairs={{0,1},{1,0},{2,3},{3,2},{4,5},{5,4},{6,7},{7,6},{8,9},{9,8},{10,11... | collective-permute-start | bytes 2359304 | tf_op jit(solution)/shard_map/ppermute | solution.py:252
  39.9 39.8 %collective-permute-start.12 = (bf16[192,2048]{1,0:T(8,128)(2,1)S(1)}, bf16[192,2048]{1,0:T(8,128)(2,1)S(1)}, u32[]{:S(2)}, u32[]{:S(2)}) collective-permute-start(bf16[192,2048]{1,0:T(8,128)(2,1)S(1)} %get-tuple-element.68), channel_id=1, source_target_pairs={{0,2},{1,3},{2,0},{3,1},{4,6},{5,7},{6,4},{7,5},{8,10},{9,11},{10,... | collective-permute-start | bytes 2359304 | tf_op jit(solution)/shard_map/ppermute | solution.py:252
  47.5 34.1 %collective-permute-start.14 = (bf16[192,2048]{1,0:T(8,128)(2,1)S(1)}, bf16[192,2048]{1,0:T(8,128)(2,1)S(1)}, u32[]{:S(2)}, u32[]{:S(2)}) collective-permute-start(bf16[192,2048]{1,0:T(8,128)(2,1)S(1)} %get-tuple-element.71), channel_id=1, source_target_pairs={{0,3},{1,2},{2,1},{3,0},{4,7},{5,6},{6,5},{7,4},{8,11},{9,10},{10,... | collective-permute-start | bytes 2359304 | tf_op jit(solution)/shard_map/ppermute | solution.py:252
  57.8 26.1 %collective-permute-start.16 = (bf16[512,512]{1,0:T(8,128)(2,1)S(1)}, bf16[512,512]{1,0:T(8,128)(2,1)S(1)}, u32[]{:S(2)}, u32[]{:S(2)}) collective-permute-start(bf16[512,512]{1,0:T(8,128)(2,1)S(1)} %get-tuple-element.57.refs_5_), channel_id=1, source_target_pairs={{0,4},{1,5},{2,6},{3,7},{4,8},{5,9},{6,10},{7,11},{8,12},{9,13},{1... | collective-permute-start | bytes 1572872 | tf_op jit(solution)/shard_map/ppermute | solution.py:246
  57.9 26.1 %collective-permute-start.17 = (bf16[512,512]{1,0:T(8,128)(2,1)S(1)}, bf16[512,512]{1,0:T(8,128)(2,1)S(1)}, u32[]{:S(2)}, u32[]{:S(2)}) collective-permute-start(bf16[512,512]{1,0:T(8,128)(2,1)S(1)} %get-tuple-element.79), channel_id=1, source_target_pairs={{4,0},{5,1},{6,2},{7,3},{8,4},{9,5},{10,6},{11,7},{12,8},{13,9},{1... | collective-permute-start | bytes 1572872 | tf_op jit(solution)/shard_map/ppermute | solution.py:249
  64.0 23.7 %collective-permute-start.11 = (bf16[192,512]{1,0:T(8,128)(2,1)S(1)}, bf16[192,512]{1,0:T(8,128)(2,1)S(1)}, u32[]{:S(2)}, u32[]{:S(2)}) collective-permute-start(bf16[192,512]{1,0:T(8,128)(2,1)S(1)} %get-tuple-element.66), channel_id=1, source_target_pairs={{0,1},{1,0},{2,3},{3,2},{4,5},{5,4},{6,7},{7,6},{8,9},{9,8},{10,11... | collective-permute-start | bytes 589832 | tf_op jit(solution)/shard_map/ppermute | solution.py:252
  79.7 9.5 %collective-permute-start.13 = (bf16[192,512]{1,0:T(8,128)(2,1)S(1)}, bf16[192,512]{1,0:T(8,128)(2,1)S(1)}, u32[]{:S(2)}, u32[]{:S(2)}) collective-permute-start(bf16[192,512]{1,0:T(8,128)(2,1)S(1)} %get-tuple-element.69), channel_id=1, source_target_pairs={{0,2},{1,3},{2,0},{3,1},{4,6},{5,7},{6,4},{7,5},{8,10},{9,11},{10,... | collective-permute-start | bytes 589832 | tf_op jit(solution)/shard_map/ppermute | solution.py:252
  81.5 7.7 %collective-permute-start.15 = (bf16[192,512]{1,0:T(8,128)(2,1)S(1)}, bf16[192,512]{1,0:T(8,128)(2,1)S(1)}, u32[]{:S(2)}, u32[]{:S(2)}) collective-permute-start(bf16[192,512]{1,0:T(8,128)(2,1)S(1)} %get-tuple-element.72), channel_id=1, source_target_pairs={{0,3},{1,2},{2,1},{3,0},{4,7},{5,6},{6,5},{7,4},{8,11},{9,10},{10,... | collective-permute-start | bytes 589832 | tf_op jit(solution)/shard_map/ppermute | solution.py:252
  83.9 1.5 %copy-start.3 = (f32[1,512,512]{2,1,0:T(8,128)S(1)}, f32[1,512,512]{2,1,0:T(8,128)}, u32[]{:S(2)}) copy-start(f32[1,512,512]{2,1,0:T(8,128)} %param.12) | copy-start | bytes 3145732
  84.0 1.5 %copy-start.4 = (f32[1,512,512]{2,1,0:T(8,128)S(1)}, f32[1,512,512]{2,1,0:T(8,128)}, u32[]{:S(2)}) copy-start(f32[1,512,512]{2,1,0:T(8,128)} %param.11) | copy-start | bytes 3145732
  87.6 2.9 %copy-start = (f32[512,512]{1,0:T(8,128)}, f32[512,512]{1,0:T(8,128)S(1)}, u32[]{:S(2)}) copy-start(f32[512,512]{1,0:T(8,128)S(1)} %get-tuple-element.83.refs_5_) | copy-start | bytes 3145732

commit v7 on v6

--- a/solution.py
+++ b/solution.py
@@ -19,8 +19,8 @@
 PLANE = 4
 WEIGHT_SCALE = 2.0**17
 WIRE = jnp.bfloat16
-ORDER = (1, 2, 3)
-C_PARTIAL, C_PRODUCT, C_UNPACK = (36, 32, 34), (36, 20), (32, 20)
+PEERS = (0, 2, 3, 1)
+C_PARTIAL, C_PRODUCT, C_UNPACK = (32, 32, 36), (33, 20), (36, 20)
 
 
 def cost(log_flops):
@@ -78,7 +78,7 @@
             first[:, : cot.shape[1]] = cot[...]
         for at, distance in enumerate(distances):
             block = lax.rem(z + planes + distance, planes)
-            start = pl.multiple_of((block * PLANE + (p ^ k)) * columns, 128)
+            start = pl.multiple_of((block * PLANE + (p ^ PEERS[k])) * columns, 128)
             value = features[:, pl.ds(start, columns)]
             if k == 0:
                 own[:, at * columns : (at + 1) * columns] = value
@@ -195,7 +195,7 @@
             else:
                 buffer[i] = decode(pieces[k][:, span]) * factor
                 source = buffer.at[i]
-            start = pl.multiple_of((block * PLANE + (p ^ k)) * columns, 128)
+            start = pl.multiple_of((block * PLANE + (p ^ PEERS[k])) * columns, 128)
             copy = pltpu.make_async_copy(source, out.at[:, pl.ds(start, columns)], sem.at[i])
             copy.start()
             copies.append(copy)
@@ -249,11 +249,10 @@
         return lax.ppermute(x, "fsdp", [(to, source) for source, to in ring])
 
     def across(x, k):
-        return lax.ppermute(x, "fsdp", [(i, i ^ k) for i in range(size)])
+        return lax.ppermute(x, "fsdp", [(i, i ^ PEERS[k]) for i in range(size)])
 
     def across_all(parts):
-        moved = {k: across(parts[k - 1], k) for k in ORDER}
-        return [moved[k] for k in range(1, PLANE)]
+        return [across(part, k + 1) for k, part in enumerate(parts)]
 
     workers = lax.axis_size("worker")
     half = planes // 2
@@ -285,29 +284,25 @@
     def partials(spread, parts, rest, dtype, span):
         return plane_partial(spread, own, cot, firsts, parts, rest, columns, gradient_scale, dtype, span)
 
-    plus, minus = partials([(0, cot.shape[1], 0, half > 1)], firsts, [behind], WIRE, C_PARTIAL[0])[0], None
+    plus, minus = partials([(0, cot.shape[1], 0, False)], firsts, [], WIRE, C_PARTIAL[0])[0], None
     early = plane_product(weights, cot, firsts, riders, new_momentum, columns, product_scale, C_PRODUCT[0])
     early[1:] = across_all(early[1:])
     late_weights, late_offsets = [], []
     for step in range(half - 1, 0, -1):
         plus = around(plus)
-        late_weights.append(plus)
+        if step == half - 1:
+            behind, plus = lax.optimization_barrier((behind, plus))
+        behind = around(behind)
+        late_weights.append(behind)
         late_offsets.append(step - half - 1)
         at = (planes - 1 - 2 * step) * columns
-        spread, rest = [(at, at - columns, 1, step > 1)], [plus]
-        if step > 1:
-            rest.append(plus)
-        if minus is None:
-            carried = ahead
-            spread.append((at + columns, at, 0, step > 1))
-        else:
-            carried = minus = back(minus)
-            late_weights.append(minus)
+        spread, rest = [(at, at - columns, 1, False), (at + columns, at, 0, False)], [plus]
+        if minus is not None:
+            minus, ahead = back(minus), back(ahead)
+            late_weights.append(ahead)
             late_offsets.append(half - step)
-            spread.append((at + columns, at, 1, step > 1))
+            spread[1] = (at + columns, at, 1, False)
             rest.append(minus)
-        if step > 1:
-            rest.append(carried)
         plus, minus = partials(spread, middles, rest, WIRE, C_PARTIAL[1])
     factor = 1.0 / product_scale
     late = plane_product(late_weights, cot, firsts, [], plus, columns, product_scale, C_PRODUCT[1])

time: 90.9 us -> 92.1 us (1.013)
  starting transfers between devices: 24.2 us -> 32.6 us
  waiting for transfers between devices: 43.2 us -> 36 us
    ppermute x12, waiting for transfers between devices: 33.9 us -> 25 us  [across(): return lax.ppermute(x, 'fsdp', [(i, i ^ PEERS[k]) for i in range(size)])]
    ppermute x3 -> x4, starting transfers between devices: 4.33 us -> 12.6 us  [around(): return lax.ppermute(x, 'fsdp', ring)]
    ppermute x3 -> x4, waiting for transfers between devices: 8.39 us -> 10.9 us  [around(): return lax.ppermute(x, 'fsdp', ring)]
    ppermute x12, starting transfers between devices: 13.2 us -> 15.1 us  [across(): return lax.ppermute(x, 'fsdp', [(i, i ^ PEERS[k]) for i in range(size)])]
    ppermute x2, starting transfers between devices: 6.15 us -> 4.4 us  [back(): return lax.ppermute(x, 'fsdp', [(to, source) for source, to in ring])]
  transfers between devices with their start and end apart: 18 -> 19, of which waited for: 7 -> 6; matrix products, arithmetic and copies ran while one was open for 4% -> 4% of each run, Pallas kernels for 18% -> 18%
where the time goes in v7:
time: 92.1 us; the launch traced here: 92 us
  waiting for transfers between devices  36 us (39%)
  starting transfers between devices  32.6 us (35%)
  Pallas kernels  17.8 us (19%)
  other arithmetic  3.64 us (4%)
  local copies, waits for them, and re-layouts  0.96 us (1%)
  between operations  0.93 us (1%)
    ppermute x12, waiting for transfers between devices, across(): return lax.ppermute(x, 'fsdp', [(i, i ^ PEERS[k]) for i in range(size)])  25 us
    ppermute x12, starting transfers between devices, across(): return lax.ppermute(x, 'fsdp', [(i, i ^ PEERS[k]) for i in range(size)])  15.1 us
    ppermute x4, starting transfers between devices, around(): return lax.ppermute(x, 'fsdp', ring)  12.6 us
    ppermute x4, waiting for transfers between devices, around(): return lax.ppermute(x, 'fsdp', ring)  10.9 us
    pallas_call x2, Pallas kernels, plane_product(): pl.pallas_call(functools.partial(product_kernel, columns, len(weights), s...  7.11 us
    ppermute x2, starting transfers between devices, back(): return lax.ppermute(x, 'fsdp', [(to, source) for source, to in ring])  4.4 us
    pallas_call x3, Pallas kernels, plane_partial(): pl.pallas_call(functools.partial(partial_kernel, columns, scale, spread),...  4.34 us
    pallas_call x2, Pallas kernels, unpack(): pl.pallas_call(functools.partial(unpack_kernel, columns, planes, 'fsdp',...  3.67 us
  transfers between devices with their start and end apart: 19, of which 6 were waited for; matrix products, arithmetic and copies ran while one was open for 4% of the time, Pallas kernels for 18%

profile of v7, /device:TPU:0, one launch (start us, length us, event | category | flops | bytes accessed | tf_op | source)
XLA Modules:
  0.0 92.0 jit_solution(6661033919448208442)
XLA Ops:
  1.2 0.9 %copy-done.2 = bf16[192,512]{1,0:T(8,128)(2,1)S(1)} copy-done((bf16[192,512]{1,0:T(8,128)(2,1)S(1)}, bf16[192,512]{1,0:T(8,128)(2,1)}, u32[]{:S(2)}) %copy-start.2) | copy-done | bytes 196632
  2.1 2.7 %pack.1 = (bf16[512,512]{1,0:T(8,128)(2,1)S(1)}, f32[512,512]{1,0:T(8,128)S(1)}, bf16[192,512]{1,0:T(8,128)(2,1)S(1)}, bf16[192,2048]{1,0:T(8,128)(2,1)S(1)}, bf...) custom-call(bf16[192,8192]{1,0:T(8,128)(2,1)} %features_far.1, ...), custom_call_target="tpu_custom_call" | custom-call | flops 68719476736 | bytes 1048576 | tf_op jit(solution)/shard_map/pack/pallas_call | solution.py:96
  4.8 2.6 %collective-permute-start = (bf16[512,512]{1,0:T(8,128)(2,1)S(1)}, bf16[512,512]{1,0:T(8,128)(2,1)S(1)}, u32[]{:S(2)}, u32[]{:S(2)}) collective-permute-start(bf16[512,512]{1,0:T(8,128)(2,1)S(1)} %get-tuple-element.45), channel_id=1, source_target_pairs={{0,4},{1,5},{2,6},{3,7},{4,8},{5,9},{6,10},{7,11},{8,12},{9,13},{1... | collective-permute-start | bytes 1572872 | tf_op jit(solution)/shard_map/ppermute | solution.py:246
  7.4 1.5 %collective-permute-start.1 = (bf16[192,1024]{1,0:T(8,128)(2,1)S(1)}, bf16[192,1024]{1,0:T(8,128)(2,1)S(1)}, u32[]{:S(2)}, u32[]{:S(2)}) collective-permute-start(bf16[192,1024]{1,0:T(8,128)(2,1)S(1)} %get-tuple-element.46), channel_id=1, source_target_pairs={{0,2},{1,3},{2,0},{3,1},{4,6},{5,7},{6,4},{7,5},{8,10},{9,11},{10,... | collective-permute-start | bytes 1179656 | tf_op jit(solution)/shard_map/ppermute | solution.py:252
  8.9 1.4 %collective-permute-start.2 = (bf16[192,1024]{1,0:T(8,128)(2,1)S(1)}, bf16[192,1024]{1,0:T(8,128)(2,1)S(1)}, u32[]{:S(2)}, u32[]{:S(2)}) collective-permute-start(bf16[192,1024]{1,0:T(8,128)(2,1)S(1)} %get-tuple-element.47), channel_id=1, source_target_pairs={{0,3},{1,2},{2,1},{3,0},{4,7},{5,6},{6,5},{7,4},{8,11},{9,10},{10,... | collective-permute-start | bytes 1179656 | tf_op jit(solution)/shard_map/ppermute | solution.py:252
  10.9 2.1 %collective-permute-start.10 = (bf16[512,512]{1,0:T(8,128)(2,1)S(1)}, bf16[512,512]{1,0:T(8,128)(2,1)S(1)}, u32[]{:S(2)}, u32[]{:S(2)}) collective-permute-start(bf16[512,512]{1,0:T(8,128)(2,1)S(1)} %get-tuple-element.45), channel_id=1, source_target_pairs={{4,0},{5,1},{6,2},{7,3},{8,4},{9,5},{10,6},{11,7},{12,8},{13,9},{1... | collective-permute-start | bytes 1572872 | tf_op jit(solution)/shard_map/ppermute | solution.py:249
  13.0 1.5 %multiply_subtract_fusion = (f32[512,512]{1,0:T(8,128)}, f32[512,512]{1,0:T(8,128)S(1)}) fusion(f32[512,512]{1,0:T(8,128)S(1)} %copy-done.5, f32[1,512,512]{2,1,0:T(8,128)S(1)} %collective-permute-done.3, f32[1,512,512]{2,1,0:T(8,128)S(1)} %copy-done.6, f32[512,512]{1,0:T(8,128)S(1)} %copy-done.7), kind=kLoop, calls=%fused_computation.6 | loop fusion | flops 2621440 | bytes 6291456 | tf_op jit(solution)/shard_map/sub | solution.py:278
  14.5 12.5 %collective-permute-done.1.refs_0_.refs_3_.refs_2_.refs_4_ = bf16[192,1024]{1,0:T(8,128)(2,1)S(1)} collective-permute-done((bf16[192,1024]{1,0:T(8,128)(2,1)S(1)}, bf16[192,1024]{1,0:T(8,128)(2,1)S(1)}, u32[]{:S(2)}, u32[]{:S(2)}) %collective-permute-start.1) | collective-permute-done | bytes 393248 | tf_op jit(solution)/shard_map/ppermute | solution.py:252
  27.1 1.5 %collective-permute-start.7 = (bf16[192,1024]{1,0:T(8,128)(2,1)S(1)}, bf16[192,1024]{1,0:T(8,128)(2,1)S(1)}, u32[]{:S(2)}, u32[]{:S(2)}) collective-permute-start(bf16[192,1024]{1,0:T(8,128)(2,1)S(1)} %get-tuple-element.57), channel_id=1, source_target_pairs={{0,2},{1,3},{2,0},{3,1},{4,6},{5,7},{6,4},{7,5},{8,10},{9,11},{10,... | collective-permute-start | bytes 1179656 | tf_op jit(solution)/shard_map/ppermute | solution.py:252
  28.6 1.4 %collective-permute-start.8 = (bf16[192,1024]{1,0:T(8,128)(2,1)S(1)}, bf16[192,1024]{1,0:T(8,128)(2,1)S(1)}, u32[]{:S(2)}, u32[]{:S(2)}) collective-permute-start(bf16[192,1024]{1,0:T(8,128)(2,1)S(1)} %get-tuple-element.58), channel_id=1, source_target_pairs={{0,3},{1,2},{2,1},{3,0},{4,7},{5,6},{6,5},{7,4},{8,11},{9,10},{10,... | collective-permute-start | bytes 1179656 | tf_op jit(solution)/shard_map/ppermute | solution.py:252
  30.6 0.9 plane_partial.3
  31.5 1.6 %collective-permute-start.5 = (bf16[512,512]{1,0:T(8,128)(2,1)S(1)}, bf16[512,512]{1,0:T(8,128)(2,1)S(1)}, u32[]{:S(2)}, u32[]{:S(2)}) collective-permute-start(bf16[512,512]{1,0:T(8,128)(2,1)S(1)} %plane_partial.3), channel_id=1, source_target_pairs={{0,4},{1,5},{2,6},{3,7},{4,8},{5,9},{6,10},{7,11},{8,12},{9,13},{1... | collective-permute-start | bytes 1572872 | tf_op jit(solution)/shard_map/ppermute | solution.py:246
  33.3 5.1 %plane_product.3 = (f32[192,1536]{1,0:T(8,128)S(1)}, bf16[192,2048]{1,0:T(8,128)(2,1)S(1)}, bf16[192,2048]{1,0:T(8,128)(2,1)S(1)}, bf16[192,2048]{1,0:T(8,128)(2,1)S(1)}) custom-call(f32[512,512]{1,0:T(8,128)S(1)} %get-tuple-element.64.refs_0_, bf16[512,512]{1,0:T(8,128)(2,1)S(1)} %collective-permute-done.refs_1_, ...), custom_call_target="tpu_custom_call" | custom-call | flops 8589934592 | bytes 1048576 | tf_op jit(solution)/shard_map/plane_product/pallas_call | solution.py:169
  38.4 1.6 %collective-permute-start.11 = (bf16[192,2048]{1,0:T(8,128)(2,1)S(1)}, bf16[192,2048]{1,0:T(8,128)(2,1)S(1)}, u32[]{:S(2)}, u32[]{:S(2)}) collective-permute-start(bf16[192,2048]{1,0:T(8,128)(2,1)S(1)} %get-tuple-element.69), channel_id=1, source_target_pairs={{0,2},{1,3},{2,0},{3,1},{4,6},{5,7},{6,4},{7,5},{8,10},{9,11},{10,... | collective-permute-start | bytes 2359304 | tf_op jit(solution)/shard_map/ppermute | solution.py:252
  40.0 7.6 %collective-permute-done.7.refs_3_ = bf16[192,1024]{1,0:T(8,128)(2,1)S(1)} collective-permute-done((bf16[192,1024]{1,0:T(8,128)(2,1)S(1)}, bf16[192,1024]{1,0:T(8,128)(2,1)S(1)}, u32[]{:S(2)}, u32[]{:S(2)}) %collective-permute-start.7) | collective-permute-done | bytes 393248 | tf_op jit(solution)/shard_map/ppermute | solution.py:252
  47.5 2.1 %collective-permute-start.13 = (bf16[192,2048]{1,0:T(8,128)(2,1)S(1)}, bf16[192,2048]{1,0:T(8,128)(2,1)S(1)}, u32[]{:S(2)}, u32[]{:S(2)}) collective-permute-start(bf16[192,2048]{1,0:T(8,128)(2,1)S(1)} %get-tuple-element.72), channel_id=1, source_target_pairs={{0,3},{1,2},{2,1},{3,0},{4,7},{5,6},{6,5},{7,4},{8,11},{9,10},{10,... | collective-permute-start | bytes 2359304 | tf_op jit(solution)/shard_map/ppermute | solution.py:252
  49.6 0.5 collective-permute-start.15
  50.2 1.6 %collective-permute-start.6 = (bf16[512,512]{1,0:T(8,128)(2,1)S(1)}, bf16[512,512]{1,0:T(8,128)(2,1)S(1)}, u32[]{:S(2)}, u32[]{:S(2)}) collective-permute-start(bf16[512,512]{1,0:T(8,128)(2,1)S(1)} %collective-permute-done.refs_1_), channel_id=1, source_target_pairs={{0,4},{1,5},{2,6},{3,7},{4,8},{5,9},{6,10},{7,11},{8,12},{9,13},{1... | collective-permute-start | bytes 1572872 | tf_op jit(solution)/shard_map/ppermute | solution.py:246
  51.8 2.0 %plane_partial.4 = (bf16[512,512]{1,0:T(8,128)(2,1)S(1)}, bf16[512,512]{1,0:T(8,128)(2,1)S(1)}) custom-call(bf16[192,2048]{1,0:T(8,128)(2,1)S(1)} %get-tuple-element.51.own, bf16[192,512]{1,0:T(8,128)(2,1)S(1)} %get-tuple-element.52.cot.refs_1_.refs_3_, bf16[192,1024]{1,0:T(8,128)(2,1)S(1)} %collective-permute-done.1.refs_0_.refs_3_.refs_2_.refs_4_, ...), custom_call_target="tpu_custom_call" | custom-call | flops 4294967296 | bytes 1048576 | tf_op jit(solution)/shard_map/plane_partial/pallas_call | solution.py:133
  53.8 2.3 %collective-permute-start.18 = (bf16[512,512]{1,0:T(8,128)(2,1)S(1)}, bf16[512,512]{1,0:T(8,128)(2,1)S(1)}, u32[]{:S(2)}, u32[]{:S(2)}) collective-permute-start(bf16[512,512]{1,0:T(8,128)(2,1)S(1)} %get-tuple-element.83), channel_id=1, source_target_pairs={{4,0},{5,1},{6,2},{7,3},{8,4},{9,5},{10,6},{11,7},{12,8},{13,9},{1... | collective-permute-start | bytes 1572872 | tf_op jit(solution)/shard_map/ppermute | solution.py:249
  56.1 10.8 %collective-permute-done.6.refs_0_ = bf16[512,512]{1,0:T(8,128)(2,1)S(1)} collective-permute-done((bf16[512,512]{1,0:T(8,128)(2,1)S(1)}, bf16[512,512]{1,0:T(8,128)(2,1)S(1)}, u32[]{:S(2)}, u32[]{:S(2)}) %collective-permute-start.6) | collective-permute-done | bytes 524320 | tf_op jit(solution)/shard_map/ppermute | solution.py:246
  66.9 6.8 %collective-permute-start.17 = (bf16[512,512]{1,0:T(8,128)(2,1)S(1)}, bf16[512,512]{1,0:T(8,128)(2,1)S(1)}, u32[]{:S(2)}, u32[]{:S(2)}) collective-permute-start(bf16[512,512]{1,0:T(8,128)(2,1)S(1)} %get-tuple-element.61.refs_5_), channel_id=1, source_target_pairs={{0,4},{1,5},{2,6},{3,7},{4,8},{5,9},{6,10},{7,11},{8,12},{9,13},{1... | collective-permute-start | bytes 1572872 | tf_op jit(solution)/shard_map/ppermute | solution.py:246
  73.7 2.0 %plane_product.2 = (f32[192,512]{1,0:T(8,128)S(1)}, bf16[192,512]{1,0:T(8,128)(2,1)S(1)}, bf16[192,512]{1,0:T(8,128)(2,1)S(1)}, bf16[192,512]{1,0:T(8,128)(2,1)S(1)}) custom-call(bf16[512,512]{1,0:T(8,128)(2,1)S(1)} %collective-permute-done.6.refs_0_, bf16[192,512]{1,0:T(8,128)(2,1)S(1)} %get-tuple-element.52.cot.refs_1_.refs_3_, ...), custom_call_target="tpu_custom_call" | custom-call | flops 1048576 | bytes 1048576 | tf_op jit(solution)/shard_map/plane_product/pallas_call | solution.py:169
  75.7 3.9 %collective-permute-done.11.refs_1_.refs_3_ = bf16[192,2048]{1,0:T(8,128)(2,1)S(1)} collective-permute-done((bf16[192,2048]{1,0:T(8,128)(2,1)S(1)}, bf16[192,2048]{1,0:T(8,128)(2,1)S(1)}, u32[]{:S(2)}, u32[]{:S(2)}) %collective-permute-start.11) | collective-permute-done | bytes 786464 | tf_op jit(solution)/shard_map/ppermute | solution.py:252
  79.6 1.5 %collective-permute-start.12 = (bf16[192,512]{1,0:T(8,128)(2,1)S(1)}, bf16[192,512]{1,0:T(8,128)(2,1)S(1)}, u32[]{:S(2)}, u32[]{:S(2)}) collective-permute-start(bf16[192,512]{1,0:T(8,128)(2,1)S(1)} %get-tuple-element.70), channel_id=1, source_target_pairs={{0,2},{1,3},{2,0},{3,1},{4,6},{5,7},{6,4},{7,5},{8,10},{9,11},{10,... | collective-permute-start | bytes 589832 | tf_op jit(solution)/shard_map/ppermute | solution.py:252
  81.1 1.4 %collective-permute-start.14 = (bf16[192,512]{1,0:T(8,128)(2,1)S(1)}, bf16[192,512]{1,0:T(8,128)(2,1)S(1)}, u32[]{:S(2)}, u32[]{:S(2)}) collective-permute-start(bf16[192,512]{1,0:T(8,128)(2,1)S(1)} %get-tuple-element.73), channel_id=1, source_target_pairs={{0,3},{1,2},{2,1},{3,0},{4,7},{5,6},{6,5},{7,4},{8,11},{9,10},{10,... | collective-permute-start | bytes 589832 | tf_op jit(solution)/shard_map/ppermute | solution.py:252
  82.6 0.9 %collective-permute-start.16 = (bf16[192,512]{1,0:T(8,128)(2,1)S(1)}, bf16[192,512]{1,0:T(8,128)(2,1)S(1)}, u32[]{:S(2)}, u32[]{:S(2)}) collective-permute-start(bf16[192,512]{1,0:T(8,128)(2,1)S(1)} %get-tuple-element.76), channel_id=1, source_target_pairs={{0,1},{1,0},{2,3},{3,2},{4,5},{5,4},{6,7},{7,6},{8,9},{9,8},{10,11... | collective-permute-start | bytes 589832 | tf_op jit(solution)/shard_map/ppermute | solution.py:252
  83.5 2.4 %unpack.2.refs_4_ = f32[192,8192]{1,0:T(8,128)} custom-call(f32[192,1536]{1,0:T(8,128)S(1)} %get-tuple-element.77.refs_0_, bf16[192,2048]{1,0:T(8,128)(2,1)S(1)} %collective-permute-done.11.refs_1_.refs_3_, bf16[192,2048]{1,0:T(8,128)(2,1)S(1)} %collective-permute-done.13.refs_2_.refs_4_, bf16[192,2048]{1,0:T(8,128)(2,1)S(1)} %collective-permute-done.15.refs_3_.refs_5_), custom_call_target="tpu_custom_call" | custom-call | flops 68719476736 | bytes 1048576 | tf_op jit(solution)/shard_map/unpack/pallas_call | solution.py:210
  85.9 1.5 %plane_partial.5 = f32[512,512]{1,0:T(8,128)S(1)} custom-call(bf16[192,2048]{1,0:T(8,128)(2,1)S(1)} %get-tuple-element.51.own, bf16[192,512]{1,0:T(8,128)(2,1)S(1)} %get-tuple-element.52.cot.refs_1_.refs_3_, bf16[192,1024]{1,0:T(8,128)(2,1)S(1)} %collective-permute-done.1.refs_0_.refs_3_.refs_2_.refs_4_, ...), custom_call_target="tpu_custom_call" | custom-call | flops 68719476736 | bytes 1048576 | tf_op jit(solution)/shard_map/plane_partial/pallas_call | solution.py:133
  87.4 2.1 %subtract_bitcast_fusion = (f32[1,512,512]{2,1,0:T(8,128)}, f32[512,512]{1,0:T(8,128)S(1)}, f32[1,512,512]{2,1,0:T(8,128)}) fusion(f32[512,512]{1,0:T(8,128)S(1)} %get-tuple-element.64.refs_0_, f32[512,512]{1,0:T(8,128)S(1)} %plane_partial.5, f32[1,512,512]{2,1,0:T(8,128)S(1)} %copy-done.3, f32[1,512,512]{2,1,0:T(8,128)S(1)} %copy-done.4), kind=kLoop, calls=%fused_computation.7 | loop fusion | flops 4194304 | bytes 7340032 | tf_op jit(solution)/shard_map/broadcast_in_dim | solution.py:331
  89.6 0.9 collective-permute-done.16.refs_3_
  90.5 1.3 %unpack.3 = f32[192,8192]{1,0:T(8,128)} custom-call(f32[192,512]{1,0:T(8,128)S(1)} %get-tuple-element.62.refs_0_, bf16[192,512]{1,0:T(8,128)(2,1)S(1)} %collective-permute-done.12.refs_1_, bf16[192,512]{1,0:T(8,128)(2,1)S(1)} %collective-permute-done.14.refs_2_, ...), custom_call_target="tpu_custom_call", output_to_operand_aliasing={{}: (4, {})} | custom-call | flops 1048576 | bytes 1048576 | tf_op jit(solution)/shard_map/unpack/pallas_call | solution.py:210
  (32 shorter events, 1.8 us)
Async XLA Ops:
  0.6 9.7 %collective-permute-start.3 = (f32[1,512,512]{2,1,0:T(8,128)}, f32[1,512,512]{2,1,0:T(8,128)S(1)}, u32[]{:S(2)}, u32[]{:S(2)}) collective-permute-start(f32[1,512,512]{2,1,0:T(8,128)} %param.13), channel_id=1, source_target_pairs={{0,16},{16,0},{1,17},{17,1},{2,18},{18,2},{3,19},{19,3},{4,20},{20... | collective-permute-start | bytes 3145736 | tf_op jit(solution)/shard_map/ppermute | solution.py:266
  1.2 0.9 %copy-start.2 = (bf16[192,512]{1,0:T(8,128)(2,1)S(1)}, bf16[192,512]{1,0:T(8,128)(2,1)}, u32[]{:S(2)}) copy-start(bf16[192,512]{1,0:T(8,128)(2,1)} %cot_in.1) | copy-start | bytes 589828
  2.1 10.9 %copy-start.5 = (f32[512,512]{1,0:T(8,128)S(1)}, f32[512,512]{1,0:T(8,128)}, u32[]{:S(2)}) copy-start(f32[512,512]{1,0:T(8,128)} %param.14) | copy-start | bytes 3145732
  2.1 10.9 %copy-start.6 = (f32[1,512,512]{2,1,0:T(8,128)S(1)}, f32[1,512,512]{2,1,0:T(8,128)}, u32[]{:S(2)}) copy-start(f32[1,512,512]{2,1,0:T(8,128)} %param.13) | copy-start | bytes 3145732
  2.1 10.9 %copy-start.7 = (f32[512,512]{1,0:T(8,128)S(1)}, f32[512,512]{1,0:T(8,128)}, u32[]{:S(2)}) copy-start(f32[512,512]{1,0:T(8,128)} %param.15) | copy-start | bytes 3145732
  4.8 25.3 %collective-permute-start = (bf16[512,512]{1,0:T(8,128)(2,1)S(1)}, bf16[512,512]{1,0:T(8,128)(2,1)S(1)}, u32[]{:S(2)}, u32[]{:S(2)}) collective-permute-start(bf16[512,512]{1,0:T(8,128)(2,1)S(1)} %get-tuple-element.45), channel_id=1, source_target_pairs={{0,4},{1,5},{2,6},{3,7},{4,8},{5,9},{6,10},{7,11},{8,12},{9,13},{1... | collective-permute-start | bytes 1572872 | tf_op jit(solution)/shard_map/ppermute | solution.py:246
  7.4 19.7 %collective-permute-start.1 = (bf16[192,1024]{1,0:T(8,128)(2,1)S(1)}, bf16[192,1024]{1,0:T(8,128)(2,1)S(1)}, u32[]{:S(2)}, u32[]{:S(2)}) collective-permute-start(bf16[192,1024]{1,0:T(8,128)(2,1)S(1)} %get-tuple-element.46), channel_id=1, source_target_pairs={{0,2},{1,3},{2,0},{3,1},{4,6},{5,7},{6,4},{7,5},{8,10},{9,11},{10,... | collective-permute-start | bytes 1179656 | tf_op jit(solution)/shard_map/ppermute | solution.py:252
  8.9 19.7 %collective-permute-start.2 = (bf16[192,1024]{1,0:T(8,128)(2,1)S(1)}, bf16[192,1024]{1,0:T(8,128)(2,1)S(1)}, u32[]{:S(2)}, u32[]{:S(2)}) collective-permute-start(bf16[192,1024]{1,0:T(8,128)(2,1)S(1)} %get-tuple-element.47), channel_id=1, source_target_pairs={{0,3},{1,2},{2,1},{3,0},{4,7},{5,6},{6,5},{7,4},{8,11},{9,10},{10,... | collective-permute-start | bytes 1179656 | tf_op jit(solution)/shard_map/ppermute | solution.py:252
  10.4 20.2 %collective-permute-start.4 = (bf16[192,1024]{1,0:T(8,128)(2,1)S(1)}, bf16[192,1024]{1,0:T(8,128)(2,1)S(1)}, u32[]{:S(2)}, u32[]{:S(2)}) collective-permute-start(bf16[192,1024]{1,0:T(8,128)(2,1)S(1)} %get-tuple-element.49), channel_id=1, source_target_pairs={{0,1},{1,0},{2,3},{3,2},{4,5},{5,4},{6,7},{7,6},{8,9},{9,8},{10,11... | collective-permute-start | bytes 1179656 | tf_op jit(solution)/shard_map/ppermute | solution.py:252
  10.9 22.4 %collective-permute-start.10 = (bf16[512,512]{1,0:T(8,128)(2,1)S(1)}, bf16[512,512]{1,0:T(8,128)(2,1)S(1)}, u32[]{:S(2)}, u32[]{:S(2)}) collective-permute-start(bf16[512,512]{1,0:T(8,128)(2,1)S(1)} %get-tuple-element.45), channel_id=1, source_target_pairs={{4,0},{5,1},{6,2},{7,3},{8,4},{9,5},{10,6},{11,7},{12,8},{13,9},{1... | collective-permute-start | bytes 1572872 | tf_op jit(solution)/shard_map/ppermute | solution.py:249
  14.5 18.7 %copy-start.1 = (f32[512,512]{1,0:T(8,128)}, f32[512,512]{1,0:T(8,128)S(1)}, u32[]{:S(2)}) copy-start(f32[512,512]{1,0:T(8,128)S(1)} %get-tuple-element.85.refs_10_) | copy-start | bytes 3145732
  27.1 20.5 %collective-permute-start.7 = (bf16[192,1024]{1,0:T(8,128)(2,1)S(1)}, bf16[192,1024]{1,0:T(8,128)(2,1)S(1)}, u32[]{:S(2)}, u32[]{:S(2)}) collective-permute-start(bf16[192,1024]{1,0:T(8,128)(2,1)S(1)} %get-tuple-element.57), channel_id=1, source_target_pairs={{0,2},{1,3},{2,0},{3,1},{4,6},{5,7},{6,4},{7,5},{8,10},{9,11},{10,... | collective-permute-start | bytes 1179656 | tf_op jit(solution)/shard_map/ppermute | solution.py:252
  28.6 21.6 %collective-permute-start.8 = (bf16[192,1024]{1,0:T(8,128)(2,1)S(1)}, bf16[192,1024]{1,0:T(8,128)(2,1)S(1)}, u32[]{:S(2)}, u32[]{:S(2)}) collective-permute-start(bf16[192,1024]{1,0:T(8,128)(2,1)S(1)} %get-tuple-element.58), channel_id=1, source_target_pairs={{0,3},{1,2},{2,1},{3,0},{4,7},{5,6},{6,5},{7,4},{8,11},{9,10},{10,... | collective-permute-start | bytes 1179656 | tf_op jit(solution)/shard_map/ppermute | solution.py:252
  30.0 21.8 %collective-permute-start.9 = (bf16[192,1024]{1,0:T(8,128)(2,1)S(1)}, bf16[192,1024]{1,0:T(8,128)(2,1)S(1)}, u32[]{:S(2)}, u32[]{:S(2)}) collective-permute-start(bf16[192,1024]{1,0:T(8,128)(2,1)S(1)} %get-tuple-element.59), channel_id=1, source_target_pairs={{0,1},{1,0},{2,3},{3,2},{4,5},{5,4},{6,7},{7,6},{8,9},{9,8},{10,11... | collective-permute-start | bytes 1179656 | tf_op jit(solution)/shard_map/ppermute | solution.py:252
  31.5 18.2 %collective-permute-start.5 = (bf16[512,512]{1,0:T(8,128)(2,1)S(1)}, bf16[512,512]{1,0:T(8,128)(2,1)S(1)}, u32[]{:S(2)}, u32[]{:S(2)}) collective-permute-start(bf16[512,512]{1,0:T(8,128)(2,1)S(1)} %plane_partial.3), channel_id=1, source_target_pairs={{0,4},{1,5},{2,6},{3,7},{4,8},{5,9},{6,10},{7,11},{8,12},{9,13},{1... | collective-permute-start | bytes 1572872 | tf_op jit(solution)/shard_map/ppermute | solution.py:246
  38.4 41.2 %collective-permute-start.11 = (bf16[192,2048]{1,0:T(8,128)(2,1)S(1)}, bf16[192,2048]{1,0:T(8,128)(2,1)S(1)}, u32[]{:S(2)}, u32[]{:S(2)}) collective-permute-start(bf16[192,2048]{1,0:T(8,128)(2,1)S(1)} %get-tuple-element.69), channel_id=1, source_target_pairs={{0,2},{1,3},{2,0},{3,1},{4,6},{5,7},{6,4},{7,5},{8,10},{9,11},{10,... | collective-permute-start | bytes 2359304 | tf_op jit(solution)/shard_map/ppermute | solution.py:252
  47.5 33.6 %collective-permute-start.13 = (bf16[192,2048]{1,0:T(8,128)(2,1)S(1)}, bf16[192,2048]{1,0:T(8,128)(2,1)S(1)}, u32[]{:S(2)}, u32[]{:S(2)}) collective-permute-start(bf16[192,2048]{1,0:T(8,128)(2,1)S(1)} %get-tuple-element.72), channel_id=1, source_target_pairs={{0,3},{1,2},{2,1},{3,0},{4,7},{5,6},{6,5},{7,4},{8,11},{9,10},{10,... | collective-permute-start | bytes 2359304 | tf_op jit(solution)/shard_map/ppermute | solution.py:252
  49.6 32.9 %collective-permute-start.15 = (bf16[192,2048]{1,0:T(8,128)(2,1)S(1)}, bf16[192,2048]{1,0:T(8,128)(2,1)S(1)}, u32[]{:S(2)}, u32[]{:S(2)}) collective-permute-start(bf16[192,2048]{1,0:T(8,128)(2,1)S(1)} %get-tuple-element.75), channel_id=1, source_target_pairs={{0,1},{1,0},{2,3},{3,2},{4,5},{5,4},{6,7},{7,6},{8,9},{9,8},{10,11... | collective-permute-start | bytes 2359304 | tf_op jit(solution)/shard_map/ppermute | solution.py:252
  50.2 16.7 %collective-permute-start.6 = (bf16[512,512]{1,0:T(8,128)(2,1)S(1)}, bf16[512,512]{1,0:T(8,128)(2,1)S(1)}, u32[]{:S(2)}, u32[]{:S(2)}) collective-permute-start(bf16[512,512]{1,0:T(8,128)(2,1)S(1)} %collective-permute-done.refs_1_), channel_id=1, source_target_pairs={{0,4},{1,5},{2,6},{3,7},{4,8},{5,9},{6,10},{7,11},{8,12},{9,13},{1... | collective-permute-start | bytes 1572872 | tf_op jit(solution)/shard_map/ppermute | solution.py:246
  53.8 32.2 %collective-permute-start.18 = (bf16[512,512]{1,0:T(8,128)(2,1)S(1)}, bf16[512,512]{1,0:T(8,128)(2,1)S(1)}, u32[]{:S(2)}, u32[]{:S(2)}) collective-permute-start(bf16[512,512]{1,0:T(8,128)(2,1)S(1)} %get-tuple-element.83), channel_id=1, source_target_pairs={{4,0},{5,1},{6,2},{7,3},{8,4},{9,5},{10,6},{11,7},{12,8},{13,9},{1... | collective-permute-start | bytes 1572872 | tf_op jit(solution)/shard_map/ppermute | solution.py:249
  66.9 19.0 %collective-permute-start.17 = (bf16[512,512]{1,0:T(8,128)(2,1)S(1)}, bf16[512,512]{1,0:T(8,128)(2,1)S(1)}, u32[]{:S(2)}, u32[]{:S(2)}) collective-permute-start(bf16[512,512]{1,0:T(8,128)(2,1)S(1)} %get-tuple-element.61.refs_5_), channel_id=1, source_target_pairs={{0,4},{1,5},{2,6},{3,7},{4,8},{5,9},{6,10},{7,11},{8,12},{9,13},{1... | collective-permute-start | bytes 1572872 | tf_op jit(solution)/shard_map/ppermute | solution.py:246
  79.6 10.0 %collective-permute-start.12 = (bf16[192,512]{1,0:T(8,128)(2,1)S(1)}, bf16[192,512]{1,0:T(8,128)(2,1)S(1)}, u32[]{:S(2)}, u32[]{:S(2)}) collective-permute-start(bf16[192,512]{1,0:T(8,128)(2,1)S(1)} %get-tuple-element.70), channel_id=1, source_target_pairs={{0,2},{1,3},{2,0},{3,1},{4,6},{5,7},{6,4},{7,5},{8,10},{9,11},{10,... | collective-permute-start | bytes 589832 | tf_op jit(solution)/shard_map/ppermute | solution.py:252
  81.1 8.4 %collective-permute-start.14 = (bf16[192,512]{1,0:T(8,128)(2,1)S(1)}, bf16[192,512]{1,0:T(8,128)(2,1)S(1)}, u32[]{:S(2)}, u32[]{:S(2)}) collective-permute-start(bf16[192,512]{1,0:T(8,128)(2,1)S(1)} %get-tuple-element.73), channel_id=1, source_target_pairs={{0,3},{1,2},{2,1},{3,0},{4,7},{5,6},{6,5},{7,4},{8,11},{9,10},{10,... | collective-permute-start | bytes 589832 | tf_op jit(solution)/shard_map/ppermute | solution.py:252
  82.6 7.9 %collective-permute-start.16 = (bf16[192,512]{1,0:T(8,128)(2,1)S(1)}, bf16[192,512]{1,0:T(8,128)(2,1)S(1)}, u32[]{:S(2)}, u32[]{:S(2)}) collective-permute-start(bf16[192,512]{1,0:T(8,128)(2,1)S(1)} %get-tuple-element.76), channel_id=1, source_target_pairs={{0,1},{1,0},{2,3},{3,2},{4,5},{5,4},{6,7},{7,6},{8,9},{9,8},{10,11... | collective-permute-start | bytes 589832 | tf_op jit(solution)/shard_map/ppermute | solution.py:252
  85.9 1.5 %copy-start.3 = (f32[1,512,512]{2,1,0:T(8,128)S(1)}, f32[1,512,512]{2,1,0:T(8,128)}, u32[]{:S(2)}) copy-start(f32[1,512,512]{2,1,0:T(8,128)} %param.12) | copy-start | bytes 3145732
  85.9 1.5 %copy-start.4 = (f32[1,512,512]{2,1,0:T(8,128)S(1)}, f32[1,512,512]{2,1,0:T(8,128)}, u32[]{:S(2)}) copy-start(f32[1,512,512]{2,1,0:T(8,128)} %param.11) | copy-start | bytes 3145732
  89.6 2.2 %copy-start = (f32[512,512]{1,0:T(8,128)}, f32[512,512]{1,0:T(8,128)S(1)}, u32[]{:S(2)}) copy-start(f32[512,512]{1,0:T(8,128)S(1)} %get-tuple-element.87.refs_5_) | copy-start | bytes 3145732

commit v8 on v6

--- a/solution.py
+++ b/solution.py
@@ -19,8 +19,8 @@
 PLANE = 4
 WEIGHT_SCALE = 2.0**17
 WIRE = jnp.bfloat16
-ORDER = (1, 2, 3)
-C_PARTIAL, C_PRODUCT, C_UNPACK = (36, 32, 34), (36, 20), (32, 20)
+PEERS = (0, 2, 3, 1)
+C_PARTIAL, C_PRODUCT, C_UNPACK = (32, 33, 34), (36, 34), (33, 20)
 
 
 def cost(log_flops):
@@ -75,15 +75,14 @@
     for k in range(PLANE):
         if k > 0:
             first, middle, last = chunks[3 * k - 3 : 3 * k]
-            first[:, : cot.shape[1]] = cot[...]
         for at, distance in enumerate(distances):
             block = lax.rem(z + planes + distance, planes)
-            start = pl.multiple_of((block * PLANE + (p ^ k)) * columns, 128)
+            start = pl.multiple_of((block * PLANE + (p ^ PEERS[k])) * columns, 128)
             value = features[:, pl.ds(start, columns)]
             if k == 0:
                 own[:, at * columns : (at + 1) * columns] = value
             elif at == 0:
-                first[:, cot.shape[1] :] = value
+                first[...] = value
             elif at == planes - 1:
                 last[...] = value
             else:
@@ -92,7 +91,7 @@
 
 def pack(features, cot, weight, columns, distances):
     rows, planes = features.shape[0], len(distances)
-    widths = [planes * columns] + [cot.shape[1] + columns, (planes - 2) * columns, columns] * (PLANE - 1)
+    widths = [planes * columns] + [columns, (planes - 2) * columns, columns] * (PLANE - 1)
     coded, weight, cot, own, *chunks = pl.pallas_call(
         functools.partial(pack_kernel, columns, distances, "fsdp"),
         out_shape=[
@@ -111,14 +110,13 @@
     return coded, weight, cot, own, [chunks[k::3] for k in range(3)]
 
 
-def partial_kernel(columns, scale, spread, own, cot, *refs):
-    firsts, parts = refs[: PLANE - 1], refs[PLANE - 1 : 2 * PLANE - 2]
-    rest, outs = refs[2 * PLANE - 2 : -len(spread)], refs[-len(spread) :]
-    depth = cot.shape[1]
+def partial_kernel(columns, scale, spread, own, *refs):
+    cots, parts = refs[:PLANE], refs[PLANE : 2 * PLANE - 1]
+    rest, outs = refs[2 * PLANE - 1 : -len(spread)], refs[-len(spread) :]
     for (at, start, count, rides), out in zip(spread, outs):
-        total = contract(own[:, at : at + columns], cot[...], ((0,), (0,)))
-        for part, first in zip(parts, firsts):
-            total += contract(part[:, start : start + columns], first[:, :depth], ((0,), (0,)))
+        total = contract(own[:, at : at + columns], cots[0][...], ((0,), (0,)))
+        for part, cot in zip(parts, cots[1:]):
+            total += contract(part[:, start : start + columns], cot[...], ((0,), (0,)))
         total = total * scale
         for ref in rest[:count]:
             total += decode(ref[:columns, :])
@@ -128,12 +126,12 @@
         rest = rest[count + rides :]
 
 
-def plane_partial(spread, own, cot, firsts, parts, rest, columns, scale, dtype, span):
-    operands = [own, cot, *firsts, *parts, *rest]
+def plane_partial(spread, own, cots, parts, rest, columns, scale, dtype, span):
+    operands = [own, *cots, *parts, *rest]
     outs = pl.pallas_call(
         functools.partial(partial_kernel, columns, scale, spread),
         out_shape=[
-            jax.ShapeDtypeStruct((columns * (1 + rides), cot.shape[1]), dtype) for *_, rides in spread
+            jax.ShapeDtypeStruct((columns * (1 + rides), cots[0].shape[1]), dtype) for *_, rides in spread
         ],
         in_specs=vmem(len(operands)),
         out_specs=vmem(len(spread)),
@@ -145,10 +143,9 @@
 
 
 def product_kernel(columns, count, scale, *refs):
-    weights, cot, firsts, outs = refs[:count], refs[count], refs[count + 1 : count + PLANE], refs[-PLANE:]
+    weights, cots, outs = refs[:count], refs[count : count + PLANE], refs[-PLANE:]
     for rider, out in zip(refs[count + PLANE : -PLANE - 1], outs[1:]):
         out[:, count * columns :] = rider[...]
-    depth = cot.shape[1]
     for i, weight in enumerate(weights):
         if weight.dtype == WIRE:
             wide, factor = decode(weight[-columns:, :]), 1.0 / WEIGHT_SCALE
@@ -157,14 +154,14 @@
         high = wide.astype(jnp.bfloat16)
         low = (wide - high.astype(jnp.float32)).astype(jnp.bfloat16)
         for k in range(PLANE):
-            rows = cot[...] if k == 0 else firsts[k - 1][:, :depth]
+            rows = cots[k][...]
             result = contract(rows, high, ((1,), (1,))) + contract(rows, low, ((1,), (1,)))
             result = result * factor if k == 0 else encode(result * (factor * scale))
             outs[k][:, i * columns : (i + 1) * columns] = result
 
 
-def plane_product(weights, cot, firsts, riders, after, columns, scale, span):
-    rows, width = cot.shape[0], columns * len(weights)
+def plane_product(weights, cots, riders, after, columns, scale, span):
+    rows, width = cots[0].shape[0], columns * len(weights)
     sizes = [width] + [width + (columns if riders else 0)] * (PLANE - 1)
     outs = pl.pallas_call(
         functools.partial(product_kernel, columns, len(weights), scale),
@@ -176,7 +173,7 @@
         cost_estimate=cost(span),
         compiler_params=pltpu.CompilerParams(vmem_limit_bytes=32 << 20),
         name="plane_product",
-    )(*weights, cot, *firsts, *riders, after)
+    )(*weights, *cots, *riders, after)
     return list(outs)
 
 
@@ -195,7 +192,7 @@
             else:
                 buffer[i] = decode(pieces[k][:, span]) * factor
                 source = buffer.at[i]
-            start = pl.multiple_of((block * PLANE + (p ^ k)) * columns, 128)
+            start = pl.multiple_of((block * PLANE + (p ^ PEERS[k])) * columns, 128)
             copy = pltpu.make_async_copy(source, out.at[:, pl.ds(start, columns)], sem.at[i])
             copy.start()
             copies.append(copy)
@@ -249,11 +246,10 @@
         return lax.ppermute(x, "fsdp", [(to, source) for source, to in ring])
 
     def across(x, k):
-        return lax.ppermute(x, "fsdp", [(i, i ^ k) for i in range(size)])
+        return lax.ppermute(x, "fsdp", [(i, i ^ PEERS[k]) for i in range(size)])
 
     def across_all(parts):
-        moved = {k: across(parts[k - 1], k) for k in ORDER}
-        return [moved[k] for k in range(1, PLANE)]
+        return [across(part, k + 1) for k, part in enumerate(parts)]
 
     workers = lax.axis_size("worker")
     half = planes // 2
@@ -265,7 +261,10 @@
     firsts, middles, riders = chunks
     if workers == 2:
         partner_local = lax.ppermute(fragment_local, "worker", [(0, 1), (1, 0)])
-        firsts[-1], partner_local = lax.optimization_barrier((firsts[-1], partner_local))
+        coded, partner_local = lax.optimization_barrier((coded, partner_local))
+    by_y = across(cot, 1)
+    by_x = across(cot, 3)
+    cots = [cot, by_y, across(by_y, 3), by_x]
     firsts = across_all(firsts)
     middles = across_all(middles)
 
@@ -283,10 +282,10 @@
     weights, offsets = [weight, behind, ahead], [0, -1, 1]
 
     def partials(spread, parts, rest, dtype, span):
-        return plane_partial(spread, own, cot, firsts, parts, rest, columns, gradient_scale, dtype, span)
-
-    plus, minus = partials([(0, cot.shape[1], 0, half > 1)], firsts, [behind], WIRE, C_PARTIAL[0])[0], None
-    early = plane_product(weights, cot, firsts, riders, new_momentum, columns, product_scale, C_PRODUCT[0])
+        return plane_partial(spread, own, cots, parts, rest, columns, gradient_scale, dtype, span)
+
+    plus, minus = partials([(0, 0, 0, half > 1)], firsts, [behind], WIRE, C_PARTIAL[0])[0], None
+    early = plane_product(weights, cots, riders, new_momentum, columns, product_scale, C_PRODUCT[0])
     early[1:] = across_all(early[1:])
     late_weights, late_offsets = [], []
     for step in range(half - 1, 0, -1):
@@ -310,7 +309,7 @@
             rest.append(carried)
         plus, minus = partials(spread, middles, rest, WIRE, C_PARTIAL[1])
     factor = 1.0 / product_scale
-    late = plane_product(late_weights, cot, firsts, [], plus, columns, product_scale, C_PRODUCT[1])
+    late = plane_product(late_weights, cots, [], plus, columns, product_scale, C_PRODUCT[1])
     for k in range(1, PLANE):
         late[k], early[k] = lax.optimization_barrier((late[k], early[k]))
     late[1:] = across_all(late[1:])

time: 90.9 us -> 96.3 us (1.059)
  starting transfers between devices: 24.2 us -> 29.4 us
  local copies, waits for them, and re-layouts: 0.96 us -> 2.18 us
    ppermute x12 -> x15, waiting for transfers between devices: 33.9 us -> 22.8 us  [across(): return lax.ppermute(x, 'fsdp', [(i, i ^ PEERS[k]) for i in range(size)])]
    ppermute x12 -> x15, starting transfers between devices: 13.2 us -> 20.2 us  [across(): return lax.ppermute(x, 'fsdp', [(i, i ^ PEERS[k]) for i in range(size)])]
    ppermute x2, waiting for transfers between devices: 0.92 us -> 6.45 us  [back(): return lax.ppermute(x, 'fsdp', [(to, source) for source, to in ring])]
    ppermute x3, waiting for transfers between devices: 8.39 us -> 13.2 us  [around(): return lax.ppermute(x, 'fsdp', ring)]
    ppermute x3, starting transfers between devices: 4.33 us -> 1.64 us  [around(): return lax.ppermute(x, 'fsdp', ring)]
    unnamed x16 -> x18, local copies, waits for them, and re-layouts: 0.96 us -> 2.18 us
  transfers between devices with their start and end apart: 18 -> 21, of which waited for: 7 -> 8; matrix products, arithmetic and copies ran while one was open for 4% -> 4% of each run, Pallas kernels for 18% -> 17%
where the time goes in v8:
time: 96.3 us; the launch traced here: 96.1 us
  waiting for transfers between devices  42.4 us (44%)
  starting transfers between devices  29.4 us (31%)
  Pallas kernels  17.6 us (18%)
  other arithmetic  3.64 us (4%)
  local copies, waits for them, and re-layouts  2.18 us (2%)
    ppermute x15, waiting for transfers between devices, across(): return lax.ppermute(x, 'fsdp', [(i, i ^ PEERS[k]) for i in range(size)])  22.8 us
    ppermute x15, starting transfers between devices, across(): return lax.ppermute(x, 'fsdp', [(i, i ^ PEERS[k]) for i in range(size)])  20.2 us
    ppermute x3, waiting for transfers between devices, around(): return lax.ppermute(x, 'fsdp', ring)  13.2 us
    ppermute x2, starting transfers between devices, back(): return lax.ppermute(x, 'fsdp', [(to, source) for source, to in ring])  7.03 us
    pallas_call x2, Pallas kernels, plane_product(): pl.pallas_call(functools.partial(product_kernel, columns, len(weights), s...  6.96 us
    ppermute x2, waiting for transfers between devices, back(): return lax.ppermute(x, 'fsdp', [(to, source) for source, to in ring])  6.45 us
    pallas_call x3, Pallas kernels, plane_partial(): pl.pallas_call(functools.partial(partial_kernel, columns, scale, spread),...  4.34 us
    pallas_call x2, Pallas kernels, unpack(): pl.pallas_call(functools.partial(unpack_kernel, columns, planes, 'fsdp',...  3.88 us
  transfers between devices with their start and end apart: 21, of which 8 were waited for; matrix products, arithmetic and copies ran while one was open for 4% of the time, Pallas kernels for 17%

profile of v8, /device:TPU:0, one launch (start us, length us, event | category | flops | bytes accessed | tf_op | source)
XLA Modules:
  0.0 96.1 jit_solution(7940186659333735777)
XLA Ops:
  1.2 1.2 %copy-done.2 = f32[1,512,512]{2,1,0:T(8,128)S(1)} copy-done((f32[1,512,512]{2,1,0:T(8,128)S(1)}, f32[1,512,512]{2,1,0:T(8,128)}, u32[]{:S(2)}) %copy-start.2) | copy-done | bytes 1048600
  2.4 0.9 copy-done.3
  3.3 2.4 %pack.1 = (bf16[512,512]{1,0:T(8,128)(2,1)S(1)}, f32[512,512]{1,0:T(8,128)S(1)}, bf16[192,512]{1,0:T(8,128)(2,1)S(1)}, bf16[192,2048]{1,0:T(8,128)(2,1)S(1)}, bf...) custom-call(bf16[192,8192]{1,0:T(8,128)(2,1)} %features_far.1, ...), custom_call_target="tpu_custom_call" | custom-call | flops 68719476736 | bytes 1048576 | tf_op jit(solution)/shard_map/pack/pallas_call | solution.py:95
  5.7 2.6 %collective-permute-start.5 = (bf16[192,512]{1,0:T(8,128)(2,1)S(1)}, bf16[192,512]{1,0:T(8,128)(2,1)S(1)}, u32[]{:S(2)}, u32[]{:S(2)}) collective-permute-start(bf16[192,512]{1,0:T(8,128)(2,1)S(1)} %get-tuple-element.47), channel_id=1, source_target_pairs={{0,2},{1,3},{2,0},{3,1},{4,6},{5,7},{6,4},{7,5},{8,10},{9,11},{10,... | collective-permute-start | bytes 589832 | tf_op jit(solution)/shard_map/ppermute | solution.py:249
  8.4 2.9 %collective-permute-start.6 = (bf16[192,512]{1,0:T(8,128)(2,1)S(1)}, bf16[192,512]{1,0:T(8,128)(2,1)S(1)}, u32[]{:S(2)}, u32[]{:S(2)}) collective-permute-start(bf16[192,512]{1,0:T(8,128)(2,1)S(1)} %get-tuple-element.48), channel_id=1, source_target_pairs={{0,3},{1,2},{2,1},{3,0},{4,7},{5,6},{6,5},{7,4},{8,11},{9,10},{10,... | collective-permute-start | bytes 589832 | tf_op jit(solution)/shard_map/ppermute | solution.py:249
  11.2 1.6 %collective-permute-start.4 = (bf16[512,512]{1,0:T(8,128)(2,1)S(1)}, bf16[512,512]{1,0:T(8,128)(2,1)S(1)}, u32[]{:S(2)}, u32[]{:S(2)}) collective-permute-start(bf16[512,512]{1,0:T(8,128)(2,1)S(1)} %get-tuple-element.46), channel_id=1, source_target_pairs={{0,4},{1,5},{2,6},{3,7},{4,8},{5,9},{6,10},{7,11},{8,12},{9,13},{1... | collective-permute-start | bytes 1572872 | tf_op jit(solution)/shard_map/ppermute | solution.py:243
  13.4 4.9 %collective-permute-done.5.refs_4_ = bf16[192,512]{1,0:T(8,128)(2,1)S(1)} collective-permute-done((bf16[192,512]{1,0:T(8,128)(2,1)S(1)}, bf16[192,512]{1,0:T(8,128)(2,1)S(1)}, u32[]{:S(2)}, u32[]{:S(2)}) %collective-permute-start.5) | collective-permute-done | bytes 196640 | tf_op jit(solution)/shard_map/ppermute | solution.py:249
  18.3 1.9 %collective-permute-start.7 = (bf16[192,512]{1,0:T(8,128)(2,1)S(1)}, bf16[192,512]{1,0:T(8,128)(2,1)S(1)}, u32[]{:S(2)}, u32[]{:S(2)}) collective-permute-start(bf16[192,512]{1,0:T(8,128)(2,1)S(1)} %get-tuple-element.49), channel_id=1, source_target_pairs={{0,1},{1,0},{2,3},{3,2},{4,5},{5,4},{6,7},{7,6},{8,9},{9,8},{10,11... | collective-permute-start | bytes 589832 | tf_op jit(solution)/shard_map/ppermute | solution.py:249
  20.2 2.1 %collective-permute-done.refs_1_.refs_2_.refs_4_ = bf16[192,512]{1,0:T(8,128)(2,1)S(1)} collective-permute-done((bf16[192,512]{1,0:T(8,128)(2,1)S(1)}, bf16[192,512]{1,0:T(8,128)(2,1)S(1)}, u32[]{:S(2)}, u32[]{:S(2)}) %collective-permute-start) | collective-permute-done | bytes 196640 | tf_op jit(solution)/shard_map/ppermute | solution.py:249
  22.3 1.7 %collective-permute-start.1 = (bf16[192,512]{1,0:T(8,128)(2,1)S(1)}, bf16[192,512]{1,0:T(8,128)(2,1)S(1)}, u32[]{:S(2)}, u32[]{:S(2)}) collective-permute-start(bf16[192,512]{1,0:T(8,128)(2,1)S(1)} %collective-permute-done.refs_1_.refs_2_.refs_4_), channel_id=1, source_target_pairs={{0,1},{1,0},{2,3},{3,2},{4,5},{5,4},{6,7},{7,6},{8,9},{9,8},{10,11... | collective-permute-start | bytes 589832 | tf_op jit(solution)/shard_map/ppermute | solution.py:249
  24.0 3.6 %collective-permute-start.12 = (bf16[512,512]{1,0:T(8,128)(2,1)S(1)}, bf16[512,512]{1,0:T(8,128)(2,1)S(1)}, u32[]{:S(2)}, u32[]{:S(2)}) collective-permute-start(bf16[512,512]{1,0:T(8,128)(2,1)S(1)} %get-tuple-element.46), channel_id=1, source_target_pairs={{4,0},{5,1},{6,2},{7,3},{8,4},{9,5},{10,6},{11,7},{12,8},{13,9},{1... | collective-permute-start | bytes 1572872 | tf_op jit(solution)/shard_map/ppermute | solution.py:246
  27.6 1.5 %multiply_subtract_fusion = (f32[512,512]{1,0:T(8,128)}, f32[512,512]{1,0:T(8,128)S(1)}) fusion(f32[512,512]{1,0:T(8,128)S(1)} %copy-done.6, f32[1,512,512]{2,1,0:T(8,128)S(1)} %collective-permute-done.3, f32[1,512,512]{2,1,0:T(8,128)S(1)} %copy-done.7, f32[512,512]{1,0:T(8,128)S(1)} %copy-done.8), kind=kLoop, calls=%fused_computation.6 | loop fusion | flops 2621440 | bytes 6291456 | tf_op jit(solution)/shard_map/sub | solution.py:278
  29.1 1.5 %collective-permute-start.9 = (bf16[192,1024]{1,0:T(8,128)(2,1)S(1)}, bf16[192,1024]{1,0:T(8,128)(2,1)S(1)}, u32[]{:S(2)}, u32[]{:S(2)}) collective-permute-start(bf16[192,1024]{1,0:T(8,128)(2,1)S(1)} %get-tuple-element.54), channel_id=1, source_target_pairs={{0,2},{1,3},{2,0},{3,1},{4,6},{5,7},{6,4},{7,5},{8,10},{9,11},{10,... | collective-permute-start | bytes 1179656 | tf_op jit(solution)/shard_map/ppermute | solution.py:249
  31.1 1.5 %collective-permute-start.11 = (bf16[192,1024]{1,0:T(8,128)(2,1)S(1)}, bf16[192,1024]{1,0:T(8,128)(2,1)S(1)}, u32[]{:S(2)}, u32[]{:S(2)}) collective-permute-start(bf16[192,1024]{1,0:T(8,128)(2,1)S(1)} %get-tuple-element.56), channel_id=1, source_target_pairs={{0,1},{1,0},{2,3},{3,2},{4,5},{5,4},{6,7},{7,6},{8,9},{9,8},{10,11... | collective-permute-start | bytes 1179656 | tf_op jit(solution)/shard_map/ppermute | solution.py:249
  32.6 0.9 plane_partial.3
  33.6 6.4 %collective-permute-done.12.refs_2_ = bf16[512,512]{1,0:T(8,128)(2,1)S(1)} collective-permute-done((bf16[512,512]{1,0:T(8,128)(2,1)S(1)}, bf16[512,512]{1,0:T(8,128)(2,1)S(1)}, u32[]{:S(2)}, u32[]{:S(2)}) %collective-permute-start.12) | collective-permute-done | bytes 524320 | tf_op jit(solution)/shard_map/ppermute | solution.py:246
  40.0 5.0 %plane_product.3 = (f32[192,1536]{1,0:T(8,128)S(1)}, bf16[192,2048]{1,0:T(8,128)(2,1)S(1)}, bf16[192,2048]{1,0:T(8,128)(2,1)S(1)}, bf16[192,2048]{1,0:T(8,128)(2,1)S(1)}) custom-call(f32[512,512]{1,0:T(8,128)S(1)} %get-tuple-element.60.refs_0_, bf16[512,512]{1,0:T(8,128)(2,1)S(1)} %collective-permute-done.4.refs_7_.refs_1_, ...), custom_call_target="tpu_custom_call" | custom-call | flops 68719476736 | bytes 1048576 | tf_op jit(solution)/shard_map/plane_product/pallas_call | solution.py:166
  45.1 1.6 %collective-permute-start.13 = (bf16[192,2048]{1,0:T(8,128)(2,1)S(1)}, bf16[192,2048]{1,0:T(8,128)(2,1)S(1)}, u32[]{:S(2)}, u32[]{:S(2)}) collective-permute-start(bf16[192,2048]{1,0:T(8,128)(2,1)S(1)} %get-tuple-element.65), channel_id=1, source_target_pairs={{0,2},{1,3},{2,0},{3,1},{4,6},{5,7},{6,4},{7,5},{8,10},{9,11},{10,... | collective-permute-start | bytes 2359304 | tf_op jit(solution)/shard_map/ppermute | solution.py:249
  46.6 3.1 %collective-permute-done.9.refs_4_ = bf16[192,1024]{1,0:T(8,128)(2,1)S(1)} collective-permute-done((bf16[192,1024]{1,0:T(8,128)(2,1)S(1)}, bf16[192,1024]{1,0:T(8,128)(2,1)S(1)}, u32[]{:S(2)}, u32[]{:S(2)}) %collective-permute-start.9) | collective-permute-done | bytes 393248 | tf_op jit(solution)/shard_map/ppermute | solution.py:249
  50.5 1.5 %collective-permute-start.17 = (bf16[192,2048]{1,0:T(8,128)(2,1)S(1)}, bf16[192,2048]{1,0:T(8,128)(2,1)S(1)}, u32[]{:S(2)}, u32[]{:S(2)}) collective-permute-start(bf16[192,2048]{1,0:T(8,128)(2,1)S(1)} %get-tuple-element.71), channel_id=1, source_target_pairs={{0,1},{1,0},{2,3},{3,2},{4,5},{5,4},{6,7},{7,6},{8,9},{9,8},{10,11... | collective-permute-start | bytes 2359304 | tf_op jit(solution)/shard_map/ppermute | solution.py:249
  52.0 9.8 %collective-permute-done.8.refs_7_.refs_0_ = bf16[1024,512]{1,0:T(8,128)(2,1)S(1)} collective-permute-done((bf16[1024,512]{1,0:T(8,128)(2,1)S(1)}, bf16[1024,512]{1,0:T(8,128)(2,1)S(1)}, u32[]{:S(2)}, u32[]{:S(2)}) %collective-permute-start.8) | collective-permute-done | bytes 1048608 | tf_op jit(solution)/shard_map/ppermute | solution.py:243
  61.8 2.0 %plane_partial.4 = (bf16[512,512]{1,0:T(8,128)(2,1)S(1)}, bf16[512,512]{1,0:T(8,128)(2,1)S(1)}) custom-call(bf16[192,2048]{1,0:T(8,128)(2,1)S(1)} %get-tuple-element.43.own, bf16[192,512]{1,0:T(8,128)(2,1)S(1)} %get-tuple-element.44.refs_0_.refs_1_.refs_3_, bf16[192,512]{1,0:T(8,128)(2,1)S(1)} %collective-permute-done.refs_1_.refs_2_.refs_4_, ...), custom_call_target="tpu_custom_call" | custom-call | flops 8589934592 | bytes 1048576 | tf_op jit(solution)/shard_map/plane_partial/pallas_call | solution.py:131
  63.7 3.4 %collective-permute-start.20 = (bf16[512,512]{1,0:T(8,128)(2,1)S(1)}, bf16[512,512]{1,0:T(8,128)(2,1)S(1)}, u32[]{:S(2)}, u32[]{:S(2)}) collective-permute-start(bf16[512,512]{1,0:T(8,128)(2,1)S(1)} %get-tuple-element.79), channel_id=1, source_target_pairs={{4,0},{5,1},{6,2},{7,3},{8,4},{9,5},{10,6},{11,7},{12,8},{13,9},{1... | collective-permute-start | bytes 1572872 | tf_op jit(solution)/shard_map/ppermute | solution.py:246
  67.2 1.9 %plane_product.2 = (f32[192,512]{1,0:T(8,128)S(1)}, bf16[192,512]{1,0:T(8,128)(2,1)S(1)}, bf16[192,512]{1,0:T(8,128)(2,1)S(1)}, bf16[192,512]{1,0:T(8,128)(2,1)S(1)}) custom-call(bf16[1024,512]{1,0:T(8,128)(2,1)S(1)} %collective-permute-done.8.refs_7_.refs_0_, bf16[192,512]{1,0:T(8,128)(2,1)S(1)} %get-tuple-element.44.refs_0_.refs_1_.refs_3_, ...), custom_call_target="tpu_custom_call" | custom-call | flops 17179869184 | bytes 1048576 | tf_op jit(solution)/shard_map/plane_product/pallas_call | solution.py:166
  69.1 12.3 %collective-permute-done.13.refs_1_.refs_4_ = bf16[192,2048]{1,0:T(8,128)(2,1)S(1)} collective-permute-done((bf16[192,2048]{1,0:T(8,128)(2,1)S(1)}, bf16[192,2048]{1,0:T(8,128)(2,1)S(1)}, u32[]{:S(2)}, u32[]{:S(2)}) %collective-permute-start.13) | collective-permute-done | bytes 786464 | tf_op jit(solution)/shard_map/ppermute | solution.py:249
  81.4 1.5 %collective-permute-start.14 = (bf16[192,512]{1,0:T(8,128)(2,1)S(1)}, bf16[192,512]{1,0:T(8,128)(2,1)S(1)}, u32[]{:S(2)}, u32[]{:S(2)}) collective-permute-start(bf16[192,512]{1,0:T(8,128)(2,1)S(1)} %get-tuple-element.66), channel_id=1, source_target_pairs={{0,2},{1,3},{2,0},{3,1},{4,6},{5,7},{6,4},{7,5},{8,10},{9,11},{10,... | collective-permute-start | bytes 589832 | tf_op jit(solution)/shard_map/ppermute | solution.py:249
  83.8 1.1 %collective-permute-start.18 = (bf16[192,512]{1,0:T(8,128)(2,1)S(1)}, bf16[192,512]{1,0:T(8,128)(2,1)S(1)}, u32[]{:S(2)}, u32[]{:S(2)}) collective-permute-start(bf16[192,512]{1,0:T(8,128)(2,1)S(1)} %get-tuple-element.72), channel_id=1, source_target_pairs={{0,1},{1,0},{2,3},{3,2},{4,5},{5,4},{6,7},{7,6},{8,9},{9,8},{10,11... | collective-permute-start | bytes 589832 | tf_op jit(solution)/shard_map/ppermute | solution.py:249
  84.9 2.4 %unpack.2.refs_4_ = f32[192,8192]{1,0:T(8,128)} custom-call(f32[192,1536]{1,0:T(8,128)S(1)} %get-tuple-element.73.refs_0_, bf16[192,2048]{1,0:T(8,128)(2,1)S(1)} %collective-permute-done.13.refs_1_.refs_4_, bf16[192,2048]{1,0:T(8,128)(2,1)S(1)} %collective-permute-done.15.refs_2_.refs_5_, bf16[192,2048]{1,0:T(8,128)(2,1)S(1)} %collective-permute-done.17.refs_3_.refs_6_), custom_call_target="tpu_custom_call" | custom-call | flops 8589934592 | bytes 1048576 | tf_op jit(solution)/shard_map/unpack/pallas_call | solution.py:207
  87.3 3.4 %collective-permute-done.19.refs_7_ = bf16[512,512]{1,0:T(8,128)(2,1)S(1)} collective-permute-done((bf16[512,512]{1,0:T(8,128)(2,1)S(1)}, bf16[512,512]{1,0:T(8,128)(2,1)S(1)}, u32[]{:S(2)}, u32[]{:S(2)}) %collective-permute-start.19) | collective-permute-done | bytes 524320 | tf_op jit(solution)/shard_map/ppermute | solution.py:243
  90.8 1.5 %plane_partial.5 = f32[512,512]{1,0:T(8,128)S(1)} custom-call(bf16[192,2048]{1,0:T(8,128)(2,1)S(1)} %get-tuple-element.43.own, bf16[192,512]{1,0:T(8,128)(2,1)S(1)} %get-tuple-element.44.refs_0_.refs_1_.refs_3_, bf16[192,512]{1,0:T(8,128)(2,1)S(1)} %collective-permute-done.refs_1_.refs_2_.refs_4_, ...), custom_call_target="tpu_custom_call" | custom-call | flops 17179869184 | bytes 1048576 | tf_op jit(solution)/shard_map/plane_partial/pallas_call | solution.py:131
  92.3 2.1 %subtract_bitcast_fusion = (f32[1,512,512]{2,1,0:T(8,128)}, f32[512,512]{1,0:T(8,128)S(1)}, f32[1,512,512]{2,1,0:T(8,128)}) fusion(f32[512,512]{1,0:T(8,128)S(1)} %get-tuple-element.60.refs_0_, f32[512,512]{1,0:T(8,128)S(1)} %plane_partial.5, f32[1,512,512]{2,1,0:T(8,128)S(1)} %copy-done.4, f32[1,512,512]{2,1,0:T(8,128)S(1)} %copy-done.5), kind=kLoop, calls=%fused_computation.7 | loop fusion | flops 4194304 | bytes 7340032 | tf_op jit(solution)/shard_map/broadcast_in_dim | solution.py:335
  94.5 1.5 %unpack.3 = f32[192,8192]{1,0:T(8,128)} custom-call(f32[192,512]{1,0:T(8,128)S(1)} %get-tuple-element.58.refs_0_, bf16[192,512]{1,0:T(8,128)(2,1)S(1)} %collective-permute-done.14.refs_1_, bf16[192,512]{1,0:T(8,128)(2,1)S(1)} %collective-permute-done.16.refs_2_, ...), custom_call_target="tpu_custom_call", output_to_operand_aliasing={{}: (4, {})} | custom-call | flops 1048576 | bytes 1048576 | tf_op jit(solution)/shard_map/unpack/pallas_call | solution.py:207
  (38 shorter events, 3.4 us)
Async XLA Ops:
  0.6 10.6 %collective-permute-start.3 = (f32[1,512,512]{2,1,0:T(8,128)}, f32[1,512,512]{2,1,0:T(8,128)S(1)}, u32[]{:S(2)}, u32[]{:S(2)}) collective-permute-start(f32[1,512,512]{2,1,0:T(8,128)} %param.13), channel_id=1, source_target_pairs={{0,16},{16,0},{1,17},{17,1},{2,18},{18,2},{3,19},{19,3},{4,20},{20... | collective-permute-start | bytes 3145736 | tf_op jit(solution)/shard_map/ppermute | solution.py:263
  1.2 1.2 %copy-start.2 = (f32[1,512,512]{2,1,0:T(8,128)S(1)}, f32[1,512,512]{2,1,0:T(8,128)}, u32[]{:S(2)}) copy-start(f32[1,512,512]{2,1,0:T(8,128)} %weight_far.1) | copy-start | bytes 3145732
  2.4 0.9 copy-start.3
  3.3 24.3 %copy-start.6 = (f32[512,512]{1,0:T(8,128)S(1)}, f32[512,512]{1,0:T(8,128)}, u32[]{:S(2)}) copy-start(f32[512,512]{1,0:T(8,128)} %param.14) | copy-start | bytes 3145732
  3.3 24.3 %copy-start.7 = (f32[1,512,512]{2,1,0:T(8,128)S(1)}, f32[1,512,512]{2,1,0:T(8,128)}, u32[]{:S(2)}) copy-start(f32[1,512,512]{2,1,0:T(8,128)} %param.13) | copy-start | bytes 3145732
  3.3 24.3 %copy-start.8 = (f32[512,512]{1,0:T(8,128)S(1)}, f32[512,512]{1,0:T(8,128)}, u32[]{:S(2)}) copy-start(f32[512,512]{1,0:T(8,128)} %param.15) | copy-start | bytes 3145732
  5.7 12.6 %collective-permute-start.5 = (bf16[192,512]{1,0:T(8,128)(2,1)S(1)}, bf16[192,512]{1,0:T(8,128)(2,1)S(1)}, u32[]{:S(2)}, u32[]{:S(2)}) collective-permute-start(bf16[192,512]{1,0:T(8,128)(2,1)S(1)} %get-tuple-element.47), channel_id=1, source_target_pairs={{0,2},{1,3},{2,0},{3,1},{4,6},{5,7},{6,4},{7,5},{8,10},{9,11},{10,... | collective-permute-start | bytes 589832 | tf_op jit(solution)/shard_map/ppermute | solution.py:249
  8.3 14.0 %collective-permute-start = (bf16[192,512]{1,0:T(8,128)(2,1)S(1)}, bf16[192,512]{1,0:T(8,128)(2,1)S(1)}, u32[]{:S(2)}, u32[]{:S(2)}) collective-permute-start(bf16[192,512]{1,0:T(8,128)(2,1)S(1)} %get-tuple-element.44.refs_0_.refs_1_.refs_3_), channel_id=1, source_target_pairs={{0,2},{1,3},{2,0},{3,1},{4,6},{5,7},{6,4},{7,5},{8,10},{9,11},{10,... | collective-permute-start | bytes 589832 | tf_op jit(solution)/shard_map/ppermute | solution.py:249
  8.4 15.6 %collective-permute-start.6 = (bf16[192,512]{1,0:T(8,128)(2,1)S(1)}, bf16[192,512]{1,0:T(8,128)(2,1)S(1)}, u32[]{:S(2)}, u32[]{:S(2)}) collective-permute-start(bf16[192,512]{1,0:T(8,128)(2,1)S(1)} %get-tuple-element.48), channel_id=1, source_target_pairs={{0,3},{1,2},{2,1},{3,0},{4,7},{5,6},{6,5},{7,4},{8,11},{9,10},{10,... | collective-permute-start | bytes 589832 | tf_op jit(solution)/shard_map/ppermute | solution.py:249
  11.2 19.4 %collective-permute-start.4 = (bf16[512,512]{1,0:T(8,128)(2,1)S(1)}, bf16[512,512]{1,0:T(8,128)(2,1)S(1)}, u32[]{:S(2)}, u32[]{:S(2)}) collective-permute-start(bf16[512,512]{1,0:T(8,128)(2,1)S(1)} %get-tuple-element.46), channel_id=1, source_target_pairs={{0,4},{1,5},{2,6},{3,7},{4,8},{5,9},{6,10},{7,11},{8,12},{9,13},{1... | collective-permute-start | bytes 1572872 | tf_op jit(solution)/shard_map/ppermute | solution.py:243
  12.8 18.3 %collective-permute-start.2 = (bf16[192,512]{1,0:T(8,128)(2,1)S(1)}, bf16[192,512]{1,0:T(8,128)(2,1)S(1)}, u32[]{:S(2)}, u32[]{:S(2)}) collective-permute-start(bf16[192,512]{1,0:T(8,128)(2,1)S(1)} %get-tuple-element.44.refs_0_.refs_1_.refs_3_), channel_id=1, source_target_pairs={{0,1},{1,0},{2,3},{3,2},{4,5},{5,4},{6,7},{7,6},{8,9},{9,8},{10,11... | collective-permute-start | bytes 589832 | tf_op jit(solution)/shard_map/ppermute | solution.py:249
  18.3 10.9 %collective-permute-start.7 = (bf16[192,512]{1,0:T(8,128)(2,1)S(1)}, bf16[192,512]{1,0:T(8,128)(2,1)S(1)}, u32[]{:S(2)}, u32[]{:S(2)}) collective-permute-start(bf16[192,512]{1,0:T(8,128)(2,1)S(1)} %get-tuple-element.49), channel_id=1, source_target_pairs={{0,1},{1,0},{2,3},{3,2},{4,5},{5,4},{6,7},{7,6},{8,9},{9,8},{10,11... | collective-permute-start | bytes 589832 | tf_op jit(solution)/shard_map/ppermute | solution.py:249
  22.3 10.3 %collective-permute-start.1 = (bf16[192,512]{1,0:T(8,128)(2,1)S(1)}, bf16[192,512]{1,0:T(8,128)(2,1)S(1)}, u32[]{:S(2)}, u32[]{:S(2)}) collective-permute-start(bf16[192,512]{1,0:T(8,128)(2,1)S(1)} %collective-permute-done.refs_1_.refs_2_.refs_4_), channel_id=1, source_target_pairs={{0,1},{1,0},{2,3},{3,2},{4,5},{5,4},{6,7},{7,6},{8,9},{9,8},{10,11... | collective-permute-start | bytes 589832 | tf_op jit(solution)/shard_map/ppermute | solution.py:249
  24.0 16.0 %collective-permute-start.12 = (bf16[512,512]{1,0:T(8,128)(2,1)S(1)}, bf16[512,512]{1,0:T(8,128)(2,1)S(1)}, u32[]{:S(2)}, u32[]{:S(2)}) collective-permute-start(bf16[512,512]{1,0:T(8,128)(2,1)S(1)} %get-tuple-element.46), channel_id=1, source_target_pairs={{4,0},{5,1},{6,2},{7,3},{8,4},{9,5},{10,6},{11,7},{12,8},{13,9},{1... | collective-permute-start | bytes 1572872 | tf_op jit(solution)/shard_map/ppermute | solution.py:246
  29.1 10.9 %copy-start.1 = (f32[512,512]{1,0:T(8,128)}, f32[512,512]{1,0:T(8,128)S(1)}, u32[]{:S(2)}) copy-start(f32[512,512]{1,0:T(8,128)S(1)} %get-tuple-element.81.refs_10_) | copy-start | bytes 3145732
  29.1 20.6 %collective-permute-start.9 = (bf16[192,1024]{1,0:T(8,128)(2,1)S(1)}, bf16[192,1024]{1,0:T(8,128)(2,1)S(1)}, u32[]{:S(2)}, u32[]{:S(2)}) collective-permute-start(bf16[192,1024]{1,0:T(8,128)(2,1)S(1)} %get-tuple-element.54), channel_id=1, source_target_pairs={{0,2},{1,3},{2,0},{3,1},{4,6},{5,7},{6,4},{7,5},{8,10},{9,11},{10,... | collective-permute-start | bytes 1179656 | tf_op jit(solution)/shard_map/ppermute | solution.py:249
  30.6 19.9 %collective-permute-start.10 = (bf16[192,1024]{1,0:T(8,128)(2,1)S(1)}, bf16[192,1024]{1,0:T(8,128)(2,1)S(1)}, u32[]{:S(2)}, u32[]{:S(2)}) collective-permute-start(bf16[192,1024]{1,0:T(8,128)(2,1)S(1)} %get-tuple-element.55), channel_id=1, source_target_pairs={{0,3},{1,2},{2,1},{3,0},{4,7},{5,6},{6,5},{7,4},{8,11},{9,10},{10,... | collective-permute-start | bytes 1179656 | tf_op jit(solution)/shard_map/ppermute | solution.py:249
  31.1 20.9 %collective-permute-start.11 = (bf16[192,1024]{1,0:T(8,128)(2,1)S(1)}, bf16[192,1024]{1,0:T(8,128)(2,1)S(1)}, u32[]{:S(2)}, u32[]{:S(2)}) collective-permute-start(bf16[192,1024]{1,0:T(8,128)(2,1)S(1)} %get-tuple-element.56), channel_id=1, source_target_pairs={{0,1},{1,0},{2,3},{3,2},{4,5},{5,4},{6,7},{7,6},{8,9},{9,8},{10,11... | collective-permute-start | bytes 1179656 | tf_op jit(solution)/shard_map/ppermute | solution.py:249
  33.5 28.3 %collective-permute-start.8 = (bf16[1024,512]{1,0:T(8,128)(2,1)S(1)}, bf16[1024,512]{1,0:T(8,128)(2,1)S(1)}, u32[]{:S(2)}, u32[]{:S(2)}) collective-permute-start(bf16[1024,512]{1,0:T(8,128)(2,1)S(1)} %plane_partial.3), channel_id=1, source_target_pairs={{0,4},{1,5},{2,6},{3,7},{4,8},{5,9},{6,10},{7,11},{8,12},{9,13},{1... | collective-permute-start | bytes 3145736 | tf_op jit(solution)/shard_map/ppermute | solution.py:243
  45.1 36.4 %collective-permute-start.13 = (bf16[192,2048]{1,0:T(8,128)(2,1)S(1)}, bf16[192,2048]{1,0:T(8,128)(2,1)S(1)}, u32[]{:S(2)}, u32[]{:S(2)}) collective-permute-start(bf16[192,2048]{1,0:T(8,128)(2,1)S(1)} %get-tuple-element.65), channel_id=1, source_target_pairs={{0,2},{1,3},{2,0},{3,1},{4,6},{5,7},{6,4},{7,5},{8,10},{9,11},{10,... | collective-permute-start | bytes 2359304 | tf_op jit(solution)/shard_map/ppermute | solution.py:249
  49.7 33.3 %collective-permute-start.15 = (bf16[192,2048]{1,0:T(8,128)(2,1)S(1)}, bf16[192,2048]{1,0:T(8,128)(2,1)S(1)}, u32[]{:S(2)}, u32[]{:S(2)}) collective-permute-start(bf16[192,2048]{1,0:T(8,128)(2,1)S(1)} %get-tuple-element.68), channel_id=1, source_target_pairs={{0,3},{1,2},{2,1},{3,0},{4,7},{5,6},{6,5},{7,4},{8,11},{9,10},{10,... | collective-permute-start | bytes 2359304 | tf_op jit(solution)/shard_map/ppermute | solution.py:249
  50.5 33.3 %collective-permute-start.17 = (bf16[192,2048]{1,0:T(8,128)(2,1)S(1)}, bf16[192,2048]{1,0:T(8,128)(2,1)S(1)}, u32[]{:S(2)}, u32[]{:S(2)}) collective-permute-start(bf16[192,2048]{1,0:T(8,128)(2,1)S(1)} %get-tuple-element.71), channel_id=1, source_target_pairs={{0,1},{1,0},{2,3},{3,2},{4,5},{5,4},{6,7},{7,6},{8,9},{9,8},{10,11... | collective-permute-start | bytes 2359304 | tf_op jit(solution)/shard_map/ppermute | solution.py:249
  63.7 27.0 %collective-permute-start.20 = (bf16[512,512]{1,0:T(8,128)(2,1)S(1)}, bf16[512,512]{1,0:T(8,128)(2,1)S(1)}, u32[]{:S(2)}, u32[]{:S(2)}) collective-permute-start(bf16[512,512]{1,0:T(8,128)(2,1)S(1)} %get-tuple-element.79), channel_id=1, source_target_pairs={{4,0},{5,1},{6,2},{7,3},{8,4},{9,5},{10,6},{11,7},{12,8},{13,9},{1... | collective-permute-start | bytes 1572872 | tf_op jit(solution)/shard_map/ppermute | solution.py:246
  67.2 23.6 %collective-permute-start.19 = (bf16[512,512]{1,0:T(8,128)(2,1)S(1)}, bf16[512,512]{1,0:T(8,128)(2,1)S(1)}, u32[]{:S(2)}, u32[]{:S(2)}) collective-permute-start(bf16[512,512]{1,0:T(8,128)(2,1)S(1)} %get-tuple-element.57.refs_5_), channel_id=1, source_target_pairs={{0,4},{1,5},{2,6},{3,7},{4,8},{5,9},{6,10},{7,11},{8,12},{9,13},{1... | collective-permute-start | bytes 1572872 | tf_op jit(solution)/shard_map/ppermute | solution.py:243
  81.4 13.0 %collective-permute-start.14 = (bf16[192,512]{1,0:T(8,128)(2,1)S(1)}, bf16[192,512]{1,0:T(8,128)(2,1)S(1)}, u32[]{:S(2)}, u32[]{:S(2)}) collective-permute-start(bf16[192,512]{1,0:T(8,128)(2,1)S(1)} %get-tuple-element.66), channel_id=1, source_target_pairs={{0,2},{1,3},{2,0},{3,1},{4,6},{5,7},{6,4},{7,5},{8,10},{9,11},{10,... | collective-permute-start | bytes 589832 | tf_op jit(solution)/shard_map/ppermute | solution.py:249
  82.9 11.5 %collective-permute-start.16 = (bf16[192,512]{1,0:T(8,128)(2,1)S(1)}, bf16[192,512]{1,0:T(8,128)(2,1)S(1)}, u32[]{:S(2)}, u32[]{:S(2)}) collective-permute-start(bf16[192,512]{1,0:T(8,128)(2,1)S(1)} %get-tuple-element.69), channel_id=1, source_target_pairs={{0,3},{1,2},{2,1},{3,0},{4,7},{5,6},{6,5},{7,4},{8,11},{9,10},{10,... | collective-permute-start | bytes 589832 | tf_op jit(solution)/shard_map/ppermute | solution.py:249
  83.8 10.6 %collective-permute-start.18 = (bf16[192,512]{1,0:T(8,128)(2,1)S(1)}, bf16[192,512]{1,0:T(8,128)(2,1)S(1)}, u32[]{:S(2)}, u32[]{:S(2)}) collective-permute-start(bf16[192,512]{1,0:T(8,128)(2,1)S(1)} %get-tuple-element.72), channel_id=1, source_target_pairs={{0,1},{1,0},{2,3},{3,2},{4,5},{5,4},{6,7},{7,6},{8,9},{9,8},{10,11... | collective-permute-start | bytes 589832 | tf_op jit(solution)/shard_map/ppermute | solution.py:249
  87.3 5.0 %copy-start.4 = (f32[1,512,512]{2,1,0:T(8,128)S(1)}, f32[1,512,512]{2,1,0:T(8,128)}, u32[]{:S(2)}) copy-start(f32[1,512,512]{2,1,0:T(8,128)} %param.12) | copy-start | bytes 3145732
  87.3 5.0 %copy-start.5 = (f32[1,512,512]{2,1,0:T(8,128)S(1)}, f32[1,512,512]{2,1,0:T(8,128)}, u32[]{:S(2)}) copy-start(f32[1,512,512]{2,1,0:T(8,128)} %param.11) | copy-start | bytes 3145732
  94.4 1.5 %copy-start = (f32[512,512]{1,0:T(8,128)}, f32[512,512]{1,0:T(8,128)S(1)}, u32[]{:S(2)}) copy-start(f32[512,512]{1,0:T(8,128)S(1)} %get-tuple-element.83.refs_5_) | copy-start | bytes 3145732

commit v9 on v8

--- a/solution.py
+++ b/solution.py
@@ -20,7 +20,7 @@
 WEIGHT_SCALE = 2.0**17
 WIRE = jnp.bfloat16
 PEERS = (0, 2, 3, 1)
-C_PARTIAL, C_PRODUCT, C_UNPACK = (32, 33, 34), (36, 34), (33, 20)
+C_PARTIAL, C_PRODUCT, C_UNPACK = (33, 34, 32), (33, 34), (32, 20)
 
 
 def cost(log_flops):
@@ -278,7 +278,7 @@
     new_anchor = fragment_anchor - outer_rate * (pseudo_mean + outer_mass * new_momentum)
 
     behind, ahead = around(coded), back(coded)
-    behind, firsts = lax.optimization_barrier((behind, firsts))
+    behind, ahead, firsts = lax.optimization_barrier((behind, ahead, firsts))
     weights, offsets = [weight, behind, ahead], [0, -1, 1]
 
     def partials(spread, parts, rest, dtype, span):

time: 96.3 us -> 98.6 us (1.024)
  waiting for transfers between devices: 42.4 us -> 45.5 us
  starting transfers between devices: 29.4 us -> 27.8 us
    ppermute x15, waiting for transfers between devices: 22.8 us -> 36.4 us  [across(): return lax.ppermute(x, 'fsdp', [(i, i ^ PEERS[k]) for i in range(size)])]
    ppermute x2, waiting for transfers between devices: 6.45 us -> 0.01 us  [back(): return lax.ppermute(x, 'fsdp', [(to, source) for source, to in ring])]
    ppermute x3, waiting for transfers between devices: 13.2 us -> 9.08 us  [around(): return lax.ppermute(x, 'fsdp', ring)]
    ppermute x2, starting transfers between devices: 7.03 us -> 4.72 us  [back(): return lax.ppermute(x, 'fsdp', [(to, source) for source, to in ring])]
  transfers between devices with their start and end apart: 21 -> 21, of which waited for: 8 -> 9; matrix products, arithmetic and copies ran while one was open for 4% -> 4% of each run, Pallas kernels for 17% -> 16%
where the time goes in v9:
time: 98.6 us; the launch traced here: 98.3 us
  waiting for transfers between devices  45.5 us (46%)
  starting transfers between devices  27.8 us (28%)
  Pallas kernels  17.4 us (18%)
  other arithmetic  3.64 us (4%)
  local copies, waits for them, and re-layouts  3.04 us (3%)
    ppermute x15, waiting for transfers between devices, across(): return lax.ppermute(x, 'fsdp', [(i, i ^ PEERS[k]) for i in range(size)])  36.4 us
    ppermute x15, starting transfers between devices, across(): return lax.ppermute(x, 'fsdp', [(i, i ^ PEERS[k]) for i in range(size)])  20.5 us
    ppermute x3, waiting for transfers between devices, around(): return lax.ppermute(x, 'fsdp', ring)  9.08 us
    pallas_call x2, Pallas kernels, plane_product(): pl.pallas_call(functools.partial(product_kernel, columns, len(weights), s...  6.95 us
    ppermute x2, starting transfers between devices, back(): return lax.ppermute(x, 'fsdp', [(to, source) for source, to in ring])  4.72 us
    pallas_call x3, Pallas kernels, plane_partial(): pl.pallas_call(functools.partial(partial_kernel, columns, scale, spread),...  4.33 us
    pallas_call x2, Pallas kernels, unpack(): pl.pallas_call(functools.partial(unpack_kernel, columns, planes, 'fsdp',...  3.88 us
    unnamed x18, local copies, waits for them, and re-layouts  3.04 us
  transfers between devices with their start and end apart: 21, of which 9 were waited for; matrix products, arithmetic and copies ran while one was open for 4% of the time, Pallas kernels for 16%

profile of v9, /device:TPU:0, one launch (start us, length us, event | category | flops | bytes accessed | tf_op | source)
XLA Modules:
  0.0 98.3 jit_solution(16725000835231311454)
XLA Ops:
  3.3 2.2 %pack.1 = (bf16[512,512]{1,0:T(8,128)(2,1)S(1)}, f32[512,512]{1,0:T(8,128)S(1)}, bf16[192,512]{1,0:T(8,128)(2,1)S(1)}, bf16[192,2048]{1,0:T(8,128)(2,1)S(1)}, bf...) custom-call(bf16[192,8192]{1,0:T(8,128)(2,1)} %features_far.1, ...), custom_call_target="tpu_custom_call" | custom-call | flops 68719476736 | bytes 1048576 | tf_op jit(solution)/shard_map/pack/pallas_call | solution.py:95
  5.5 4.7 %collective-permute-start.5 = (bf16[512,512]{1,0:T(8,128)(2,1)S(1)}, bf16[512,512]{1,0:T(8,128)(2,1)S(1)}, u32[]{:S(2)}, u32[]{:S(2)}) collective-permute-start(bf16[512,512]{1,0:T(8,128)(2,1)S(1)} %get-tuple-element.47), channel_id=1, source_target_pairs={{4,0},{5,1},{6,2},{7,3},{8,4},{9,5},{10,6},{11,7},{12,8},{13,9},{1... | collective-permute-start | bytes 1572872 | tf_op jit(solution)/shard_map/ppermute | solution.py:246
  10.2 1.5 %collective-permute-start.6 = (bf16[192,512]{1,0:T(8,128)(2,1)S(1)}, bf16[192,512]{1,0:T(8,128)(2,1)S(1)}, u32[]{:S(2)}, u32[]{:S(2)}) collective-permute-start(bf16[192,512]{1,0:T(8,128)(2,1)S(1)} %get-tuple-element.48), channel_id=1, source_target_pairs={{0,2},{1,3},{2,0},{3,1},{4,6},{5,7},{6,4},{7,5},{8,10},{9,11},{10,... | collective-permute-start | bytes 589832 | tf_op jit(solution)/shard_map/ppermute | solution.py:249
  11.7 1.4 %collective-permute-start.7 = (bf16[192,512]{1,0:T(8,128)(2,1)S(1)}, bf16[192,512]{1,0:T(8,128)(2,1)S(1)}, u32[]{:S(2)}, u32[]{:S(2)}) collective-permute-start(bf16[192,512]{1,0:T(8,128)(2,1)S(1)} %get-tuple-element.49), channel_id=1, source_target_pairs={{0,3},{1,2},{2,1},{3,0},{4,7},{5,6},{6,5},{7,4},{8,11},{9,10},{10,... | collective-permute-start | bytes 589832 | tf_op jit(solution)/shard_map/ppermute | solution.py:249
  13.2 1.5 %collective-permute-start = (bf16[192,512]{1,0:T(8,128)(2,1)S(1)}, bf16[192,512]{1,0:T(8,128)(2,1)S(1)}, u32[]{:S(2)}, u32[]{:S(2)}) collective-permute-start(bf16[192,512]{1,0:T(8,128)(2,1)S(1)} %get-tuple-element.45.refs_0_.refs_1_.refs_3_), channel_id=1, source_target_pairs={{0,2},{1,3},{2,0},{3,1},{4,6},{5,7},{6,4},{7,5},{8,10},{9,11},{10,... | collective-permute-start | bytes 589832 | tf_op jit(solution)/shard_map/ppermute | solution.py:249
  14.7 7.5 %collective-permute-done.6.refs_4_ = bf16[192,512]{1,0:T(8,128)(2,1)S(1)} collective-permute-done((bf16[192,512]{1,0:T(8,128)(2,1)S(1)}, bf16[192,512]{1,0:T(8,128)(2,1)S(1)}, u32[]{:S(2)}, u32[]{:S(2)}) %collective-permute-start.6) | collective-permute-done | bytes 196640 | tf_op jit(solution)/shard_map/ppermute | solution.py:249
  22.2 1.5 %collective-permute-start.8 = (bf16[192,512]{1,0:T(8,128)(2,1)S(1)}, bf16[192,512]{1,0:T(8,128)(2,1)S(1)}, u32[]{:S(2)}, u32[]{:S(2)}) collective-permute-start(bf16[192,512]{1,0:T(8,128)(2,1)S(1)} %get-tuple-element.50), channel_id=1, source_target_pairs={{0,1},{1,0},{2,3},{3,2},{4,5},{5,4},{6,7},{7,6},{8,9},{9,8},{10,11... | collective-permute-start | bytes 589832 | tf_op jit(solution)/shard_map/ppermute | solution.py:249
  24.2 1.5 %collective-permute-done.refs_1_.refs_2_.refs_4_ = bf16[192,512]{1,0:T(8,128)(2,1)S(1)} collective-permute-done((bf16[192,512]{1,0:T(8,128)(2,1)S(1)}, bf16[192,512]{1,0:T(8,128)(2,1)S(1)}, u32[]{:S(2)}, u32[]{:S(2)}) %collective-permute-start) | collective-permute-done | bytes 196640 | tf_op jit(solution)/shard_map/ppermute | solution.py:249
  25.7 1.5 %collective-permute-start.1 = (bf16[192,512]{1,0:T(8,128)(2,1)S(1)}, bf16[192,512]{1,0:T(8,128)(2,1)S(1)}, u32[]{:S(2)}, u32[]{:S(2)}) collective-permute-start(bf16[192,512]{1,0:T(8,128)(2,1)S(1)} %collective-permute-done.refs_1_.refs_2_.refs_4_), channel_id=1, source_target_pairs={{0,1},{1,0},{2,3},{3,2},{4,5},{5,4},{6,7},{7,6},{8,9},{9,8},{10,11... | collective-permute-start | bytes 589832 | tf_op jit(solution)/shard_map/ppermute | solution.py:249
  27.2 2.8 %collective-permute-done.8.refs_6_ = bf16[192,512]{1,0:T(8,128)(2,1)S(1)} collective-permute-done((bf16[192,512]{1,0:T(8,128)(2,1)S(1)}, bf16[192,512]{1,0:T(8,128)(2,1)S(1)}, u32[]{:S(2)}, u32[]{:S(2)}) %collective-permute-start.8) | collective-permute-done | bytes 196640 | tf_op jit(solution)/shard_map/ppermute | solution.py:249
  30.0 1.5 %collective-permute-start.10 = (bf16[192,1024]{1,0:T(8,128)(2,1)S(1)}, bf16[192,1024]{1,0:T(8,128)(2,1)S(1)}, u32[]{:S(2)}, u32[]{:S(2)}) collective-permute-start(bf16[192,1024]{1,0:T(8,128)(2,1)S(1)} %get-tuple-element.55), channel_id=1, source_target_pairs={{0,2},{1,3},{2,0},{3,1},{4,6},{5,7},{6,4},{7,5},{8,10},{9,11},{10,... | collective-permute-start | bytes 1179656 | tf_op jit(solution)/shard_map/ppermute | solution.py:249
  31.5 1.4 %collective-permute-start.11 = (bf16[192,1024]{1,0:T(8,128)(2,1)S(1)}, bf16[192,1024]{1,0:T(8,128)(2,1)S(1)}, u32[]{:S(2)}, u32[]{:S(2)}) collective-permute-start(bf16[192,1024]{1,0:T(8,128)(2,1)S(1)} %get-tuple-element.56), channel_id=1, source_target_pairs={{0,3},{1,2},{2,1},{3,0},{4,7},{5,6},{6,5},{7,4},{8,11},{9,10},{10,... | collective-permute-start | bytes 1179656 | tf_op jit(solution)/shard_map/ppermute | solution.py:249
  34.2 1.5 %collective-permute-start.12 = (bf16[192,1024]{1,0:T(8,128)(2,1)S(1)}, bf16[192,1024]{1,0:T(8,128)(2,1)S(1)}, u32[]{:S(2)}, u32[]{:S(2)}) collective-permute-start(bf16[192,1024]{1,0:T(8,128)(2,1)S(1)} %get-tuple-element.57), channel_id=1, source_target_pairs={{0,1},{1,0},{2,3},{3,2},{4,5},{5,4},{6,7},{7,6},{8,9},{9,8},{10,11... | collective-permute-start | bytes 1179656 | tf_op jit(solution)/shard_map/ppermute | solution.py:249
  35.7 2.7 %collective-permute-done.1.refs_2_.refs_3_.refs_5_ = bf16[192,512]{1,0:T(8,128)(2,1)S(1)} collective-permute-done((bf16[192,512]{1,0:T(8,128)(2,1)S(1)}, bf16[192,512]{1,0:T(8,128)(2,1)S(1)}, u32[]{:S(2)}, u32[]{:S(2)}) %collective-permute-start.1) | collective-permute-done | bytes 196640 | tf_op jit(solution)/shard_map/ppermute | solution.py:249
  40.3 1.5 %multiply_subtract_fusion = (f32[512,512]{1,0:T(8,128)}, f32[512,512]{1,0:T(8,128)S(1)}) fusion(f32[512,512]{1,0:T(8,128)S(1)} %copy-done.6, f32[1,512,512]{2,1,0:T(8,128)S(1)} %collective-permute-done.3, f32[1,512,512]{2,1,0:T(8,128)S(1)} %copy-done.7, f32[512,512]{1,0:T(8,128)S(1)} %copy-done.8), kind=kLoop, calls=%fused_computation.6 | loop fusion | flops 2621440 | bytes 6291456 | tf_op jit(solution)/shard_map/sub | solution.py:278
  41.8 5.0 %plane_product.3 = (f32[192,1536]{1,0:T(8,128)S(1)}, bf16[192,2048]{1,0:T(8,128)(2,1)S(1)}, bf16[192,2048]{1,0:T(8,128)(2,1)S(1)}, bf16[192,2048]{1,0:T(8,128)(2,1)S(1)}) custom-call(f32[512,512]{1,0:T(8,128)S(1)} %get-tuple-element.61.refs_0_, bf16[512,512]{1,0:T(8,128)(2,1)S(1)} %collective-permute-done.4.refs_7_.refs_1_, ...), custom_call_target="tpu_custom_call" | custom-call | flops 8589934592 | bytes 1048576 | tf_op jit(solution)/shard_map/plane_product/pallas_call | solution.py:166
  46.8 1.6 %collective-permute-start.13 = (bf16[192,2048]{1,0:T(8,128)(2,1)S(1)}, bf16[192,2048]{1,0:T(8,128)(2,1)S(1)}, u32[]{:S(2)}, u32[]{:S(2)}) collective-permute-start(bf16[192,2048]{1,0:T(8,128)(2,1)S(1)} %get-tuple-element.67), channel_id=1, source_target_pairs={{0,2},{1,3},{2,0},{3,1},{4,6},{5,7},{6,4},{7,5},{8,10},{9,11},{10,... | collective-permute-start | bytes 2359304 | tf_op jit(solution)/shard_map/ppermute | solution.py:249
  48.4 1.4 %collective-permute-start.15 = (bf16[192,2048]{1,0:T(8,128)(2,1)S(1)}, bf16[192,2048]{1,0:T(8,128)(2,1)S(1)}, u32[]{:S(2)}, u32[]{:S(2)}) collective-permute-start(bf16[192,2048]{1,0:T(8,128)(2,1)S(1)} %get-tuple-element.70), channel_id=1, source_target_pairs={{0,3},{1,2},{2,1},{3,0},{4,7},{5,6},{6,5},{7,4},{8,11},{9,10},{10,... | collective-permute-start | bytes 2359304 | tf_op jit(solution)/shard_map/ppermute | solution.py:249
  50.4 4.9 %collective-permute-done.12.refs_6_ = bf16[192,1024]{1,0:T(8,128)(2,1)S(1)} collective-permute-done((bf16[192,1024]{1,0:T(8,128)(2,1)S(1)}, bf16[192,1024]{1,0:T(8,128)(2,1)S(1)}, u32[]{:S(2)}, u32[]{:S(2)}) %collective-permute-start.12) | collective-permute-done | bytes 393248 | tf_op jit(solution)/shard_map/ppermute | solution.py:249
  55.3 7.9 %collective-permute-done.9.refs_7_.refs_0_ = bf16[1024,512]{1,0:T(8,128)(2,1)S(1)} collective-permute-done((bf16[1024,512]{1,0:T(8,128)(2,1)S(1)}, bf16[1024,512]{1,0:T(8,128)(2,1)S(1)}, u32[]{:S(2)}, u32[]{:S(2)}) %collective-permute-start.9) | collective-permute-done | bytes 1048608 | tf_op jit(solution)/shard_map/ppermute | solution.py:243
  63.2 2.0 %plane_partial.4 = (bf16[512,512]{1,0:T(8,128)(2,1)S(1)}, bf16[512,512]{1,0:T(8,128)(2,1)S(1)}) custom-call(bf16[192,2048]{1,0:T(8,128)(2,1)S(1)} %get-tuple-element.44.own, bf16[192,512]{1,0:T(8,128)(2,1)S(1)} %get-tuple-element.45.refs_0_.refs_1_.refs_3_, bf16[192,512]{1,0:T(8,128)(2,1)S(1)} %collective-permute-done.refs_1_.refs_2_.refs_4_, ...), custom_call_target="tpu_custom_call" | custom-call | flops 17179869184 | bytes 1048576 | tf_op jit(solution)/shard_map/plane_partial/pallas_call | solution.py:131
  65.2 2.0 %collective-permute-start.19 = (bf16[512,512]{1,0:T(8,128)(2,1)S(1)}, bf16[512,512]{1,0:T(8,128)(2,1)S(1)}, u32[]{:S(2)}, u32[]{:S(2)}) collective-permute-start(bf16[512,512]{1,0:T(8,128)(2,1)S(1)} %get-tuple-element.58.refs_5_), channel_id=1, source_target_pairs={{0,4},{1,5},{2,6},{3,7},{4,8},{5,9},{6,10},{7,11},{8,12},{9,13},{1... | collective-permute-start | bytes 1572872 | tf_op jit(solution)/shard_map/ppermute | solution.py:243
  67.2 1.9 %plane_product.2 = (f32[192,512]{1,0:T(8,128)S(1)}, bf16[192,512]{1,0:T(8,128)(2,1)S(1)}, bf16[192,512]{1,0:T(8,128)(2,1)S(1)}, bf16[192,512]{1,0:T(8,128)(2,1)S(1)}) custom-call(bf16[1024,512]{1,0:T(8,128)(2,1)S(1)} %collective-permute-done.9.refs_7_.refs_0_, bf16[192,512]{1,0:T(8,128)(2,1)S(1)} %get-tuple-element.45.refs_0_.refs_1_.refs_3_, ...), custom_call_target="tpu_custom_call" | custom-call | flops 17179869184 | bytes 1048576 | tf_op jit(solution)/shard_map/plane_product/pallas_call | solution.py:166
  69.2 12.3 %collective-permute-done.13.refs_1_.refs_4_ = bf16[192,2048]{1,0:T(8,128)(2,1)S(1)} collective-permute-done((bf16[192,2048]{1,0:T(8,128)(2,1)S(1)}, bf16[192,2048]{1,0:T(8,128)(2,1)S(1)}, u32[]{:S(2)}, u32[]{:S(2)}) %collective-permute-start.13) | collective-permute-done | bytes 786464 | tf_op jit(solution)/shard_map/ppermute | solution.py:249
  81.5 1.5 %collective-permute-start.14 = (bf16[192,512]{1,0:T(8,128)(2,1)S(1)}, bf16[192,512]{1,0:T(8,128)(2,1)S(1)}, u32[]{:S(2)}, u32[]{:S(2)}) collective-permute-start(bf16[192,512]{1,0:T(8,128)(2,1)S(1)} %get-tuple-element.68), channel_id=1, source_target_pairs={{0,2},{1,3},{2,0},{3,1},{4,6},{5,7},{6,4},{7,5},{8,10},{9,11},{10,... | collective-permute-start | bytes 589832 | tf_op jit(solution)/shard_map/ppermute | solution.py:249
  83.0 1.5 %collective-permute-start.16 = (bf16[192,512]{1,0:T(8,128)(2,1)S(1)}, bf16[192,512]{1,0:T(8,128)(2,1)S(1)}, u32[]{:S(2)}, u32[]{:S(2)}) collective-permute-start(bf16[192,512]{1,0:T(8,128)(2,1)S(1)} %get-tuple-element.71), channel_id=1, source_target_pairs={{0,3},{1,2},{2,1},{3,0},{4,7},{5,6},{6,5},{7,4},{8,11},{9,10},{10,... | collective-permute-start | bytes 589832 | tf_op jit(solution)/shard_map/ppermute | solution.py:249
  84.4 4.7 %collective-permute-done.17.refs_3_.refs_6_ = bf16[192,2048]{1,0:T(8,128)(2,1)S(1)} collective-permute-done((bf16[192,2048]{1,0:T(8,128)(2,1)S(1)}, bf16[192,2048]{1,0:T(8,128)(2,1)S(1)}, u32[]{:S(2)}, u32[]{:S(2)}) %collective-permute-start.17) | collective-permute-done | bytes 786464 | tf_op jit(solution)/shard_map/ppermute | solution.py:249
  89.1 1.5 %collective-permute-start.18 = (bf16[192,512]{1,0:T(8,128)(2,1)S(1)}, bf16[192,512]{1,0:T(8,128)(2,1)S(1)}, u32[]{:S(2)}, u32[]{:S(2)}) collective-permute-start(bf16[192,512]{1,0:T(8,128)(2,1)S(1)} %get-tuple-element.74), channel_id=1, source_target_pairs={{0,1},{1,0},{2,3},{3,2},{4,5},{5,4},{6,7},{7,6},{8,9},{9,8},{10,11... | collective-permute-start | bytes 589832 | tf_op jit(solution)/shard_map/ppermute | solution.py:249
  90.6 2.4 %unpack.2.refs_4_ = f32[192,8192]{1,0:T(8,128)} custom-call(f32[192,1536]{1,0:T(8,128)S(1)} %get-tuple-element.75.refs_0_, bf16[192,2048]{1,0:T(8,128)(2,1)S(1)} %collective-permute-done.13.refs_1_.refs_4_, bf16[192,2048]{1,0:T(8,128)(2,1)S(1)} %collective-permute-done.15.refs_2_.refs_5_, bf16[192,2048]{1,0:T(8,128)(2,1)S(1)} %collective-permute-done.17.refs_3_.refs_6_), custom_call_target="tpu_custom_call" | custom-call | flops 4294967296 | bytes 1048576 | tf_op jit(solution)/shard_map/unpack/pallas_call | solution.py:207
  93.0 1.5 %plane_partial.5 = f32[512,512]{1,0:T(8,128)S(1)} custom-call(bf16[192,2048]{1,0:T(8,128)(2,1)S(1)} %get-tuple-element.44.own, bf16[192,512]{1,0:T(8,128)(2,1)S(1)} %get-tuple-element.45.refs_0_.refs_1_.refs_3_, bf16[192,512]{1,0:T(8,128)(2,1)S(1)} %collective-permute-done.refs_1_.refs_2_.refs_4_, ...), custom_call_target="tpu_custom_call" | custom-call | flops 4294967296 | bytes 1048576 | tf_op jit(solution)/shard_map/plane_partial/pallas_call | solution.py:131
  94.5 2.1 %subtract_bitcast_fusion = (f32[1,512,512]{2,1,0:T(8,128)}, f32[512,512]{1,0:T(8,128)S(1)}, f32[1,512,512]{2,1,0:T(8,128)}) fusion(f32[512,512]{1,0:T(8,128)S(1)} %get-tuple-element.61.refs_0_, f32[512,512]{1,0:T(8,128)S(1)} %plane_partial.5, f32[1,512,512]{2,1,0:T(8,128)S(1)} %copy-done.4, f32[1,512,512]{2,1,0:T(8,128)S(1)} %copy-done.5), kind=kLoop, calls=%fused_computation.7 | loop fusion | flops 4194304 | bytes 7340032 | tf_op jit(solution)/shard_map/broadcast_in_dim | solution.py:335
  96.7 1.5 %unpack.3 = f32[192,8192]{1,0:T(8,128)} custom-call(f32[192,512]{1,0:T(8,128)S(1)} %get-tuple-element.59.refs_0_, bf16[192,512]{1,0:T(8,128)(2,1)S(1)} %collective-permute-done.14.refs_1_, bf16[192,512]{1,0:T(8,128)(2,1)S(1)} %collective-permute-done.16.refs_2_, ...), custom_call_target="tpu_custom_call", output_to_operand_aliasing={{}: (4, {})} | custom-call | flops 1048576 | bytes 1048576 | tf_op jit(solution)/shard_map/unpack/pallas_call | solution.py:207
  (38 shorter events, 6.9 us)
Async XLA Ops:
  0.6 4.9 %collective-permute-start.3 = (f32[1,512,512]{2,1,0:T(8,128)}, f32[1,512,512]{2,1,0:T(8,128)S(1)}, u32[]{:S(2)}, u32[]{:S(2)}) collective-permute-start(f32[1,512,512]{2,1,0:T(8,128)} %param.13), channel_id=1, source_target_pairs={{0,16},{16,0},{1,17},{17,1},{2,18},{18,2},{3,19},{19,3},{4,20},{20... | collective-permute-start | bytes 3145736 | tf_op jit(solution)/shard_map/ppermute | solution.py:263
  1.1 1.2 %copy-start.2 = (f32[1,512,512]{2,1,0:T(8,128)S(1)}, f32[1,512,512]{2,1,0:T(8,128)}, u32[]{:S(2)}) copy-start(f32[1,512,512]{2,1,0:T(8,128)} %weight_far.1) | copy-start | bytes 3145732
  2.4 0.9 copy-start.3
  5.5 26.0 %collective-permute-start.5 = (bf16[512,512]{1,0:T(8,128)(2,1)S(1)}, bf16[512,512]{1,0:T(8,128)(2,1)S(1)}, u32[]{:S(2)}, u32[]{:S(2)}) collective-permute-start(bf16[512,512]{1,0:T(8,128)(2,1)S(1)} %get-tuple-element.47), channel_id=1, source_target_pairs={{4,0},{5,1},{6,2},{7,3},{8,4},{9,5},{10,6},{11,7},{12,8},{13,9},{1... | collective-permute-start | bytes 1572872 | tf_op jit(solution)/shard_map/ppermute | solution.py:246
  10.2 24.0 %collective-permute-start.4 = (bf16[512,512]{1,0:T(8,128)(2,1)S(1)}, bf16[512,512]{1,0:T(8,128)(2,1)S(1)}, u32[]{:S(2)}, u32[]{:S(2)}) collective-permute-start(bf16[512,512]{1,0:T(8,128)(2,1)S(1)} %get-tuple-element.47), channel_id=1, source_target_pairs={{0,4},{1,5},{2,6},{3,7},{4,8},{5,9},{6,10},{7,11},{8,12},{9,13},{1... | collective-permute-start | bytes 1572872 | tf_op jit(solution)/shard_map/ppermute | solution.py:243
  10.2 11.9 %collective-permute-start.6 = (bf16[192,512]{1,0:T(8,128)(2,1)S(1)}, bf16[192,512]{1,0:T(8,128)(2,1)S(1)}, u32[]{:S(2)}, u32[]{:S(2)}) collective-permute-start(bf16[192,512]{1,0:T(8,128)(2,1)S(1)} %get-tuple-element.48), channel_id=1, source_target_pairs={{0,2},{1,3},{2,0},{3,1},{4,6},{5,7},{6,4},{7,5},{8,10},{9,11},{10,... | collective-permute-start | bytes 589832 | tf_op jit(solution)/shard_map/ppermute | solution.py:249
  11.7 11.9 %collective-permute-start.7 = (bf16[192,512]{1,0:T(8,128)(2,1)S(1)}, bf16[192,512]{1,0:T(8,128)(2,1)S(1)}, u32[]{:S(2)}, u32[]{:S(2)}) collective-permute-start(bf16[192,512]{1,0:T(8,128)(2,1)S(1)} %get-tuple-element.49), channel_id=1, source_target_pairs={{0,3},{1,2},{2,1},{3,0},{4,7},{5,6},{6,5},{7,4},{8,11},{9,10},{10,... | collective-permute-start | bytes 589832 | tf_op jit(solution)/shard_map/ppermute | solution.py:249
  13.2 12.5 %collective-permute-start = (bf16[192,512]{1,0:T(8,128)(2,1)S(1)}, bf16[192,512]{1,0:T(8,128)(2,1)S(1)}, u32[]{:S(2)}, u32[]{:S(2)}) collective-permute-start(bf16[192,512]{1,0:T(8,128)(2,1)S(1)} %get-tuple-element.45.refs_0_.refs_1_.refs_3_), channel_id=1, source_target_pairs={{0,2},{1,3},{2,0},{3,1},{4,6},{5,7},{6,4},{7,5},{8,10},{9,11},{10,... | collective-permute-start | bytes 589832 | tf_op jit(solution)/shard_map/ppermute | solution.py:249
  22.2 7.8 %collective-permute-start.8 = (bf16[192,512]{1,0:T(8,128)(2,1)S(1)}, bf16[192,512]{1,0:T(8,128)(2,1)S(1)}, u32[]{:S(2)}, u32[]{:S(2)}) collective-permute-start(bf16[192,512]{1,0:T(8,128)(2,1)S(1)} %get-tuple-element.50), channel_id=1, source_target_pairs={{0,1},{1,0},{2,3},{3,2},{4,5},{5,4},{6,7},{7,6},{8,9},{9,8},{10,11... | collective-permute-start | bytes 589832 | tf_op jit(solution)/shard_map/ppermute | solution.py:249
  23.7 12.0 %collective-permute-start.2 = (bf16[192,512]{1,0:T(8,128)(2,1)S(1)}, bf16[192,512]{1,0:T(8,128)(2,1)S(1)}, u32[]{:S(2)}, u32[]{:S(2)}) collective-permute-start(bf16[192,512]{1,0:T(8,128)(2,1)S(1)} %get-tuple-element.45.refs_0_.refs_1_.refs_3_), channel_id=1, source_target_pairs={{0,1},{1,0},{2,3},{3,2},{4,5},{5,4},{6,7},{7,6},{8,9},{9,8},{10,11... | collective-permute-start | bytes 589832 | tf_op jit(solution)/shard_map/ppermute | solution.py:249
  25.7 12.8 %collective-permute-start.1 = (bf16[192,512]{1,0:T(8,128)(2,1)S(1)}, bf16[192,512]{1,0:T(8,128)(2,1)S(1)}, u32[]{:S(2)}, u32[]{:S(2)}) collective-permute-start(bf16[192,512]{1,0:T(8,128)(2,1)S(1)} %collective-permute-done.refs_1_.refs_2_.refs_4_), channel_id=1, source_target_pairs={{0,1},{1,0},{2,3},{3,2},{4,5},{5,4},{6,7},{7,6},{8,9},{9,8},{10,11... | collective-permute-start | bytes 589832 | tf_op jit(solution)/shard_map/ppermute | solution.py:249
  30.0 18.4 %collective-permute-start.10 = (bf16[192,1024]{1,0:T(8,128)(2,1)S(1)}, bf16[192,1024]{1,0:T(8,128)(2,1)S(1)}, u32[]{:S(2)}, u32[]{:S(2)}) collective-permute-start(bf16[192,1024]{1,0:T(8,128)(2,1)S(1)} %get-tuple-element.55), channel_id=1, source_target_pairs={{0,2},{1,3},{2,0},{3,1},{4,6},{5,7},{6,4},{7,5},{8,10},{9,11},{10,... | collective-permute-start | bytes 1179656 | tf_op jit(solution)/shard_map/ppermute | solution.py:249
  31.5 18.3 %collective-permute-start.11 = (bf16[192,1024]{1,0:T(8,128)(2,1)S(1)}, bf16[192,1024]{1,0:T(8,128)(2,1)S(1)}, u32[]{:S(2)}, u32[]{:S(2)}) collective-permute-start(bf16[192,1024]{1,0:T(8,128)(2,1)S(1)} %get-tuple-element.56), channel_id=1, source_target_pairs={{0,3},{1,2},{2,1},{3,0},{4,7},{5,6},{6,5},{7,4},{8,11},{9,10},{10,... | collective-permute-start | bytes 1179656 | tf_op jit(solution)/shard_map/ppermute | solution.py:249
  34.2 21.1 %collective-permute-start.12 = (bf16[192,1024]{1,0:T(8,128)(2,1)S(1)}, bf16[192,1024]{1,0:T(8,128)(2,1)S(1)}, u32[]{:S(2)}, u32[]{:S(2)}) collective-permute-start(bf16[192,1024]{1,0:T(8,128)(2,1)S(1)} %get-tuple-element.57), channel_id=1, source_target_pairs={{0,1},{1,0},{2,3},{3,2},{4,5},{5,4},{6,7},{7,6},{8,9},{9,8},{10,11... | collective-permute-start | bytes 1179656 | tf_op jit(solution)/shard_map/ppermute | solution.py:249
  38.4 1.2 %copy-start.6 = (f32[512,512]{1,0:T(8,128)S(1)}, f32[512,512]{1,0:T(8,128)}, u32[]{:S(2)}) copy-start(f32[512,512]{1,0:T(8,128)} %param.14) | copy-start | bytes 3145732
  38.4 1.5 %copy-start.7 = (f32[1,512,512]{2,1,0:T(8,128)S(1)}, f32[1,512,512]{2,1,0:T(8,128)}, u32[]{:S(2)}) copy-start(f32[1,512,512]{2,1,0:T(8,128)} %param.13) | copy-start | bytes 3145732
  38.4 1.9 %copy-start.8 = (f32[512,512]{1,0:T(8,128)S(1)}, f32[512,512]{1,0:T(8,128)}, u32[]{:S(2)}) copy-start(f32[512,512]{1,0:T(8,128)} %param.15) | copy-start | bytes 3145732
  39.3 23.9 %collective-permute-start.9 = (bf16[1024,512]{1,0:T(8,128)(2,1)S(1)}, bf16[1024,512]{1,0:T(8,128)(2,1)S(1)}, u32[]{:S(2)}, u32[]{:S(2)}) collective-permute-start(bf16[1024,512]{1,0:T(8,128)(2,1)S(1)} %plane_partial.3), channel_id=1, source_target_pairs={{0,4},{1,5},{2,6},{3,7},{4,8},{5,9},{6,10},{7,11},{8,12},{9,13},{1... | collective-permute-start | bytes 3145736 | tf_op jit(solution)/shard_map/ppermute | solution.py:243
  41.8 5.0 %copy-start.1 = (f32[512,512]{1,0:T(8,128)}, f32[512,512]{1,0:T(8,128)S(1)}, u32[]{:S(2)}) copy-start(f32[512,512]{1,0:T(8,128)S(1)} %get-tuple-element.83.refs_10_) | copy-start | bytes 3145732
  46.8 34.6 %collective-permute-start.13 = (bf16[192,2048]{1,0:T(8,128)(2,1)S(1)}, bf16[192,2048]{1,0:T(8,128)(2,1)S(1)}, u32[]{:S(2)}, u32[]{:S(2)}) collective-permute-start(bf16[192,2048]{1,0:T(8,128)(2,1)S(1)} %get-tuple-element.67), channel_id=1, source_target_pairs={{0,2},{1,3},{2,0},{3,1},{4,6},{5,7},{6,4},{7,5},{8,10},{9,11},{10,... | collective-permute-start | bytes 2359304 | tf_op jit(solution)/shard_map/ppermute | solution.py:249
  48.4 34.6 %collective-permute-start.15 = (bf16[192,2048]{1,0:T(8,128)(2,1)S(1)}, bf16[192,2048]{1,0:T(8,128)(2,1)S(1)}, u32[]{:S(2)}, u32[]{:S(2)}) collective-permute-start(bf16[192,2048]{1,0:T(8,128)(2,1)S(1)} %get-tuple-element.70), channel_id=1, source_target_pairs={{0,3},{1,2},{2,1},{3,0},{4,7},{5,6},{6,5},{7,4},{8,11},{9,10},{10,... | collective-permute-start | bytes 2359304 | tf_op jit(solution)/shard_map/ppermute | solution.py:249
  49.9 39.2 %collective-permute-start.17 = (bf16[192,2048]{1,0:T(8,128)(2,1)S(1)}, bf16[192,2048]{1,0:T(8,128)(2,1)S(1)}, u32[]{:S(2)}, u32[]{:S(2)}) collective-permute-start(bf16[192,2048]{1,0:T(8,128)(2,1)S(1)} %get-tuple-element.73), channel_id=1, source_target_pairs={{0,1},{1,0},{2,3},{3,2},{4,5},{5,4},{6,7},{7,6},{8,9},{9,8},{10,11... | collective-permute-start | bytes 2359304 | tf_op jit(solution)/shard_map/ppermute | solution.py:249
  65.2 27.9 %collective-permute-start.20 = (bf16[512,512]{1,0:T(8,128)(2,1)S(1)}, bf16[512,512]{1,0:T(8,128)(2,1)S(1)}, u32[]{:S(2)}, u32[]{:S(2)}) collective-permute-start(bf16[512,512]{1,0:T(8,128)(2,1)S(1)} %get-tuple-element.81), channel_id=1, source_target_pairs={{4,0},{5,1},{6,2},{7,3},{8,4},{9,5},{10,6},{11,7},{12,8},{13,9},{1... | collective-permute-start | bytes 1572872 | tf_op jit(solution)/shard_map/ppermute | solution.py:246
  65.2 27.8 %collective-permute-start.19 = (bf16[512,512]{1,0:T(8,128)(2,1)S(1)}, bf16[512,512]{1,0:T(8,128)(2,1)S(1)}, u32[]{:S(2)}, u32[]{:S(2)}) collective-permute-start(bf16[512,512]{1,0:T(8,128)(2,1)S(1)} %get-tuple-element.58.refs_5_), channel_id=1, source_target_pairs={{0,4},{1,5},{2,6},{3,7},{4,8},{5,9},{6,10},{7,11},{8,12},{9,13},{1... | collective-permute-start | bytes 1572872 | tf_op jit(solution)/shard_map/ppermute | solution.py:243
  81.5 15.2 %collective-permute-start.14 = (bf16[192,512]{1,0:T(8,128)(2,1)S(1)}, bf16[192,512]{1,0:T(8,128)(2,1)S(1)}, u32[]{:S(2)}, u32[]{:S(2)}) collective-permute-start(bf16[192,512]{1,0:T(8,128)(2,1)S(1)} %get-tuple-element.68), channel_id=1, source_target_pairs={{0,2},{1,3},{2,0},{3,1},{4,6},{5,7},{6,4},{7,5},{8,10},{9,11},{10,... | collective-permute-start | bytes 589832 | tf_op jit(solution)/shard_map/ppermute | solution.py:249
  83.0 13.7 %collective-permute-start.16 = (bf16[192,512]{1,0:T(8,128)(2,1)S(1)}, bf16[192,512]{1,0:T(8,128)(2,1)S(1)}, u32[]{:S(2)}, u32[]{:S(2)}) collective-permute-start(bf16[192,512]{1,0:T(8,128)(2,1)S(1)} %get-tuple-element.71), channel_id=1, source_target_pairs={{0,3},{1,2},{2,1},{3,0},{4,7},{5,6},{6,5},{7,4},{8,11},{9,10},{10,... | collective-permute-start | bytes 589832 | tf_op jit(solution)/shard_map/ppermute | solution.py:249
  89.1 7.6 %collective-permute-start.18 = (bf16[192,512]{1,0:T(8,128)(2,1)S(1)}, bf16[192,512]{1,0:T(8,128)(2,1)S(1)}, u32[]{:S(2)}, u32[]{:S(2)}) collective-permute-start(bf16[192,512]{1,0:T(8,128)(2,1)S(1)} %get-tuple-element.74), channel_id=1, source_target_pairs={{0,1},{1,0},{2,3},{3,2},{4,5},{5,4},{6,7},{7,6},{8,9},{9,8},{10,11... | collective-permute-start | bytes 589832 | tf_op jit(solution)/shard_map/ppermute | solution.py:249
  93.0 1.5 %copy-start.4 = (f32[1,512,512]{2,1,0:T(8,128)S(1)}, f32[1,512,512]{2,1,0:T(8,128)}, u32[]{:S(2)}) copy-start(f32[1,512,512]{2,1,0:T(8,128)} %param.12) | copy-start | bytes 3145732
  93.0 1.5 %copy-start.5 = (f32[1,512,512]{2,1,0:T(8,128)S(1)}, f32[1,512,512]{2,1,0:T(8,128)}, u32[]{:S(2)}) copy-start(f32[1,512,512]{2,1,0:T(8,128)} %param.11) | copy-start | bytes 3145732
  96.7 1.5 %copy-start = (f32[512,512]{1,0:T(8,128)}, f32[512,512]{1,0:T(8,128)S(1)}, u32[]{:S(2)}) copy-start(f32[512,512]{1,0:T(8,128)S(1)} %get-tuple-element.85.refs_5_) | copy-start | bytes 3145732

commit v10 on v5

--- a/solution.py
+++ b/solution.py
@@ -19,7 +19,7 @@
 PLANE = 4
 WEIGHT_SCALE = 2.0**17
 WIRE = jnp.bfloat16
-ORDER = (3, 1, 2)
+PEERS = (0, 2, 3, 1)
 C_PARTIAL, C_PRODUCT, C_UNPACK = (33, 34, 20), (33, 20), (36, 30)
 
 
@@ -78,7 +78,7 @@
             first[:, : cot.shape[1]] = cot[...]
         for at, distance in enumerate(distances):
             block = lax.rem(z + planes + distance, planes)
-            start = pl.multiple_of((block * PLANE + (p ^ k)) * columns, 128)
+            start = pl.multiple_of((block * PLANE + (p ^ PEERS[k])) * columns, 128)
             value = features[:, pl.ds(start, columns)]
             if k == 0:
                 own[:, at * columns : (at + 1) * columns] = value
@@ -195,7 +195,7 @@
             else:
                 buffer[i] = decode(pieces[k][:, span]) * factor
                 source = buffer.at[i]
-            start = pl.multiple_of((block * PLANE + (p ^ k)) * columns, 128)
+            start = pl.multiple_of((block * PLANE + (p ^ PEERS[k])) * columns, 128)
             copy = pltpu.make_async_copy(source, out.at[:, pl.ds(start, columns)], sem.at[i])
             copy.start()
             copies.append(copy)
@@ -249,11 +249,10 @@
         return lax.ppermute(x, "fsdp", [(to, source) for source, to in ring])
 
     def across(x, k):
-        return lax.ppermute(x, "fsdp", [(i, i ^ k) for i in range(size)])
+        return lax.ppermute(x, "fsdp", [(i, i ^ PEERS[k]) for i in range(size)])
 
     def across_all(parts):
-        moved = {k: across(parts[k - 1], k) for k in ORDER}
-        return [moved[k] for k in range(1, PLANE)]
+        return [across(part, k + 1) for k, part in enumerate(parts)]
 
     workers = lax.axis_size("worker")
     half = planes // 2

time: 89.5 us -> 96.9 us (1.083)
  waiting for transfers between devices: 44.8 us -> 48.9 us
  starting transfers between devices: 21.3 us -> 23.7 us
    ppermute x12, waiting for transfers between devices: 37 us -> 27.2 us  [across(): return lax.ppermute(x, 'fsdp', [(i, i ^ PEERS[k]) for i in range(size)])]
    ppermute x3, waiting for transfers between devices: 7.78 us -> 15.9 us  [around(): return lax.ppermute(x, 'fsdp', ring)]
    ppermute x2, waiting for transfers between devices: 0.01 us -> 5.87 us  [back(): return lax.ppermute(x, 'fsdp', [(to, source) for source, to in ring])]
    ppermute x12, starting transfers between devices: 12.4 us -> 15.7 us  [across(): return lax.ppermute(x, 'fsdp', [(i, i ^ PEERS[k]) for i in range(size)])]
    ppermute x3, starting transfers between devices: 5.57 us -> 3.14 us  [around(): return lax.ppermute(x, 'fsdp', ring)]
    ppermute x2, starting transfers between devices: 3.28 us -> 4.91 us  [back(): return lax.ppermute(x, 'fsdp', [(to, source) for source, to in ring])]
  transfers between devices with their start and end apart: 18 -> 18, of which waited for: 10 -> 6; matrix products, arithmetic and copies ran while one was open for 4% -> 4% of each run, Pallas kernels for 15% -> 14%
where the time goes in v10:
time: 96.9 us; the launch traced here: 96.7 us
  waiting for transfers between devices  48.9 us (50%)
  starting transfers between devices  23.7 us (24%)
  Pallas kernels  17.9 us (18%)
  other arithmetic  3.64 us (4%)
  local copies, waits for them, and re-layouts  1.52 us (2%)
    ppermute x12, waiting for transfers between devices, across(): return lax.ppermute(x, 'fsdp', [(i, i ^ PEERS[k]) for i in range(size)])  27.2 us
    ppermute x3, waiting for transfers between devices, around(): return lax.ppermute(x, 'fsdp', ring)  15.9 us
    ppermute x12, starting transfers between devices, across(): return lax.ppermute(x, 'fsdp', [(i, i ^ PEERS[k]) for i in range(size)])  15.7 us
    pallas_call x2, Pallas kernels, plane_product(): pl.pallas_call(functools.partial(product_kernel, columns, len(weights), s...  7.1 us
    ppermute x2, waiting for transfers between devices, back(): return lax.ppermute(x, 'fsdp', [(to, source) for source, to in ring])  5.87 us
    ppermute x2, starting transfers between devices, back(): return lax.ppermute(x, 'fsdp', [(to, source) for source, to in ring])  4.91 us
    pallas_call x3, Pallas kernels, plane_partial(): pl.pallas_call(functools.partial(partial_kernel, columns, scale, spread),...  4.33 us
    pallas_call x2, Pallas kernels, unpack(): pl.pallas_call(functools.partial(unpack_kernel, columns, planes, 'fsdp',...  3.88 us
  transfers between devices with their start and end apart: 18, of which 6 were waited for; matrix products, arithmetic and copies ran while one was open for 4% of the time, Pallas kernels for 14%

profile of v10, /device:TPU:0, one launch (start us, length us, event | category | flops | bytes accessed | tf_op | source)
XLA Modules:
  0.0 96.7 jit_solution(17948439915411553767)
XLA Ops:
  0.6 0.9 copy-done.2
  1.6 2.6 %pack.1 = (bf16[512,512]{1,0:T(8,128)(2,1)S(1)}, f32[512,512]{1,0:T(8,128)S(1)}, bf16[192,512]{1,0:T(8,128)(2,1)S(1)}, bf16[192,2048]{1,0:T(8,128)(2,1)S(1)}, bf...) custom-call(bf16[192,8192]{1,0:T(8,128)(2,1)} %features_far.1, ...), custom_call_target="tpu_custom_call" | custom-call | flops 68719476736 | bytes 1048576 | tf_op jit(solution)/shard_map/pack/pallas_call | solution.py:96
  4.2 3.1 %collective-permute-start = (bf16[512,512]{1,0:T(8,128)(2,1)S(1)}, bf16[512,512]{1,0:T(8,128)(2,1)S(1)}, u32[]{:S(2)}, u32[]{:S(2)}) collective-permute-start(bf16[512,512]{1,0:T(8,128)(2,1)S(1)} %get-tuple-element.43), channel_id=1, source_target_pairs={{0,4},{1,5},{2,6},{3,7},{4,8},{5,9},{6,10},{7,11},{8,12},{9,13},{1... | collective-permute-start | bytes 1572872 | tf_op jit(solution)/shard_map/ppermute | solution.py:246
  7.3 1.5 %collective-permute-start.1 = (bf16[192,1024]{1,0:T(8,128)(2,1)S(1)}, bf16[192,1024]{1,0:T(8,128)(2,1)S(1)}, u32[]{:S(2)}, u32[]{:S(2)}) collective-permute-start(bf16[192,1024]{1,0:T(8,128)(2,1)S(1)} %get-tuple-element.44), channel_id=1, source_target_pairs={{0,2},{1,3},{2,0},{3,1},{4,6},{5,7},{6,4},{7,5},{8,10},{9,11},{10,... | collective-permute-start | bytes 1179656 | tf_op jit(solution)/shard_map/ppermute | solution.py:252
  8.8 1.4 %collective-permute-start.2 = (bf16[192,1024]{1,0:T(8,128)(2,1)S(1)}, bf16[192,1024]{1,0:T(8,128)(2,1)S(1)}, u32[]{:S(2)}, u32[]{:S(2)}) collective-permute-start(bf16[192,1024]{1,0:T(8,128)(2,1)S(1)} %get-tuple-element.45), channel_id=1, source_target_pairs={{0,3},{1,2},{2,1},{3,0},{4,7},{5,6},{6,5},{7,4},{8,11},{9,10},{10,... | collective-permute-start | bytes 1179656 | tf_op jit(solution)/shard_map/ppermute | solution.py:252
  10.2 0.5 collective-permute-start.3
  10.8 15.5 %collective-permute-done.1.refs_0_.refs_3_.refs_2_.refs_4_ = bf16[192,1024]{1,0:T(8,128)(2,1)S(1)} collective-permute-done((bf16[192,1024]{1,0:T(8,128)(2,1)S(1)}, bf16[192,1024]{1,0:T(8,128)(2,1)S(1)}, u32[]{:S(2)}, u32[]{:S(2)}) %collective-permute-start.1) | collective-permute-done | bytes 393248 | tf_op jit(solution)/shard_map/ppermute | solution.py:252
  26.3 2.4 %collective-permute-start.8 = (bf16[512,512]{1,0:T(8,128)(2,1)S(1)}, bf16[512,512]{1,0:T(8,128)(2,1)S(1)}, u32[]{:S(2)}, u32[]{:S(2)}) collective-permute-start(bf16[512,512]{1,0:T(8,128)(2,1)S(1)} %get-tuple-element.43), channel_id=1, source_target_pairs={{4,0},{5,1},{6,2},{7,3},{8,4},{9,5},{10,6},{11,7},{12,8},{13,9},{1... | collective-permute-start | bytes 1572872 | tf_op jit(solution)/shard_map/ppermute | solution.py:249
  28.7 1.5 %collective-permute-start.5 = (bf16[192,1024]{1,0:T(8,128)(2,1)S(1)}, bf16[192,1024]{1,0:T(8,128)(2,1)S(1)}, u32[]{:S(2)}, u32[]{:S(2)}) collective-permute-start(bf16[192,1024]{1,0:T(8,128)(2,1)S(1)} %get-tuple-element.51), channel_id=1, source_target_pairs={{0,2},{1,3},{2,0},{3,1},{4,6},{5,7},{6,4},{7,5},{8,10},{9,11},{10,... | collective-permute-start | bytes 1179656 | tf_op jit(solution)/shard_map/ppermute | solution.py:252
  30.2 1.4 %collective-permute-start.6 = (bf16[192,1024]{1,0:T(8,128)(2,1)S(1)}, bf16[192,1024]{1,0:T(8,128)(2,1)S(1)}, u32[]{:S(2)}, u32[]{:S(2)}) collective-permute-start(bf16[192,1024]{1,0:T(8,128)(2,1)S(1)} %get-tuple-element.52), channel_id=1, source_target_pairs={{0,3},{1,2},{2,1},{3,0},{4,7},{5,6},{6,5},{7,4},{8,11},{9,10},{10,... | collective-permute-start | bytes 1179656 | tf_op jit(solution)/shard_map/ppermute | solution.py:252
  31.6 0.5 collective-permute-start.7
  32.2 0.9 plane_partial.3
  33.7 1.5 %multiply_subtract_fusion = (f32[512,512]{1,0:T(8,128)}, f32[512,512]{1,0:T(8,128)S(1)}) fusion(f32[512,512]{1,0:T(8,128)S(1)} %copy-done.5, f32[1,512,512]{2,1,0:T(8,128)S(1)} %collective-permute-done.9, f32[1,512,512]{2,1,0:T(8,128)S(1)} %copy-done.6, f32[512,512]{1,0:T(8,128)S(1)} %copy-done.7), kind=kLoop, calls=%fused_computation.6 | loop fusion | flops 2621440 | bytes 6291456 | tf_op jit(solution)/shard_map/sub | solution.py:276
  35.2 5.9 %collective-permute-done.8.refs_2_ = bf16[512,512]{1,0:T(8,128)(2,1)S(1)} collective-permute-done((bf16[512,512]{1,0:T(8,128)(2,1)S(1)}, bf16[512,512]{1,0:T(8,128)(2,1)S(1)}, u32[]{:S(2)}, u32[]{:S(2)}) %collective-permute-start.8) | collective-permute-done | bytes 524320 | tf_op jit(solution)/shard_map/ppermute | solution.py:249
  41.1 5.1 %plane_product.3 = (f32[192,1536]{1,0:T(8,128)S(1)}, bf16[192,2048]{1,0:T(8,128)(2,1)S(1)}, bf16[192,2048]{1,0:T(8,128)(2,1)S(1)}, bf16[192,2048]{1,0:T(8,128)(2,1)S(1)}) custom-call(f32[512,512]{1,0:T(8,128)S(1)} %get-tuple-element.57.refs_0_, bf16[512,512]{1,0:T(8,128)(2,1)S(1)} %collective-permute-done.refs_6_.refs_1_, ...), custom_call_target="tpu_custom_call" | custom-call | flops 8589934592 | bytes 1048576 | tf_op jit(solution)/shard_map/plane_product/pallas_call | solution.py:169
  46.2 1.6 %collective-permute-start.10 = (bf16[192,2048]{1,0:T(8,128)(2,1)S(1)}, bf16[192,2048]{1,0:T(8,128)(2,1)S(1)}, u32[]{:S(2)}, u32[]{:S(2)}) collective-permute-start(bf16[192,2048]{1,0:T(8,128)(2,1)S(1)} %get-tuple-element.61), channel_id=1, source_target_pairs={{0,2},{1,3},{2,0},{3,1},{4,6},{5,7},{6,4},{7,5},{8,10},{9,11},{10,... | collective-permute-start | bytes 2359304 | tf_op jit(solution)/shard_map/ppermute | solution.py:252
  47.8 0.9 collective-permute-done.5.refs_3_
  48.7 1.7 %collective-permute-start.12 = (bf16[192,2048]{1,0:T(8,128)(2,1)S(1)}, bf16[192,2048]{1,0:T(8,128)(2,1)S(1)}, u32[]{:S(2)}, u32[]{:S(2)}) collective-permute-start(bf16[192,2048]{1,0:T(8,128)(2,1)S(1)} %get-tuple-element.64), channel_id=1, source_target_pairs={{0,3},{1,2},{2,1},{3,0},{4,7},{5,6},{6,5},{7,4},{8,11},{9,10},{10,... | collective-permute-start | bytes 2359304 | tf_op jit(solution)/shard_map/ppermute | solution.py:252
  50.3 0.7 collective-permute-start.14
  51.1 12.2 %collective-permute-done.4.refs_6_.refs_0_ = bf16[1024,512]{1,0:T(8,128)(2,1)S(1)} collective-permute-done((bf16[1024,512]{1,0:T(8,128)(2,1)S(1)}, bf16[1024,512]{1,0:T(8,128)(2,1)S(1)}, u32[]{:S(2)}, u32[]{:S(2)}) %collective-permute-start.4) | collective-permute-done | bytes 1048608 | tf_op jit(solution)/shard_map/ppermute | solution.py:246
  63.2 2.0 %plane_partial.4 = (bf16[512,512]{1,0:T(8,128)(2,1)S(1)}, bf16[512,512]{1,0:T(8,128)(2,1)S(1)}) custom-call(bf16[192,2048]{1,0:T(8,128)(2,1)S(1)} %get-tuple-element.41.own, bf16[192,512]{1,0:T(8,128)(2,1)S(1)} %get-tuple-element.42.cot.refs_1_.refs_3_, bf16[192,1024]{1,0:T(8,128)(2,1)S(1)} %collective-permute-done.1.refs_0_.refs_3_.refs_2_.refs_4_, ...), custom_call_target="tpu_custom_call" | custom-call | flops 17179869184 | bytes 1048576 | tf_op jit(solution)/shard_map/plane_partial/pallas_call | solution.py:133
  65.2 2.5 %collective-permute-start.17 = (bf16[512,512]{1,0:T(8,128)(2,1)S(1)}, bf16[512,512]{1,0:T(8,128)(2,1)S(1)}, u32[]{:S(2)}, u32[]{:S(2)}) collective-permute-start(bf16[512,512]{1,0:T(8,128)(2,1)S(1)} %get-tuple-element.75), channel_id=1, source_target_pairs={{4,0},{5,1},{6,2},{7,3},{8,4},{9,5},{10,6},{11,7},{12,8},{13,9},{1... | collective-permute-start | bytes 1572872 | tf_op jit(solution)/shard_map/ppermute | solution.py:249
  67.7 2.0 %plane_product.2 = (f32[192,512]{1,0:T(8,128)S(1)}, bf16[192,512]{1,0:T(8,128)(2,1)S(1)}, bf16[192,512]{1,0:T(8,128)(2,1)S(1)}, bf16[192,512]{1,0:T(8,128)(2,1)S(1)}) custom-call(bf16[1024,512]{1,0:T(8,128)(2,1)S(1)} %collective-permute-done.4.refs_6_.refs_0_, bf16[192,512]{1,0:T(8,128)(2,1)S(1)} %get-tuple-element.42.cot.refs_1_.refs_3_, ...), custom_call_target="tpu_custom_call" | custom-call | flops 1048576 | bytes 1048576 | tf_op jit(solution)/shard_map/plane_product/pallas_call | solution.py:169
  69.7 10.8 %collective-permute-done.10.refs_1_.refs_3_ = bf16[192,2048]{1,0:T(8,128)(2,1)S(1)} collective-permute-done((bf16[192,2048]{1,0:T(8,128)(2,1)S(1)}, bf16[192,2048]{1,0:T(8,128)(2,1)S(1)}, u32[]{:S(2)}, u32[]{:S(2)}) %collective-permute-start.10) | collective-permute-done | bytes 786464 | tf_op jit(solution)/shard_map/ppermute | solution.py:252
  80.5 1.4 %collective-permute-start.11 = (bf16[192,512]{1,0:T(8,128)(2,1)S(1)}, bf16[192,512]{1,0:T(8,128)(2,1)S(1)}, u32[]{:S(2)}, u32[]{:S(2)}) collective-permute-start(bf16[192,512]{1,0:T(8,128)(2,1)S(1)} %get-tuple-element.62), channel_id=1, source_target_pairs={{0,2},{1,3},{2,0},{3,1},{4,6},{5,7},{6,4},{7,5},{8,10},{9,11},{10,... | collective-permute-start | bytes 589832 | tf_op jit(solution)/shard_map/ppermute | solution.py:252
  81.9 1.4 %collective-permute-start.13 = (bf16[192,512]{1,0:T(8,128)(2,1)S(1)}, bf16[192,512]{1,0:T(8,128)(2,1)S(1)}, u32[]{:S(2)}, u32[]{:S(2)}) collective-permute-start(bf16[192,512]{1,0:T(8,128)(2,1)S(1)} %get-tuple-element.65), channel_id=1, source_target_pairs={{0,3},{1,2},{2,1},{3,0},{4,7},{5,6},{6,5},{7,4},{8,11},{9,10},{10,... | collective-permute-start | bytes 589832 | tf_op jit(solution)/shard_map/ppermute | solution.py:252
  83.3 1.9 %collective-permute-start.15 = (bf16[192,512]{1,0:T(8,128)(2,1)S(1)}, bf16[192,512]{1,0:T(8,128)(2,1)S(1)}, u32[]{:S(2)}, u32[]{:S(2)}) collective-permute-start(bf16[192,512]{1,0:T(8,128)(2,1)S(1)} %get-tuple-element.68), channel_id=1, source_target_pairs={{0,1},{1,0},{2,3},{3,2},{4,5},{5,4},{6,7},{7,6},{8,9},{9,8},{10,11... | collective-permute-start | bytes 589832 | tf_op jit(solution)/shard_map/ppermute | solution.py:252
  85.2 2.4 %unpack.2.refs_4_ = f32[192,8192]{1,0:T(8,128)} custom-call(f32[192,1536]{1,0:T(8,128)S(1)} %get-tuple-element.69.refs_0_, bf16[192,2048]{1,0:T(8,128)(2,1)S(1)} %collective-permute-done.10.refs_1_.refs_3_, bf16[192,2048]{1,0:T(8,128)(2,1)S(1)} %collective-permute-done.12.refs_2_.refs_4_, bf16[192,2048]{1,0:T(8,128)(2,1)S(1)} %collective-permute-done.14.refs_3_.refs_5_), custom_call_target="tpu_custom_call" | custom-call | flops 68719476736 | bytes 1048576 | tf_op jit(solution)/shard_map/unpack/pallas_call | solution.py:210
  87.6 3.7 %collective-permute-done.16.refs_6_ = bf16[512,512]{1,0:T(8,128)(2,1)S(1)} collective-permute-done((bf16[512,512]{1,0:T(8,128)(2,1)S(1)}, bf16[512,512]{1,0:T(8,128)(2,1)S(1)}, u32[]{:S(2)}, u32[]{:S(2)}) %collective-permute-start.16) | collective-permute-done | bytes 524320 | tf_op jit(solution)/shard_map/ppermute | solution.py:246
  91.4 1.5 %plane_partial.5 = f32[512,512]{1,0:T(8,128)S(1)} custom-call(bf16[192,2048]{1,0:T(8,128)(2,1)S(1)} %get-tuple-element.41.own, bf16[192,512]{1,0:T(8,128)(2,1)S(1)} %get-tuple-element.42.cot.refs_1_.refs_3_, bf16[192,1024]{1,0:T(8,128)(2,1)S(1)} %collective-permute-done.1.refs_0_.refs_3_.refs_2_.refs_4_, ...), custom_call_target="tpu_custom_call" | custom-call | flops 1048576 | bytes 1048576 | tf_op jit(solution)/shard_map/plane_partial/pallas_call | solution.py:133
  92.9 2.1 %subtract_bitcast_fusion = (f32[1,512,512]{2,1,0:T(8,128)}, f32[512,512]{1,0:T(8,128)S(1)}, f32[1,512,512]{2,1,0:T(8,128)}) fusion(f32[512,512]{1,0:T(8,128)S(1)} %get-tuple-element.57.refs_0_, f32[512,512]{1,0:T(8,128)S(1)} %plane_partial.5, f32[1,512,512]{2,1,0:T(8,128)S(1)} %copy-done.3, f32[1,512,512]{2,1,0:T(8,128)S(1)} %copy-done.4), kind=kLoop, calls=%fused_computation.7 | loop fusion | flops 4194304 | bytes 7340032 | tf_op jit(solution)/shard_map/broadcast_in_dim | solution.py:333
  95.0 1.5 %unpack.3 = f32[192,8192]{1,0:T(8,128)} custom-call(f32[192,512]{1,0:T(8,128)S(1)} %get-tuple-element.55.refs_0_, bf16[192,512]{1,0:T(8,128)(2,1)S(1)} %collective-permute-done.11.refs_1_, bf16[192,512]{1,0:T(8,128)(2,1)S(1)} %collective-permute-done.13.refs_2_, ...), custom_call_target="tpu_custom_call", output_to_operand_aliasing={{}: (4, {})} | custom-call | flops 1073741824 | bytes 1048576 | tf_op jit(solution)/shard_map/unpack/pallas_call | solution.py:210
  (30 shorter events, 0.7 us)
Async XLA Ops:
  0.6 0.9 copy-start.2
  1.6 9.2 %copy-start.6 = (f32[1,512,512]{2,1,0:T(8,128)S(1)}, f32[1,512,512]{2,1,0:T(8,128)}, u32[]{:S(2)}) copy-start(f32[1,512,512]{2,1,0:T(8,128)} %param.13) | copy-start | bytes 3145732
  4.2 27.4 %collective-permute-start = (bf16[512,512]{1,0:T(8,128)(2,1)S(1)}, bf16[512,512]{1,0:T(8,128)(2,1)S(1)}, u32[]{:S(2)}, u32[]{:S(2)}) collective-permute-start(bf16[512,512]{1,0:T(8,128)(2,1)S(1)} %get-tuple-element.43), channel_id=1, source_target_pairs={{0,4},{1,5},{2,6},{3,7},{4,8},{5,9},{6,10},{7,11},{8,12},{9,13},{1... | collective-permute-start | bytes 1572872 | tf_op jit(solution)/shard_map/ppermute | solution.py:246
  7.3 19.0 %collective-permute-start.1 = (bf16[192,1024]{1,0:T(8,128)(2,1)S(1)}, bf16[192,1024]{1,0:T(8,128)(2,1)S(1)}, u32[]{:S(2)}, u32[]{:S(2)}) collective-permute-start(bf16[192,1024]{1,0:T(8,128)(2,1)S(1)} %get-tuple-element.44), channel_id=1, source_target_pairs={{0,2},{1,3},{2,0},{3,1},{4,6},{5,7},{6,4},{7,5},{8,10},{9,11},{10,... | collective-permute-start | bytes 1179656 | tf_op jit(solution)/shard_map/ppermute | solution.py:252
  8.8 19.9 %collective-permute-start.2 = (bf16[192,1024]{1,0:T(8,128)(2,1)S(1)}, bf16[192,1024]{1,0:T(8,128)(2,1)S(1)}, u32[]{:S(2)}, u32[]{:S(2)}) collective-permute-start(bf16[192,1024]{1,0:T(8,128)(2,1)S(1)} %get-tuple-element.45), channel_id=1, source_target_pairs={{0,3},{1,2},{2,1},{3,0},{4,7},{5,6},{6,5},{7,4},{8,11},{9,10},{10,... | collective-permute-start | bytes 1179656 | tf_op jit(solution)/shard_map/ppermute | solution.py:252
  10.2 20.0 %collective-permute-start.3 = (bf16[192,1024]{1,0:T(8,128)(2,1)S(1)}, bf16[192,1024]{1,0:T(8,128)(2,1)S(1)}, u32[]{:S(2)}, u32[]{:S(2)}) collective-permute-start(bf16[192,1024]{1,0:T(8,128)(2,1)S(1)} %get-tuple-element.46), channel_id=1, source_target_pairs={{0,1},{1,0},{2,3},{3,2},{4,5},{5,4},{6,7},{7,6},{8,9},{9,8},{10,11... | collective-permute-start | bytes 1179656 | tf_op jit(solution)/shard_map/ppermute | solution.py:252
  10.8 22.3 %collective-permute-start.9 = (f32[1,512,512]{2,1,0:T(8,128)S(1)}, f32[1,512,512]{2,1,0:T(8,128)S(1)}, u32[]{:S(2)}, u32[]{:S(2)}) collective-permute-start(f32[1,512,512]{2,1,0:T(8,128)S(1)} %copy-done.6), channel_id=1, source_target_pairs={{0,16},{16,0},{1,17},{17,1},{2,18},{18,2},{3,19},{19,3},{4,20},{20... | collective-permute-start | bytes 3145736 | tf_op jit(solution)/shard_map/ppermute | solution.py:270
  26.3 14.8 %collective-permute-start.8 = (bf16[512,512]{1,0:T(8,128)(2,1)S(1)}, bf16[512,512]{1,0:T(8,128)(2,1)S(1)}, u32[]{:S(2)}, u32[]{:S(2)}) collective-permute-start(bf16[512,512]{1,0:T(8,128)(2,1)S(1)} %get-tuple-element.43), channel_id=1, source_target_pairs={{4,0},{5,1},{6,2},{7,3},{8,4},{9,5},{10,6},{11,7},{12,8},{13,9},{1... | collective-permute-start | bytes 1572872 | tf_op jit(solution)/shard_map/ppermute | solution.py:249
  28.7 20.0 %collective-permute-start.5 = (bf16[192,1024]{1,0:T(8,128)(2,1)S(1)}, bf16[192,1024]{1,0:T(8,128)(2,1)S(1)}, u32[]{:S(2)}, u32[]{:S(2)}) collective-permute-start(bf16[192,1024]{1,0:T(8,128)(2,1)S(1)} %get-tuple-element.51), channel_id=1, source_target_pairs={{0,2},{1,3},{2,0},{3,1},{4,6},{5,7},{6,4},{7,5},{8,10},{9,11},{10,... | collective-permute-start | bytes 1179656 | tf_op jit(solution)/shard_map/ppermute | solution.py:252
  30.2 20.2 %collective-permute-start.6 = (bf16[192,1024]{1,0:T(8,128)(2,1)S(1)}, bf16[192,1024]{1,0:T(8,128)(2,1)S(1)}, u32[]{:S(2)}, u32[]{:S(2)}) collective-permute-start(bf16[192,1024]{1,0:T(8,128)(2,1)S(1)} %get-tuple-element.52), channel_id=1, source_target_pairs={{0,3},{1,2},{2,1},{3,0},{4,7},{5,6},{6,5},{7,4},{8,11},{9,10},{10,... | collective-permute-start | bytes 1179656 | tf_op jit(solution)/shard_map/ppermute | solution.py:252
  31.6 19.5 %collective-permute-start.7 = (bf16[192,1024]{1,0:T(8,128)(2,1)S(1)}, bf16[192,1024]{1,0:T(8,128)(2,1)S(1)}, u32[]{:S(2)}, u32[]{:S(2)}) collective-permute-start(bf16[192,1024]{1,0:T(8,128)(2,1)S(1)} %get-tuple-element.53), channel_id=1, source_target_pairs={{0,1},{1,0},{2,3},{3,2},{4,5},{5,4},{6,7},{7,6},{8,9},{9,8},{10,11... | collective-permute-start | bytes 1179656 | tf_op jit(solution)/shard_map/ppermute | solution.py:252
  32.1 1.2 %copy-start.5 = (f32[512,512]{1,0:T(8,128)S(1)}, f32[512,512]{1,0:T(8,128)}, u32[]{:S(2)}) copy-start(f32[512,512]{1,0:T(8,128)} %param.14) | copy-start | bytes 3145732
  32.2 1.5 %copy-start.7 = (f32[512,512]{1,0:T(8,128)S(1)}, f32[512,512]{1,0:T(8,128)}, u32[]{:S(2)}) copy-start(f32[512,512]{1,0:T(8,128)} %param.15) | copy-start | bytes 3145732
  33.1 30.2 %collective-permute-start.4 = (bf16[1024,512]{1,0:T(8,128)(2,1)S(1)}, bf16[1024,512]{1,0:T(8,128)(2,1)S(1)}, u32[]{:S(2)}, u32[]{:S(2)}) collective-permute-start(bf16[1024,512]{1,0:T(8,128)(2,1)S(1)} %plane_partial.3), channel_id=1, source_target_pairs={{0,4},{1,5},{2,6},{3,7},{4,8},{5,9},{6,10},{7,11},{8,12},{9,13},{1... | collective-permute-start | bytes 3145736 | tf_op jit(solution)/shard_map/ppermute | solution.py:246
  35.2 11.0 %copy-start.1 = (f32[512,512]{1,0:T(8,128)}, f32[512,512]{1,0:T(8,128)S(1)}, u32[]{:S(2)}) copy-start(f32[512,512]{1,0:T(8,128)S(1)} %get-tuple-element.77.refs_10_) | copy-start | bytes 3145732
  46.2 34.3 %collective-permute-start.10 = (bf16[192,2048]{1,0:T(8,128)(2,1)S(1)}, bf16[192,2048]{1,0:T(8,128)(2,1)S(1)}, u32[]{:S(2)}, u32[]{:S(2)}) collective-permute-start(bf16[192,2048]{1,0:T(8,128)(2,1)S(1)} %get-tuple-element.61), channel_id=1, source_target_pairs={{0,2},{1,3},{2,0},{3,1},{4,6},{5,7},{6,4},{7,5},{8,10},{9,11},{10,... | collective-permute-start | bytes 2359304 | tf_op jit(solution)/shard_map/ppermute | solution.py:252
  48.7 33.2 %collective-permute-start.12 = (bf16[192,2048]{1,0:T(8,128)(2,1)S(1)}, bf16[192,2048]{1,0:T(8,128)(2,1)S(1)}, u32[]{:S(2)}, u32[]{:S(2)}) collective-permute-start(bf16[192,2048]{1,0:T(8,128)(2,1)S(1)} %get-tuple-element.64), channel_id=1, source_target_pairs={{0,3},{1,2},{2,1},{3,0},{4,7},{5,6},{6,5},{7,4},{8,11},{9,10},{10,... | collective-permute-start | bytes 2359304 | tf_op jit(solution)/shard_map/ppermute | solution.py:252
  50.3 32.9 %collective-permute-start.14 = (bf16[192,2048]{1,0:T(8,128)(2,1)S(1)}, bf16[192,2048]{1,0:T(8,128)(2,1)S(1)}, u32[]{:S(2)}, u32[]{:S(2)}) collective-permute-start(bf16[192,2048]{1,0:T(8,128)(2,1)S(1)} %get-tuple-element.67), channel_id=1, source_target_pairs={{0,1},{1,0},{2,3},{3,2},{4,5},{5,4},{6,7},{7,6},{8,9},{9,8},{10,11... | collective-permute-start | bytes 2359304 | tf_op jit(solution)/shard_map/ppermute | solution.py:252
  65.2 26.1 %collective-permute-start.17 = (bf16[512,512]{1,0:T(8,128)(2,1)S(1)}, bf16[512,512]{1,0:T(8,128)(2,1)S(1)}, u32[]{:S(2)}, u32[]{:S(2)}) collective-permute-start(bf16[512,512]{1,0:T(8,128)(2,1)S(1)} %get-tuple-element.75), channel_id=1, source_target_pairs={{4,0},{5,1},{6,2},{7,3},{8,4},{9,5},{10,6},{11,7},{12,8},{13,9},{1... | collective-permute-start | bytes 1572872 | tf_op jit(solution)/shard_map/ppermute | solution.py:249
  67.7 23.6 %collective-permute-start.16 = (bf16[512,512]{1,0:T(8,128)(2,1)S(1)}, bf16[512,512]{1,0:T(8,128)(2,1)S(1)}, u32[]{:S(2)}, u32[]{:S(2)}) collective-permute-start(bf16[512,512]{1,0:T(8,128)(2,1)S(1)} %get-tuple-element.54.refs_5_), channel_id=1, source_target_pairs={{0,4},{1,5},{2,6},{3,7},{4,8},{5,9},{6,10},{7,11},{8,12},{9,13},{1... | collective-permute-start | bytes 1572872 | tf_op jit(solution)/shard_map/ppermute | solution.py:246
  80.5 14.5 %collective-permute-start.11 = (bf16[192,512]{1,0:T(8,128)(2,1)S(1)}, bf16[192,512]{1,0:T(8,128)(2,1)S(1)}, u32[]{:S(2)}, u32[]{:S(2)}) collective-permute-start(bf16[192,512]{1,0:T(8,128)(2,1)S(1)} %get-tuple-element.62), channel_id=1, source_target_pairs={{0,2},{1,3},{2,0},{3,1},{4,6},{5,7},{6,4},{7,5},{8,10},{9,11},{10,... | collective-permute-start | bytes 589832 | tf_op jit(solution)/shard_map/ppermute | solution.py:252
  81.9 13.1 %collective-permute-start.13 = (bf16[192,512]{1,0:T(8,128)(2,1)S(1)}, bf16[192,512]{1,0:T(8,128)(2,1)S(1)}, u32[]{:S(2)}, u32[]{:S(2)}) collective-permute-start(bf16[192,512]{1,0:T(8,128)(2,1)S(1)} %get-tuple-element.65), channel_id=1, source_target_pairs={{0,3},{1,2},{2,1},{3,0},{4,7},{5,6},{6,5},{7,4},{8,11},{9,10},{10,... | collective-permute-start | bytes 589832 | tf_op jit(solution)/shard_map/ppermute | solution.py:252
  83.3 11.7 %collective-permute-start.15 = (bf16[192,512]{1,0:T(8,128)(2,1)S(1)}, bf16[192,512]{1,0:T(8,128)(2,1)S(1)}, u32[]{:S(2)}, u32[]{:S(2)}) collective-permute-start(bf16[192,512]{1,0:T(8,128)(2,1)S(1)} %get-tuple-element.68), channel_id=1, source_target_pairs={{0,1},{1,0},{2,3},{3,2},{4,5},{5,4},{6,7},{7,6},{8,9},{9,8},{10,11... | collective-permute-start | bytes 589832 | tf_op jit(solution)/shard_map/ppermute | solution.py:252
  87.6 5.2 %copy-start.3 = (f32[1,512,512]{2,1,0:T(8,128)S(1)}, f32[1,512,512]{2,1,0:T(8,128)}, u32[]{:S(2)}) copy-start(f32[1,512,512]{2,1,0:T(8,128)} %param.12) | copy-start | bytes 3145732
  87.6 5.2 %copy-start.4 = (f32[1,512,512]{2,1,0:T(8,128)S(1)}, f32[1,512,512]{2,1,0:T(8,128)}, u32[]{:S(2)}) copy-start(f32[1,512,512]{2,1,0:T(8,128)} %param.11) | copy-start | bytes 3145732
  95.0 1.5 %copy-start = (f32[512,512]{1,0:T(8,128)}, f32[512,512]{1,0:T(8,128)S(1)}, u32[]{:S(2)}) copy-start(f32[512,512]{1,0:T(8,128)S(1)} %get-tuple-element.79.refs_5_) | copy-start | bytes 3145732
